TPU v7x, 32 devices: a whole 2x2x4 slice. The times are simulated.
32 devices in a mesh: dp: 4 (over y, x), expert: 8 (over z, core).
Axes of the slice: x: 2, y: 2, z: 4, core: 2. Of those that a mesh axis runs over, the one named last changes fastest.
Arguments:
- tokens: bfloat16 [1024, 4096], P('expert', 'dp'), may hold values from -6 to 6
- expert_ids: int32 [1024, 2], P('expert'), may hold values from 0 to 7, all different within a row; in each aligned block of 128 rows (0 to 127, 128 to 255, ...) at most 40 rows name the same one
- route_weights: float32 [1024, 2], P('expert'), may hold values from 0.1 to 1
- w_gate: bfloat16 [14336, 4096], P('expert', 'dp'), may hold values from -0.09375 to 0.09375
- w_up: bfloat16 [14336, 4096], P('expert', 'dp'), may hold values from -0.09375 to 0.09375
- w_down: bfloat16 [14336, 4096], P('expert', 'dp'), may hold values from -0.125 to 0.125
- out_grad: bfloat16 [1024, 4096], P('expert', 'dp'), may hold values from -0.59765625 to 0.59765625
Outputs:
- output: bfloat16 [1024, 4096], P('expert', 'dp')
- grad_gate: bfloat16 [14336, 4096], P('expert', 'dp')
- grad_up: bfloat16 [14336, 4096], P('expert', 'dp')
- grad_down: bfloat16 [14336, 4096], P('expert', 'dp')
Inputs may be any that keep to these rules, and one draw needn't show every extreme that they name: `expert_ids`: each token names two different experts. Among the 128 tokens of one index of expert (aligned blocks of 128 rows), no expert is named more than 40 times, a bound that some block reaches.
All inputs are finite; a program needn't handle non-finite values.
Results may differ from a plain program's by a relative error of at most 0.029.
Values may be sent and summed in bfloat16 or wider, within the bound.
No kernel may reach another device: no remote copies, remote signals or barrier semaphores. Data moves between devices by JAX's collectives and lax.ppermute only.
A program may use at most 128 MiB of HBM per device.

v0:
```python
import jax
import jax.numpy as jnp
from jax import lax
from jax.sharding import PartitionSpec as P


def as_sent(array):

    def short(part):
        return part.astype(jnp.bfloat16) if part.dtype == jnp.float32 else part

    return jax.tree.map(short, array)


def from_partner(block, axis, bit):
    count = lax.axis_size(axis)
    route = []
    for low in range(count):
        high = low | 1 << bit
        if high != low and high < count:
            route += [(low, high), (high, low)]
    return lax.ppermute(block, axis, route)


def silu_parts(gate_sum):
    gate_sigmoid = jax.nn.sigmoid(gate_sum)
    return (gate_sum * gate_sigmoid, gate_sigmoid * (1.0 + gate_sum * (1.0 - gate_sigmoid)))


def relay_join(own_part, their_part, is_upper, join_axis):
    lower_first = jnp.concatenate([own_part, their_part], axis=join_axis)
    upper_first = jnp.concatenate([their_part, own_part], axis=join_axis)
    return jnp.where(is_upper, upper_first, lower_first)


def add_round(own_part, their_part):
    return (own_part.astype(jnp.float32) + their_part.astype(jnp.float32)).astype(jnp.bfloat16)


def forward_sums(in_rows, gate_w, up_w):
    contract_feats = (((1,), (1,)), ((), ()))
    part_gate = lax.dot_general(in_rows, gate_w, contract_feats, preferred_element_type=jnp.float32)
    part_up = lax.dot_general(in_rows, up_w, contract_feats, preferred_element_type=jnp.float32)
    gate_sum, up_sum = (
        lax.psum(part_gate.astype(jnp.bfloat16), "dp").astype(jnp.float32),
        lax.psum(part_up.astype(jnp.bfloat16), "dp").astype(jnp.float32),
    )
    active, slope_term = silu_parts(gate_sum)
    hidden = (active * up_sum).astype(jnp.bfloat16)
    return (up_sum, active, slope_term, hidden)


def backward_rows(cot_rows, down_w, up_sum, active, slope_term):
    contract_feats = (((1,), (1,)), ((), ()))
    part_hidden = lax.dot_general(
        cot_rows, down_w, contract_feats, preferred_element_type=jnp.float32
    )
    grad_hidden = lax.psum(part_hidden.astype(jnp.bfloat16), "dp").astype(jnp.float32)
    grad_gate_rows = (grad_hidden * up_sum * slope_term).astype(jnp.bfloat16)
    grad_up_rows = (grad_hidden * active).astype(jnp.bfloat16)
    return (grad_gate_rows, grad_up_rows)


def per_device(tokens, expert_ids, route_weights, w_gate, w_up, w_down, out_grad):
    experts = lax.axis_size("expert")
    copies = experts // 8
    levels = copies.bit_length() - 1
    owner_index = lax.axis_index("expert")
    copy_index = owner_index % copies
    tok_rows = tokens.shape[0]
    feat_cols = tokens.shape[1]
    shard_width = w_gate.shape[0]
    pair_count = 2 * tok_rows
    capacity = max(2, 5 * tok_rows // (2 * experts))
    buckets = experts * capacity
    flat_ids = expert_ids.reshape(pair_count)
    choose = (flat_ids[:, None] == jnp.arange(experts, dtype=jnp.int32)[None, :]).astype(jnp.int32)
    before = jnp.cumsum(choose, axis=0) - choose
    slot_index = jnp.sum(before * choose, axis=1)
    target = flat_ids * capacity + slot_index
    placer = (jnp.arange(buckets, dtype=jnp.int32)[:, None] == target[None, :]).astype(jnp.bfloat16)
    token_placer = jnp.sum(placer.reshape(buckets, tok_rows, 2), axis=2)
    send_rows = jnp.dot(token_placer, tokens, preferred_element_type=jnp.float32).astype(
        jnp.bfloat16
    )
    arrived = lax.all_to_all(
        send_rows.reshape(experts, capacity, feat_cols),
        "expert",
        split_axis=0,
        concat_axis=0,
        tiled=True,
    )
    in_rows = arrived.reshape(buckets, feat_cols)
    pieces = (w_gate, w_up, w_down)
    for bit_index in range(levels):
        partner = from_partner(
            (as_sent(pieces[0]), as_sent(pieces[1]), as_sent(pieces[2])), "expert", bit_index
        )
        is_upper = owner_index // 2**bit_index % 2 == 1
        pieces = (
            relay_join(pieces[0], partner[0], is_upper, 0),
            relay_join(pieces[1], partner[1], is_upper, 0),
            relay_join(pieces[2], partner[2], is_upper, 0),
        )
    gate_w, up_w, down_w = pieces
    up_sum, active, slope_term, hidden = forward_sums(in_rows, gate_w, up_w)
    out_rows = jnp.dot(hidden, down_w, preferred_element_type=jnp.float32).astype(jnp.bfloat16)
    returned = lax.all_to_all(
        out_rows.reshape(experts, capacity, feat_cols),
        "expert",
        split_axis=0,
        concat_axis=0,
        tiled=True,
    )
    picked = jnp.dot(
        placer.T, returned.reshape(buckets, feat_cols), preferred_element_type=jnp.float32
    )
    combined = jnp.sum(route_weights[:, :, None] * picked.reshape(tok_rows, 2, feat_cols), axis=1)
    output = combined.astype(jnp.bfloat16)
    cot_pairs = (route_weights[:, :, None] * out_grad[:, None, :].astype(jnp.float32)).astype(
        jnp.bfloat16
    )
    cot_send = jnp.dot(
        placer, cot_pairs.reshape(pair_count, feat_cols), preferred_element_type=jnp.float32
    ).astype(jnp.bfloat16)
    cot_arrived = lax.all_to_all(
        cot_send.reshape(experts, capacity, feat_cols),
        "expert",
        split_axis=0,
        concat_axis=0,
        tiled=True,
    )
    cot_rows = cot_arrived.reshape(buckets, feat_cols)
    contract_rows = (((0,), (0,)), ((), ()))
    grad_gate_rows, grad_up_rows = backward_rows(cot_rows, down_w, up_sum, active, slope_term)
    gate_term = lax.dot_general(
        grad_gate_rows, in_rows, contract_rows, preferred_element_type=jnp.float32
    ).astype(jnp.bfloat16)
    up_term = lax.dot_general(
        grad_up_rows, in_rows, contract_rows, preferred_element_type=jnp.float32
    ).astype(jnp.bfloat16)
    down_term = lax.dot_general(
        hidden, cot_rows, contract_rows, preferred_element_type=jnp.float32
    ).astype(jnp.bfloat16)
    grad_terms = (gate_term, up_term, down_term)
    for bit_index in range(levels):
        partner = from_partner((grad_terms[0], grad_terms[1], grad_terms[2]), "expert", bit_index)
        grad_terms = (
            add_round(grad_terms[0], partner[0]),
            add_round(grad_terms[1], partner[1]),
            add_round(grad_terms[2], partner[2]),
        )
    start_row = copy_index * shard_width
    grad_gate = lax.dynamic_slice_in_dim(grad_terms[0], start_row, shard_width, 0)
    grad_up = lax.dynamic_slice_in_dim(grad_terms[1], start_row, shard_width, 0)
    grad_down = lax.dynamic_slice_in_dim(grad_terms[2], start_row, shard_width, 0)
    return (output, grad_gate, grad_up, grad_down)


def solution(mesh):
    placed = (
        P("expert", "dp"),
        P("expert", None),
        P("expert", None),
        P("expert", "dp"),
        P("expert", "dp"),
        P("expert", "dp"),
        P("expert", "dp"),
    )
    return jax.shard_map(
        per_device,
        mesh=mesh,
        in_specs=placed,
        out_specs=(P("expert", "dp"), P("expert", "dp"), P("expert", "dp"), P("expert", "dp")),
        check_vma=False,
    )
```

profile of v0, /device:TPU:0, one launch (start us, length us, event | category | flops | bytes accessed | tf_op | source)
XLA Modules:
  0.0 193.9 jit_solution(6475174479888714914)
XLA Ops:
  7.2 0.8 copy.25
  8.3 0.6 reduce-window.6
  8.9 0.2 slice_reduce_fusion
  9.3 0.1 reduce_sum.33
  9.5 0.7 multiply_add_fusion
  10.2 1.2 convolution_convert_fusion.6
  11.4 6.3 %all-to-all-start = ((bf16[8,40,1024]{2,1,0:T(8,128)(2,1)}), bf16[8,40,1024]{2,1,0:T(8,128)(2,1)S(1)}, u32[]{:S(2)}, u32[]{:S(2)}) async-start(bf16[8,40,1024]{2,1,0:T(8,128)(2,1)} %bitcast.2), calls=%async_computation | async-start | bytes 1310720 | tf_op jit(solution)/shard_map/all_to_all | solution.py:86
  18.0 0.3 mul.77
  18.3 0.7 mul.78
  19.0 1.3 convolution_convert_fusion.7
  20.3 15.6 %all-to-all-done = bf16[8,40,1024]{2,1,0:T(8,128)(2,1)S(1)} async-done(((bf16[8,40,1024]{2,1,0:T(8,128)(2,1)}), bf16[8,40,1024]{2,1,0:T(8,128)(2,1)S(1)}, u32[]{:S(2)}, u32[]{:S(2)}) %all-to-all-start) | async-done | bytes 655392 | tf_op jit(solution)/shard_map/all_to_all | solution.py:86
  35.9 3.5 %all-to-all-start.2 = ((bf16[8,40,1024]{2,1,0:T(8,128)(2,1)}), bf16[8,40,1024]{2,1,0:T(8,128)(2,1)S(1)}, u32[]{:S(2)}, u32[]{:S(2)}) async-start(bf16[8,40,1024]{2,1,0:T(8,128)(2,1)} %bitcast.7), calls=%async_computation.2 | async-start | bytes 1310720 | tf_op jit(solution)/shard_map/all_to_all | solution.py:126
  39.5 4.6 %convolution_convert_fusion.4 = bf16[320,1792]{1,0:T(8,128)(2,1)} fusion(bf16[320,1024]{1,0:T(8,128)(2,1)S(1)} %bitcast.29, bf16[1792,1024]{1,0:T(8,128)(2,1)} %param.11), kind=kOutput, calls=%fused_computation.10 | convolution fusion | flops 1174978560 | bytes 5472256 | tf_op jit(solution)/shard_map/dot_general | solution.py:43
  44.1 2.4 %convolution_convert_fusion.5 = bf16[320,1792]{1,0:T(8,128)(2,1)} fusion(bf16[320,1024]{1,0:T(8,128)(2,1)S(1)} %bitcast.30, bf16[1792,1024]{1,0:T(8,128)(2,1)S(1)} %copy-done.3), kind=kOutput, calls=%fused_computation.11 | convolution fusion | flops 1174978560 | bytes 5472256 | tf_op jit(solution)/shard_map/dot_general | solution.py:42
  46.5 11.0 %all-to-all-done.2 = bf16[8,40,1024]{2,1,0:T(8,128)(2,1)S(1)} async-done(((bf16[8,40,1024]{2,1,0:T(8,128)(2,1)}), bf16[8,40,1024]{2,1,0:T(8,128)(2,1)S(1)}, u32[]{:S(2)}, u32[]{:S(2)}) %all-to-all-start.2) | async-done | bytes 655392 | tf_op jit(solution)/shard_map/all_to_all | solution.py:126
  57.5 4.4 %convolution_convert_fusion.3 = bf16[320,1792]{1,0:T(8,128)(2,1)} fusion(bf16[320,1024]{1,0:T(8,128)(2,1)S(1)} %bitcast.33, bf16[1792,1024]{1,0:T(8,128)(2,1)} %param.12), kind=kOutput, calls=%fused_computation.9 | convolution fusion | flops 1174978560 | bytes 5472256 | tf_op jit(solution)/shard_map/dot_general | solution.py:55
  62.3 91.4 %all-reduce.3.cloned.1.call-done = (bf16[320,1792]{1,0:T(8,128)(2,1)}, bf16[320,1792]{1,0:T(8,128)(2,1)}, bf16[320,1792]{1,0:T(8,128)(2,1)}) async-done(((bf16[320,1792]{1,0:T(8,128)(2,1)}, bf16[320,1792]{1,0:T(8,128)(2,1)}, bf16[320,1792]{1,0:T(8,128)(2,1)}), (bf16[320,1792]{1,0:T(8,128)(2,1)}, bf16[320,1792]{1,0:T(8,128)(2,1)}, bf16[320,1792]{1,0:T(8,128)(2,1)})) %all-reduce.3.cloned.1.call-update) | async-done | bytes 3440656 | tf_op jit(solution)/shard_map/psum | solution.py:46
  153.7 5.3 %convolution_convert_fusion.8 = bf16[320,1024]{1,0:T(8,128)(2,1)} fusion(bf16[1792,1024]{1,0:T(8,128)(2,1)} %param.12, bf16[320,1792]{1,0:T(8,128)(2,1)} %get-tuple-element.4, bf16[320,1792]{1,0:T(8,128)(2,1)} %get-tuple-element.5), kind=kOutput, calls=%fused_computation.24 | convolution fusion | flops 1179320320 | bytes 6619136 | tf_op jit(solution)/shard_map/dot_general | solution.py:107
  159.0 4.1 %convolution_convert_fusion = bf16[1792,1024]{1,0:T(8,128)(2,1)} fusion(bf16[320,1024]{1,0:T(8,128)(2,1)S(1)} %bitcast.34, bf16[320,1792]{1,0:T(8,128)(2,1)S(1)} %copy-done.4, bf16[320,1792]{1,0:T(8,128)(2,1)S(1)} %copy-done.5), kind=kOutput, calls=%fused_computation | convolution fusion | flops 1180827648 | bytes 6619136 | tf_op jit(solution)/shard_map/dot_general | solution.py:142
  163.1 4.6 %all-to-all-start.1 = ((bf16[8,40,1024]{2,1,0:T(8,128)(2,1)}), bf16[8,40,1024]{2,1,0:T(8,128)(2,1)S(1)}, u32[]{:S(2)}, u32[]{:S(2)}) async-start(bf16[8,40,1024]{2,1,0:T(8,128)(2,1)} %bitcast.4), calls=%async_computation.1 | async-start | bytes 1310720 | tf_op jit(solution)/shard_map/all_to_all | solution.py:108
  167.7 5.9 %convolution_convert_fusion.1 = bf16[1792,1024]{1,0:T(8,128)(2,1)} fusion(bf16[320,1024]{1,0:T(8,128)(2,1)S(1)} %bitcast.31, bf16[320,1792]{1,0:T(8,128)(2,1)} %get-tuple-element.6, bf16[320,1792]{1,0:T(8,128)(2,1)} %get-tuple-element.5), kind=kOutput, calls=%fused_computation.1 | convolution fusion | flops 1180827648 | bytes 6619136 | tf_op jit(solution)/shard_map/dot_general | solution.py:139
  173.6 4.6 %convolution_convert_fusion.2 = bf16[1792,1024]{1,0:T(8,128)(2,1)} fusion(bf16[320,1024]{1,0:T(8,128)(2,1)S(1)} %bitcast.32, bf16[320,1792]{1,0:T(8,128)(2,1)S(1)} %copy-done.4, bf16[320,1792]{1,0:T(8,128)(2,1)S(1)} %copy-done.7, bf16[320,1792]{1,0:T(8,128)(2,1)S(1)} %copy-done.6), kind=kOutput, calls=%fused_computation.2 | convolution fusion | flops 1183694848 | bytes 7766016 | tf_op jit(solution)/shard_map/dot_general | solution.py:136
  178.2 7.7 %all-to-all-done.1 = bf16[8,40,1024]{2,1,0:T(8,128)(2,1)S(1)} async-done(((bf16[8,40,1024]{2,1,0:T(8,128)(2,1)}), bf16[8,40,1024]{2,1,0:T(8,128)(2,1)S(1)}, u32[]{:S(2)}, u32[]{:S(2)}) %all-to-all-start.1) | async-done | bytes 655392 | tf_op jit(solution)/shard_map/all_to_all | solution.py:108
  185.9 1.2 fusion.9
  (31 shorter events, 1.1 us)
Async XLA Ops:
  7.2 3.1 %copy-start = (bf16[128,1024]{1,0:T(8,128)(2,1)S(1)}, bf16[128,1024]{1,0:T(8,128)(2,1)}, u32[]{:S(2)}) copy-start(bf16[128,1024]{1,0:T(8,128)(2,1)} %param.7) | copy-start | bytes 786436
  7.2 10.6 %copy-start.2 = (f32[128,2]{0,1:T(2,128)S(1)}, f32[128,2]{0,1:T(2,128)}, u32[]{:S(2)}) copy-start(f32[128,2]{0,1:T(2,128)} %param.9) | copy-start | bytes 3076
  7.2 10.8 %copy-start.1 = (bf16[128,1024]{1,0:T(8,128)(2,1)S(1)}, bf16[128,1024]{1,0:T(8,128)(2,1)}, u32[]{:S(2)}) copy-start(bf16[128,1024]{1,0:T(8,128)(2,1)} %param.13) | copy-start | bytes 786436
  11.4 24.5 %all-to-all-start = ((bf16[8,40,1024]{2,1,0:T(8,128)(2,1)}), bf16[8,40,1024]{2,1,0:T(8,128)(2,1)S(1)}, u32[]{:S(2)}, u32[]{:S(2)}) async-start(bf16[8,40,1024]{2,1,0:T(8,128)(2,1)} %bitcast.2), calls=%async_computation | async-start | bytes 1310720 | tf_op jit(solution)/shard_map/all_to_all | solution.py:86
  35.9 21.6 %all-to-all-start.2 = ((bf16[8,40,1024]{2,1,0:T(8,128)(2,1)}), bf16[8,40,1024]{2,1,0:T(8,128)(2,1)S(1)}, u32[]{:S(2)}, u32[]{:S(2)}) async-start(bf16[8,40,1024]{2,1,0:T(8,128)(2,1)} %bitcast.7), calls=%async_computation.2 | async-start | bytes 1310720 | tf_op jit(solution)/shard_map/all_to_all | solution.py:126
  39.4 114.2 %all-reduce.3.cloned.1.call-start = ((), (), s32[]{:S(2)}) async-start(), calls=%async_computation.3 | async-start | bytes 6881280 | tf_op jit(solution)/shard_map/psum | solution.py:46
  39.5 4.6 %copy-start.3 = (bf16[1792,1024]{1,0:T(8,128)(2,1)S(1)}, bf16[1792,1024]{1,0:T(8,128)(2,1)}, u32[]{:S(2)}) copy-start(bf16[1792,1024]{1,0:T(8,128)(2,1)} %param.10) | copy-start | bytes 11010052
  153.7 5.3 %copy-start.4 = (bf16[320,1792]{1,0:T(8,128)(2,1)S(1)}, bf16[320,1792]{1,0:T(8,128)(2,1)}, u32[]{:S(2)}) copy-start(bf16[320,1792]{1,0:T(8,128)(2,1)} %get-tuple-element.4) | copy-start | bytes 3440644
  153.7 5.3 %copy-start.5 = (bf16[320,1792]{1,0:T(8,128)(2,1)S(1)}, bf16[320,1792]{1,0:T(8,128)(2,1)}, u32[]{:S(2)}) copy-start(bf16[320,1792]{1,0:T(8,128)(2,1)} %get-tuple-element.5) | copy-start | bytes 3440644
  163.1 22.8 %all-to-all-start.1 = ((bf16[8,40,1024]{2,1,0:T(8,128)(2,1)}), bf16[8,40,1024]{2,1,0:T(8,128)(2,1)S(1)}, u32[]{:S(2)}, u32[]{:S(2)}) async-start(bf16[8,40,1024]{2,1,0:T(8,128)(2,1)} %bitcast.4), calls=%async_computation.1 | async-start | bytes 1310720 | tf_op jit(solution)/shard_map/all_to_all | solution.py:108
  167.7 5.9 %copy-start.6 = (bf16[320,1792]{1,0:T(8,128)(2,1)S(1)}, bf16[320,1792]{1,0:T(8,128)(2,1)}, u32[]{:S(2)}) copy-start(bf16[320,1792]{1,0:T(8,128)(2,1)} %get-tuple-element.5) | copy-start | bytes 3440644
  167.7 5.9 %copy-start.7 = (bf16[320,1792]{1,0:T(8,128)(2,1)S(1)}, bf16[320,1792]{1,0:T(8,128)(2,1)}, u32[]{:S(2)}) copy-start(bf16[320,1792]{1,0:T(8,128)(2,1)} %get-tuple-element.6) | copy-start | bytes 3440644
Sparse Core Ops, SparseCore 0:
  62.1 91.5 all-reduce.2
where the time goes:
time: 194 us
  waiting for transfers between devices  126 us (65%)
  matrix products  34.9 us (18%)
  starting transfers between devices  14.5 us (7%)
  between operations  14.2 us (7%)
  local copies, waits for them, and re-layouts  2.95 us (2%)
    psum x1, waiting for transfers between devices, forward_sums(): lax.psum(part_up.astype(jnp.bfloat16), 'dp').astype(jnp.float32)  91.4 us
    all_to_all x1, waiting for transfers between devices, per_device(): lax.all_to_all(send_rows.reshape(experts, capacity, feat_cols), 'expert',...  15.6 us
    all_to_all x1, waiting for transfers between devices, per_device(): lax.all_to_all(cot_send.reshape(experts, capacity, feat_cols), 'expert',...  11 us
    all_to_all x1, waiting for transfers between devices, per_device(): lax.all_to_all(out_rows.reshape(experts, capacity, feat_cols), 'expert',...  7.7 us
    all_to_all x1, starting transfers between devices, per_device(): lax.all_to_all(send_rows.reshape(experts, capacity, feat_cols), 'expert',...  6.32 us
    dot_general x1, matrix products, per_device(): lax.dot_general(grad_up_rows, in_rows, contract_rows, preferred_element_t...  5.86 us
    dot_general x1, matrix products, per_device(): jnp.dot(hidden, down_w, preferred_element_type=jnp.float32)  5.28 us
    all_to_all x1, starting transfers between devices, per_device(): lax.all_to_all(out_rows.reshape(experts, capacity, feat_cols), 'expert',...  4.61 us
  transfers between devices with their start and end apart: 4, of which 4 were waited for; matrix products, arithmetic and copies ran while one was open for 10% of the time, Pallas kernels for 0%

commit v1 on v0

v1 whole, which is shorter than its diff:
```python
import jax
import jax.numpy as jnp
from jax import lax
from jax.sharding import PartitionSpec as P

BF = jnp.bfloat16
F32 = jnp.float32


def as_sent(array):

    def short(part):
        return part.astype(BF) if part.dtype == F32 else part

    return jax.tree.map(short, array)


def from_partner(block, axis, bit):
    count = lax.axis_size(axis)
    route = []
    for low in range(count):
        high = low | 1 << bit
        if high != low and high < count:
            route += [(low, high), (high, low)]
    return lax.ppermute(block, axis, route)


def swap(block, axis, mask):
    count = lax.axis_size(axis)
    return lax.ppermute(block, axis, [(i, i ^ mask) for i in range(count)])


def after(value, *earlier):
    return lax.optimization_barrier((value, earlier))[0]


def silu_parts(gate_sum):
    gate_sigmoid = jax.nn.sigmoid(gate_sum)
    return (gate_sum * gate_sigmoid, gate_sigmoid * (1.0 + gate_sum * (1.0 - gate_sigmoid)))


def relay_join(own_part, their_part, is_upper, join_axis):
    lower_first = jnp.concatenate([own_part, their_part], axis=join_axis)
    upper_first = jnp.concatenate([their_part, own_part], axis=join_axis)
    return jnp.where(is_upper, upper_first, lower_first)


def add_round(own_part, their_part):
    return (own_part.astype(F32) + their_part.astype(F32)).astype(BF)


def reorder(rows, key, parts):
    blocks = rows.reshape(parts, rows.shape[0] // parts, rows.shape[1])
    return jnp.concatenate(
        [lax.dynamic_index_in_dim(blocks, key ^ i, 0, keepdims=False) for i in range(parts)], axis=0
    )


def all_to_all(rows, experts):
    moved = lax.all_to_all(
        rows.reshape(experts, rows.shape[0] // experts, rows.shape[1]),
        "expert",
        split_axis=0,
        concat_axis=0,
        tiled=True,
    )
    return moved.reshape(rows.shape)


def pair_core(rows):
    n = rows.shape[0] // 2
    return rows[:n], swap(rows[n:], "expert", 1)


def to_chips(own, other):
    n = own.shape[0] // 4
    blocks = [
        jnp.concatenate([own[m * n:(m + 1) * n], other[m * n:(m + 1) * n]], axis=0) for m in range(4)
    ]
    return jnp.concatenate(
        [blocks[0]] + [swap(blocks[m], "expert", 2 * m) for m in range(1, 4)], axis=0
    )


def from_chips(rows, *earlier):
    n = rows.shape[0] // 8
    blocks = [rows[2 * m * n:2 * (m + 1) * n] for m in range(4)]
    back = after([blocks[0]] + [swap(blocks[m], "expert", 2 * m) for m in range(1, 4)], *earlier)
    other = swap(jnp.concatenate([each[n:] for each in back], axis=0), "expert", 1)
    return jnp.concatenate([each[:n] for each in back] + [other], axis=0)


def scatter_far(first, second):
    n = first.shape[0] // 4
    via_x = swap(first[3 * n:], "dp", 1)
    via_y = swap(second[3 * n:], "dp", 2)
    to_x = jnp.concatenate([first[n:2 * n], add_round(second[n:2 * n], via_y)], axis=1)
    to_y = jnp.concatenate([add_round(first[2 * n:3 * n], via_x), second[2 * n:3 * n]], axis=1)
    return to_x, to_y


def scatter_near(first, second, to_x, to_y):
    n = first.shape[0] // 4
    c = first.shape[1]
    from_x = swap(to_x, "dp", 1)
    from_y = swap(to_y, "dp", 2)
    return tuple(
        own[:n].astype(F32) + x.astype(F32) + y.astype(F32)
        for own, x, y in ((first, from_x[:, :c], from_y[:, :c]), (second, from_x[:, c:], from_y[:, c:]))
    )


def gather_near(first, second):
    own = jnp.concatenate([first, second], axis=1)
    return swap(own, "dp", 1), swap(own, "dp", 2)


def gather_far(first, second, from_x, from_y):
    c = first.shape[1]
    far_first = swap(from_y[:, :c], "dp", 1)
    far_second = swap(from_x[:, c:], "dp", 2)
    return (
        jnp.concatenate([first, from_x[:, :c], from_y[:, :c], far_first], axis=0),
        jnp.concatenate([second, from_x[:, c:], from_y[:, c:], far_second], axis=0),
    )


CONTRACT_FEATS = (((1,), (1,)), ((), ()))
CONTRACT_ROWS = (((0,), (0,)), ((), ()))


def per_device(tokens, expert_ids, route_weights, w_gate, w_up, w_down, out_grad):
    experts = lax.axis_size("expert")
    copies = experts // 8
    levels = copies.bit_length() - 1
    owner_index = lax.axis_index("expert")
    me = lax.axis_index("dp")
    copy_index = owner_index % copies
    tok_rows = tokens.shape[0]
    shard_width = w_gate.shape[0]
    capacity = max(2, 5 * tok_rows // (2 * experts))
    buckets = experts * capacity
    near = experts <= 8
    keys = expert_ids
    if near:
        keys = expert_ids ^ owner_index
        keys = (keys & 1) * 4 + (keys >> 1)

    lanes = jnp.arange(experts, dtype=jnp.int32)[None, :]
    first = keys[:, :1] == lanes
    second = keys[:, 1:] == lanes
    named = (first | second).astype(BF)
    earlier = (
        jnp.arange(tok_rows, dtype=jnp.int32)[None, :] < jnp.arange(tok_rows, dtype=jnp.int32)[:, None]
    ).astype(BF)
    before = jnp.dot(earlier, named, preferred_element_type=F32)
    slots = jnp.arange(buckets, dtype=jnp.int32)[None, :]

    def place(chosen, key):
        rank = jnp.sum(jnp.where(chosen, before, 0.0), axis=1, keepdims=True).astype(jnp.int32)
        return (slots == key * capacity + rank).astype(BF)

    place_0 = place(first, keys[:, :1])
    place_1 = place(second, keys[:, 1:])
    send_rows = lax.dot_general(
        place_0 + place_1, tokens, CONTRACT_ROWS, preferred_element_type=F32
    ).astype(BF)
    grad_f32 = out_grad.astype(F32)
    cot_0 = (route_weights[:, :1] * grad_f32).astype(BF)
    cot_1 = (route_weights[:, 1:] * grad_f32).astype(BF)
    cot_send = (
        lax.dot_general(place_0, cot_0, CONTRACT_ROWS, preferred_element_type=F32)
        + lax.dot_general(place_1, cot_1, CONTRACT_ROWS, preferred_element_type=F32)
    ).astype(BF)
    if near:
        in_rows = reorder(to_chips(*pair_core(send_rows)), me, 4)
        own_cot, other_cot = pair_core(cot_send)
        own_cot, other_cot = after((own_cot, other_cot), in_rows)
        cot_rows = reorder(to_chips(own_cot, other_cot), me, 4)
    else:
        in_rows = reorder(all_to_all(send_rows, experts), me, 4)
        cot_rows = reorder(all_to_all(cot_send, experts), me, 4)

    pieces = (w_gate, w_up, w_down)
    for bit_index in range(levels):
        partner = from_partner(as_sent(pieces), "expert", bit_index)
        is_upper = owner_index // 2**bit_index % 2 == 1
        pieces = tuple(relay_join(own, their, is_upper, 0) for own, their in zip(pieces, partner))
    gate_w, up_w, down_w = pieces

    def partial_product(rows, weights):
        return lax.dot_general(rows, weights, CONTRACT_FEATS, preferred_element_type=F32).astype(BF)

    half = gate_w.shape[0] // 2
    part_gate, part_up = partial_product(in_rows, gate_w), partial_product(in_rows, up_w)
    to_x, to_y = scatter_far(part_gate, part_up)
    gate_sum, up_sum = scatter_near(part_gate, part_up, to_x, to_y)
    cot_rows = after(cot_rows, gate_sum, up_sum)

    active, slope_term = silu_parts(gate_sum)
    own_hidden = (active * up_sum).astype(BF)
    own_hidden = (own_hidden[:, :half], own_hidden[:, half:])
    near_hidden = gather_near(*own_hidden)

    part_hidden = partial_product(cot_rows, down_w)
    part_first, part_second = part_hidden[:, :half], part_hidden[:, half:]
    to_x, to_y = scatter_far(part_first, part_second)
    to_x, to_y = after((to_x, to_y), near_hidden)
    hidden = jnp.concatenate(gather_far(*own_hidden, *near_hidden), axis=1)
    grad_hidden = jnp.concatenate(scatter_near(part_first, part_second, to_x, to_y), axis=1)
    out_rows = jnp.dot(hidden, down_w, preferred_element_type=F32).astype(BF)

    own_grads = ((grad_hidden * up_sum * slope_term).astype(BF), (grad_hidden * active).astype(BF))
    near_grads = gather_near(*own_grads)
    grad_gate_rows, grad_up_rows = gather_far(*own_grads, *near_grads)

    if near:
        returned = from_chips(reorder(out_rows, me, 4), near_grads)
    else:
        returned = all_to_all(reorder(out_rows, me, 4), experts)
    picked_0 = jnp.dot(place_0, returned, preferred_element_type=F32)
    picked_1 = jnp.dot(place_1, returned, preferred_element_type=F32)
    output = (route_weights[:, :1] * picked_0 + route_weights[:, 1:] * picked_1).astype(BF)

    def term(left, right):
        return lax.dot_general(left, right, CONTRACT_ROWS, preferred_element_type=F32).astype(BF)

    grad_terms = (term(grad_gate_rows, in_rows), term(grad_up_rows, in_rows), term(hidden, cot_rows))
    for bit_index in range(levels):
        partner = from_partner(grad_terms, "expert", bit_index)
        grad_terms = tuple(add_round(own, their) for own, their in zip(grad_terms, partner))
    start_row = copy_index * shard_width
    grads = [lax.dynamic_slice_in_dim(each, start_row, shard_width, 0) for each in grad_terms]
    return (output, *grads)


def solution(mesh):
    split = P("expert", "dp")
    pairs = P("expert", None)
    return jax.shard_map(
        per_device,
        mesh=mesh,
        in_specs=(split, pairs, pairs, split, split, split, split),
        out_specs=(split, split, split, split),
        check_vma=False,
    )
```

time: 194 us -> 114 us (0.59)
  waiting for transfers between devices: 126 us -> 44.7 us
  starting transfers between devices: 14.5 us -> 43.9 us
  matrix products: 34.9 us -> 20.5 us
  between operations: 14.2 us -> 1.14 us
    psum x1 -> x0, waiting for transfers between devices: 91.4 us -> none  [forward_sums(): lax.psum(part_up.astype(jnp.bfloat16), 'dp').astype(jnp.float32)]
    ppermute x0 -> x28, waiting for transfers between devices: none -> 44.7 us  [swap(): return lax.ppermute(block, axis, [(i, i ^ mask) for i in range(count)])]
    ppermute x0 -> x28, starting transfers between devices: none -> 43.9 us  [swap(): return lax.ppermute(block, axis, [(i, i ^ mask) for i in range(count)])]
    all_to_all x3 -> x0, waiting for transfers between devices: 34.3 us -> none  [the longest x1 15.6 us: per_device(): lax.all_to_all(send_rows.reshape(experts, capacity, feat_cols), 'expert',...]
    all_to_all x3 -> x0, starting transfers between devices: 14.5 us -> none  [the longest x1 6.32 us: per_device(): lax.all_to_all(send_rows.reshape(experts, capacity, feat_cols), 'expert',...]
    dot_general x10 -> x13, matrix products: 34.9 us -> 20.5 us  [the longest x3 12 us: term(): lax.dot_general(left, right, CONTRACT_ROWS, preferred_element_type=F32)]
  transfers between devices with their start and end apart: 4 -> 28, of which waited for: 4 -> 18; matrix products, arithmetic and copies ran while one was open for 10% -> 17% of each run, Pallas kernels for 0% -> 0%
where the time goes in v1:
time: 114 us
  waiting for transfers between devices  44.7 us (39%)
  starting transfers between devices  43.9 us (39%)
  matrix products  20.5 us (18%)
  other arithmetic  2.05 us (2%)
  local copies, waits for them, and re-layouts  1.42 us (1%)
    ppermute x28, waiting for transfers between devices, swap(): return lax.ppermute(block, axis, [(i, i ^ mask) for i in range(count)])  44.7 us
    ppermute x28, starting transfers between devices, swap(): return lax.ppermute(block, axis, [(i, i ^ mask) for i in range(count)])  43.9 us
    dot_general x3, matrix products, term(): lax.dot_general(left, right, CONTRACT_ROWS, preferred_element_type=F32)  12 us
    dot_general x3, matrix products, partial_product(): lax.dot_general(rows, weights, CONTRACT_FEATS, preferred_element_type=F32)  4.2 us
  transfers between devices with their start and end apart: 28, of which 18 were waited for; matrix products, arithmetic and copies ran while one was open for 17% of the time, Pallas kernels for 0%

profile of v1, /device:TPU:0, one launch (start us, length us, event | category | flops | bytes accessed | tf_op | source)
XLA Modules:
  0.0 113.7 jit_solution(17510255237962122635)
XLA Ops:
  3.9 3.0 %collective-permute-start.1 = (bf16[80,1024]{1,0:T(8,128)(2,1)S(1)}, bf16[80,1024]{1,0:T(8,128)(2,1)S(1)}, u32[]{:S(2)}, u32[]{:S(2)}) collective-permute-start(bf16[80,1024]{1,0:T(8,128)(2,1)S(1)} %pad_maximum_fusion.9), channel_id=1, source_target_pairs={{0,2},{1,3},{2,0},{3,1},{4,6},{5,7},{6,4},{7,5},{8,10},{9,11},{10,... | collective-permute-start | bytes 491528 | tf_op jit(solution)/shard_map/ppermute | solution.py:30
  6.9 2.7 %collective-permute-start.2 = (bf16[80,1024]{1,0:T(8,128)(2,1)S(1)}, bf16[80,1024]{1,0:T(8,128)(2,1)S(1)}, u32[]{:S(2)}, u32[]{:S(2)}) collective-permute-start(bf16[80,1024]{1,0:T(8,128)(2,1)S(1)} %pad_maximum_fusion.10), channel_id=1, source_target_pairs={{0,4},{1,5},{2,6},{3,7},{4,0},{5,1},{6,2},{7,3},{8,12},{9,13},{10,... | collective-permute-start | bytes 491528 | tf_op jit(solution)/shard_map/ppermute | solution.py:30
  10.7 3.6 %collective-permute-start.17 = (bf16[80,1024]{1,0:T(8,128)(2,1)S(1)}, bf16[80,1024]{1,0:T(8,128)(2,1)S(1)}, u32[]{:S(2)}, u32[]{:S(2)}) collective-permute-start(bf16[80,1024]{1,0:T(8,128)(2,1)S(1)} %pad_maximum_fusion.13), channel_id=1, source_target_pairs={{0,4},{1,5},{2,6},{3,7},{4,0},{5,1},{6,2},{7,3},{8,12},{9,13},{10,... | collective-permute-start | bytes 491528 | tf_op jit(solution)/shard_map/ppermute | solution.py:30
  14.8 3.8 %collective-permute-start.18 = (bf16[80,1024]{1,0:T(8,128)(2,1)S(1)}, bf16[80,1024]{1,0:T(8,128)(2,1)S(1)}, u32[]{:S(2)}, u32[]{:S(2)}) collective-permute-start(bf16[80,1024]{1,0:T(8,128)(2,1)S(1)} %pad_maximum_fusion.14), channel_id=1, source_target_pairs={{0,6},{1,7},{2,4},{3,5},{4,2},{5,3},{6,0},{7,1},{8,14},{9,15},{10,... | collective-permute-start | bytes 491528 | tf_op jit(solution)/shard_map/ppermute | solution.py:30
  18.6 3.4 %collective-permute-done.2 = bf16[80,1024]{1,0:T(8,128)(2,1)S(1)} collective-permute-done((bf16[80,1024]{1,0:T(8,128)(2,1)S(1)}, bf16[80,1024]{1,0:T(8,128)(2,1)S(1)}, u32[]{:S(2)}, u32[]{:S(2)}) %collective-permute-start.2) | collective-permute-done | bytes 163872 | tf_op jit(solution)/shard_map/ppermute | solution.py:30
  25.6 1.6 %collective-permute-start.6 = (bf16[80,1792]{1,0:T(8,128)(2,1)S(1)}, bf16[80,1792]{1,0:T(8,128)(2,1)S(1)}, u32[]{:S(2)}, u32[]{:S(2)}) collective-permute-start(bf16[80,1792]{1,0:T(8,128)(2,1)S(1)} %get-tuple-element.38), channel_id=1, source_target_pairs={{0,8},{8,0},{16,24},{24,16},{1,9},{9,1},{17,25},{25,17},{2,10},{10... | collective-permute-start | bytes 860168 | tf_op jit(solution)/shard_map/ppermute | solution.py:30
  27.2 1.6 %collective-permute-start.4 = (bf16[80,1792]{1,0:T(8,128)(2,1)S(1)}, bf16[80,1792]{1,0:T(8,128)(2,1)S(1)}, u32[]{:S(2)}, u32[]{:S(2)}) collective-permute-start(bf16[80,1792]{1,0:T(8,128)(2,1)S(1)} %get-tuple-element.39), channel_id=1, source_target_pairs={{0,16},{8,24},{16,0},{24,8},{1,17},{9,25},{17,1},{25,9},{2,18},{10... | collective-permute-start | bytes 860168 | tf_op jit(solution)/shard_map/ppermute | solution.py:30
  28.8 3.5 %collective-permute-done.6 = bf16[80,1792]{1,0:T(8,128)(2,1)S(1)} collective-permute-done((bf16[80,1792]{1,0:T(8,128)(2,1)S(1)}, bf16[80,1792]{1,0:T(8,128)(2,1)S(1)}, u32[]{:S(2)}, u32[]{:S(2)}) %collective-permute-start.6) | collective-permute-done | bytes 286752 | tf_op jit(solution)/shard_map/ppermute | solution.py:30
  32.5 1.6 %collective-permute-start.7 = (bf16[80,3584]{1,0:T(8,128)(2,1)S(1)}, bf16[80,3584]{1,0:T(8,128)(2,1)S(1)}, u32[]{:S(2)}, u32[]{:S(2)}) collective-permute-start(bf16[80,3584]{1,0:T(8,128)(2,1)S(1)} %pad_maximum_fusion.3), channel_id=1, source_target_pairs={{0,16},{8,24},{16,0},{24,8},{1,17},{9,25},{17,1},{25,9},{2,18},{10... | collective-permute-start | bytes 1720328 | tf_op jit(solution)/shard_map/ppermute | solution.py:30
  34.1 1.6 %collective-permute-done.4 = bf16[80,1792]{1,0:T(8,128)(2,1)S(1)} collective-permute-done((bf16[80,1792]{1,0:T(8,128)(2,1)S(1)}, bf16[80,1792]{1,0:T(8,128)(2,1)S(1)}, u32[]{:S(2)}, u32[]{:S(2)}) %collective-permute-start.4) | collective-permute-done | bytes 286752 | tf_op jit(solution)/shard_map/ppermute | solution.py:30
  36.2 10.0 %collective-permute-done.7 = bf16[80,3584]{1,0:T(8,128)(2,1)S(1)} collective-permute-done((bf16[80,3584]{1,0:T(8,128)(2,1)S(1)}, bf16[80,3584]{1,0:T(8,128)(2,1)S(1)}, u32[]{:S(2)}, u32[]{:S(2)}) %collective-permute-start.7) | collective-permute-done | bytes 573472 | tf_op jit(solution)/shard_map/ppermute | solution.py:30
  46.5 1.6 %collective-permute-start.9 = (bf16[80,1792]{1,0:T(8,128)(2,1)S(1)}, bf16[80,1792]{1,0:T(8,128)(2,1)S(1)}, u32[]{:S(2)}, u32[]{:S(2)}) collective-permute-start(bf16[80,1792]{1,0:T(8,128)(2,1)S(1)} %get-tuple-element.24), channel_id=1, source_target_pairs={{0,16},{8,24},{16,0},{24,8},{1,17},{9,25},{17,1},{25,9},{2,18},{10... | collective-permute-start | bytes 860168 | tf_op jit(solution)/shard_map/ppermute | solution.py:30
  52.3 3.7 %collective-permute-done.20 = bf16[80,896]{1,0:T(8,128)(2,1)S(1)} collective-permute-done((bf16[80,896]{1,0:T(8,128)(2,1)S(1)}, bf16[80,896]{1,0:T(8,128)(2,1)S(1)}, u32[]{:S(2)}, u32[]{:S(2)}) %collective-permute-start.20) | collective-permute-done | bytes 143392 | tf_op jit(solution)/shard_map/ppermute | solution.py:30
  57.7 4.4 %collective-permute-done.8 = bf16[80,1792]{1,0:T(8,128)(2,1)S(1)} collective-permute-done((bf16[80,1792]{1,0:T(8,128)(2,1)S(1)}, bf16[80,1792]{1,0:T(8,128)(2,1)S(1)}, u32[]{:S(2)}, u32[]{:S(2)}) %collective-permute-start.8) | collective-permute-done | bytes 286752 | tf_op jit(solution)/shard_map/ppermute | solution.py:30
  62.2 2.2 %collective-permute-start.21 = (bf16[80,1792]{1,0:T(8,128)(2,1)S(1)}, bf16[80,1792]{1,0:T(8,128)(2,1)S(1)}, u32[]{:S(2)}, u32[]{:S(2)}) collective-permute-start(bf16[80,1792]{1,0:T(8,128)(2,1)S(1)} %get-tuple-element.16), channel_id=1, source_target_pairs={{0,8},{8,0},{16,24},{24,16},{1,9},{9,1},{17,25},{25,17},{2,10},{10... | collective-permute-start | bytes 860168 | tf_op jit(solution)/shard_map/ppermute | solution.py:30
  65.1 2.1 %collective-permute-done.11 = bf16[80,896]{1,0:T(8,128)(2,1)S(1)} collective-permute-done((bf16[80,896]{1,0:T(8,128)(2,1)S(1)}, bf16[80,896]{1,0:T(8,128)(2,1)S(1)}, u32[]{:S(2)}, u32[]{:S(2)}) %collective-permute-start.11) | collective-permute-done | bytes 143392 | tf_op jit(solution)/shard_map/ppermute | solution.py:30
  69.0 4.7 %collective-permute-done.22 = bf16[80,1792]{1,0:T(8,128)(2,1)S(1)} collective-permute-done((bf16[80,1792]{1,0:T(8,128)(2,1)S(1)}, bf16[80,1792]{1,0:T(8,128)(2,1)S(1)}, u32[]{:S(2)}, u32[]{:S(2)}) %collective-permute-start.22) | collective-permute-done | bytes 286752 | tf_op jit(solution)/shard_map/ppermute | solution.py:30
  74.4 1.7 %collective-permute-start.14 = (bf16[80,1024]{1,0:T(8,128)(2,1)S(1)}, bf16[80,1024]{1,0:T(8,128)(2,1)S(1)}, u32[]{:S(2)}, u32[]{:S(2)}) collective-permute-start(bf16[80,1024]{1,0:T(8,128)(2,1)S(1)} %get-tuple-element.47), channel_id=1, source_target_pairs={{0,6},{1,7},{2,4},{3,5},{4,2},{5,3},{6,0},{7,1},{8,14},{9,15},{10,... | collective-permute-start | bytes 491528 | tf_op jit(solution)/shard_map/ppermute | solution.py:30
  76.1 11.6 %collective-permute-start.13 = (bf16[80,1024]{1,0:T(8,128)(2,1)S(1)}, bf16[80,1024]{1,0:T(8,128)(2,1)S(1)}, u32[]{:S(2)}, u32[]{:S(2)}) collective-permute-start(bf16[80,1024]{1,0:T(8,128)(2,1)S(1)} %get-tuple-element.48), channel_id=1, source_target_pairs={{0,4},{1,5},{2,6},{3,7},{4,0},{5,1},{6,2},{7,3},{8,12},{9,13},{10,... | collective-permute-start | bytes 491528 | tf_op jit(solution)/shard_map/ppermute | solution.py:30
  88.8 3.9 %convolution_convert_fusion = bf16[1792,1024]{1,0:T(8,128)(2,1)} fusion(bf16[320,1024]{1,0:T(8,128)(2,1)S(1)} %pad_maximum_fusion.1, bf16[80,896]{1,0:T(8,128)(2,1)S(1)} %collective-permute-done.11, bf16[80,896]{1,0:T(8,128)(2,1)S(1)} %get-tuple-element.80, bf16[80,896]{1,0:T(8,128)(2,1)S(1)} %get-tuple-element.78, bf16[80,896]{1,0:T(8,128)(2,1)S(1)} %get-tuple-element.76, ...), kind=kOutput, calls=%fused_computation | convolution fusion | flops 1185415168 | bytes 5472256 | tf_op jit(solution)/shard_map/dot_general | solution.py:226
  94.8 2.6 %collective-permute-done.23 = bf16[80,3584]{1,0:T(8,128)(2,1)S(1)} collective-permute-done((bf16[80,3584]{1,0:T(8,128)(2,1)S(1)}, bf16[80,3584]{1,0:T(8,128)(2,1)S(1)}, u32[]{:S(2)}, u32[]{:S(2)}) %collective-permute-start.23) | collective-permute-done | bytes 573472 | tf_op jit(solution)/shard_map/ppermute | solution.py:30
  98.7 5.4 %collective-permute-done.27 = bf16[80,1792]{1,0:T(8,128)(2,1)S(1)} collective-permute-done((bf16[80,1792]{1,0:T(8,128)(2,1)S(1)}, bf16[80,1792]{1,0:T(8,128)(2,1)S(1)}, u32[]{:S(2)}, u32[]{:S(2)}) %collective-permute-start.27) | collective-permute-done | bytes 286752 | tf_op jit(solution)/shard_map/ppermute | solution.py:30
  104.2 4.1 %convolution_convert_fusion.1 = bf16[1792,1024]{1,0:T(8,128)(2,1)} fusion(bf16[80,1792]{1,0:T(8,128)(2,1)S(1)} %collective-permute-done.27, bf16[80,1792]{1,0:T(8,128)(2,1)S(1)} %get-tuple-element.59, bf16[80,1792]{1,0:T(8,128)(2,1)S(1)} %get-tuple-element.61, bf16[80,1792]{1,0:T(8,128)(2,1)S(1)} %get-tuple-element.30, ...), kind=kOutput, calls=%fused_computation.1 | convolution fusion | flops 1183449088 | bytes 5472256 | tf_op jit(solution)/shard_map/dot_general | solution.py:226
  108.3 3.9 %convolution_convert_fusion.2 = bf16[1792,1024]{1,0:T(8,128)(2,1)} fusion(bf16[80,1792]{1,0:T(8,128)(2,1)S(1)} %collective-permute-done.26, bf16[80,1792]{1,0:T(8,128)(2,1)S(1)} %get-tuple-element.60, bf16[80,1792]{1,0:T(8,128)(2,1)S(1)} %get-tuple-element.62, bf16[80,1792]{1,0:T(8,128)(2,1)S(1)} %get-tuple-element.29, ...), kind=kOutput, calls=%fused_computation.2 | convolution fusion | flops 1183449088 | bytes 5472256 | tf_op jit(solution)/shard_map/dot_general | solution.py:226
  (107 shorter events, 24.2 us)
Async XLA Ops:
  3.9 10.9 %collective-permute-start.1 = (bf16[80,1024]{1,0:T(8,128)(2,1)S(1)}, bf16[80,1024]{1,0:T(8,128)(2,1)S(1)}, u32[]{:S(2)}, u32[]{:S(2)}) collective-permute-start(bf16[80,1024]{1,0:T(8,128)(2,1)S(1)} %pad_maximum_fusion.9), channel_id=1, source_target_pairs={{0,2},{1,3},{2,0},{3,1},{4,6},{5,7},{6,4},{7,5},{8,10},{9,11},{10,... | collective-permute-start | bytes 491528 | tf_op jit(solution)/shard_map/ppermute | solution.py:30
  6.9 15.1 %collective-permute-start.2 = (bf16[80,1024]{1,0:T(8,128)(2,1)S(1)}, bf16[80,1024]{1,0:T(8,128)(2,1)S(1)}, u32[]{:S(2)}, u32[]{:S(2)}) collective-permute-start(bf16[80,1024]{1,0:T(8,128)(2,1)S(1)} %pad_maximum_fusion.10), channel_id=1, source_target_pairs={{0,4},{1,5},{2,6},{3,7},{4,0},{5,1},{6,2},{7,3},{8,12},{9,13},{10,... | collective-permute-start | bytes 491528 | tf_op jit(solution)/shard_map/ppermute | solution.py:30
  9.6 12.5 %collective-permute-start.3 = (bf16[80,1024]{1,0:T(8,128)(2,1)S(1)}, bf16[80,1024]{1,0:T(8,128)(2,1)S(1)}, u32[]{:S(2)}, u32[]{:S(2)}) collective-permute-start(bf16[80,1024]{1,0:T(8,128)(2,1)S(1)} %pad_maximum_fusion.11), channel_id=1, source_target_pairs={{0,6},{1,7},{2,4},{3,5},{4,2},{5,3},{6,0},{7,1},{8,14},{9,15},{10,... | collective-permute-start | bytes 491528 | tf_op jit(solution)/shard_map/ppermute | solution.py:30
  9.8 26.1 %collective-permute-start.16 = (bf16[80,1024]{1,0:T(8,128)(2,1)S(1)}, bf16[80,1024]{1,0:T(8,128)(2,1)S(1)}, u32[]{:S(2)}, u32[]{:S(2)}) collective-permute-start(bf16[80,1024]{1,0:T(8,128)(2,1)S(1)} %pad_maximum_fusion.12), channel_id=1, source_target_pairs={{0,2},{1,3},{2,0},{3,1},{4,6},{5,7},{6,4},{7,5},{8,10},{9,11},{10,... | collective-permute-start | bytes 491528 | tf_op jit(solution)/shard_map/ppermute | solution.py:30
  10.7 25.3 %collective-permute-start.17 = (bf16[80,1024]{1,0:T(8,128)(2,1)S(1)}, bf16[80,1024]{1,0:T(8,128)(2,1)S(1)}, u32[]{:S(2)}, u32[]{:S(2)}) collective-permute-start(bf16[80,1024]{1,0:T(8,128)(2,1)S(1)} %pad_maximum_fusion.13), channel_id=1, source_target_pairs={{0,4},{1,5},{2,6},{3,7},{4,0},{5,1},{6,2},{7,3},{8,12},{9,13},{10,... | collective-permute-start | bytes 491528 | tf_op jit(solution)/shard_map/ppermute | solution.py:30
  14.8 21.3 %collective-permute-start.18 = (bf16[80,1024]{1,0:T(8,128)(2,1)S(1)}, bf16[80,1024]{1,0:T(8,128)(2,1)S(1)}, u32[]{:S(2)}, u32[]{:S(2)}) collective-permute-start(bf16[80,1024]{1,0:T(8,128)(2,1)S(1)} %pad_maximum_fusion.14), channel_id=1, source_target_pairs={{0,6},{1,7},{2,4},{3,5},{4,2},{5,3},{6,0},{7,1},{8,14},{9,15},{10,... | collective-permute-start | bytes 491528 | tf_op jit(solution)/shard_map/ppermute | solution.py:30
  25.6 6.7 %collective-permute-start.6 = (bf16[80,1792]{1,0:T(8,128)(2,1)S(1)}, bf16[80,1792]{1,0:T(8,128)(2,1)S(1)}, u32[]{:S(2)}, u32[]{:S(2)}) collective-permute-start(bf16[80,1792]{1,0:T(8,128)(2,1)S(1)} %get-tuple-element.38), channel_id=1, source_target_pairs={{0,8},{8,0},{16,24},{24,16},{1,9},{9,1},{17,25},{25,17},{2,10},{10... | collective-permute-start | bytes 860168 | tf_op jit(solution)/shard_map/ppermute | solution.py:30
  27.2 8.4 %collective-permute-start.4 = (bf16[80,1792]{1,0:T(8,128)(2,1)S(1)}, bf16[80,1792]{1,0:T(8,128)(2,1)S(1)}, u32[]{:S(2)}, u32[]{:S(2)}) collective-permute-start(bf16[80,1792]{1,0:T(8,128)(2,1)S(1)} %get-tuple-element.39), channel_id=1, source_target_pairs={{0,16},{8,24},{16,0},{24,8},{1,17},{9,25},{17,1},{25,9},{2,18},{10... | collective-permute-start | bytes 860168 | tf_op jit(solution)/shard_map/ppermute | solution.py:30
  32.5 13.7 %collective-permute-start.7 = (bf16[80,3584]{1,0:T(8,128)(2,1)S(1)}, bf16[80,3584]{1,0:T(8,128)(2,1)S(1)}, u32[]{:S(2)}, u32[]{:S(2)}) collective-permute-start(bf16[80,3584]{1,0:T(8,128)(2,1)S(1)} %pad_maximum_fusion.3), channel_id=1, source_target_pairs={{0,16},{8,24},{16,0},{24,8},{1,17},{9,25},{17,1},{25,9},{2,18},{10... | collective-permute-start | bytes 1720328 | tf_op jit(solution)/shard_map/ppermute | solution.py:30
  35.8 10.4 %collective-permute-start.5 = (bf16[80,3584]{1,0:T(8,128)(2,1)S(1)}, bf16[80,3584]{1,0:T(8,128)(2,1)S(1)}, u32[]{:S(2)}, u32[]{:S(2)}) collective-permute-start(bf16[80,3584]{1,0:T(8,128)(2,1)S(1)} %pad_maximum_fusion.2), channel_id=1, source_target_pairs={{0,8},{8,0},{16,24},{24,16},{1,9},{9,1},{17,25},{25,17},{2,10},{10... | collective-permute-start | bytes 1720328 | tf_op jit(solution)/shard_map/ppermute | solution.py:30
  46.5 9.8 %collective-permute-start.9 = (bf16[80,1792]{1,0:T(8,128)(2,1)S(1)}, bf16[80,1792]{1,0:T(8,128)(2,1)S(1)}, u32[]{:S(2)}, u32[]{:S(2)}) collective-permute-start(bf16[80,1792]{1,0:T(8,128)(2,1)S(1)} %get-tuple-element.24), channel_id=1, source_target_pairs={{0,16},{8,24},{16,0},{24,8},{1,17},{9,25},{17,1},{25,9},{2,18},{10... | collective-permute-start | bytes 860168 | tf_op jit(solution)/shard_map/ppermute | solution.py:30
  49.6 6.4 %collective-permute-start.20 = (bf16[80,896]{1,0:T(8,128)(2,1)S(1)}, bf16[80,896]{1,0:T(8,128)(2,1)S(1)}, u32[]{:S(2)}, u32[]{:S(2)}) collective-permute-start(bf16[80,896]{1,0:T(8,128)(2,1)S(1)} %get-tuple-element.33), channel_id=1, source_target_pairs={{0,8},{8,0},{16,24},{24,16},{1,9},{9,1},{17,25},{25,17},{2,10},{10... | collective-permute-start | bytes 430088 | tf_op jit(solution)/shard_map/ppermute | solution.py:30
  51.4 10.7 %collective-permute-start.8 = (bf16[80,1792]{1,0:T(8,128)(2,1)S(1)}, bf16[80,1792]{1,0:T(8,128)(2,1)S(1)}, u32[]{:S(2)}, u32[]{:S(2)}) collective-permute-start(bf16[80,1792]{1,0:T(8,128)(2,1)S(1)} %get-tuple-element.24), channel_id=1, source_target_pairs={{0,8},{8,0},{16,24},{24,16},{1,9},{9,1},{17,25},{25,17},{2,10},{10... | collective-permute-start | bytes 860168 | tf_op jit(solution)/shard_map/ppermute | solution.py:30
  56.4 8.7 %collective-permute-start.10 = (bf16[80,896]{1,0:T(8,128)(2,1)S(1)}, bf16[80,896]{1,0:T(8,128)(2,1)S(1)}, u32[]{:S(2)}, u32[]{:S(2)}) collective-permute-start(bf16[80,896]{1,0:T(8,128)(2,1)S(1)} %get-tuple-element.79), channel_id=1, source_target_pairs={{0,8},{8,0},{16,24},{24,16},{1,9},{9,1},{17,25},{25,17},{2,10},{10... | collective-permute-start | bytes 430088 | tf_op jit(solution)/shard_map/ppermute | solution.py:30
  62.2 6.8 %collective-permute-start.21 = (bf16[80,1792]{1,0:T(8,128)(2,1)S(1)}, bf16[80,1792]{1,0:T(8,128)(2,1)S(1)}, u32[]{:S(2)}, u32[]{:S(2)}) collective-permute-start(bf16[80,1792]{1,0:T(8,128)(2,1)S(1)} %get-tuple-element.16), channel_id=1, source_target_pairs={{0,8},{8,0},{16,24},{24,16},{1,9},{9,1},{17,25},{25,17},{2,10},{10... | collective-permute-start | bytes 860168 | tf_op jit(solution)/shard_map/ppermute | solution.py:30
  64.4 9.4 %collective-permute-start.22 = (bf16[80,1792]{1,0:T(8,128)(2,1)S(1)}, bf16[80,1792]{1,0:T(8,128)(2,1)S(1)}, u32[]{:S(2)}, u32[]{:S(2)}) collective-permute-start(bf16[80,1792]{1,0:T(8,128)(2,1)S(1)} %get-tuple-element.17), channel_id=1, source_target_pairs={{0,16},{8,24},{16,0},{24,8},{1,17},{9,25},{17,1},{25,9},{2,18},{10... | collective-permute-start | bytes 860168 | tf_op jit(solution)/shard_map/ppermute | solution.py:30
  74.2 18.5 %collective-permute-start.24 = (bf16[80,3584]{1,0:T(8,128)(2,1)S(1)}, bf16[80,3584]{1,0:T(8,128)(2,1)S(1)}, u32[]{:S(2)}, u32[]{:S(2)}) collective-permute-start(bf16[80,3584]{1,0:T(8,128)(2,1)S(1)} %pad_maximum_fusion.5), channel_id=1, source_target_pairs={{0,16},{8,24},{16,0},{24,8},{1,17},{9,25},{17,1},{25,9},{2,18},{10... | collective-permute-start | bytes 1720328 | tf_op jit(solution)/shard_map/ppermute | solution.py:30
  74.4 19.4 %collective-permute-start.14 = (bf16[80,1024]{1,0:T(8,128)(2,1)S(1)}, bf16[80,1024]{1,0:T(8,128)(2,1)S(1)}, u32[]{:S(2)}, u32[]{:S(2)}) collective-permute-start(bf16[80,1024]{1,0:T(8,128)(2,1)S(1)} %get-tuple-element.47), channel_id=1, source_target_pairs={{0,6},{1,7},{2,4},{3,5},{4,2},{5,3},{6,0},{7,1},{8,14},{9,15},{10,... | collective-permute-start | bytes 491528 | tf_op jit(solution)/shard_map/ppermute | solution.py:30
  76.1 18.5 %collective-permute-start.13 = (bf16[80,1024]{1,0:T(8,128)(2,1)S(1)}, bf16[80,1024]{1,0:T(8,128)(2,1)S(1)}, u32[]{:S(2)}, u32[]{:S(2)}) collective-permute-start(bf16[80,1024]{1,0:T(8,128)(2,1)S(1)} %get-tuple-element.48), channel_id=1, source_target_pairs={{0,4},{1,5},{2,6},{3,7},{4,0},{5,1},{6,2},{7,3},{8,12},{9,13},{10,... | collective-permute-start | bytes 491528 | tf_op jit(solution)/shard_map/ppermute | solution.py:30
  87.7 7.1 %collective-permute-start.12 = (bf16[80,1024]{1,0:T(8,128)(2,1)S(1)}, bf16[80,1024]{1,0:T(8,128)(2,1)S(1)}, u32[]{:S(2)}, u32[]{:S(2)}) collective-permute-start(bf16[80,1024]{1,0:T(8,128)(2,1)S(1)} %get-tuple-element.49), channel_id=1, source_target_pairs={{0,2},{1,3},{2,0},{3,1},{4,6},{5,7},{6,4},{7,5},{8,10},{9,11},{10,... | collective-permute-start | bytes 491528 | tf_op jit(solution)/shard_map/ppermute | solution.py:30
  87.7 9.7 %collective-permute-start.23 = (bf16[80,3584]{1,0:T(8,128)(2,1)S(1)}, bf16[80,3584]{1,0:T(8,128)(2,1)S(1)}, u32[]{:S(2)}, u32[]{:S(2)}) collective-permute-start(bf16[80,3584]{1,0:T(8,128)(2,1)S(1)} %pad_maximum_fusion.5), channel_id=1, source_target_pairs={{0,8},{8,0},{16,24},{24,16},{1,9},{9,1},{17,25},{25,17},{2,10},{10... | collective-permute-start | bytes 1720328 | tf_op jit(solution)/shard_map/ppermute | solution.py:30
  92.8 15.5 %collective-permute-start.26 = (bf16[80,1792]{1,0:T(8,128)(2,1)S(1)}, bf16[80,1792]{1,0:T(8,128)(2,1)S(1)}, u32[]{:S(2)}, u32[]{:S(2)}) collective-permute-start(bf16[80,1792]{1,0:T(8,128)(2,1)S(1)} %get-tuple-element.60), channel_id=1, source_target_pairs={{0,8},{8,0},{16,24},{24,16},{1,9},{9,1},{17,25},{25,17},{2,10},{10... | collective-permute-start | bytes 860168 | tf_op jit(solution)/shard_map/ppermute | solution.py:30
  97.5 6.7 %collective-permute-start.27 = (bf16[80,1792]{1,0:T(8,128)(2,1)S(1)}, bf16[80,1792]{1,0:T(8,128)(2,1)S(1)}, u32[]{:S(2)}, u32[]{:S(2)}) collective-permute-start(bf16[80,1792]{1,0:T(8,128)(2,1)S(1)} %get-tuple-element.61), channel_id=1, source_target_pairs={{0,16},{8,24},{16,0},{24,8},{1,17},{9,25},{17,1},{25,9},{2,18},{10... | collective-permute-start | bytes 860168 | tf_op jit(solution)/shard_map/ppermute | solution.py:30
  98.7 13.6 %collective-permute-start.25 = (bf16[160,1024]{1,0:T(8,128)(2,1)S(1)}, bf16[160,1024]{1,0:T(8,128)(2,1)S(1)}, u32[]{:S(2)}, u32[]{:S(2)}) collective-permute-start(bf16[160,1024]{1,0:T(8,128)(2,1)S(1)} %pad_maximum_fusion.6), channel_id=1, source_target_pairs={{0,1},{1,0},{2,3},{3,2},{4,5},{5,4},{6,7},{7,6},{8,9},{9,8},{10,11... | collective-permute-start | bytes 983048 | tf_op jit(solution)/shard_map/ppermute | solution.py:30
  (10 other events, 50.4 us)

commit v2 on v1

--- a/solution.py
+++ b/solution.py
@@ -30,8 +30,8 @@
     return lax.ppermute(block, axis, [(i, i ^ mask) for i in range(count)])
 
 
-def after(value, *earlier):
-    return lax.optimization_barrier((value, earlier))[0]
+def after(values):
+    return lax.optimization_barrier(values)
 
 
 def silu_parts(gate_sum):
@@ -82,47 +82,39 @@
     )
 
 
-def from_chips(rows, *earlier):
+def swap_places(rows):
     n = rows.shape[0] // 8
-    blocks = [rows[2 * m * n:2 * (m + 1) * n] for m in range(4)]
-    back = after([blocks[0]] + [swap(blocks[m], "expert", 2 * m) for m in range(1, 4)], *earlier)
-    other = swap(jnp.concatenate([each[n:] for each in back], axis=0), "expert", 1)
-    return jnp.concatenate([each[:n] for each in back] + [other], axis=0)
-
-
-def scatter_far(first, second):
-    n = first.shape[0] // 4
-    via_x = swap(first[3 * n:], "dp", 1)
-    via_y = swap(second[3 * n:], "dp", 2)
-    to_x = jnp.concatenate([first[n:2 * n], add_round(second[n:2 * n], via_y)], axis=1)
-    to_y = jnp.concatenate([add_round(first[2 * n:3 * n], via_x), second[2 * n:3 * n]], axis=1)
+    return rows.reshape(2, 4, n, rows.shape[1]).swapaxes(0, 1).reshape(rows.shape)
+
+
+def swap_back(rows):
+    n = rows.shape[0] // 8
+    return rows.reshape(4, 2, n, rows.shape[1]).swapaxes(0, 1).reshape(rows.shape)
+
+
+def scatter_far(part):
+    n, c = part.shape[0] // 4, part.shape[1] // 2
+    via_x = swap(part[3 * n:, :c], "dp", 1)
+    via_y = swap(part[3 * n:, c:], "dp", 2)
+    to_x = jnp.concatenate([part[n:2 * n, :c], add_round(part[n:2 * n, c:], via_y)], axis=1)
+    to_y = jnp.concatenate([add_round(part[2 * n:3 * n, :c], via_x), part[2 * n:3 * n, c:]], axis=1)
     return to_x, to_y
 
 
-def scatter_near(first, second, to_x, to_y):
-    n = first.shape[0] // 4
-    c = first.shape[1]
-    from_x = swap(to_x, "dp", 1)
-    from_y = swap(to_y, "dp", 2)
-    return tuple(
-        own[:n].astype(F32) + x.astype(F32) + y.astype(F32)
-        for own, x, y in ((first, from_x[:, :c], from_y[:, :c]), (second, from_x[:, c:], from_y[:, c:]))
-    )
-
-
-def gather_near(first, second):
-    own = jnp.concatenate([first, second], axis=1)
+def scatter_near(part, to_x, to_y):
+    n = part.shape[0] // 4
+    return part[:n].astype(F32) + swap(to_x, "dp", 1).astype(F32) + swap(to_y, "dp", 2).astype(F32)
+
+
+def gather_near(own):
     return swap(own, "dp", 1), swap(own, "dp", 2)
 
 
-def gather_far(first, second, from_x, from_y):
-    c = first.shape[1]
+def gather_far(own, from_x, from_y):
+    c = own.shape[1] // 2
     far_first = swap(from_y[:, :c], "dp", 1)
     far_second = swap(from_x[:, c:], "dp", 2)
-    return (
-        jnp.concatenate([first, from_x[:, :c], from_y[:, :c], far_first], axis=0),
-        jnp.concatenate([second, from_x[:, c:], from_y[:, c:], far_second], axis=0),
-    )
+    return jnp.concatenate([own, from_x, from_y, jnp.concatenate([far_first, far_second], axis=1)], axis=0)
 
 
 CONTRACT_FEATS = (((1,), (1,)), ((), ()))
@@ -174,12 +166,9 @@
     ).astype(BF)
     if near:
         in_rows = reorder(to_chips(*pair_core(send_rows)), me, 4)
-        own_cot, other_cot = pair_core(cot_send)
-        own_cot, other_cot = after((own_cot, other_cot), in_rows)
-        cot_rows = reorder(to_chips(own_cot, other_cot), me, 4)
+        cot_send = reorder(swap_places(cot_send), owner_index, 8)
     else:
         in_rows = reorder(all_to_all(send_rows, experts), me, 4)
-        cot_rows = reorder(all_to_all(cot_send, experts), me, 4)
 
     pieces = (w_gate, w_up, w_down)
     for bit_index in range(levels):
@@ -191,33 +180,38 @@
     def partial_product(rows, weights):
         return lax.dot_general(rows, weights, CONTRACT_FEATS, preferred_element_type=F32).astype(BF)
 
-    half = gate_w.shape[0] // 2
     part_gate, part_up = partial_product(in_rows, gate_w), partial_product(in_rows, up_w)
-    to_x, to_y = scatter_far(part_gate, part_up)
-    gate_sum, up_sum = scatter_near(part_gate, part_up, to_x, to_y)
-    cot_rows = after(cot_rows, gate_sum, up_sum)
-
+    way_gate, way_up = scatter_far(part_gate), scatter_far(part_up)
+    cot_send, way_up = after((cot_send, way_up))
+    cot_rows = all_to_all(cot_send, experts)
+    gate_sum, up_sum = scatter_near(part_gate, *way_gate), scatter_near(part_up, *way_up)
     active, slope_term = silu_parts(gate_sum)
     own_hidden = (active * up_sum).astype(BF)
-    own_hidden = (own_hidden[:, :half], own_hidden[:, half:])
-    near_hidden = gather_near(*own_hidden)
-
-    part_hidden = partial_product(cot_rows, down_w)
-    part_first, part_second = part_hidden[:, :half], part_hidden[:, half:]
-    to_x, to_y = scatter_far(part_first, part_second)
-    to_x, to_y = after((to_x, to_y), near_hidden)
-    hidden = jnp.concatenate(gather_far(*own_hidden, *near_hidden), axis=1)
-    grad_hidden = jnp.concatenate(scatter_near(part_first, part_second, to_x, to_y), axis=1)
+    near_hidden = gather_near(own_hidden)
+
+    cot_rows, near_hidden = after((cot_rows, near_hidden))
+    if near:
+        cot_rows = reorder(cot_rows, owner_index ^ (2 * me), 8)
+    else:
+        cot_rows = reorder(cot_rows, me, 4)
+    part = partial_product(cot_rows, down_w)
+    on_way = scatter_far(part)
+    hidden = gather_far(own_hidden, *near_hidden)
     out_rows = jnp.dot(hidden, down_w, preferred_element_type=F32).astype(BF)
-
-    own_grads = ((grad_hidden * up_sum * slope_term).astype(BF), (grad_hidden * active).astype(BF))
-    near_grads = gather_near(*own_grads)
-    grad_gate_rows, grad_up_rows = gather_far(*own_grads, *near_grads)
-
-    if near:
-        returned = from_chips(reorder(out_rows, me, 4), near_grads)
+    grad_hidden = scatter_near(part, *on_way)
+
+    own_gate = (grad_hidden * up_sum * slope_term).astype(BF)
+    own_up = (grad_hidden * active).astype(BF)
+    near_gate, near_up = gather_near(own_gate), gather_near(own_up)
+    if near:
+        returned = all_to_all(reorder(out_rows, owner_index ^ (2 * me), 8), experts)
     else:
         returned = all_to_all(reorder(out_rows, me, 4), experts)
+    hidden, returned, near_gate = after((hidden, returned, near_gate))
+    if near:
+        returned = swap_back(reorder(returned, owner_index, 8))
+    gate_rows = gather_far(own_gate, *near_gate)
+    up_rows = gather_far(own_up, *near_up)
     picked_0 = jnp.dot(place_0, returned, preferred_element_type=F32)
     picked_1 = jnp.dot(place_1, returned, preferred_element_type=F32)
     output = (route_weights[:, :1] * picked_0 + route_weights[:, 1:] * picked_1).astype(BF)
@@ -225,7 +219,7 @@
     def term(left, right):
         return lax.dot_general(left, right, CONTRACT_ROWS, preferred_element_type=F32).astype(BF)
 
-    grad_terms = (term(grad_gate_rows, in_rows), term(grad_up_rows, in_rows), term(hidden, cot_rows))
+    grad_terms = (term(gate_rows, in_rows), term(up_rows, in_rows), term(hidden, cot_rows))
     for bit_index in range(levels):
         partner = from_partner(grad_terms, "expert", bit_index)
         grad_terms = tuple(add_round(own, their) for own, their in zip(grad_terms, partner))

time: 114 us -> 132 us (1.16)
  other arithmetic: 2.05 us -> 9.9 us
  local copies, waits for them, and re-layouts: 1.42 us -> 6.82 us
  matrix products: 20.5 us -> 24.8 us
  starting transfers between devices: 43.9 us -> 40.6 us
  waiting for transfers between devices: 44.7 us -> 47.4 us
    ppermute x28, starting transfers between devices: 43.9 us -> 30.5 us  [swap(): return lax.ppermute(block, axis, [(i, i ^ mask) for i in range(count)])]
    all_to_all x0 -> x2, starting transfers between devices: none -> 10.1 us  [all_to_all(): lax.all_to_all(rows.reshape(experts, rows.shape[0] // experts, rows.shape...]
    concatenate x6, other arithmetic: 0.24 us -> 5.27 us  [the longest x3 2.59 us: scatter_far(): jnp.concatenate([part[n:2 * n, :c], add_round(part[n:2 * n, c:], via_y)],...]
    slice x12 -> x9, local copies, waits for them, and re-layouts: 0.33 us -> 3.71 us  [the longest x3 1.96 us: gather_far(): far_second = swap(from_x[:, c:], 'dp', 2)]
    ppermute x28, waiting for transfers between devices: 44.7 us -> 47.4 us  [swap(): return lax.ppermute(block, axis, [(i, i ^ mask) for i in range(count)])]
    dot_general x3, matrix products: 4.2 us -> 6.49 us  [partial_product(): lax.dot_general(rows, weights, CONTRACT_FEATS, preferred_element_type=F32)]
    unnamed x16 -> x90, local copies, waits for them, and re-layouts: 0.71 us -> 2.8 us
    convert_element_type x1, other arithmetic: 0.33 us -> 1.91 us  [per_device(): own_up = (grad_hidden * active).astype(BF)]
  transfers between devices with their start and end apart: 28 -> 30, of which waited for: 18 -> 15; matrix products, arithmetic and copies ran while one was open for 17% -> 19% of each run, Pallas kernels for 0% -> 0%
where the time goes in v2:
time: 132 us; the launch traced here: 131 us
  waiting for transfers between devices  47.4 us (36%)
  starting transfers between devices  40.6 us (31%)
  matrix products  24.8 us (19%)
  other arithmetic  9.9 us (8%)
  local copies, waits for them, and re-layouts  6.82 us (5%)
  between operations  1.5 us (1%)
    ppermute x28, waiting for transfers between devices, swap(): return lax.ppermute(block, axis, [(i, i ^ mask) for i in range(count)])  47.4 us
    ppermute x28, starting transfers between devices, swap(): return lax.ppermute(block, axis, [(i, i ^ mask) for i in range(count)])  30.5 us
    dot_general x3, matrix products, term(): lax.dot_general(left, right, CONTRACT_ROWS, preferred_element_type=F32)  12.8 us
    all_to_all x2, starting transfers between devices, all_to_all(): lax.all_to_all(rows.reshape(experts, rows.shape[0] // experts, rows.shape...  10.1 us
    dot_general x3, matrix products, partial_product(): lax.dot_general(rows, weights, CONTRACT_FEATS, preferred_element_type=F32)  6.49 us
    unnamed x90, local copies, waits for them, and re-layouts  2.8 us
  transfers between devices with their start and end apart: 30, of which 15 were waited for; matrix products, arithmetic and copies ran while one was open for 19% of the time, Pallas kernels for 0%

profile of v2, /device:TPU:0, one launch (start us, length us, event | category | flops | bytes accessed | tf_op | source)
XLA Modules:
  0.0 131.1 jit_solution(6955976879076410561)
XLA Ops:
  3.9 3.0 %collective-permute-start.1 = (bf16[80,1024]{1,0:T(8,128)(2,1)S(1)}, bf16[80,1024]{1,0:T(8,128)(2,1)S(1)}, u32[]{:S(2)}, u32[]{:S(2)}) collective-permute-start(bf16[80,1024]{1,0:T(8,128)(2,1)S(1)} %pad_maximum_fusion.7), channel_id=1, source_target_pairs={{0,2},{1,3},{2,0},{3,1},{4,6},{5,7},{6,4},{7,5},{8,10},{9,11},{10,... | collective-permute-start | bytes 491528 | tf_op jit(solution)/shard_map/ppermute | solution.py:30
  6.9 2.6 %collective-permute-start.2 = (bf16[80,1024]{1,0:T(8,128)(2,1)S(1)}, bf16[80,1024]{1,0:T(8,128)(2,1)S(1)}, u32[]{:S(2)}, u32[]{:S(2)}) collective-permute-start(bf16[80,1024]{1,0:T(8,128)(2,1)S(1)} %pad_maximum_fusion.8), channel_id=1, source_target_pairs={{0,4},{1,5},{2,6},{3,7},{4,0},{5,1},{6,2},{7,3},{8,12},{9,13},{10,... | collective-permute-start | bytes 491528 | tf_op jit(solution)/shard_map/ppermute | solution.py:30
  9.7 4.6 %collective-permute-done.1 = bf16[80,1024]{1,0:T(8,128)(2,1)S(1)} collective-permute-done((bf16[80,1024]{1,0:T(8,128)(2,1)S(1)}, bf16[80,1024]{1,0:T(8,128)(2,1)S(1)}, u32[]{:S(2)}, u32[]{:S(2)}) %collective-permute-start.1) | collective-permute-done | bytes 163872 | tf_op jit(solution)/shard_map/ppermute | solution.py:30
  14.3 7.7 %collective-permute-done.2 = bf16[80,1024]{1,0:T(8,128)(2,1)S(1)} collective-permute-done((bf16[80,1024]{1,0:T(8,128)(2,1)S(1)}, bf16[80,1024]{1,0:T(8,128)(2,1)S(1)}, u32[]{:S(2)}, u32[]{:S(2)}) %collective-permute-start.2) | collective-permute-done | bytes 163872 | tf_op jit(solution)/shard_map/ppermute | solution.py:30
  26.5 1.5 %collective-permute-start.6 = (bf16[80,896]{1,0:T(8,128)(2,1)S(1)}, bf16[80,896]{1,0:T(8,128)(2,1)S(1)}, u32[]{:S(2)}, u32[]{:S(2)}) collective-permute-start(bf16[80,896]{1,0:T(8,128)(2,1)S(1)} %get-tuple-element.36), channel_id=1, source_target_pairs={{0,8},{8,0},{16,24},{24,16},{1,9},{9,1},{17,25},{25,17},{2,10},{10... | collective-permute-start | bytes 430088 | tf_op jit(solution)/shard_map/ppermute | solution.py:30
  28.0 1.5 %collective-permute-start.4 = (bf16[80,896]{1,0:T(8,128)(2,1)S(1)}, bf16[80,896]{1,0:T(8,128)(2,1)S(1)}, u32[]{:S(2)}, u32[]{:S(2)}) collective-permute-start(bf16[80,896]{1,0:T(8,128)(2,1)S(1)} %get-tuple-element.37), channel_id=1, source_target_pairs={{0,16},{8,24},{16,0},{24,8},{1,17},{9,25},{17,1},{25,9},{2,18},{10... | collective-permute-start | bytes 430088 | tf_op jit(solution)/shard_map/ppermute | solution.py:30
  30.7 2.1 %collective-permute-done.6 = bf16[80,896]{1,0:T(8,128)(2,1)S(1)} collective-permute-done((bf16[80,896]{1,0:T(8,128)(2,1)S(1)}, bf16[80,896]{1,0:T(8,128)(2,1)S(1)}, u32[]{:S(2)}, u32[]{:S(2)}) %collective-permute-start.6) | collective-permute-done | bytes 143392 | tf_op jit(solution)/shard_map/ppermute | solution.py:30
  34.6 1.5 %collective-permute-start.7 = (bf16[80,1792]{1,0:T(8,128)(2,1)}, bf16[80,1792]{1,0:T(8,128)(2,1)S(1)}, u32[]{:S(2)}, u32[]{:S(2)}) collective-permute-start(bf16[80,1792]{1,0:T(8,128)(2,1)} %pad_maximum_fusion.2), channel_id=1, source_target_pairs={{0,16},{8,24},{16,0},{24,8},{1,17},{9,25},{17,1},{25,9},{2,18},{10... | collective-permute-start | bytes 860168 | tf_op jit(solution)/shard_map/ppermute | solution.py:30
  37.5 5.8 %all-to-all-start = ((bf16[8,40,1024]{2,1,0:T(8,128)(2,1)}), bf16[8,40,1024]{2,1,0:T(8,128)(2,1)S(1)}, u32[]{:S(2)}, u32[]{:S(2)}) async-start(bf16[8,40,1024]{2,1,0:T(8,128)(2,1)} %bitcast.132), calls=%async_computation | async-start | bytes 1310720 | tf_op jit(solution)/shard_map/all_to_all | solution.py:60
  46.9 7.0 %collective-permute-done.5 = bf16[80,1792]{1,0:T(8,128)(2,1)S(1)} collective-permute-done((bf16[80,1792]{1,0:T(8,128)(2,1)S(1)}, bf16[80,1792]{1,0:T(8,128)(2,1)S(1)}, u32[]{:S(2)}, u32[]{:S(2)}) %collective-permute-start.5) | collective-permute-done | bytes 286752 | tf_op jit(solution)/shard_map/ppermute | solution.py:30
  53.9 5.8 %collective-permute-done.10 = bf16[80,1792]{1,0:T(8,128)(2,1)S(1)} collective-permute-done((bf16[80,1792]{1,0:T(8,128)(2,1)}, bf16[80,1792]{1,0:T(8,128)(2,1)S(1)}, u32[]{:S(2)}, u32[]{:S(2)}) %collective-permute-start.10) | collective-permute-done | bytes 286752 | tf_op jit(solution)/shard_map/ppermute | solution.py:30
  62.1 7.5 %collective-permute-done.13 = bf16[80,1792]{1,0:T(8,128)(2,1)} collective-permute-done((bf16[80,1792]{1,0:T(8,128)(2,1)}, bf16[80,1792]{1,0:T(8,128)(2,1)}, u32[]{:S(2)}, u32[]{:S(2)}) %collective-permute-start.13) | collective-permute-done | bytes 286752 | tf_op jit(solution)/shard_map/ppermute | solution.py:30
  72.5 1.7 %collective-permute-start.15 = (bf16[80,896]{1,0:T(8,128)(2,1)S(1)}, bf16[80,896]{1,0:T(8,128)(2,1)S(1)}, u32[]{:S(2)}, u32[]{:S(2)}) collective-permute-start(bf16[80,896]{1,0:T(8,128)(2,1)S(1)} %slice.157), channel_id=1, source_target_pairs={{0,16},{8,24},{16,0},{24,8},{1,17},{9,25},{17,1},{25,9},{2,18},{10... | collective-permute-start | bytes 430088 | tf_op jit(solution)/shard_map/ppermute | solution.py:30
  74.3 3.7 %convolution_convert_fusion.3 = bf16[320,1792]{1,0:T(8,128)(2,1)S(1)} fusion(bf16[320,1024]{1,0:T(8,128)(2,1)S(1)} %bitcast_dynamic-update-slice_fusion.8, bf16[1792,1024]{1,0:T(8,128)(2,1)} %param.12), kind=kOutput, calls=%fused_computation.3 | convolution fusion | flops 1174978560 | bytes 5472256 | tf_op jit(solution)/shard_map/dot_general | solution.py:181
  79.9 2.6 %convolution_convert_fusion.7 = bf16[320,1024]{1,0:T(8,128)(2,1)S(1)} fusion(bf16[1792,1024]{1,0:T(8,128)(2,1)S(1)} %copy-done.29, bf16[80,896]{1,0:T(8,128)(2,1)S(1)} %collective-permute-done.15, bf16[80,896]{1,0:T(8,128)(2,1)S(1)} %collective-permute-done.14, bf16[80,1792]{1,0:T(8,128)(2,1)} %collective-permute-done.13, ...), kind=kOutput, calls=%fused_computation.9 | convolution fusion | flops 1180467200 | bytes 5472256 | tf_op jit(solution)/shard_map/dot_general | solution.py:200
  88.1 4.3 %all-to-all-start.1 = ((bf16[8,40,1024]{2,1,0:T(8,128)(2,1)}), bf16[8,40,1024]{2,1,0:T(8,128)(2,1)S(1)}, u32[]{:S(2)}, u32[]{:S(2)}) async-start(bf16[8,40,1024]{2,1,0:T(8,128)(2,1)} %bitcast.130), calls=%async_computation.1 | async-start | bytes 1310720 | tf_op jit(solution)/shard_map/all_to_all | solution.py:60
  93.5 1.9 %multiply_convert_fusion = (bf16[80,1792]{1,0:T(8,128)(2,1)S(1)}, bf16[80,1792]{1,0:T(8,128)(2,1)S(1)}) fusion(bf16[80,1792]{1,0:T(8,128)(2,1)} %collective-permute-done.19, bf16[80,1792]{1,0:T(8,128)(2,1)} %collective-permute-done.17, bf16[320,1792]{1,0:T(8,128)(2,1)} %copy-done.1, bf16[80,1792]{1,0:T(8,128)(2,1)S(1)} %collective-permute-done.7, ...), kind=kLoop, calls=%fused_computation.36 | loop fusion | flops 4014080 | bytes 3153920 | tf_op jit(solution)/shard_map/convert_element_type | solution.py:204
  95.4 1.5 %collective-permute-start.25 = (bf16[80,1792]{1,0:T(8,128)(2,1)S(1)}, bf16[80,1792]{1,0:T(8,128)(2,1)S(1)}, u32[]{:S(2)}, u32[]{:S(2)}) collective-permute-start(bf16[80,1792]{1,0:T(8,128)(2,1)S(1)} %get-tuple-element.26), channel_id=1, source_target_pairs={{0,16},{8,24},{16,0},{24,8},{1,17},{9,25},{17,1},{25,9},{2,18},{10... | collective-permute-start | bytes 860168 | tf_op jit(solution)/shard_map/ppermute | solution.py:30
  97.9 6.0 %collective-permute-done.25 = bf16[80,1792]{1,0:T(8,128)(2,1)S(1)} collective-permute-done((bf16[80,1792]{1,0:T(8,128)(2,1)S(1)}, bf16[80,1792]{1,0:T(8,128)(2,1)S(1)}, u32[]{:S(2)}, u32[]{:S(2)}) %collective-permute-start.25) | collective-permute-done | bytes 286752 | tf_op jit(solution)/shard_map/ppermute | solution.py:30
  105.4 1.5 %collective-permute-start.27 = (bf16[80,896]{1,0:T(8,128)(2,1)S(1)}, bf16[80,896]{1,0:T(8,128)(2,1)S(1)}, u32[]{:S(2)}, u32[]{:S(2)}) collective-permute-start(bf16[80,896]{1,0:T(8,128)(2,1)S(1)} %slice.200), channel_id=1, source_target_pairs={{0,16},{8,24},{16,0},{24,8},{1,17},{9,25},{17,1},{25,9},{2,18},{10... | collective-permute-start | bytes 430088 | tf_op jit(solution)/shard_map/ppermute | solution.py:30
  109.8 1.9 %collective-permute-done.27 = bf16[80,896]{1,0:T(8,128)(2,1)S(1)} collective-permute-done((bf16[80,896]{1,0:T(8,128)(2,1)S(1)}, bf16[80,896]{1,0:T(8,128)(2,1)S(1)}, u32[]{:S(2)}, u32[]{:S(2)}) %collective-permute-start.27) | collective-permute-done | bytes 143392 | tf_op jit(solution)/shard_map/ppermute | solution.py:30
  111.7 4.0 %convolution_convert_fusion.1 = bf16[1792,1024]{1,0:T(8,128)(2,1)} fusion(bf16[80,896]{1,0:T(8,128)(2,1)S(1)} %collective-permute-done.27, bf16[80,896]{1,0:T(8,128)(2,1)S(1)} %collective-permute-done.26, bf16[80,1792]{1,0:T(8,128)(2,1)S(1)} %collective-permute-done.25, bf16[80,1792]{1,0:T(8,128)(2,1)S(1)} %collective-permute-done.24, ...), kind=kOutput, calls=%fused_computation.1 | convolution fusion | flops 1184595968 | bytes 5472256 | tf_op jit(solution)/shard_map/dot_general | solution.py:220
  121.1 3.9 %convolution_convert_fusion = bf16[1792,1024]{1,0:T(8,128)(2,1)} fusion(bf16[320,1792]{1,0:T(8,128)(2,1)S(1)} %maximum_maximum_fusion, bf16[320,1024]{1,0:T(8,128)(2,1)S(1)} %copy-done.25), kind=kOutput, calls=%fused_computation | convolution fusion | flops 1176240128 | bytes 5472256 | tf_op jit(solution)/shard_map/dot_general | solution.py:220
  126.1 4.9 %convolution_convert_fusion.2 = bf16[1792,1024]{1,0:T(8,128)(2,1)} fusion(bf16[80,896]{1,0:T(8,128)(2,1)S(1)} %collective-permute-done.23, bf16[80,896]{1,0:T(8,128)(2,1)S(1)} %collective-permute-done.22, bf16[80,1792]{1,0:T(8,128)(2,1)S(1)} %copy-done.23, bf16[80,1792]{1,0:T(8,128)(2,1)} %collective-permute-done.20, bf16[80,1792]{1,0:T(8,128)(2,1)S(1)} %copy-done.9, ...), kind=kOutput, calls=%fused_computation.2 | convolution fusion | flops 1184595968 | bytes 5472256 | tf_op jit(solution)/shard_map/dot_general | solution.py:220
  (177 shorter events, 41.0 us)
Async XLA Ops:
  3.9 10.3 %collective-permute-start.1 = (bf16[80,1024]{1,0:T(8,128)(2,1)S(1)}, bf16[80,1024]{1,0:T(8,128)(2,1)S(1)}, u32[]{:S(2)}, u32[]{:S(2)}) collective-permute-start(bf16[80,1024]{1,0:T(8,128)(2,1)S(1)} %pad_maximum_fusion.7), channel_id=1, source_target_pairs={{0,2},{1,3},{2,0},{3,1},{4,6},{5,7},{6,4},{7,5},{8,10},{9,11},{10,... | collective-permute-start | bytes 491528 | tf_op jit(solution)/shard_map/ppermute | solution.py:30
  6.9 15.1 %collective-permute-start.2 = (bf16[80,1024]{1,0:T(8,128)(2,1)S(1)}, bf16[80,1024]{1,0:T(8,128)(2,1)S(1)}, u32[]{:S(2)}, u32[]{:S(2)}) collective-permute-start(bf16[80,1024]{1,0:T(8,128)(2,1)S(1)} %pad_maximum_fusion.8), channel_id=1, source_target_pairs={{0,4},{1,5},{2,6},{3,7},{4,0},{5,1},{6,2},{7,3},{8,12},{9,13},{10,... | collective-permute-start | bytes 491528 | tf_op jit(solution)/shard_map/ppermute | solution.py:30
  9.6 12.4 %collective-permute-start.3 = (bf16[80,1024]{1,0:T(8,128)(2,1)S(1)}, bf16[80,1024]{1,0:T(8,128)(2,1)S(1)}, u32[]{:S(2)}, u32[]{:S(2)}) collective-permute-start(bf16[80,1024]{1,0:T(8,128)(2,1)S(1)} %pad_maximum_fusion.9), channel_id=1, source_target_pairs={{0,6},{1,7},{2,4},{3,5},{4,2},{5,3},{6,0},{7,1},{8,14},{9,15},{10,... | collective-permute-start | bytes 491528 | tf_op jit(solution)/shard_map/ppermute | solution.py:30
  29.6 6.5 %collective-permute-start.9 = (bf16[80,896]{1,0:T(8,128)(2,1)S(1)}, bf16[80,896]{1,0:T(8,128)(2,1)S(1)}, u32[]{:S(2)}, u32[]{:S(2)}) collective-permute-start(bf16[80,896]{1,0:T(8,128)(2,1)S(1)} %get-tuple-element.42), channel_id=1, source_target_pairs={{0,8},{8,0},{16,24},{24,16},{1,9},{9,1},{17,25},{25,17},{2,10},{10... | collective-permute-start | bytes 430088 | tf_op jit(solution)/shard_map/ppermute | solution.py:30
  30.2 6.4 %collective-permute-start.8 = (bf16[80,896]{1,0:T(8,128)(2,1)S(1)}, bf16[80,896]{1,0:T(8,128)(2,1)S(1)}, u32[]{:S(2)}, u32[]{:S(2)}) collective-permute-start(bf16[80,896]{1,0:T(8,128)(2,1)S(1)} %get-tuple-element.44), channel_id=1, source_target_pairs={{0,16},{8,24},{16,0},{24,8},{1,17},{9,25},{17,1},{25,9},{2,18},{10... | collective-permute-start | bytes 430088 | tf_op jit(solution)/shard_map/ppermute | solution.py:30
  34.6 12.4 %collective-permute-start.7 = (bf16[80,1792]{1,0:T(8,128)(2,1)}, bf16[80,1792]{1,0:T(8,128)(2,1)S(1)}, u32[]{:S(2)}, u32[]{:S(2)}) collective-permute-start(bf16[80,1792]{1,0:T(8,128)(2,1)} %pad_maximum_fusion.2), channel_id=1, source_target_pairs={{0,16},{8,24},{16,0},{24,8},{1,17},{9,25},{17,1},{25,9},{2,18},{10... | collective-permute-start | bytes 860168 | tf_op jit(solution)/shard_map/ppermute | solution.py:30
  37.5 32.4 %all-to-all-start = ((bf16[8,40,1024]{2,1,0:T(8,128)(2,1)}), bf16[8,40,1024]{2,1,0:T(8,128)(2,1)S(1)}, u32[]{:S(2)}, u32[]{:S(2)}) async-start(bf16[8,40,1024]{2,1,0:T(8,128)(2,1)} %bitcast.132), calls=%async_computation | async-start | bytes 1310720 | tf_op jit(solution)/shard_map/all_to_all | solution.py:60
  44.2 9.7 %collective-permute-start.5 = (bf16[80,1792]{1,0:T(8,128)(2,1)S(1)}, bf16[80,1792]{1,0:T(8,128)(2,1)S(1)}, u32[]{:S(2)}, u32[]{:S(2)}) collective-permute-start(bf16[80,1792]{1,0:T(8,128)(2,1)S(1)} %pad_maximum_fusion.1), channel_id=1, source_target_pairs={{0,8},{8,0},{16,24},{24,16},{1,9},{9,1},{17,25},{25,17},{2,10},{10... | collective-permute-start | bytes 860168 | tf_op jit(solution)/shard_map/ppermute | solution.py:30
  45.3 14.4 %collective-permute-start.10 = (bf16[80,1792]{1,0:T(8,128)(2,1)}, bf16[80,1792]{1,0:T(8,128)(2,1)S(1)}, u32[]{:S(2)}, u32[]{:S(2)}) collective-permute-start(bf16[80,1792]{1,0:T(8,128)(2,1)} %get-tuple-element.14), channel_id=1, source_target_pairs={{0,8},{8,0},{16,24},{24,16},{1,9},{9,1},{17,25},{25,17},{2,10},{10... | collective-permute-start | bytes 860168 | tf_op jit(solution)/shard_map/ppermute | solution.py:30
  46.3 13.4 %collective-permute-start.11 = (bf16[80,1792]{1,0:T(8,128)(2,1)}, bf16[80,1792]{1,0:T(8,128)(2,1)S(1)}, u32[]{:S(2)}, u32[]{:S(2)}) collective-permute-start(bf16[80,1792]{1,0:T(8,128)(2,1)} %get-tuple-element.15), channel_id=1, source_target_pairs={{0,16},{8,24},{16,0},{24,8},{1,17},{9,25},{17,1},{25,9},{2,18},{10... | collective-permute-start | bytes 860168 | tf_op jit(solution)/shard_map/ppermute | solution.py:30
  60.7 8.8 %collective-permute-start.13 = (bf16[80,1792]{1,0:T(8,128)(2,1)}, bf16[80,1792]{1,0:T(8,128)(2,1)}, u32[]{:S(2)}, u32[]{:S(2)}) collective-permute-start(bf16[80,1792]{1,0:T(8,128)(2,1)} %multiply_convert_fusion.2), channel_id=1, source_target_pairs={{0,16},{8,24},{16,0},{24,8},{1,17},{9,25},{17,1},{25,9},{2,18},{10... | collective-permute-start | bytes 860168 | tf_op jit(solution)/shard_map/ppermute | solution.py:30
  61.3 8.5 %collective-permute-start.12 = (bf16[80,1792]{1,0:T(8,128)(2,1)}, bf16[80,1792]{1,0:T(8,128)(2,1)}, u32[]{:S(2)}, u32[]{:S(2)}) collective-permute-start(bf16[80,1792]{1,0:T(8,128)(2,1)} %multiply_convert_fusion.2), channel_id=1, source_target_pairs={{0,8},{8,0},{16,24},{24,16},{1,9},{9,1},{17,25},{25,17},{2,10},{10... | collective-permute-start | bytes 860168 | tf_op jit(solution)/shard_map/ppermute | solution.py:30
  71.7 8.2 %collective-permute-start.14 = (bf16[80,896]{1,0:T(8,128)(2,1)S(1)}, bf16[80,896]{1,0:T(8,128)(2,1)S(1)}, u32[]{:S(2)}, u32[]{:S(2)}) collective-permute-start(bf16[80,896]{1,0:T(8,128)(2,1)S(1)} %slice.156), channel_id=1, source_target_pairs={{0,8},{8,0},{16,24},{24,16},{1,9},{9,1},{17,25},{25,17},{2,10},{10... | collective-permute-start | bytes 430088 | tf_op jit(solution)/shard_map/ppermute | solution.py:30
  72.5 7.4 %collective-permute-start.15 = (bf16[80,896]{1,0:T(8,128)(2,1)S(1)}, bf16[80,896]{1,0:T(8,128)(2,1)S(1)}, u32[]{:S(2)}, u32[]{:S(2)}) collective-permute-start(bf16[80,896]{1,0:T(8,128)(2,1)S(1)} %slice.157), channel_id=1, source_target_pairs={{0,16},{8,24},{16,0},{24,8},{1,17},{9,25},{17,1},{25,9},{2,18},{10... | collective-permute-start | bytes 430088 | tf_op jit(solution)/shard_map/ppermute | solution.py:30
  85.2 7.3 %collective-permute-start.19 = (bf16[80,1792]{1,0:T(8,128)(2,1)}, bf16[80,1792]{1,0:T(8,128)(2,1)}, u32[]{:S(2)}, u32[]{:S(2)}) collective-permute-start(bf16[80,1792]{1,0:T(8,128)(2,1)} %pad_maximum_fusion.6), channel_id=1, source_target_pairs={{0,16},{8,24},{16,0},{24,8},{1,17},{9,25},{17,1},{25,9},{2,18},{10... | collective-permute-start | bytes 860168 | tf_op jit(solution)/shard_map/ppermute | solution.py:30
  86.5 7.0 %collective-permute-start.17 = (bf16[80,1792]{1,0:T(8,128)(2,1)}, bf16[80,1792]{1,0:T(8,128)(2,1)}, u32[]{:S(2)}, u32[]{:S(2)}) collective-permute-start(bf16[80,1792]{1,0:T(8,128)(2,1)} %pad_maximum_fusion.5), channel_id=1, source_target_pairs={{0,8},{8,0},{16,24},{24,16},{1,9},{9,1},{17,25},{25,17},{2,10},{10... | collective-permute-start | bytes 860168 | tf_op jit(solution)/shard_map/ppermute | solution.py:30
  88.1 28.6 %all-to-all-start.1 = ((bf16[8,40,1024]{2,1,0:T(8,128)(2,1)}), bf16[8,40,1024]{2,1,0:T(8,128)(2,1)S(1)}, u32[]{:S(2)}, u32[]{:S(2)}) async-start(bf16[8,40,1024]{2,1,0:T(8,128)(2,1)} %bitcast.130), calls=%async_computation.1 | async-start | bytes 1310720 | tf_op jit(solution)/shard_map/all_to_all | solution.py:60
  95.4 8.5 %collective-permute-start.25 = (bf16[80,1792]{1,0:T(8,128)(2,1)S(1)}, bf16[80,1792]{1,0:T(8,128)(2,1)S(1)}, u32[]{:S(2)}, u32[]{:S(2)}) collective-permute-start(bf16[80,1792]{1,0:T(8,128)(2,1)S(1)} %get-tuple-element.26), channel_id=1, source_target_pairs={{0,16},{8,24},{16,0},{24,8},{1,17},{9,25},{17,1},{25,9},{2,18},{10... | collective-permute-start | bytes 860168 | tf_op jit(solution)/shard_map/ppermute | solution.py:30
  96.9 8.5 %collective-permute-start.24 = (bf16[80,1792]{1,0:T(8,128)(2,1)S(1)}, bf16[80,1792]{1,0:T(8,128)(2,1)S(1)}, u32[]{:S(2)}, u32[]{:S(2)}) collective-permute-start(bf16[80,1792]{1,0:T(8,128)(2,1)S(1)} %get-tuple-element.26), channel_id=1, source_target_pairs={{0,8},{8,0},{16,24},{24,16},{1,9},{9,1},{17,25},{25,17},{2,10},{10... | collective-permute-start | bytes 860168 | tf_op jit(solution)/shard_map/ppermute | solution.py:30
  105.4 6.3 %collective-permute-start.27 = (bf16[80,896]{1,0:T(8,128)(2,1)S(1)}, bf16[80,896]{1,0:T(8,128)(2,1)S(1)}, u32[]{:S(2)}, u32[]{:S(2)}) collective-permute-start(bf16[80,896]{1,0:T(8,128)(2,1)S(1)} %slice.200), channel_id=1, source_target_pairs={{0,16},{8,24},{16,0},{24,8},{1,17},{9,25},{17,1},{25,9},{2,18},{10... | collective-permute-start | bytes 430088 | tf_op jit(solution)/shard_map/ppermute | solution.py:30
  108.1 8.6 %collective-permute-start.21 = (bf16[80,1792]{1,0:T(8,128)(2,1)S(1)}, bf16[80,1792]{1,0:T(8,128)(2,1)S(1)}, u32[]{:S(2)}, u32[]{:S(2)}) collective-permute-start(bf16[80,1792]{1,0:T(8,128)(2,1)S(1)} %get-tuple-element.27), channel_id=1, source_target_pairs={{0,16},{8,24},{16,0},{24,8},{1,17},{9,25},{17,1},{25,9},{2,18},{10... | collective-permute-start | bytes 860168 | tf_op jit(solution)/shard_map/ppermute | solution.py:30
  108.8 7.9 %collective-permute-start.20 = (bf16[80,1792]{1,0:T(8,128)(2,1)S(1)}, bf16[80,1792]{1,0:T(8,128)(2,1)}, u32[]{:S(2)}, u32[]{:S(2)}) collective-permute-start(bf16[80,1792]{1,0:T(8,128)(2,1)S(1)} %get-tuple-element.27), channel_id=1, source_target_pairs={{0,8},{8,0},{16,24},{24,16},{1,9},{9,1},{17,25},{25,17},{2,10},{10... | collective-permute-start | bytes 860168 | tf_op jit(solution)/shard_map/ppermute | solution.py:30
  117.8 8.3 %collective-permute-start.22 = (bf16[80,896]{1,0:T(8,128)(2,1)S(1)}, bf16[80,896]{1,0:T(8,128)(2,1)S(1)}, u32[]{:S(2)}, u32[]{:S(2)}) collective-permute-start(bf16[80,896]{1,0:T(8,128)(2,1)S(1)} %slice.165), channel_id=1, source_target_pairs={{0,8},{8,0},{16,24},{24,16},{1,9},{9,1},{17,25},{25,17},{2,10},{10... | collective-permute-start | bytes 430088 | tf_op jit(solution)/shard_map/ppermute | solution.py:30
  118.9 7.2 %collective-permute-start.23 = (bf16[80,896]{1,0:T(8,128)(2,1)S(1)}, bf16[80,896]{1,0:T(8,128)(2,1)S(1)}, u32[]{:S(2)}, u32[]{:S(2)}) collective-permute-start(bf16[80,896]{1,0:T(8,128)(2,1)S(1)} %slice.166), channel_id=1, source_target_pairs={{0,16},{8,24},{16,0},{24,8},{1,17},{9,25},{17,1},{25,9},{2,18},{10... | collective-permute-start | bytes 430088 | tf_op jit(solution)/shard_map/ppermute | solution.py:30
  (36 other events, 181.0 us)

commit v3 on v1

--- a/solution.py
+++ b/solution.py
@@ -30,8 +30,13 @@
     return lax.ppermute(block, axis, [(i, i ^ mask) for i in range(count)])
 
 
-def after(value, *earlier):
-    return lax.optimization_barrier((value, earlier))[0]
+def after(values):
+    return lax.optimization_barrier(values)
+
+
+def after_start(value, earlier):
+    value, column = after((value, earlier))
+    return value, 0.0 * column.astype(F32)
 
 
 def silu_parts(gate_sum):
@@ -77,23 +82,44 @@
     blocks = [
         jnp.concatenate([own[m * n:(m + 1) * n], other[m * n:(m + 1) * n]], axis=0) for m in range(4)
     ]
-    return jnp.concatenate(
-        [blocks[0]] + [swap(blocks[m], "expert", 2 * m) for m in range(1, 4)], axis=0
-    )
-
-
-def from_chips(rows, *earlier):
+    return [blocks[0]] + [swap(blocks[m], "expert", 2 * m) for m in range(1, 4)]
+
+
+def to_chips_first(rows):
     n = rows.shape[0] // 8
-    blocks = [rows[2 * m * n:2 * (m + 1) * n] for m in range(4)]
-    back = after([blocks[0]] + [swap(blocks[m], "expert", 2 * m) for m in range(1, 4)], *earlier)
+    blocks = [
+        jnp.concatenate([rows[m * n:(m + 1) * n], rows[(4 + m) * n:(5 + m) * n]], axis=0) for m in range(4)
+    ]
+    return [blocks[0]] + [swap(blocks[m], "expert", 2 * m) for m in range(1, 4)]
+
+
+def core_last(got):
+    n = got[0].shape[0] // 2
+    other = swap(jnp.concatenate([each[n:] for each in got], axis=0), "expert", 1)
+    rows = []
+    for m, each in enumerate(got):
+        rows += [each[:n], other[m * n:(m + 1) * n]]
+    return rows
+
+
+def from_chips(rows):
+    n = rows.shape[0] // 4
+    return [rows[:n]] + [swap(rows[m * n:(m + 1) * n], "expert", 2 * m) for m in range(1, 4)]
+
+
+def from_core(back):
+    n = back[0].shape[0] // 2
     other = swap(jnp.concatenate([each[n:] for each in back], axis=0), "expert", 1)
     return jnp.concatenate([each[:n] for each in back] + [other], axis=0)
 
 
 def scatter_far(first, second):
     n = first.shape[0] // 4
-    via_x = swap(first[3 * n:], "dp", 1)
-    via_y = swap(second[3 * n:], "dp", 2)
+    return swap(first[3 * n:], "dp", 1), swap(second[3 * n:], "dp", 2)
+
+
+def scatter_add(first, second, via_x, via_y):
+    n = first.shape[0] // 4
     to_x = jnp.concatenate([first[n:2 * n], add_round(second[n:2 * n], via_y)], axis=1)
     to_y = jnp.concatenate([add_round(first[2 * n:3 * n], via_x), second[2 * n:3 * n]], axis=1)
     return to_x, to_y
@@ -173,13 +199,13 @@
         + lax.dot_general(place_1, cot_1, CONTRACT_ROWS, preferred_element_type=F32)
     ).astype(BF)
     if near:
-        in_rows = reorder(to_chips(*pair_core(send_rows)), me, 4)
-        own_cot, other_cot = pair_core(cot_send)
-        own_cot, other_cot = after((own_cot, other_cot), in_rows)
-        cot_rows = reorder(to_chips(own_cot, other_cot), me, 4)
+        in_rows = to_chips(*pair_core(send_rows))
+        cot_send, in_rows = after((cot_send, in_rows))
+        cot_rows = to_chips_first(cot_send)
     else:
-        in_rows = reorder(all_to_all(send_rows, experts), me, 4)
-        cot_rows = reorder(all_to_all(cot_send, experts), me, 4)
+        in_rows = [all_to_all(send_rows, experts)]
+        cot_rows = [all_to_all(cot_send, experts)]
+    in_rows = reorder(jnp.concatenate(in_rows, axis=0), me, 4)
 
     pieces = (w_gate, w_up, w_down)
     for bit_index in range(levels):
@@ -193,31 +219,35 @@
 
     half = gate_w.shape[0] // 2
     part_gate, part_up = partial_product(in_rows, gate_w), partial_product(in_rows, up_w)
-    to_x, to_y = scatter_far(part_gate, part_up)
+    to_x, to_y = scatter_add(part_gate, part_up, *scatter_far(part_gate, part_up))
     gate_sum, up_sum = scatter_near(part_gate, part_up, to_x, to_y)
-    cot_rows = after(cot_rows, gate_sum, up_sum)
+    cot_rows, zeros = after_start(cot_rows, to_x[:, -1:] + to_y[:, :1])
+    if near:
+        cot_rows = core_last(cot_rows)
+    cot_rows = reorder(jnp.concatenate(cot_rows, axis=0), me, 4)
 
     active, slope_term = silu_parts(gate_sum)
     own_hidden = (active * up_sum).astype(BF)
+
+    part_hidden = partial_product(cot_rows, down_w)
+    part_first, part_second = part_hidden[:, :half], part_hidden[:, half:]
+    via, more_zeros = after_start(scatter_far(part_first, part_second), own_hidden[:, :1])
+    to_x, to_y = scatter_add(part_first, part_second, *via)
     own_hidden = (own_hidden[:, :half], own_hidden[:, half:])
     near_hidden = gather_near(*own_hidden)
-
-    part_hidden = partial_product(cot_rows, down_w)
-    part_first, part_second = part_hidden[:, :half], part_hidden[:, half:]
-    to_x, to_y = scatter_far(part_first, part_second)
-    to_x, to_y = after((to_x, to_y), near_hidden)
     hidden = jnp.concatenate(gather_far(*own_hidden, *near_hidden), axis=1)
-    grad_hidden = jnp.concatenate(scatter_near(part_first, part_second, to_x, to_y), axis=1)
+    grad_hidden = jnp.concatenate(scatter_near(part_first, part_second, to_x, to_y), axis=1) + zeros + more_zeros
     out_rows = jnp.dot(hidden, down_w, preferred_element_type=F32).astype(BF)
 
     own_grads = ((grad_hidden * up_sum * slope_term).astype(BF), (grad_hidden * active).astype(BF))
-    near_grads = gather_near(*own_grads)
-    grad_gate_rows, grad_up_rows = gather_far(*own_grads, *near_grads)
-
-    if near:
-        returned = from_chips(reorder(out_rows, me, 4), near_grads)
+    hidden, near_grads = after((hidden, gather_near(*own_grads)))
+    grad_rows = gather_far(*own_grads, *near_grads)
+    back = reorder(out_rows, me, 4)
+    if near:
+        back, grad_rows = after((from_chips(back), grad_rows))
+        returned = from_core(back)
     else:
-        returned = all_to_all(reorder(out_rows, me, 4), experts)
+        returned = all_to_all(back, experts)
     picked_0 = jnp.dot(place_0, returned, preferred_element_type=F32)
     picked_1 = jnp.dot(place_1, returned, preferred_element_type=F32)
     output = (route_weights[:, :1] * picked_0 + route_weights[:, 1:] * picked_1).astype(BF)
@@ -225,7 +255,7 @@
     def term(left, right):
         return lax.dot_general(left, right, CONTRACT_ROWS, preferred_element_type=F32).astype(BF)
 
-    grad_terms = (term(grad_gate_rows, in_rows), term(grad_up_rows, in_rows), term(hidden, cot_rows))
+    grad_terms = (term(grad_rows[0], in_rows), term(grad_rows[1], in_rows), term(hidden, cot_rows))
     for bit_index in range(levels):
         partner = from_partner(grad_terms, "expert", bit_index)
         grad_terms = tuple(add_round(own, their) for own, their in zip(grad_terms, partner))

time: 114 us -> 105 us (0.921)
  starting transfers between devices: 43.9 us -> 36 us
    ppermute x28, starting transfers between devices: 43.9 us -> 36 us  [swap(): return lax.ppermute(block, axis, [(i, i ^ mask) for i in range(count)])]
  transfers between devices with their start and end apart: 28 -> 28, of which waited for: 18 -> 15; matrix products, arithmetic and copies ran while one was open for 17% -> 20% of each run, Pallas kernels for 0% -> 0%
where the time goes in v3:
time: 105 us
  waiting for transfers between devices  43.9 us (42%)
  starting transfers between devices  36 us (34%)
  matrix products  20.5 us (20%)
  other arithmetic  2.75 us (3%)
  between operations  1.26 us (1%)
    ppermute x28, waiting for transfers between devices, swap(): return lax.ppermute(block, axis, [(i, i ^ mask) for i in range(count)])  43.9 us
    ppermute x28, starting transfers between devices, swap(): return lax.ppermute(block, axis, [(i, i ^ mask) for i in range(count)])  36 us
    dot_general x3, matrix products, term(): lax.dot_general(left, right, CONTRACT_ROWS, preferred_element_type=F32)  12 us
    dot_general x3, matrix products, partial_product(): lax.dot_general(rows, weights, CONTRACT_FEATS, preferred_element_type=F32)  4.18 us
  transfers between devices with their start and end apart: 28, of which 15 were waited for; matrix products, arithmetic and copies ran while one was open for 20% of the time, Pallas kernels for 0%

profile of v3, /device:TPU:0, one launch (start us, length us, event | category | flops | bytes accessed | tf_op | source)
XLA Modules:
  0.0 105.2 jit_solution(1610979026587211804)
XLA Ops:
  3.9 3.0 %collective-permute-start.1 = (bf16[80,1024]{1,0:T(8,128)(2,1)S(1)}, bf16[80,1024]{1,0:T(8,128)(2,1)S(1)}, u32[]{:S(2)}, u32[]{:S(2)}) collective-permute-start(bf16[80,1024]{1,0:T(8,128)(2,1)S(1)} %pad_maximum_fusion.13), channel_id=1, source_target_pairs={{0,2},{1,3},{2,0},{3,1},{4,6},{5,7},{6,4},{7,5},{8,10},{9,11},{10,... | collective-permute-start | bytes 491528 | tf_op jit(solution)/shard_map/ppermute | solution.py:30
  6.9 2.7 %collective-permute-start.2 = (bf16[80,1024]{1,0:T(8,128)(2,1)S(1)}, bf16[80,1024]{1,0:T(8,128)(2,1)S(1)}, u32[]{:S(2)}, u32[]{:S(2)}) collective-permute-start(bf16[80,1024]{1,0:T(8,128)(2,1)S(1)} %pad_maximum_fusion.14), channel_id=1, source_target_pairs={{0,4},{1,5},{2,6},{3,7},{4,0},{5,1},{6,2},{7,3},{8,12},{9,13},{10,... | collective-permute-start | bytes 491528 | tf_op jit(solution)/shard_map/ppermute | solution.py:30
  10.2 4.0 %collective-permute-done.1 = bf16[80,1024]{1,0:T(8,128)(2,1)S(1)} collective-permute-done((bf16[80,1024]{1,0:T(8,128)(2,1)S(1)}, bf16[80,1024]{1,0:T(8,128)(2,1)S(1)}, u32[]{:S(2)}, u32[]{:S(2)}) %collective-permute-start.1) | collective-permute-done | bytes 163872 | tf_op jit(solution)/shard_map/ppermute | solution.py:30
  14.2 7.8 %collective-permute-done.2 = bf16[80,1024]{1,0:T(8,128)(2,1)S(1)} collective-permute-done((bf16[80,1024]{1,0:T(8,128)(2,1)S(1)}, bf16[80,1024]{1,0:T(8,128)(2,1)S(1)}, u32[]{:S(2)}, u32[]{:S(2)}) %collective-permute-start.2) | collective-permute-done | bytes 163872 | tf_op jit(solution)/shard_map/ppermute | solution.py:30
  22.1 3.1 %collective-permute-start.15 = (bf16[80,1024]{1,0:T(8,128)(2,1)S(1)}, bf16[80,1024]{1,0:T(8,128)(2,1)S(1)}, u32[]{:S(2)}, u32[]{:S(2)}) collective-permute-start(bf16[80,1024]{1,0:T(8,128)(2,1)S(1)} %pad_maximum_fusion.17), channel_id=1, source_target_pairs={{0,2},{1,3},{2,0},{3,1},{4,6},{5,7},{6,4},{7,5},{8,10},{9,11},{10,... | collective-permute-start | bytes 491528 | tf_op jit(solution)/shard_map/ppermute | solution.py:30
  26.2 1.5 %collective-permute-start.17 = (bf16[80,1024]{1,0:T(8,128)(2,1)S(1)}, bf16[80,1024]{1,0:T(8,128)(2,1)S(1)}, u32[]{:S(2)}, u32[]{:S(2)}) collective-permute-start(bf16[80,1024]{1,0:T(8,128)(2,1)S(1)} %pad_maximum_fusion.19), channel_id=1, source_target_pairs={{0,6},{1,7},{2,4},{3,5},{4,2},{5,3},{6,0},{7,1},{8,14},{9,15},{10,... | collective-permute-start | bytes 491528 | tf_op jit(solution)/shard_map/ppermute | solution.py:30
  29.4 1.6 %collective-permute-start.4 = (bf16[80,1792]{1,0:T(8,128)(2,1)S(1)}, bf16[80,1792]{1,0:T(8,128)(2,1)S(1)}, u32[]{:S(2)}, u32[]{:S(2)}) collective-permute-start(bf16[80,1792]{1,0:T(8,128)(2,1)S(1)} %get-tuple-element.62), channel_id=1, source_target_pairs={{0,16},{8,24},{16,0},{24,8},{1,17},{9,25},{17,1},{25,9},{2,18},{10... | collective-permute-start | bytes 860168 | tf_op jit(solution)/shard_map/ppermute | solution.py:30
  32.4 1.6 %collective-permute-start.6 = (bf16[80,1792]{1,0:T(8,128)(2,1)S(1)}, bf16[80,1792]{1,0:T(8,128)(2,1)S(1)}, u32[]{:S(2)}, u32[]{:S(2)}) collective-permute-start(bf16[80,1792]{1,0:T(8,128)(2,1)S(1)} %get-tuple-element.61), channel_id=1, source_target_pairs={{0,8},{8,0},{16,24},{24,16},{1,9},{9,1},{17,25},{25,17},{2,10},{10... | collective-permute-start | bytes 860168 | tf_op jit(solution)/shard_map/ppermute | solution.py:30
  34.0 2.7 %collective-permute-done.4 = bf16[80,1792]{1,0:T(8,128)(2,1)S(1)} collective-permute-done((bf16[80,1792]{1,0:T(8,128)(2,1)S(1)}, bf16[80,1792]{1,0:T(8,128)(2,1)S(1)}, u32[]{:S(2)}, u32[]{:S(2)}) %collective-permute-start.4) | collective-permute-done | bytes 286752 | tf_op jit(solution)/shard_map/ppermute | solution.py:30
  36.8 2.6 %collective-permute-done.6 = bf16[80,1792]{1,0:T(8,128)(2,1)S(1)} collective-permute-done((bf16[80,1792]{1,0:T(8,128)(2,1)S(1)}, bf16[80,1792]{1,0:T(8,128)(2,1)S(1)}, u32[]{:S(2)}, u32[]{:S(2)}) %collective-permute-start.6) | collective-permute-done | bytes 286752 | tf_op jit(solution)/shard_map/ppermute | solution.py:30
  40.0 1.6 %collective-permute-start.7 = (bf16[80,3584]{1,0:T(8,128)(2,1)S(1)}, bf16[80,3584]{1,0:T(8,128)(2,1)S(1)}, u32[]{:S(2)}, u32[]{:S(2)}) collective-permute-start(bf16[80,3584]{1,0:T(8,128)(2,1)S(1)} %pad_maximum_fusion.6), channel_id=1, source_target_pairs={{0,16},{8,24},{16,0},{24,8},{1,17},{9,25},{17,1},{25,9},{2,18},{10... | collective-permute-start | bytes 1720328 | tf_op jit(solution)/shard_map/ppermute | solution.py:30
  46.4 9.4 %collective-permute-done.7 = bf16[80,3584]{1,0:T(8,128)(2,1)S(1)} collective-permute-done((bf16[80,3584]{1,0:T(8,128)(2,1)S(1)}, bf16[80,3584]{1,0:T(8,128)(2,1)S(1)}, u32[]{:S(2)}, u32[]{:S(2)}) %collective-permute-start.7) | collective-permute-done | bytes 573472 | tf_op jit(solution)/shard_map/ppermute | solution.py:30
  55.9 1.6 %collective-permute-done.5 = bf16[80,3584]{1,0:T(8,128)(2,1)S(1)} collective-permute-done((bf16[80,3584]{1,0:T(8,128)(2,1)S(1)}, bf16[80,3584]{1,0:T(8,128)(2,1)S(1)}, u32[]{:S(2)}, u32[]{:S(2)}) %collective-permute-start.5) | collective-permute-done | bytes 573472 | tf_op jit(solution)/shard_map/ppermute | solution.py:30
  58.3 1.5 %collective-permute-start.8 = (bf16[80,1792]{1,0:T(8,128)(2,1)S(1)}, bf16[80,1792]{1,0:T(8,128)(2,1)S(1)}, u32[]{:S(2)}, u32[]{:S(2)}) collective-permute-start(bf16[80,1792]{1,0:T(8,128)(2,1)S(1)} %multiply_convert_fusion.2), channel_id=1, source_target_pairs={{0,8},{8,0},{16,24},{24,16},{1,9},{9,1},{17,25},{25,17},{2,10},{10... | collective-permute-start | bytes 860168 | tf_op jit(solution)/shard_map/ppermute | solution.py:30
  62.3 5.3 %collective-permute-done.9 = bf16[80,1792]{1,0:T(8,128)(2,1)S(1)} collective-permute-done((bf16[80,1792]{1,0:T(8,128)(2,1)S(1)}, bf16[80,1792]{1,0:T(8,128)(2,1)S(1)}, u32[]{:S(2)}, u32[]{:S(2)}) %collective-permute-start.9) | collective-permute-done | bytes 286752 | tf_op jit(solution)/shard_map/ppermute | solution.py:30
  67.6 1.6 %collective-permute-start.10 = (bf16[80,896]{1,0:T(8,128)(2,1)S(1)}, bf16[80,896]{1,0:T(8,128)(2,1)S(1)}, u32[]{:S(2)}, u32[]{:S(2)}) collective-permute-start(bf16[80,896]{1,0:T(8,128)(2,1)S(1)} %get-tuple-element.100), channel_id=1, source_target_pairs={{0,8},{8,0},{16,24},{24,16},{1,9},{9,1},{17,25},{25,17},{2,10},{10... | collective-permute-start | bytes 430088 | tf_op jit(solution)/shard_map/ppermute | solution.py:30
  69.8 3.1 %collective-permute-done.22 = bf16[80,1792]{1,0:T(8,128)(2,1)S(1)} collective-permute-done((bf16[80,1792]{1,0:T(8,128)(2,1)S(1)}, bf16[80,1792]{1,0:T(8,128)(2,1)S(1)}, u32[]{:S(2)}, u32[]{:S(2)}) %collective-permute-start.22) | collective-permute-done | bytes 286752 | tf_op jit(solution)/shard_map/ppermute | solution.py:30
  78.3 2.0 %collective-permute-start.14 = (bf16[80,1024]{1,0:T(8,128)(2,1)S(1)}, bf16[80,1024]{1,0:T(8,128)(2,1)S(1)}, u32[]{:S(2)}, u32[]{:S(2)}) collective-permute-start(bf16[80,1024]{1,0:T(8,128)(2,1)S(1)} %get-tuple-element.76), channel_id=1, source_target_pairs={{0,6},{1,7},{2,4},{3,5},{4,2},{5,3},{6,0},{7,1},{8,14},{9,15},{10,... | collective-permute-start | bytes 491528 | tf_op jit(solution)/shard_map/ppermute | solution.py:30
  80.3 1.9 %collective-permute-start.13 = (bf16[80,1024]{1,0:T(8,128)(2,1)S(1)}, bf16[80,1024]{1,0:T(8,128)(2,1)S(1)}, u32[]{:S(2)}, u32[]{:S(2)}) collective-permute-start(bf16[80,1024]{1,0:T(8,128)(2,1)S(1)} %get-tuple-element.77), channel_id=1, source_target_pairs={{0,4},{1,5},{2,6},{3,7},{4,0},{5,1},{6,2},{7,3},{8,12},{9,13},{10,... | collective-permute-start | bytes 491528 | tf_op jit(solution)/shard_map/ppermute | solution.py:30
  82.9 4.1 %collective-permute-done.24 = bf16[80,3584]{1,0:T(8,128)(2,1)S(1)} collective-permute-done((bf16[80,3584]{1,0:T(8,128)(2,1)S(1)}, bf16[80,3584]{1,0:T(8,128)(2,1)S(1)}, u32[]{:S(2)}, u32[]{:S(2)}) %collective-permute-start.24) | collective-permute-done | bytes 573472 | tf_op jit(solution)/shard_map/ppermute | solution.py:30
  88.8 1.6 %collective-permute-start.25 = (bf16[80,1792]{1,0:T(8,128)(2,1)S(1)}, bf16[80,1792]{1,0:T(8,128)(2,1)S(1)}, u32[]{:S(2)}, u32[]{:S(2)}) collective-permute-start(bf16[80,1792]{1,0:T(8,128)(2,1)S(1)} %get-tuple-element.89), channel_id=1, source_target_pairs={{0,8},{8,0},{16,24},{24,16},{1,9},{9,1},{17,25},{25,17},{2,10},{10... | collective-permute-start | bytes 860168 | tf_op jit(solution)/shard_map/ppermute | solution.py:30
  90.4 4.1 %convolution_convert_fusion = bf16[1792,1024]{1,0:T(8,128)(2,1)} fusion(bf16[320,1792]{1,0:T(8,128)(2,1)S(1)} %maximum_maximum_fusion, bf16[80,1024]{1,0:T(8,128)(2,1)S(1)} %get-tuple-element.65, bf16[80,1024]{1,0:T(8,128)(2,1)S(1)} %get-tuple-element.66, bf16[80,1024]{1,0:T(8,128)(2,1)S(1)} %get-tuple-element.67, bf16[80,1024]{1,0:T(8,128)(2,1)S(1)} %get-tuple-element.64), kind=kOutput, calls=%fused_computation | convolution fusion | flops 1178861568 | bytes 5472256 | tf_op jit(solution)/shard_map/dot_general | solution.py:256
  95.8 4.0 %convolution_convert_fusion.2 = bf16[1792,1024]{1,0:T(8,128)(2,1)} fusion(bf16[320,1792]{1,0:T(8,128)(2,1)S(1)} %pad_maximum_fusion, bf16[80,1024]{1,0:T(8,128)(2,1)S(1)} %get-tuple-element.81, bf16[80,1024]{1,0:T(8,128)(2,1)S(1)} %get-tuple-element.82, bf16[80,1024]{1,0:T(8,128)(2,1)S(1)} %get-tuple-element.83, bf16[80,1024]{1,0:T(8,128)(2,1)S(1)} %get-tuple-element.80), kind=kOutput, calls=%fused_computation.2 | convolution fusion | flops 1178861568 | bytes 5472256 | tf_op jit(solution)/shard_map/dot_general | solution.py:256
  99.8 3.9 %convolution_convert_fusion.1 = bf16[1792,1024]{1,0:T(8,128)(2,1)} fusion(bf16[320,1792]{1,0:T(8,128)(2,1)S(1)} %pad_maximum_fusion.1, bf16[80,1024]{1,0:T(8,128)(2,1)S(1)} %get-tuple-element.81, bf16[80,1024]{1,0:T(8,128)(2,1)S(1)} %get-tuple-element.82, bf16[80,1024]{1,0:T(8,128)(2,1)S(1)} %get-tuple-element.83, bf16[80,1024]{1,0:T(8,128)(2,1)S(1)} %get-tuple-element.80), kind=kOutput, calls=%fused_computation.1 | convolution fusion | flops 1178861568 | bytes 5472256 | tf_op jit(solution)/shard_map/dot_general | solution.py:256
  (121 shorter events, 27.8 us)
Async XLA Ops:
  3.9 10.3 %collective-permute-start.1 = (bf16[80,1024]{1,0:T(8,128)(2,1)S(1)}, bf16[80,1024]{1,0:T(8,128)(2,1)S(1)}, u32[]{:S(2)}, u32[]{:S(2)}) collective-permute-start(bf16[80,1024]{1,0:T(8,128)(2,1)S(1)} %pad_maximum_fusion.13), channel_id=1, source_target_pairs={{0,2},{1,3},{2,0},{3,1},{4,6},{5,7},{6,4},{7,5},{8,10},{9,11},{10,... | collective-permute-start | bytes 491528 | tf_op jit(solution)/shard_map/ppermute | solution.py:30
  6.9 15.1 %collective-permute-start.2 = (bf16[80,1024]{1,0:T(8,128)(2,1)S(1)}, bf16[80,1024]{1,0:T(8,128)(2,1)S(1)}, u32[]{:S(2)}, u32[]{:S(2)}) collective-permute-start(bf16[80,1024]{1,0:T(8,128)(2,1)S(1)} %pad_maximum_fusion.14), channel_id=1, source_target_pairs={{0,4},{1,5},{2,6},{3,7},{4,0},{5,1},{6,2},{7,3},{8,12},{9,13},{10,... | collective-permute-start | bytes 491528 | tf_op jit(solution)/shard_map/ppermute | solution.py:30
  9.6 12.4 %collective-permute-start.3 = (bf16[80,1024]{1,0:T(8,128)(2,1)S(1)}, bf16[80,1024]{1,0:T(8,128)(2,1)S(1)}, u32[]{:S(2)}, u32[]{:S(2)}) collective-permute-start(bf16[80,1024]{1,0:T(8,128)(2,1)S(1)} %pad_maximum_fusion.15), channel_id=1, source_target_pairs={{0,6},{1,7},{2,4},{3,5},{4,2},{5,3},{6,0},{7,1},{8,14},{9,15},{10,... | collective-permute-start | bytes 491528 | tf_op jit(solution)/shard_map/ppermute | solution.py:30
  22.1 17.5 %collective-permute-start.15 = (bf16[80,1024]{1,0:T(8,128)(2,1)S(1)}, bf16[80,1024]{1,0:T(8,128)(2,1)S(1)}, u32[]{:S(2)}, u32[]{:S(2)}) collective-permute-start(bf16[80,1024]{1,0:T(8,128)(2,1)S(1)} %pad_maximum_fusion.17), channel_id=1, source_target_pairs={{0,2},{1,3},{2,0},{3,1},{4,6},{5,7},{6,4},{7,5},{8,10},{9,11},{10,... | collective-permute-start | bytes 491528 | tf_op jit(solution)/shard_map/ppermute | solution.py:30
  25.1 14.6 %collective-permute-start.16 = (bf16[80,1024]{1,0:T(8,128)(2,1)S(1)}, bf16[80,1024]{1,0:T(8,128)(2,1)S(1)}, u32[]{:S(2)}, u32[]{:S(2)}) collective-permute-start(bf16[80,1024]{1,0:T(8,128)(2,1)S(1)} %pad_maximum_fusion.18), channel_id=1, source_target_pairs={{0,4},{1,5},{2,6},{3,7},{4,0},{5,1},{6,2},{7,3},{8,12},{9,13},{10,... | collective-permute-start | bytes 491528 | tf_op jit(solution)/shard_map/ppermute | solution.py:30
  26.2 13.5 %collective-permute-start.17 = (bf16[80,1024]{1,0:T(8,128)(2,1)S(1)}, bf16[80,1024]{1,0:T(8,128)(2,1)S(1)}, u32[]{:S(2)}, u32[]{:S(2)}) collective-permute-start(bf16[80,1024]{1,0:T(8,128)(2,1)S(1)} %pad_maximum_fusion.19), channel_id=1, source_target_pairs={{0,6},{1,7},{2,4},{3,5},{4,2},{5,3},{6,0},{7,1},{8,14},{9,15},{10,... | collective-permute-start | bytes 491528 | tf_op jit(solution)/shard_map/ppermute | solution.py:30
  29.4 7.3 %collective-permute-start.4 = (bf16[80,1792]{1,0:T(8,128)(2,1)S(1)}, bf16[80,1792]{1,0:T(8,128)(2,1)S(1)}, u32[]{:S(2)}, u32[]{:S(2)}) collective-permute-start(bf16[80,1792]{1,0:T(8,128)(2,1)S(1)} %get-tuple-element.62), channel_id=1, source_target_pairs={{0,16},{8,24},{16,0},{24,8},{1,17},{9,25},{17,1},{25,9},{2,18},{10... | collective-permute-start | bytes 860168 | tf_op jit(solution)/shard_map/ppermute | solution.py:30
  40.0 15.8 %collective-permute-start.7 = (bf16[80,3584]{1,0:T(8,128)(2,1)S(1)}, bf16[80,3584]{1,0:T(8,128)(2,1)S(1)}, u32[]{:S(2)}, u32[]{:S(2)}) collective-permute-start(bf16[80,3584]{1,0:T(8,128)(2,1)S(1)} %pad_maximum_fusion.6), channel_id=1, source_target_pairs={{0,16},{8,24},{16,0},{24,8},{1,17},{9,25},{17,1},{25,9},{2,18},{10... | collective-permute-start | bytes 1720328 | tf_op jit(solution)/shard_map/ppermute | solution.py:30
  41.6 15.8 %collective-permute-start.5 = (bf16[80,3584]{1,0:T(8,128)(2,1)S(1)}, bf16[80,3584]{1,0:T(8,128)(2,1)S(1)}, u32[]{:S(2)}, u32[]{:S(2)}) collective-permute-start(bf16[80,3584]{1,0:T(8,128)(2,1)S(1)} %pad_maximum_fusion.5), channel_id=1, source_target_pairs={{0,8},{8,0},{16,24},{24,16},{1,9},{9,1},{17,25},{25,17},{2,10},{10... | collective-permute-start | bytes 1720328 | tf_op jit(solution)/shard_map/ppermute | solution.py:30
  44.9 15.0 %collective-permute-start.20 = (bf16[80,896]{1,0:T(8,128)(2,1)S(1)}, bf16[80,896]{1,0:T(8,128)(2,1)S(1)}, u32[]{:S(2)}, u32[]{:S(2)}) collective-permute-start(bf16[80,896]{1,0:T(8,128)(2,1)S(1)} %get-tuple-element.56), channel_id=1, source_target_pairs={{0,16},{8,24},{16,0},{24,8},{1,17},{9,25},{17,1},{25,9},{2,18},{10... | collective-permute-start | bytes 430088 | tf_op jit(solution)/shard_map/ppermute | solution.py:30
  45.4 14.6 %collective-permute-start.19 = (bf16[80,896]{1,0:T(8,128)(2,1)S(1)}, bf16[80,896]{1,0:T(8,128)(2,1)S(1)}, u32[]{:S(2)}, u32[]{:S(2)}) collective-permute-start(bf16[80,896]{1,0:T(8,128)(2,1)S(1)} %get-tuple-element.57), channel_id=1, source_target_pairs={{0,8},{8,0},{16,24},{24,16},{1,9},{9,1},{17,25},{25,17},{2,10},{10... | collective-permute-start | bytes 430088 | tf_op jit(solution)/shard_map/ppermute | solution.py:30
  57.8 9.8 %collective-permute-start.9 = (bf16[80,1792]{1,0:T(8,128)(2,1)S(1)}, bf16[80,1792]{1,0:T(8,128)(2,1)S(1)}, u32[]{:S(2)}, u32[]{:S(2)}) collective-permute-start(bf16[80,1792]{1,0:T(8,128)(2,1)S(1)} %multiply_convert_fusion.2), channel_id=1, source_target_pairs={{0,16},{8,24},{16,0},{24,8},{1,17},{9,25},{17,1},{25,9},{2,18},{10... | collective-permute-start | bytes 860168 | tf_op jit(solution)/shard_map/ppermute | solution.py:30
  58.3 10.9 %collective-permute-start.8 = (bf16[80,1792]{1,0:T(8,128)(2,1)S(1)}, bf16[80,1792]{1,0:T(8,128)(2,1)S(1)}, u32[]{:S(2)}, u32[]{:S(2)}) collective-permute-start(bf16[80,1792]{1,0:T(8,128)(2,1)S(1)} %multiply_convert_fusion.2), channel_id=1, source_target_pairs={{0,8},{8,0},{16,24},{24,16},{1,9},{9,1},{17,25},{25,17},{2,10},{10... | collective-permute-start | bytes 860168 | tf_op jit(solution)/shard_map/ppermute | solution.py:30
  60.3 12.6 %collective-permute-start.22 = (bf16[80,1792]{1,0:T(8,128)(2,1)S(1)}, bf16[80,1792]{1,0:T(8,128)(2,1)S(1)}, u32[]{:S(2)}, u32[]{:S(2)}) collective-permute-start(bf16[80,1792]{1,0:T(8,128)(2,1)S(1)} %pad_maximum_fusion.11), channel_id=1, source_target_pairs={{0,16},{8,24},{16,0},{24,8},{1,17},{9,25},{17,1},{25,9},{2,18},{10... | collective-permute-start | bytes 860168 | tf_op jit(solution)/shard_map/ppermute | solution.py:30
  61.7 11.9 %collective-permute-start.21 = (bf16[80,1792]{1,0:T(8,128)(2,1)S(1)}, bf16[80,1792]{1,0:T(8,128)(2,1)S(1)}, u32[]{:S(2)}, u32[]{:S(2)}) collective-permute-start(bf16[80,1792]{1,0:T(8,128)(2,1)S(1)} %pad_maximum_fusion.10), channel_id=1, source_target_pairs={{0,8},{8,0},{16,24},{24,16},{1,9},{9,1},{17,25},{25,17},{2,10},{10... | collective-permute-start | bytes 860168 | tf_op jit(solution)/shard_map/ppermute | solution.py:30
  67.6 9.2 %collective-permute-start.10 = (bf16[80,896]{1,0:T(8,128)(2,1)S(1)}, bf16[80,896]{1,0:T(8,128)(2,1)S(1)}, u32[]{:S(2)}, u32[]{:S(2)}) collective-permute-start(bf16[80,896]{1,0:T(8,128)(2,1)S(1)} %get-tuple-element.100), channel_id=1, source_target_pairs={{0,8},{8,0},{16,24},{24,16},{1,9},{9,1},{17,25},{25,17},{2,10},{10... | collective-permute-start | bytes 430088 | tf_op jit(solution)/shard_map/ppermute | solution.py:30
  69.2 7.7 %collective-permute-start.11 = (bf16[80,896]{1,0:T(8,128)(2,1)S(1)}, bf16[80,896]{1,0:T(8,128)(2,1)S(1)}, u32[]{:S(2)}, u32[]{:S(2)}) collective-permute-start(bf16[80,896]{1,0:T(8,128)(2,1)S(1)} %get-tuple-element.99), channel_id=1, source_target_pairs={{0,16},{8,24},{16,0},{24,8},{1,17},{9,25},{17,1},{25,9},{2,18},{10... | collective-permute-start | bytes 430088 | tf_op jit(solution)/shard_map/ppermute | solution.py:30
  74.2 12.8 %collective-permute-start.24 = (bf16[80,3584]{1,0:T(8,128)(2,1)S(1)}, bf16[80,3584]{1,0:T(8,128)(2,1)S(1)}, u32[]{:S(2)}, u32[]{:S(2)}) collective-permute-start(bf16[80,3584]{1,0:T(8,128)(2,1)S(1)} %pad_maximum_fusion.7), channel_id=1, source_target_pairs={{0,16},{8,24},{16,0},{24,8},{1,17},{9,25},{17,1},{25,9},{2,18},{10... | collective-permute-start | bytes 1720328 | tf_op jit(solution)/shard_map/ppermute | solution.py:30
  75.4 12.1 %collective-permute-start.23 = (bf16[80,3584]{1,0:T(8,128)(2,1)S(1)}, bf16[80,3584]{1,0:T(8,128)(2,1)S(1)}, u32[]{:S(2)}, u32[]{:S(2)}) collective-permute-start(bf16[80,3584]{1,0:T(8,128)(2,1)S(1)} %pad_maximum_fusion.7), channel_id=1, source_target_pairs={{0,8},{8,0},{16,24},{24,16},{1,9},{9,1},{17,25},{25,17},{2,10},{10... | collective-permute-start | bytes 1720328 | tf_op jit(solution)/shard_map/ppermute | solution.py:30
  78.3 17.3 %collective-permute-start.14 = (bf16[80,1024]{1,0:T(8,128)(2,1)S(1)}, bf16[80,1024]{1,0:T(8,128)(2,1)S(1)}, u32[]{:S(2)}, u32[]{:S(2)}) collective-permute-start(bf16[80,1024]{1,0:T(8,128)(2,1)S(1)} %get-tuple-element.76), channel_id=1, source_target_pairs={{0,6},{1,7},{2,4},{3,5},{4,2},{5,3},{6,0},{7,1},{8,14},{9,15},{10,... | collective-permute-start | bytes 491528 | tf_op jit(solution)/shard_map/ppermute | solution.py:30
  80.3 15.3 %collective-permute-start.13 = (bf16[80,1024]{1,0:T(8,128)(2,1)S(1)}, bf16[80,1024]{1,0:T(8,128)(2,1)S(1)}, u32[]{:S(2)}, u32[]{:S(2)}) collective-permute-start(bf16[80,1024]{1,0:T(8,128)(2,1)S(1)} %get-tuple-element.77), channel_id=1, source_target_pairs={{0,4},{1,5},{2,6},{3,7},{4,0},{5,1},{6,2},{7,3},{8,12},{9,13},{10,... | collective-permute-start | bytes 491528 | tf_op jit(solution)/shard_map/ppermute | solution.py:30
  82.2 13.4 %collective-permute-start.12 = (bf16[80,1024]{1,0:T(8,128)(2,1)S(1)}, bf16[80,1024]{1,0:T(8,128)(2,1)S(1)}, u32[]{:S(2)}, u32[]{:S(2)}) collective-permute-start(bf16[80,1024]{1,0:T(8,128)(2,1)S(1)} %get-tuple-element.78), channel_id=1, source_target_pairs={{0,2},{1,3},{2,0},{3,1},{4,6},{5,7},{6,4},{7,5},{8,10},{9,11},{10,... | collective-permute-start | bytes 491528 | tf_op jit(solution)/shard_map/ppermute | solution.py:30
  87.5 7.0 %collective-permute-start.26 = (bf16[80,1792]{1,0:T(8,128)(2,1)S(1)}, bf16[80,1792]{1,0:T(8,128)(2,1)S(1)}, u32[]{:S(2)}, u32[]{:S(2)}) collective-permute-start(bf16[80,1792]{1,0:T(8,128)(2,1)S(1)} %get-tuple-element.90), channel_id=1, source_target_pairs={{0,16},{8,24},{16,0},{24,8},{1,17},{9,25},{17,1},{25,9},{2,18},{10... | collective-permute-start | bytes 860168 | tf_op jit(solution)/shard_map/ppermute | solution.py:30
  95.7 8.0 %collective-permute-start.27 = (bf16[160,1024]{1,0:T(8,128)(2,1)S(1)}, bf16[160,1024]{1,0:T(8,128)(2,1)S(1)}, u32[]{:S(2)}, u32[]{:S(2)}) collective-permute-start(bf16[160,1024]{1,0:T(8,128)(2,1)S(1)} %pad_maximum_fusion.9), channel_id=1, source_target_pairs={{0,1},{1,0},{2,3},{3,2},{4,5},{5,4},{6,7},{7,6},{8,9},{9,8},{10,11... | collective-permute-start | bytes 983048 | tf_op jit(solution)/shard_map/ppermute | solution.py:30
  (10 other events, 36.2 us)

commit v4 on v3

--- a/solution.py
+++ b/solution.py
@@ -85,12 +85,12 @@
     return [blocks[0]] + [swap(blocks[m], "expert", 2 * m) for m in range(1, 4)]
 
 
-def to_chips_first(rows):
+def by_chip(rows):
     n = rows.shape[0] // 8
     blocks = [
         jnp.concatenate([rows[m * n:(m + 1) * n], rows[(4 + m) * n:(5 + m) * n]], axis=0) for m in range(4)
     ]
-    return [blocks[0]] + [swap(blocks[m], "expert", 2 * m) for m in range(1, 4)]
+    return blocks
 
 
 def core_last(got):
@@ -146,13 +146,17 @@
     far_first = swap(from_y[:, :c], "dp", 1)
     far_second = swap(from_x[:, c:], "dp", 2)
     return (
-        jnp.concatenate([first, from_x[:, :c], from_y[:, :c], far_first], axis=0),
-        jnp.concatenate([second, from_x[:, c:], from_y[:, c:], far_second], axis=0),
+        (jnp.concatenate([first, from_x[:, :c], from_y[:, :c]], axis=0), far_first),
+        (jnp.concatenate([second, from_x[:, c:], from_y[:, c:]], axis=0), far_second),
     )
 
 
 CONTRACT_FEATS = (((1,), (1,)), ((), ()))
 CONTRACT_ROWS = (((0,), (0,)), ((), ()))
+
+
+def row_product(left, right):
+    return lax.dot_general(left, right, CONTRACT_ROWS, preferred_element_type=F32)
 
 
 def per_device(tokens, expert_ids, route_weights, w_gate, w_up, w_down, out_grad):
@@ -200,11 +204,13 @@
     ).astype(BF)
     if near:
         in_rows = to_chips(*pair_core(send_rows))
-        cot_send, in_rows = after((cot_send, in_rows))
-        cot_rows = to_chips_first(cot_send)
+        in_rows[1], first_zeros = after_start(in_rows[1], in_rows[2][:, :1] + in_rows[3][:, :1])
+        cot_send, in_rows = after((by_chip(cot_send), in_rows))
+        cot_rows = [cot_send[0]] + [swap(cot_send[m], "expert", 2 * m) for m in range(1, 4)]
     else:
         in_rows = [all_to_all(send_rows, experts)]
         cot_rows = [all_to_all(cot_send, experts)]
+        first_zeros = 0.0
     in_rows = reorder(jnp.concatenate(in_rows, axis=0), me, 4)
 
     pieces = (w_gate, w_up, w_down)
@@ -235,16 +241,21 @@
     to_x, to_y = scatter_add(part_first, part_second, *via)
     own_hidden = (own_hidden[:, :half], own_hidden[:, half:])
     near_hidden = gather_near(*own_hidden)
-    hidden = jnp.concatenate(gather_far(*own_hidden, *near_hidden), axis=1)
-    grad_hidden = jnp.concatenate(scatter_near(part_first, part_second, to_x, to_y), axis=1) + zeros + more_zeros
+    hidden = jnp.concatenate(
+        [jnp.concatenate(each, axis=0) for each in gather_far(*own_hidden, *near_hidden)], axis=1
+    )
+    grad_hidden = jnp.concatenate(scatter_near(part_first, part_second, to_x, to_y), axis=1) + first_zeros + zeros + more_zeros
     out_rows = jnp.dot(hidden, down_w, preferred_element_type=F32).astype(BF)
 
     own_grads = ((grad_hidden * up_sum * slope_term).astype(BF), (grad_hidden * active).astype(BF))
-    hidden, near_grads = after((hidden, gather_near(*own_grads)))
+    down_term, near_grads = after((row_product(hidden, cot_rows).astype(BF), gather_near(*own_grads)))
     grad_rows = gather_far(*own_grads, *near_grads)
+    ready = 3 * (in_rows.shape[0] // 4)
+    near_terms = [row_product(near_rows, in_rows[:ready]) for near_rows, _ in grad_rows]
+    near_terms, far_rows = after((near_terms, [far_rows for _, far_rows in grad_rows]))
     back = reorder(out_rows, me, 4)
     if near:
-        back, grad_rows = after((from_chips(back), grad_rows))
+        back, far_rows = after((from_chips(back), far_rows))
         returned = from_core(back)
     else:
         returned = all_to_all(back, experts)
@@ -252,10 +263,8 @@
     picked_1 = jnp.dot(place_1, returned, preferred_element_type=F32)
     output = (route_weights[:, :1] * picked_0 + route_weights[:, 1:] * picked_1).astype(BF)
 
-    def term(left, right):
-        return lax.dot_general(left, right, CONTRACT_ROWS, preferred_element_type=F32).astype(BF)
-
-    grad_terms = (term(grad_rows[0], in_rows), term(grad_rows[1], in_rows), term(hidden, cot_rows))
+    grad_terms = [near + row_product(far_rows, in_rows[ready:]) for near, far_rows in zip(near_terms, far_rows)]
+    grad_terms = tuple(each.astype(BF) for each in (*grad_terms, down_term))
     for bit_index in range(levels):
         partner = from_partner(grad_terms, "expert", bit_index)
         grad_terms = tuple(add_round(own, their) for own, their in zip(grad_terms, partner))

time: 105 us -> 119 us (1.13)
  other arithmetic: 2.75 us -> 17.2 us
  waiting for transfers between devices: 43.9 us -> 38.4 us
  matrix products: 20.5 us -> 25.9 us
    convert_element_type x0 -> x2, other arithmetic: none -> 14.6 us  [per_device(): grad_terms = tuple((each.astype(BF) for each in (*grad_terms, down_term)))]
    ppermute x28, waiting for transfers between devices: 43.9 us -> 38.4 us  [swap(): return lax.ppermute(block, axis, [(i, i ^ mask) for i in range(count)])]
    dot_general x3 -> x5, matrix products: 12 us -> 17.4 us  [row_product(): lax.dot_general(left, right, CONTRACT_ROWS, preferred_element_type=F32)]
  transfers between devices with their start and end apart: 28 -> 28, of which waited for: 15 -> 12; matrix products, arithmetic and copies ran while one was open for 20% -> 34% of each run, Pallas kernels for 0% -> 0%
where the time goes in v4:
time: 119 us
  waiting for transfers between devices  38.4 us (32%)
  starting transfers between devices  35.3 us (30%)
  matrix products  25.9 us (22%)
  other arithmetic  17.2 us (14%)
  between operations  1.27 us (1%)
    ppermute x28, waiting for transfers between devices, swap(): return lax.ppermute(block, axis, [(i, i ^ mask) for i in range(count)])  38.4 us
    ppermute x28, starting transfers between devices, swap(): return lax.ppermute(block, axis, [(i, i ^ mask) for i in range(count)])  35.3 us
    dot_general x5, matrix products, row_product(): lax.dot_general(left, right, CONTRACT_ROWS, preferred_element_type=F32)  17.4 us
    convert_element_type x2, other arithmetic, per_device(): grad_terms = tuple((each.astype(BF) for each in (*grad_terms, down_term)))  14.6 us
    dot_general x3, matrix products, partial_product(): lax.dot_general(rows, weights, CONTRACT_FEATS, preferred_element_type=F32)  4.19 us
  transfers between devices with their start and end apart: 28, of which 12 were waited for; matrix products, arithmetic and copies ran while one was open for 34% of the time, Pallas kernels for 0%

profile of v4, /device:TPU:0, one launch (start us, length us, event | category | flops | bytes accessed | tf_op | source)
XLA Modules:
  0.0 119.0 jit_solution(10415979805219837634)
XLA Ops:
  3.9 5.0 %collective-permute-start.3 = (bf16[80,1024]{1,0:T(8,128)(2,1)S(1)}, bf16[80,1024]{1,0:T(8,128)(2,1)S(1)}, u32[]{:S(2)}, u32[]{:S(2)}) collective-permute-start(bf16[80,1024]{1,0:T(8,128)(2,1)S(1)} %pad_maximum_fusion.20), channel_id=1, source_target_pairs={{0,6},{1,7},{2,4},{3,5},{4,2},{5,3},{6,0},{7,1},{8,14},{9,15},{10,... | collective-permute-start | bytes 491528 | tf_op jit(solution)/shard_map/ppermute | solution.py:30
  9.7 4.3 %collective-permute-done.3 = bf16[80,1024]{1,0:T(8,128)(2,1)S(1)} collective-permute-done((bf16[80,1024]{1,0:T(8,128)(2,1)S(1)}, bf16[80,1024]{1,0:T(8,128)(2,1)S(1)}, u32[]{:S(2)}, u32[]{:S(2)}) %collective-permute-start.3) | collective-permute-done | bytes 163872 | tf_op jit(solution)/shard_map/ppermute | solution.py:30
  14.0 9.1 %collective-permute-done.2 = bf16[80,1024]{1,0:T(8,128)(2,1)S(1)} collective-permute-done((bf16[80,1024]{1,0:T(8,128)(2,1)S(1)}, bf16[80,1024]{1,0:T(8,128)(2,1)S(1)}, u32[]{:S(2)}, u32[]{:S(2)}) %collective-permute-start.2) | collective-permute-done | bytes 163872 | tf_op jit(solution)/shard_map/ppermute | solution.py:30
  23.2 3.0 %collective-permute-start.16 = (bf16[80,1024]{1,0:T(8,128)(2,1)S(1)}, bf16[80,1024]{1,0:T(8,128)(2,1)S(1)}, u32[]{:S(2)}, u32[]{:S(2)}) collective-permute-start(bf16[80,1024]{1,0:T(8,128)(2,1)S(1)} %get-tuple-element.42), channel_id=1, source_target_pairs={{0,4},{1,5},{2,6},{3,7},{4,0},{5,1},{6,2},{7,3},{8,12},{9,13},{10,... | collective-permute-start | bytes 491528 | tf_op jit(solution)/shard_map/ppermute | solution.py:30
  29.2 1.6 %collective-permute-start.4 = (bf16[80,1792]{1,0:T(8,128)(2,1)S(1)}, bf16[80,1792]{1,0:T(8,128)(2,1)S(1)}, u32[]{:S(2)}, u32[]{:S(2)}) collective-permute-start(bf16[80,1792]{1,0:T(8,128)(2,1)S(1)} %get-tuple-element.80), channel_id=1, source_target_pairs={{0,16},{8,24},{16,0},{24,8},{1,17},{9,25},{17,1},{25,9},{2,18},{10... | collective-permute-start | bytes 860168 | tf_op jit(solution)/shard_map/ppermute | solution.py:30
  32.2 1.6 %collective-permute-start.6 = (bf16[80,1792]{1,0:T(8,128)(2,1)S(1)}, bf16[80,1792]{1,0:T(8,128)(2,1)S(1)}, u32[]{:S(2)}, u32[]{:S(2)}) collective-permute-start(bf16[80,1792]{1,0:T(8,128)(2,1)S(1)} %get-tuple-element.79), channel_id=1, source_target_pairs={{0,8},{8,0},{16,24},{24,16},{1,9},{9,1},{17,25},{25,17},{2,10},{10... | collective-permute-start | bytes 860168 | tf_op jit(solution)/shard_map/ppermute | solution.py:30
  33.9 2.6 %collective-permute-done.4 = bf16[80,1792]{1,0:T(8,128)(2,1)S(1)} collective-permute-done((bf16[80,1792]{1,0:T(8,128)(2,1)S(1)}, bf16[80,1792]{1,0:T(8,128)(2,1)S(1)}, u32[]{:S(2)}, u32[]{:S(2)}) %collective-permute-start.4) | collective-permute-done | bytes 286752 | tf_op jit(solution)/shard_map/ppermute | solution.py:30
  36.6 2.6 %collective-permute-done.6 = bf16[80,1792]{1,0:T(8,128)(2,1)S(1)} collective-permute-done((bf16[80,1792]{1,0:T(8,128)(2,1)S(1)}, bf16[80,1792]{1,0:T(8,128)(2,1)S(1)}, u32[]{:S(2)}, u32[]{:S(2)}) %collective-permute-start.6) | collective-permute-done | bytes 286752 | tf_op jit(solution)/shard_map/ppermute | solution.py:30
  40.5 1.5 %collective-permute-start.5 = (bf16[80,3584]{1,0:T(8,128)(2,1)S(1)}, bf16[80,3584]{1,0:T(8,128)(2,1)S(1)}, u32[]{:S(2)}, u32[]{:S(2)}) collective-permute-start(bf16[80,3584]{1,0:T(8,128)(2,1)S(1)} %pad_maximum_fusion.3), channel_id=1, source_target_pairs={{0,8},{8,0},{16,24},{24,16},{1,9},{9,1},{17,25},{25,17},{2,10},{10... | collective-permute-start | bytes 1720328 | tf_op jit(solution)/shard_map/ppermute | solution.py:30
  42.3 1.4 %convolution_convert_fusion.1 = bf16[320,1792]{1,0:T(8,128)(2,1)S(1)} fusion(bf16[1792,1024]{1,0:T(8,128)(2,1)S(1)} %copy-done.6, bf16[80,1024]{1,0:T(8,128)(2,1)S(1)} %get-tuple-element.83, bf16[80,1024]{1,0:T(8,128)(2,1)S(1)} %get-tuple-element.84, bf16[80,1024]{1,0:T(8,128)(2,1)S(1)} %get-tuple-element.85, bf16[80,1024]{1,0:T(8,128)(2,1)S(1)} %get-tuple-element.82), kind=kOutput, calls=%fused_computation.3 | convolution fusion | flops 1177600000 | bytes 5472256 | tf_op jit(solution)/shard_map/dot_general | solution.py:224
  45.6 9.9 %collective-permute-done.7 = bf16[80,3584]{1,0:T(8,128)(2,1)S(1)} collective-permute-done((bf16[80,3584]{1,0:T(8,128)(2,1)S(1)}, bf16[80,3584]{1,0:T(8,128)(2,1)S(1)}, u32[]{:S(2)}, u32[]{:S(2)}) %collective-permute-start.7) | collective-permute-done | bytes 573472 | tf_op jit(solution)/shard_map/ppermute | solution.py:30
  57.9 1.5 %collective-permute-start.8 = (bf16[80,1792]{1,0:T(8,128)(2,1)S(1)}, bf16[80,1792]{1,0:T(8,128)(2,1)S(1)}, u32[]{:S(2)}, u32[]{:S(2)}) collective-permute-start(bf16[80,1792]{1,0:T(8,128)(2,1)S(1)} %multiply_convert_fusion.2), channel_id=1, source_target_pairs={{0,8},{8,0},{16,24},{24,16},{1,9},{9,1},{17,25},{25,17},{2,10},{10... | collective-permute-start | bytes 860168 | tf_op jit(solution)/shard_map/ppermute | solution.py:30
  61.9 4.6 %collective-permute-done.9 = bf16[80,1792]{1,0:T(8,128)(2,1)S(1)} collective-permute-done((bf16[80,1792]{1,0:T(8,128)(2,1)S(1)}, bf16[80,1792]{1,0:T(8,128)(2,1)S(1)}, u32[]{:S(2)}, u32[]{:S(2)}) %collective-permute-start.9) | collective-permute-done | bytes 286752 | tf_op jit(solution)/shard_map/ppermute | solution.py:30
  66.5 1.6 %collective-permute-start.10 = (bf16[80,896]{1,0:T(8,128)(2,1)S(1)}, bf16[80,896]{1,0:T(8,128)(2,1)S(1)}, u32[]{:S(2)}, u32[]{:S(2)}) collective-permute-start(bf16[80,896]{1,0:T(8,128)(2,1)S(1)} %get-tuple-element.118), channel_id=1, source_target_pairs={{0,8},{8,0},{16,24},{24,16},{1,9},{9,1},{17,25},{25,17},{2,10},{10... | collective-permute-start | bytes 430088 | tf_op jit(solution)/shard_map/ppermute | solution.py:30
  69.4 2.6 %collective-permute-done.22 = bf16[80,1792]{1,0:T(8,128)(2,1)S(1)} collective-permute-done((bf16[80,1792]{1,0:T(8,128)(2,1)S(1)}, bf16[80,1792]{1,0:T(8,128)(2,1)S(1)}, u32[]{:S(2)}, u32[]{:S(2)}) %collective-permute-start.22) | collective-permute-done | bytes 286752 | tf_op jit(solution)/shard_map/ppermute | solution.py:30
  74.4 1.5 %collective-permute-start.23 = (bf16[80,3584]{1,0:T(8,128)(2,1)S(1)}, bf16[80,3584]{1,0:T(8,128)(2,1)S(1)}, u32[]{:S(2)}, u32[]{:S(2)}) collective-permute-start(bf16[80,3584]{1,0:T(8,128)(2,1)S(1)} %pad_maximum_fusion.5), channel_id=1, source_target_pairs={{0,8},{8,0},{16,24},{24,16},{1,9},{9,1},{17,25},{25,17},{2,10},{10... | collective-permute-start | bytes 1720328 | tf_op jit(solution)/shard_map/ppermute | solution.py:30
  77.4 2.5 %collective-permute-start.14 = (bf16[80,1024]{1,0:T(8,128)(2,1)S(1)}, bf16[80,1024]{1,0:T(8,128)(2,1)S(1)}, u32[]{:S(2)}, u32[]{:S(2)}) collective-permute-start(bf16[80,1024]{1,0:T(8,128)(2,1)S(1)} %get-tuple-element.86), channel_id=1, source_target_pairs={{0,6},{1,7},{2,4},{3,5},{4,2},{5,3},{6,0},{7,1},{8,14},{9,15},{10,... | collective-permute-start | bytes 491528 | tf_op jit(solution)/shard_map/ppermute | solution.py:30
  81.9 4.0 %convolution_convert_fusion = bf16[1792,1024]{1,0:T(8,128)(2,1)} fusion(bf16[80,1024]{1,0:T(8,128)(2,1)S(1)} %get-tuple-element.83, bf16[80,1024]{1,0:T(8,128)(2,1)S(1)} %get-tuple-element.84, bf16[80,1024]{1,0:T(8,128)(2,1)S(1)} %get-tuple-element.85, bf16[80,1024]{1,0:T(8,128)(2,1)S(1)} %get-tuple-element.82, ...), kind=kOutput, calls=%fused_computation.2 | convolution fusion | flops 1188036608 | bytes 5472256 | tf_op jit(solution)/shard_map/dot_general | solution.py:159
  87.7 1.6 %collective-permute-start.25 = (bf16[80,1792]{1,0:T(8,128)(2,1)S(1)}, bf16[80,1792]{1,0:T(8,128)(2,1)S(1)}, u32[]{:S(2)}, u32[]{:S(2)}) collective-permute-start(bf16[80,1792]{1,0:T(8,128)(2,1)S(1)} %get-tuple-element.109), channel_id=1, source_target_pairs={{0,8},{8,0},{16,24},{24,16},{1,9},{9,1},{17,25},{25,17},{2,10},{10... | collective-permute-start | bytes 860168 | tf_op jit(solution)/shard_map/ppermute | solution.py:30
  89.3 4.1 %fusion.9 = f32[1792,1024]{1,0:T(8,128)} fusion(bf16[80,1792]{1,0:T(8,128)(2,1)S(1)} %get-tuple-element.108, bf16[80,1792]{1,0:T(8,128)(2,1)S(1)} %get-tuple-element.106, bf16[80,1792]{1,0:T(8,128)(2,1)S(1)} %get-tuple-element.69, bf16[80,1024]{1,0:T(8,128)(2,1)S(1)} %get-tuple-element.92, bf16[80,1024]{1,0:T(8,128)(2,1)S(1)} %get-tuple-element.93, ...), kind=kOutput, calls=%fused_computation.21 | convolution fusion | flops 884858880 | bytes 8691712 | tf_op jit(solution)/shard_map/dot_general | solution.py:159
  93.3 4.2 %fusion.3 = f32[1792,1024]{1,0:T(8,128)} fusion(bf16[80,1792]{1,0:T(8,128)(2,1)S(1)} %get-tuple-element.109, bf16[80,1792]{1,0:T(8,128)(2,1)S(1)} %get-tuple-element.107, bf16[80,1792]{1,0:T(8,128)(2,1)S(1)} %get-tuple-element.68, bf16[80,1024]{1,0:T(8,128)(2,1)S(1)} %get-tuple-element.92, bf16[80,1024]{1,0:T(8,128)(2,1)S(1)} %get-tuple-element.93, ...), kind=kOutput, calls=%fused_computation.15 | convolution fusion | flops 884858880 | bytes 8691712 | tf_op jit(solution)/shard_map/dot_general | solution.py:159
  97.7 4.1 %fusion.65 = f32[1792,1024]{1,0:T(8,128)} fusion(bf16[80,1792]{1,0:T(8,128)(2,1)S(1)} %collective-permute-done.25, bf16[80,1024]{1,0:T(8,128)(2,1)S(1)} %get-tuple-element.91), kind=kOutput, calls=%fused_computation.150 | convolution fusion | flops 293601280 | bytes 7790592 | tf_op jit(solution)/shard_map/dot_general | solution.py:159
  102.9 8.3 %add_convert_fusion.1 = bf16[1792,1024]{1,0:T(8,128)(2,1)} fusion(f32[1792,1024]{1,0:T(8,128)} %fusion.3, f32[1792,1024]{1,0:T(8,128)} %fusion.65), kind=kLoop, calls=%fused_computation.1 | loop fusion | flops 3670016 | bytes 18350080 | tf_op jit(solution)/shard_map/convert_element_type | solution.py:267
  111.3 6.2 %add_convert_fusion = bf16[1792,1024]{1,0:T(8,128)(2,1)} fusion(f32[1792,1024]{1,0:T(8,128)} %fusion.9, f32[1792,1024]{1,0:T(8,128)S(1)} %fusion.66), kind=kLoop, calls=%fused_computation | loop fusion | flops 3670016 | bytes 18350080 | tf_op jit(solution)/shard_map/convert_element_type | solution.py:267
  (124 shorter events, 28.4 us)
Async XLA Ops:
  3.9 10.1 %collective-permute-start.3 = (bf16[80,1024]{1,0:T(8,128)(2,1)S(1)}, bf16[80,1024]{1,0:T(8,128)(2,1)S(1)}, u32[]{:S(2)}, u32[]{:S(2)}) collective-permute-start(bf16[80,1024]{1,0:T(8,128)(2,1)S(1)} %pad_maximum_fusion.20), channel_id=1, source_target_pairs={{0,6},{1,7},{2,4},{3,5},{4,2},{5,3},{6,0},{7,1},{8,14},{9,15},{10,... | collective-permute-start | bytes 491528 | tf_op jit(solution)/shard_map/ppermute | solution.py:30
  8.9 14.2 %collective-permute-start.2 = (bf16[80,1024]{1,0:T(8,128)(2,1)S(1)}, bf16[80,1024]{1,0:T(8,128)(2,1)S(1)}, u32[]{:S(2)}, u32[]{:S(2)}) collective-permute-start(bf16[80,1024]{1,0:T(8,128)(2,1)S(1)} %pad_maximum_fusion.19), channel_id=1, source_target_pairs={{0,4},{1,5},{2,6},{3,7},{4,0},{5,1},{6,2},{7,3},{8,12},{9,13},{10,... | collective-permute-start | bytes 491528 | tf_op jit(solution)/shard_map/ppermute | solution.py:30
  9.0 14.1 %collective-permute-start.1 = (bf16[80,1024]{1,0:T(8,128)(2,1)S(1)}, bf16[80,1024]{1,0:T(8,128)(2,1)S(1)}, u32[]{:S(2)}, u32[]{:S(2)}) collective-permute-start(bf16[80,1024]{1,0:T(8,128)(2,1)S(1)} %pad_maximum_fusion.18), channel_id=1, source_target_pairs={{0,2},{1,3},{2,0},{3,1},{4,6},{5,7},{6,4},{7,5},{8,10},{9,11},{10,... | collective-permute-start | bytes 491528 | tf_op jit(solution)/shard_map/ppermute | solution.py:30
  23.1 16.2 %collective-permute-start.15 = (bf16[80,1024]{1,0:T(8,128)(2,1)S(1)}, bf16[80,1024]{1,0:T(8,128)(2,1)S(1)}, u32[]{:S(2)}, u32[]{:S(2)}) collective-permute-start(bf16[80,1024]{1,0:T(8,128)(2,1)S(1)} %get-tuple-element.41), channel_id=1, source_target_pairs={{0,2},{1,3},{2,0},{3,1},{4,6},{5,7},{6,4},{7,5},{8,10},{9,11},{10,... | collective-permute-start | bytes 491528 | tf_op jit(solution)/shard_map/ppermute | solution.py:30
  23.2 16.1 %collective-permute-start.16 = (bf16[80,1024]{1,0:T(8,128)(2,1)S(1)}, bf16[80,1024]{1,0:T(8,128)(2,1)S(1)}, u32[]{:S(2)}, u32[]{:S(2)}) collective-permute-start(bf16[80,1024]{1,0:T(8,128)(2,1)S(1)} %get-tuple-element.42), channel_id=1, source_target_pairs={{0,4},{1,5},{2,6},{3,7},{4,0},{5,1},{6,2},{7,3},{8,12},{9,13},{10,... | collective-permute-start | bytes 491528 | tf_op jit(solution)/shard_map/ppermute | solution.py:30
  26.3 13.1 %collective-permute-start.17 = (bf16[80,1024]{1,0:T(8,128)(2,1)S(1)}, bf16[80,1024]{1,0:T(8,128)(2,1)S(1)}, u32[]{:S(2)}, u32[]{:S(2)}) collective-permute-start(bf16[80,1024]{1,0:T(8,128)(2,1)S(1)} %get-tuple-element.43), channel_id=1, source_target_pairs={{0,6},{1,7},{2,4},{3,5},{4,2},{5,3},{6,0},{7,1},{8,14},{9,15},{10,... | collective-permute-start | bytes 491528 | tf_op jit(solution)/shard_map/ppermute | solution.py:30
  39.6 15.8 %collective-permute-start.7 = (bf16[80,3584]{1,0:T(8,128)(2,1)S(1)}, bf16[80,3584]{1,0:T(8,128)(2,1)S(1)}, u32[]{:S(2)}, u32[]{:S(2)}) collective-permute-start(bf16[80,3584]{1,0:T(8,128)(2,1)S(1)} %pad_maximum_fusion.4), channel_id=1, source_target_pairs={{0,16},{8,24},{16,0},{24,8},{1,17},{9,25},{17,1},{25,9},{2,18},{10... | collective-permute-start | bytes 1720328 | tf_op jit(solution)/shard_map/ppermute | solution.py:30
  40.5 15.8 %collective-permute-start.5 = (bf16[80,3584]{1,0:T(8,128)(2,1)S(1)}, bf16[80,3584]{1,0:T(8,128)(2,1)S(1)}, u32[]{:S(2)}, u32[]{:S(2)}) collective-permute-start(bf16[80,3584]{1,0:T(8,128)(2,1)S(1)} %pad_maximum_fusion.3), channel_id=1, source_target_pairs={{0,8},{8,0},{16,24},{24,16},{1,9},{9,1},{17,25},{25,17},{2,10},{10... | collective-permute-start | bytes 1720328 | tf_op jit(solution)/shard_map/ppermute | solution.py:30
  43.7 15.7 %collective-permute-start.20 = (bf16[80,896]{1,0:T(8,128)(2,1)S(1)}, bf16[80,896]{1,0:T(8,128)(2,1)S(1)}, u32[]{:S(2)}, u32[]{:S(2)}) collective-permute-start(bf16[80,896]{1,0:T(8,128)(2,1)S(1)} %get-tuple-element.74), channel_id=1, source_target_pairs={{0,16},{8,24},{16,0},{24,8},{1,17},{9,25},{17,1},{25,9},{2,18},{10... | collective-permute-start | bytes 430088 | tf_op jit(solution)/shard_map/ppermute | solution.py:30
  45.0 14.4 %collective-permute-start.19 = (bf16[80,896]{1,0:T(8,128)(2,1)S(1)}, bf16[80,896]{1,0:T(8,128)(2,1)S(1)}, u32[]{:S(2)}, u32[]{:S(2)}) collective-permute-start(bf16[80,896]{1,0:T(8,128)(2,1)S(1)} %get-tuple-element.75), channel_id=1, source_target_pairs={{0,8},{8,0},{16,24},{24,16},{1,9},{9,1},{17,25},{25,17},{2,10},{10... | collective-permute-start | bytes 430088 | tf_op jit(solution)/shard_map/ppermute | solution.py:30
  56.6 9.8 %collective-permute-start.9 = (bf16[80,1792]{1,0:T(8,128)(2,1)S(1)}, bf16[80,1792]{1,0:T(8,128)(2,1)S(1)}, u32[]{:S(2)}, u32[]{:S(2)}) collective-permute-start(bf16[80,1792]{1,0:T(8,128)(2,1)S(1)} %multiply_convert_fusion.2), channel_id=1, source_target_pairs={{0,16},{8,24},{16,0},{24,8},{1,17},{9,25},{17,1},{25,9},{2,18},{10... | collective-permute-start | bytes 860168 | tf_op jit(solution)/shard_map/ppermute | solution.py:30
  57.9 10.1 %collective-permute-start.8 = (bf16[80,1792]{1,0:T(8,128)(2,1)S(1)}, bf16[80,1792]{1,0:T(8,128)(2,1)S(1)}, u32[]{:S(2)}, u32[]{:S(2)}) collective-permute-start(bf16[80,1792]{1,0:T(8,128)(2,1)S(1)} %multiply_convert_fusion.2), channel_id=1, source_target_pairs={{0,8},{8,0},{16,24},{24,16},{1,9},{9,1},{17,25},{25,17},{2,10},{10... | collective-permute-start | bytes 860168 | tf_op jit(solution)/shard_map/ppermute | solution.py:30
  59.7 12.3 %collective-permute-start.22 = (bf16[80,1792]{1,0:T(8,128)(2,1)S(1)}, bf16[80,1792]{1,0:T(8,128)(2,1)S(1)}, u32[]{:S(2)}, u32[]{:S(2)}) collective-permute-start(bf16[80,1792]{1,0:T(8,128)(2,1)S(1)} %pad_maximum_fusion.10), channel_id=1, source_target_pairs={{0,16},{8,24},{16,0},{24,8},{1,17},{9,25},{17,1},{25,9},{2,18},{10... | collective-permute-start | bytes 860168 | tf_op jit(solution)/shard_map/ppermute | solution.py:30
  60.6 12.2 %collective-permute-start.21 = (bf16[80,1792]{1,0:T(8,128)(2,1)S(1)}, bf16[80,1792]{1,0:T(8,128)(2,1)S(1)}, u32[]{:S(2)}, u32[]{:S(2)}) collective-permute-start(bf16[80,1792]{1,0:T(8,128)(2,1)S(1)} %pad_maximum_fusion.9), channel_id=1, source_target_pairs={{0,8},{8,0},{16,24},{24,16},{1,9},{9,1},{17,25},{25,17},{2,10},{10... | collective-permute-start | bytes 860168 | tf_op jit(solution)/shard_map/ppermute | solution.py:30
  66.5 9.4 %collective-permute-start.10 = (bf16[80,896]{1,0:T(8,128)(2,1)S(1)}, bf16[80,896]{1,0:T(8,128)(2,1)S(1)}, u32[]{:S(2)}, u32[]{:S(2)}) collective-permute-start(bf16[80,896]{1,0:T(8,128)(2,1)S(1)} %get-tuple-element.118), channel_id=1, source_target_pairs={{0,8},{8,0},{16,24},{24,16},{1,9},{9,1},{17,25},{25,17},{2,10},{10... | collective-permute-start | bytes 430088 | tf_op jit(solution)/shard_map/ppermute | solution.py:30
  68.1 7.9 %collective-permute-start.11 = (bf16[80,896]{1,0:T(8,128)(2,1)S(1)}, bf16[80,896]{1,0:T(8,128)(2,1)S(1)}, u32[]{:S(2)}, u32[]{:S(2)}) collective-permute-start(bf16[80,896]{1,0:T(8,128)(2,1)S(1)} %get-tuple-element.117), channel_id=1, source_target_pairs={{0,16},{8,24},{16,0},{24,8},{1,17},{9,25},{17,1},{25,9},{2,18},{10... | collective-permute-start | bytes 430088 | tf_op jit(solution)/shard_map/ppermute | solution.py:30
  73.4 12.5 %collective-permute-start.24 = (bf16[80,3584]{1,0:T(8,128)(2,1)S(1)}, bf16[80,3584]{1,0:T(8,128)(2,1)S(1)}, u32[]{:S(2)}, u32[]{:S(2)}) collective-permute-start(bf16[80,3584]{1,0:T(8,128)(2,1)S(1)} %pad_maximum_fusion.5), channel_id=1, source_target_pairs={{0,16},{8,24},{16,0},{24,8},{1,17},{9,25},{17,1},{25,9},{2,18},{10... | collective-permute-start | bytes 1720328 | tf_op jit(solution)/shard_map/ppermute | solution.py:30
  74.4 12.3 %collective-permute-start.23 = (bf16[80,3584]{1,0:T(8,128)(2,1)S(1)}, bf16[80,3584]{1,0:T(8,128)(2,1)S(1)}, u32[]{:S(2)}, u32[]{:S(2)}) collective-permute-start(bf16[80,3584]{1,0:T(8,128)(2,1)S(1)} %pad_maximum_fusion.5), channel_id=1, source_target_pairs={{0,8},{8,0},{16,24},{24,16},{1,9},{9,1},{17,25},{25,17},{2,10},{10... | collective-permute-start | bytes 1720328 | tf_op jit(solution)/shard_map/ppermute | solution.py:30
  77.4 20.1 %collective-permute-start.14 = (bf16[80,1024]{1,0:T(8,128)(2,1)S(1)}, bf16[80,1024]{1,0:T(8,128)(2,1)S(1)}, u32[]{:S(2)}, u32[]{:S(2)}) collective-permute-start(bf16[80,1024]{1,0:T(8,128)(2,1)S(1)} %get-tuple-element.86), channel_id=1, source_target_pairs={{0,6},{1,7},{2,4},{3,5},{4,2},{5,3},{6,0},{7,1},{8,14},{9,15},{10,... | collective-permute-start | bytes 491528 | tf_op jit(solution)/shard_map/ppermute | solution.py:30
  80.0 17.5 %collective-permute-start.13 = (bf16[80,1024]{1,0:T(8,128)(2,1)S(1)}, bf16[80,1024]{1,0:T(8,128)(2,1)S(1)}, u32[]{:S(2)}, u32[]{:S(2)}) collective-permute-start(bf16[80,1024]{1,0:T(8,128)(2,1)S(1)} %get-tuple-element.87), channel_id=1, source_target_pairs={{0,4},{1,5},{2,6},{3,7},{4,0},{5,1},{6,2},{7,3},{8,12},{9,13},{10,... | collective-permute-start | bytes 491528 | tf_op jit(solution)/shard_map/ppermute | solution.py:30
  80.9 16.6 %collective-permute-start.12 = (bf16[80,1024]{1,0:T(8,128)(2,1)S(1)}, bf16[80,1024]{1,0:T(8,128)(2,1)S(1)}, u32[]{:S(2)}, u32[]{:S(2)}) collective-permute-start(bf16[80,1024]{1,0:T(8,128)(2,1)S(1)} %get-tuple-element.88), channel_id=1, source_target_pairs={{0,2},{1,3},{2,0},{3,1},{4,6},{5,7},{6,4},{7,5},{8,10},{9,11},{10,... | collective-permute-start | bytes 491528 | tf_op jit(solution)/shard_map/ppermute | solution.py:30
  86.8 10.7 %collective-permute-start.26 = (bf16[80,1792]{1,0:T(8,128)(2,1)S(1)}, bf16[80,1792]{1,0:T(8,128)(2,1)S(1)}, u32[]{:S(2)}, u32[]{:S(2)}) collective-permute-start(bf16[80,1792]{1,0:T(8,128)(2,1)S(1)} %get-tuple-element.106), channel_id=1, source_target_pairs={{0,16},{8,24},{16,0},{24,8},{1,17},{9,25},{17,1},{25,9},{2,18},{10... | collective-permute-start | bytes 860168 | tf_op jit(solution)/shard_map/ppermute | solution.py:30
  87.7 9.8 %collective-permute-start.25 = (bf16[80,1792]{1,0:T(8,128)(2,1)S(1)}, bf16[80,1792]{1,0:T(8,128)(2,1)S(1)}, u32[]{:S(2)}, u32[]{:S(2)}) collective-permute-start(bf16[80,1792]{1,0:T(8,128)(2,1)S(1)} %get-tuple-element.109), channel_id=1, source_target_pairs={{0,8},{8,0},{16,24},{24,16},{1,9},{9,1},{17,25},{25,17},{2,10},{10... | collective-permute-start | bytes 860168 | tf_op jit(solution)/shard_map/ppermute | solution.py:30
  97.6 19.9 %collective-permute-start.27 = (bf16[160,1024]{1,0:T(8,128)(2,1)S(1)}, bf16[160,1024]{1,0:T(8,128)(2,1)S(1)}, u32[]{:S(2)}, u32[]{:S(2)}) collective-permute-start(bf16[160,1024]{1,0:T(8,128)(2,1)S(1)} %pad_maximum_fusion.8), channel_id=1, source_target_pairs={{0,1},{1,0},{2,3},{3,2},{4,5},{5,4},{6,7},{7,6},{8,9},{9,8},{10,11... | collective-permute-start | bytes 983048 | tf_op jit(solution)/shard_map/ppermute | solution.py:30
  (11 other events, 49.6 us)

commit v5 on v3

--- a/solution.py
+++ b/solution.py
@@ -85,12 +85,12 @@
     return [blocks[0]] + [swap(blocks[m], "expert", 2 * m) for m in range(1, 4)]
 
 
-def to_chips_first(rows):
+def by_chip(rows):
     n = rows.shape[0] // 8
     blocks = [
         jnp.concatenate([rows[m * n:(m + 1) * n], rows[(4 + m) * n:(5 + m) * n]], axis=0) for m in range(4)
     ]
-    return [blocks[0]] + [swap(blocks[m], "expert", 2 * m) for m in range(1, 4)]
+    return blocks
 
 
 def core_last(got):
@@ -200,8 +200,10 @@
     ).astype(BF)
     if near:
         in_rows = to_chips(*pair_core(send_rows))
+        cot_send, in_rows[1] = after((by_chip(cot_send), in_rows[1]))
+        cot_next = swap(cot_send[1], "expert", 2)
         cot_send, in_rows = after((cot_send, in_rows))
-        cot_rows = to_chips_first(cot_send)
+        cot_rows = [cot_send[0], cot_next, swap(cot_send[2], "expert", 4), swap(cot_send[3], "expert", 6)]
     else:
         in_rows = [all_to_all(send_rows, experts)]
         cot_rows = [all_to_all(cot_send, experts)]
@@ -248,9 +250,8 @@
         returned = from_core(back)
     else:
         returned = all_to_all(back, experts)
-    picked_0 = jnp.dot(place_0, returned, preferred_element_type=F32)
-    picked_1 = jnp.dot(place_1, returned, preferred_element_type=F32)
-    output = (route_weights[:, :1] * picked_0 + route_weights[:, 1:] * picked_1).astype(BF)
+    weighted = (route_weights[:, :1] * place_0 + route_weights[:, 1:] * place_1).astype(BF)
+    output = jnp.dot(weighted, returned, preferred_element_type=F32).astype(BF)
 
     def term(left, right):
         return lax.dot_general(left, right, CONTRACT_ROWS, preferred_element_type=F32).astype(BF)

time: 105 us -> 106 us (level)
  waiting for transfers between devices: 43.9 us -> 41.6 us
  matrix products: 20.5 us -> 22.3 us
    ppermute x28, waiting for transfers between devices: 43.9 us -> 41.6 us  [swap(): return lax.ppermute(block, axis, [(i, i ^ mask) for i in range(count)])]
    dot_general x3, matrix products: 4.18 us -> 6.37 us  [partial_product(): lax.dot_general(rows, weights, CONTRACT_FEATS, preferred_element_type=F32)]
  transfers between devices with their start and end apart: 28 -> 28, of which waited for: 15 -> 14; matrix products, arithmetic and copies ran while one was open for 20% -> 22% of each run, Pallas kernels for 0% -> 0%
where the time goes in v5:
time: 106 us
  waiting for transfers between devices  41.6 us (39%)
  starting transfers between devices  37 us (35%)
  matrix products  22.3 us (21%)
  other arithmetic  2.76 us (3%)
  between operations  1.25 us (1%)
    ppermute x28, waiting for transfers between devices, swap(): return lax.ppermute(block, axis, [(i, i ^ mask) for i in range(count)])  41.6 us
    ppermute x28, starting transfers between devices, swap(): return lax.ppermute(block, axis, [(i, i ^ mask) for i in range(count)])  37 us
    dot_general x3, matrix products, term(): lax.dot_general(left, right, CONTRACT_ROWS, preferred_element_type=F32)  12 us
    dot_general x3, matrix products, partial_product(): lax.dot_general(rows, weights, CONTRACT_FEATS, preferred_element_type=F32)  6.37 us
  transfers between devices with their start and end apart: 28, of which 14 were waited for; matrix products, arithmetic and copies ran while one was open for 22% of the time, Pallas kernels for 0%

profile of v5, /device:TPU:0, one launch (start us, length us, event | category | flops | bytes accessed | tf_op | source)
XLA Modules:
  0.0 105.7 jit_solution(14438110659484647820)
XLA Ops:
  3.9 3.0 %collective-permute-start.1 = (bf16[80,1024]{1,0:T(8,128)(2,1)S(1)}, bf16[80,1024]{1,0:T(8,128)(2,1)S(1)}, u32[]{:S(2)}, u32[]{:S(2)}) collective-permute-start(bf16[80,1024]{1,0:T(8,128)(2,1)S(1)} %pad_maximum_fusion.16), channel_id=1, source_target_pairs={{0,2},{1,3},{2,0},{3,1},{4,6},{5,7},{6,4},{7,5},{8,10},{9,11},{10,... | collective-permute-start | bytes 491528 | tf_op jit(solution)/shard_map/ppermute | solution.py:30
  6.9 2.7 %collective-permute-start.2 = (bf16[80,1024]{1,0:T(8,128)(2,1)S(1)}, bf16[80,1024]{1,0:T(8,128)(2,1)S(1)}, u32[]{:S(2)}, u32[]{:S(2)}) collective-permute-start(bf16[80,1024]{1,0:T(8,128)(2,1)S(1)} %pad_maximum_fusion.18), channel_id=1, source_target_pairs={{0,4},{1,5},{2,6},{3,7},{4,0},{5,1},{6,2},{7,3},{8,12},{9,13},{10,... | collective-permute-start | bytes 491528 | tf_op jit(solution)/shard_map/ppermute | solution.py:30
  9.7 4.4 %collective-permute-done.1 = bf16[80,1024]{1,0:T(8,128)(2,1)S(1)} collective-permute-done((bf16[80,1024]{1,0:T(8,128)(2,1)S(1)}, bf16[80,1024]{1,0:T(8,128)(2,1)S(1)}, u32[]{:S(2)}, u32[]{:S(2)}) %collective-permute-start.1) | collective-permute-done | bytes 163872 | tf_op jit(solution)/shard_map/ppermute | solution.py:30
  14.2 7.9 %collective-permute-done.2 = bf16[80,1024]{1,0:T(8,128)(2,1)S(1)} collective-permute-done((bf16[80,1024]{1,0:T(8,128)(2,1)S(1)}, bf16[80,1024]{1,0:T(8,128)(2,1)S(1)}, u32[]{:S(2)}, u32[]{:S(2)}) %collective-permute-start.2) | collective-permute-done | bytes 163872 | tf_op jit(solution)/shard_map/ppermute | solution.py:30
  22.0 4.0 %collective-permute-start.16 = (bf16[80,1024]{1,0:T(8,128)(2,1)S(1)}, bf16[80,1024]{1,0:T(8,128)(2,1)S(1)}, u32[]{:S(2)}, u32[]{:S(2)}) collective-permute-start(bf16[80,1024]{1,0:T(8,128)(2,1)S(1)} %get-tuple-element.43), channel_id=1, source_target_pairs={{0,4},{1,5},{2,6},{3,7},{4,0},{5,1},{6,2},{7,3},{8,12},{9,13},{10,... | collective-permute-start | bytes 491528 | tf_op jit(solution)/shard_map/ppermute | solution.py:30
  27.5 3.6 %convolution_convert_fusion.4 = bf16[320,1792]{1,0:T(8,128)(2,1)S(1)} fusion(bf16[1792,1024]{1,0:T(8,128)(2,1)} %param.11, bf16[80,1024]{1,0:T(8,128)(2,1)S(1)} %get-tuple-element.87, bf16[80,1024]{1,0:T(8,128)(2,1)S(1)} %get-tuple-element.88, bf16[80,1024]{1,0:T(8,128)(2,1)S(1)} %get-tuple-element.89, bf16[80,1024]{1,0:T(8,128)(2,1)S(1)} %get-tuple-element.86), kind=kOutput, calls=%fused_computation.4 | convolution fusion | flops 1177600000 | bytes 5472256 | tf_op jit(solution)/shard_map/dot_general | solution.py:220
  31.2 1.6 %collective-permute-start.4 = (bf16[80,1792]{1,0:T(8,128)(2,1)S(1)}, bf16[80,1792]{1,0:T(8,128)(2,1)S(1)}, u32[]{:S(2)}, u32[]{:S(2)}) collective-permute-start(bf16[80,1792]{1,0:T(8,128)(2,1)S(1)} %get-tuple-element.76), channel_id=1, source_target_pairs={{0,16},{8,24},{16,0},{24,8},{1,17},{9,25},{17,1},{25,9},{2,18},{10... | collective-permute-start | bytes 860168 | tf_op jit(solution)/shard_map/ppermute | solution.py:30
  35.7 2.7 %collective-permute-done.4 = bf16[80,1792]{1,0:T(8,128)(2,1)S(1)} collective-permute-done((bf16[80,1792]{1,0:T(8,128)(2,1)S(1)}, bf16[80,1792]{1,0:T(8,128)(2,1)S(1)}, u32[]{:S(2)}, u32[]{:S(2)}) %collective-permute-start.4) | collective-permute-done | bytes 286752 | tf_op jit(solution)/shard_map/ppermute | solution.py:30
  38.6 2.6 %collective-permute-done.6 = bf16[80,1792]{1,0:T(8,128)(2,1)S(1)} collective-permute-done((bf16[80,1792]{1,0:T(8,128)(2,1)S(1)}, bf16[80,1792]{1,0:T(8,128)(2,1)S(1)}, u32[]{:S(2)}, u32[]{:S(2)}) %collective-permute-start.6) | collective-permute-done | bytes 286752 | tf_op jit(solution)/shard_map/ppermute | solution.py:30
  45.4 1.6 %collective-permute-start.20 = (bf16[80,896]{1,0:T(8,128)(2,1)S(1)}, bf16[80,896]{1,0:T(8,128)(2,1)S(1)}, u32[]{:S(2)}, u32[]{:S(2)}) collective-permute-start(bf16[80,896]{1,0:T(8,128)(2,1)S(1)} %get-tuple-element.70), channel_id=1, source_target_pairs={{0,16},{8,24},{16,0},{24,8},{1,17},{9,25},{17,1},{25,9},{2,18},{10... | collective-permute-start | bytes 430088 | tf_op jit(solution)/shard_map/ppermute | solution.py:30
  47.5 9.9 %collective-permute-done.7 = bf16[80,3584]{1,0:T(8,128)(2,1)S(1)} collective-permute-done((bf16[80,3584]{1,0:T(8,128)(2,1)S(1)}, bf16[80,3584]{1,0:T(8,128)(2,1)S(1)}, u32[]{:S(2)}, u32[]{:S(2)}) %collective-permute-start.7) | collective-permute-done | bytes 573472 | tf_op jit(solution)/shard_map/ppermute | solution.py:30
  58.3 1.6 %collective-permute-start.9 = (bf16[80,1792]{1,0:T(8,128)(2,1)S(1)}, bf16[80,1792]{1,0:T(8,128)(2,1)S(1)}, u32[]{:S(2)}, u32[]{:S(2)}) collective-permute-start(bf16[80,1792]{1,0:T(8,128)(2,1)S(1)} %multiply_convert_fusion.2), channel_id=1, source_target_pairs={{0,16},{8,24},{16,0},{24,8},{1,17},{9,25},{17,1},{25,9},{2,18},{10... | collective-permute-start | bytes 860168 | tf_op jit(solution)/shard_map/ppermute | solution.py:30
  62.5 1.6 %collective-permute-start.21 = (bf16[80,1792]{1,0:T(8,128)(2,1)S(1)}, bf16[80,1792]{1,0:T(8,128)(2,1)S(1)}, u32[]{:S(2)}, u32[]{:S(2)}) collective-permute-start(bf16[80,1792]{1,0:T(8,128)(2,1)S(1)} %pad_maximum_fusion.10), channel_id=1, source_target_pairs={{0,8},{8,0},{16,24},{24,16},{1,9},{9,1},{17,25},{25,17},{2,10},{10... | collective-permute-start | bytes 860168 | tf_op jit(solution)/shard_map/ppermute | solution.py:30
  64.0 4.1 %collective-permute-done.9 = bf16[80,1792]{1,0:T(8,128)(2,1)S(1)} collective-permute-done((bf16[80,1792]{1,0:T(8,128)(2,1)S(1)}, bf16[80,1792]{1,0:T(8,128)(2,1)S(1)}, u32[]{:S(2)}, u32[]{:S(2)}) %collective-permute-start.9) | collective-permute-done | bytes 286752 | tf_op jit(solution)/shard_map/ppermute | solution.py:30
  68.2 1.6 %collective-permute-start.10 = (bf16[80,896]{1,0:T(8,128)(2,1)S(1)}, bf16[80,896]{1,0:T(8,128)(2,1)S(1)}, u32[]{:S(2)}, u32[]{:S(2)}) collective-permute-start(bf16[80,896]{1,0:T(8,128)(2,1)S(1)} %get-tuple-element.114), channel_id=1, source_target_pairs={{0,8},{8,0},{16,24},{24,16},{1,9},{9,1},{17,25},{25,17},{2,10},{10... | collective-permute-start | bytes 430088 | tf_op jit(solution)/shard_map/ppermute | solution.py:30
  69.8 1.6 %collective-permute-start.11 = (bf16[80,896]{1,0:T(8,128)(2,1)S(1)}, bf16[80,896]{1,0:T(8,128)(2,1)S(1)}, u32[]{:S(2)}, u32[]{:S(2)}) collective-permute-start(bf16[80,896]{1,0:T(8,128)(2,1)S(1)} %get-tuple-element.113), channel_id=1, source_target_pairs={{0,16},{8,24},{16,0},{24,8},{1,17},{9,25},{17,1},{25,9},{2,18},{10... | collective-permute-start | bytes 430088 | tf_op jit(solution)/shard_map/ppermute | solution.py:30
  71.4 2.6 %collective-permute-done.22 = bf16[80,1792]{1,0:T(8,128)(2,1)S(1)} collective-permute-done((bf16[80,1792]{1,0:T(8,128)(2,1)S(1)}, bf16[80,1792]{1,0:T(8,128)(2,1)S(1)}, u32[]{:S(2)}, u32[]{:S(2)}) %collective-permute-start.22) | collective-permute-done | bytes 286752 | tf_op jit(solution)/shard_map/ppermute | solution.py:30
  79.4 2.5 %collective-permute-start.14 = (bf16[80,1024]{1,0:T(8,128)(2,1)S(1)}, bf16[80,1024]{1,0:T(8,128)(2,1)S(1)}, u32[]{:S(2)}, u32[]{:S(2)}) collective-permute-start(bf16[80,1024]{1,0:T(8,128)(2,1)S(1)} %get-tuple-element.82), channel_id=1, source_target_pairs={{0,6},{1,7},{2,4},{3,5},{4,2},{5,3},{6,0},{7,1},{8,14},{9,15},{10,... | collective-permute-start | bytes 491528 | tf_op jit(solution)/shard_map/ppermute | solution.py:30
  81.9 1.9 %collective-permute-start.12 = (bf16[80,1024]{1,0:T(8,128)(2,1)S(1)}, bf16[80,1024]{1,0:T(8,128)(2,1)S(1)}, u32[]{:S(2)}, u32[]{:S(2)}) collective-permute-start(bf16[80,1024]{1,0:T(8,128)(2,1)S(1)} %get-tuple-element.84), channel_id=1, source_target_pairs={{0,2},{1,3},{2,0},{3,1},{4,6},{5,7},{6,4},{7,5},{8,10},{9,11},{10,... | collective-permute-start | bytes 491528 | tf_op jit(solution)/shard_map/ppermute | solution.py:30
  83.9 4.0 %collective-permute-done.24 = bf16[80,3584]{1,0:T(8,128)(2,1)S(1)} collective-permute-done((bf16[80,3584]{1,0:T(8,128)(2,1)S(1)}, bf16[80,3584]{1,0:T(8,128)(2,1)S(1)}, u32[]{:S(2)}, u32[]{:S(2)}) %collective-permute-start.24) | collective-permute-done | bytes 573472 | tf_op jit(solution)/shard_map/ppermute | solution.py:30
  89.7 1.6 %collective-permute-start.25 = (bf16[80,1792]{1,0:T(8,128)(2,1)S(1)}, bf16[80,1792]{1,0:T(8,128)(2,1)S(1)}, u32[]{:S(2)}, u32[]{:S(2)}) collective-permute-start(bf16[80,1792]{1,0:T(8,128)(2,1)S(1)} %get-tuple-element.103), channel_id=1, source_target_pairs={{0,8},{8,0},{16,24},{24,16},{1,9},{9,1},{17,25},{25,17},{2,10},{10... | collective-permute-start | bytes 860168 | tf_op jit(solution)/shard_map/ppermute | solution.py:30
  91.2 4.1 %convolution_convert_fusion = bf16[1792,1024]{1,0:T(8,128)(2,1)} fusion(bf16[320,1792]{1,0:T(8,128)(2,1)S(1)} %maximum_maximum_fusion, bf16[80,1024]{1,0:T(8,128)(2,1)S(1)} %get-tuple-element.79, bf16[80,1024]{1,0:T(8,128)(2,1)S(1)} %get-tuple-element.80, bf16[80,1024]{1,0:T(8,128)(2,1)S(1)} %get-tuple-element.81, bf16[80,1024]{1,0:T(8,128)(2,1)S(1)} %get-tuple-element.78), kind=kOutput, calls=%fused_computation | convolution fusion | flops 1178861568 | bytes 5472256 | tf_op jit(solution)/shard_map/dot_general | solution.py:257
  96.7 3.9 %convolution_convert_fusion.2 = bf16[1792,1024]{1,0:T(8,128)(2,1)} fusion(bf16[320,1792]{1,0:T(8,128)(2,1)S(1)} %pad_maximum_fusion, bf16[80,1024]{1,0:T(8,128)(2,1)S(1)} %get-tuple-element.87, bf16[80,1024]{1,0:T(8,128)(2,1)S(1)} %get-tuple-element.88, bf16[80,1024]{1,0:T(8,128)(2,1)S(1)} %get-tuple-element.89, bf16[80,1024]{1,0:T(8,128)(2,1)S(1)} %get-tuple-element.86), kind=kOutput, calls=%fused_computation.2 | convolution fusion | flops 1178861568 | bytes 5472256 | tf_op jit(solution)/shard_map/dot_general | solution.py:257
  100.6 3.9 %convolution_convert_fusion.1 = bf16[1792,1024]{1,0:T(8,128)(2,1)} fusion(bf16[320,1792]{1,0:T(8,128)(2,1)S(1)} %pad_maximum_fusion.1, bf16[80,1024]{1,0:T(8,128)(2,1)S(1)} %get-tuple-element.87, bf16[80,1024]{1,0:T(8,128)(2,1)S(1)} %get-tuple-element.88, bf16[80,1024]{1,0:T(8,128)(2,1)S(1)} %get-tuple-element.89, bf16[80,1024]{1,0:T(8,128)(2,1)S(1)} %get-tuple-element.86), kind=kOutput, calls=%fused_computation.1 | convolution fusion | flops 1178861568 | bytes 5472256 | tf_op jit(solution)/shard_map/dot_general | solution.py:257
  (116 shorter events, 25.5 us)
Async XLA Ops:
  3.9 10.3 %collective-permute-start.1 = (bf16[80,1024]{1,0:T(8,128)(2,1)S(1)}, bf16[80,1024]{1,0:T(8,128)(2,1)S(1)}, u32[]{:S(2)}, u32[]{:S(2)}) collective-permute-start(bf16[80,1024]{1,0:T(8,128)(2,1)S(1)} %pad_maximum_fusion.16), channel_id=1, source_target_pairs={{0,2},{1,3},{2,0},{3,1},{4,6},{5,7},{6,4},{7,5},{8,10},{9,11},{10,... | collective-permute-start | bytes 491528 | tf_op jit(solution)/shard_map/ppermute | solution.py:30
  6.9 15.1 %collective-permute-start.2 = (bf16[80,1024]{1,0:T(8,128)(2,1)S(1)}, bf16[80,1024]{1,0:T(8,128)(2,1)S(1)}, u32[]{:S(2)}, u32[]{:S(2)}) collective-permute-start(bf16[80,1024]{1,0:T(8,128)(2,1)S(1)} %pad_maximum_fusion.18), channel_id=1, source_target_pairs={{0,4},{1,5},{2,6},{3,7},{4,0},{5,1},{6,2},{7,3},{8,12},{9,13},{10,... | collective-permute-start | bytes 491528 | tf_op jit(solution)/shard_map/ppermute | solution.py:30
  9.6 12.5 %collective-permute-start.3 = (bf16[80,1024]{1,0:T(8,128)(2,1)S(1)}, bf16[80,1024]{1,0:T(8,128)(2,1)S(1)}, u32[]{:S(2)}, u32[]{:S(2)}) collective-permute-start(bf16[80,1024]{1,0:T(8,128)(2,1)S(1)} %pad_maximum_fusion.19), channel_id=1, source_target_pairs={{0,6},{1,7},{2,4},{3,5},{4,2},{5,3},{6,0},{7,1},{8,14},{9,15},{10,... | collective-permute-start | bytes 491528 | tf_op jit(solution)/shard_map/ppermute | solution.py:30
  14.2 27.2 %collective-permute-start.15 = (bf16[80,1024]{1,0:T(8,128)(2,1)S(1)}, bf16[80,1024]{1,0:T(8,128)(2,1)S(1)}, u32[]{:S(2)}, u32[]{:S(2)}) collective-permute-start(bf16[80,1024]{1,0:T(8,128)(2,1)S(1)} %get-tuple-element.34), channel_id=1, source_target_pairs={{0,2},{1,3},{2,0},{3,1},{4,6},{5,7},{6,4},{7,5},{8,10},{9,11},{10,... | collective-permute-start | bytes 491528 | tf_op jit(solution)/shard_map/ppermute | solution.py:30
  22.0 19.3 %collective-permute-start.16 = (bf16[80,1024]{1,0:T(8,128)(2,1)S(1)}, bf16[80,1024]{1,0:T(8,128)(2,1)S(1)}, u32[]{:S(2)}, u32[]{:S(2)}) collective-permute-start(bf16[80,1024]{1,0:T(8,128)(2,1)S(1)} %get-tuple-element.43), channel_id=1, source_target_pairs={{0,4},{1,5},{2,6},{3,7},{4,0},{5,1},{6,2},{7,3},{8,12},{9,13},{10,... | collective-permute-start | bytes 491528 | tf_op jit(solution)/shard_map/ppermute | solution.py:30
  26.0 15.3 %collective-permute-start.17 = (bf16[80,1024]{1,0:T(8,128)(2,1)S(1)}, bf16[80,1024]{1,0:T(8,128)(2,1)S(1)}, u32[]{:S(2)}, u32[]{:S(2)}) collective-permute-start(bf16[80,1024]{1,0:T(8,128)(2,1)S(1)} %get-tuple-element.44), channel_id=1, source_target_pairs={{0,6},{1,7},{2,4},{3,5},{4,2},{5,3},{6,0},{7,1},{8,14},{9,15},{10,... | collective-permute-start | bytes 491528 | tf_op jit(solution)/shard_map/ppermute | solution.py:30
  31.2 7.3 %collective-permute-start.4 = (bf16[80,1792]{1,0:T(8,128)(2,1)S(1)}, bf16[80,1792]{1,0:T(8,128)(2,1)S(1)}, u32[]{:S(2)}, u32[]{:S(2)}) collective-permute-start(bf16[80,1792]{1,0:T(8,128)(2,1)S(1)} %get-tuple-element.76), channel_id=1, source_target_pairs={{0,16},{8,24},{16,0},{24,8},{1,17},{9,25},{17,1},{25,9},{2,18},{10... | collective-permute-start | bytes 860168 | tf_op jit(solution)/shard_map/ppermute | solution.py:30
  34.2 7.0 %collective-permute-start.6 = (bf16[80,1792]{1,0:T(8,128)(2,1)S(1)}, bf16[80,1792]{1,0:T(8,128)(2,1)S(1)}, u32[]{:S(2)}, u32[]{:S(2)}) collective-permute-start(bf16[80,1792]{1,0:T(8,128)(2,1)S(1)} %get-tuple-element.75), channel_id=1, source_target_pairs={{0,8},{8,0},{16,24},{24,16},{1,9},{9,1},{17,25},{25,17},{2,10},{10... | collective-permute-start | bytes 860168 | tf_op jit(solution)/shard_map/ppermute | solution.py:30
  41.6 15.8 %collective-permute-start.7 = (bf16[80,3584]{1,0:T(8,128)(2,1)S(1)}, bf16[80,3584]{1,0:T(8,128)(2,1)S(1)}, u32[]{:S(2)}, u32[]{:S(2)}) collective-permute-start(bf16[80,3584]{1,0:T(8,128)(2,1)S(1)} %pad_maximum_fusion.6), channel_id=1, source_target_pairs={{0,16},{8,24},{16,0},{24,8},{1,17},{9,25},{17,1},{25,9},{2,18},{10... | collective-permute-start | bytes 1720328 | tf_op jit(solution)/shard_map/ppermute | solution.py:30
  42.2 15.8 %collective-permute-start.5 = (bf16[80,3584]{1,0:T(8,128)(2,1)S(1)}, bf16[80,3584]{1,0:T(8,128)(2,1)S(1)}, u32[]{:S(2)}, u32[]{:S(2)}) collective-permute-start(bf16[80,3584]{1,0:T(8,128)(2,1)S(1)} %pad_maximum_fusion.5), channel_id=1, source_target_pairs={{0,8},{8,0},{16,24},{24,16},{1,9},{9,1},{17,25},{25,17},{2,10},{10... | collective-permute-start | bytes 1720328 | tf_op jit(solution)/shard_map/ppermute | solution.py:30
  45.4 16.0 %collective-permute-start.20 = (bf16[80,896]{1,0:T(8,128)(2,1)S(1)}, bf16[80,896]{1,0:T(8,128)(2,1)S(1)}, u32[]{:S(2)}, u32[]{:S(2)}) collective-permute-start(bf16[80,896]{1,0:T(8,128)(2,1)S(1)} %get-tuple-element.70), channel_id=1, source_target_pairs={{0,16},{8,24},{16,0},{24,8},{1,17},{9,25},{17,1},{25,9},{2,18},{10... | collective-permute-start | bytes 430088 | tf_op jit(solution)/shard_map/ppermute | solution.py:30
  47.0 14.4 %collective-permute-start.19 = (bf16[80,896]{1,0:T(8,128)(2,1)S(1)}, bf16[80,896]{1,0:T(8,128)(2,1)S(1)}, u32[]{:S(2)}, u32[]{:S(2)}) collective-permute-start(bf16[80,896]{1,0:T(8,128)(2,1)S(1)} %get-tuple-element.71), channel_id=1, source_target_pairs={{0,8},{8,0},{16,24},{24,16},{1,9},{9,1},{17,25},{25,17},{2,10},{10... | collective-permute-start | bytes 430088 | tf_op jit(solution)/shard_map/ppermute | solution.py:30
  58.3 9.8 %collective-permute-start.9 = (bf16[80,1792]{1,0:T(8,128)(2,1)S(1)}, bf16[80,1792]{1,0:T(8,128)(2,1)S(1)}, u32[]{:S(2)}, u32[]{:S(2)}) collective-permute-start(bf16[80,1792]{1,0:T(8,128)(2,1)S(1)} %multiply_convert_fusion.2), channel_id=1, source_target_pairs={{0,16},{8,24},{16,0},{24,8},{1,17},{9,25},{17,1},{25,9},{2,18},{10... | collective-permute-start | bytes 860168 | tf_op jit(solution)/shard_map/ppermute | solution.py:30
  59.9 9.8 %collective-permute-start.8 = (bf16[80,1792]{1,0:T(8,128)(2,1)S(1)}, bf16[80,1792]{1,0:T(8,128)(2,1)S(1)}, u32[]{:S(2)}, u32[]{:S(2)}) collective-permute-start(bf16[80,1792]{1,0:T(8,128)(2,1)S(1)} %multiply_convert_fusion.2), channel_id=1, source_target_pairs={{0,8},{8,0},{16,24},{24,16},{1,9},{9,1},{17,25},{25,17},{2,10},{10... | collective-permute-start | bytes 860168 | tf_op jit(solution)/shard_map/ppermute | solution.py:30
  61.7 12.3 %collective-permute-start.22 = (bf16[80,1792]{1,0:T(8,128)(2,1)S(1)}, bf16[80,1792]{1,0:T(8,128)(2,1)S(1)}, u32[]{:S(2)}, u32[]{:S(2)}) collective-permute-start(bf16[80,1792]{1,0:T(8,128)(2,1)S(1)} %pad_maximum_fusion.11), channel_id=1, source_target_pairs={{0,16},{8,24},{16,0},{24,8},{1,17},{9,25},{17,1},{25,9},{2,18},{10... | collective-permute-start | bytes 860168 | tf_op jit(solution)/shard_map/ppermute | solution.py:30
  62.5 12.2 %collective-permute-start.21 = (bf16[80,1792]{1,0:T(8,128)(2,1)S(1)}, bf16[80,1792]{1,0:T(8,128)(2,1)S(1)}, u32[]{:S(2)}, u32[]{:S(2)}) collective-permute-start(bf16[80,1792]{1,0:T(8,128)(2,1)S(1)} %pad_maximum_fusion.10), channel_id=1, source_target_pairs={{0,8},{8,0},{16,24},{24,16},{1,9},{9,1},{17,25},{25,17},{2,10},{10... | collective-permute-start | bytes 860168 | tf_op jit(solution)/shard_map/ppermute | solution.py:30
  68.2 9.7 %collective-permute-start.10 = (bf16[80,896]{1,0:T(8,128)(2,1)S(1)}, bf16[80,896]{1,0:T(8,128)(2,1)S(1)}, u32[]{:S(2)}, u32[]{:S(2)}) collective-permute-start(bf16[80,896]{1,0:T(8,128)(2,1)S(1)} %get-tuple-element.114), channel_id=1, source_target_pairs={{0,8},{8,0},{16,24},{24,16},{1,9},{9,1},{17,25},{25,17},{2,10},{10... | collective-permute-start | bytes 430088 | tf_op jit(solution)/shard_map/ppermute | solution.py:30
  69.8 8.1 %collective-permute-start.11 = (bf16[80,896]{1,0:T(8,128)(2,1)S(1)}, bf16[80,896]{1,0:T(8,128)(2,1)S(1)}, u32[]{:S(2)}, u32[]{:S(2)}) collective-permute-start(bf16[80,896]{1,0:T(8,128)(2,1)S(1)} %get-tuple-element.113), channel_id=1, source_target_pairs={{0,16},{8,24},{16,0},{24,8},{1,17},{9,25},{17,1},{25,9},{2,18},{10... | collective-permute-start | bytes 430088 | tf_op jit(solution)/shard_map/ppermute | solution.py:30
  75.4 12.5 %collective-permute-start.24 = (bf16[80,3584]{1,0:T(8,128)(2,1)S(1)}, bf16[80,3584]{1,0:T(8,128)(2,1)S(1)}, u32[]{:S(2)}, u32[]{:S(2)}) collective-permute-start(bf16[80,3584]{1,0:T(8,128)(2,1)S(1)} %pad_maximum_fusion.7), channel_id=1, source_target_pairs={{0,16},{8,24},{16,0},{24,8},{1,17},{9,25},{17,1},{25,9},{2,18},{10... | collective-permute-start | bytes 1720328 | tf_op jit(solution)/shard_map/ppermute | solution.py:30
  76.4 12.3 %collective-permute-start.23 = (bf16[80,3584]{1,0:T(8,128)(2,1)S(1)}, bf16[80,3584]{1,0:T(8,128)(2,1)S(1)}, u32[]{:S(2)}, u32[]{:S(2)}) collective-permute-start(bf16[80,3584]{1,0:T(8,128)(2,1)S(1)} %pad_maximum_fusion.7), channel_id=1, source_target_pairs={{0,8},{8,0},{16,24},{24,16},{1,9},{9,1},{17,25},{25,17},{2,10},{10... | collective-permute-start | bytes 1720328 | tf_op jit(solution)/shard_map/ppermute | solution.py:30
  79.4 17.1 %collective-permute-start.14 = (bf16[80,1024]{1,0:T(8,128)(2,1)S(1)}, bf16[80,1024]{1,0:T(8,128)(2,1)S(1)}, u32[]{:S(2)}, u32[]{:S(2)}) collective-permute-start(bf16[80,1024]{1,0:T(8,128)(2,1)S(1)} %get-tuple-element.82), channel_id=1, source_target_pairs={{0,6},{1,7},{2,4},{3,5},{4,2},{5,3},{6,0},{7,1},{8,14},{9,15},{10,... | collective-permute-start | bytes 491528 | tf_op jit(solution)/shard_map/ppermute | solution.py:30
  81.9 14.6 %collective-permute-start.13 = (bf16[80,1024]{1,0:T(8,128)(2,1)S(1)}, bf16[80,1024]{1,0:T(8,128)(2,1)S(1)}, u32[]{:S(2)}, u32[]{:S(2)}) collective-permute-start(bf16[80,1024]{1,0:T(8,128)(2,1)S(1)} %get-tuple-element.83), channel_id=1, source_target_pairs={{0,4},{1,5},{2,6},{3,7},{4,0},{5,1},{6,2},{7,3},{8,12},{9,13},{10,... | collective-permute-start | bytes 491528 | tf_op jit(solution)/shard_map/ppermute | solution.py:30
  81.9 14.6 %collective-permute-start.12 = (bf16[80,1024]{1,0:T(8,128)(2,1)S(1)}, bf16[80,1024]{1,0:T(8,128)(2,1)S(1)}, u32[]{:S(2)}, u32[]{:S(2)}) collective-permute-start(bf16[80,1024]{1,0:T(8,128)(2,1)S(1)} %get-tuple-element.84), channel_id=1, source_target_pairs={{0,2},{1,3},{2,0},{3,1},{4,6},{5,7},{6,4},{7,5},{8,10},{9,11},{10,... | collective-permute-start | bytes 491528 | tf_op jit(solution)/shard_map/ppermute | solution.py:30
  96.6 8.0 %collective-permute-start.27 = (bf16[160,1024]{1,0:T(8,128)(2,1)S(1)}, bf16[160,1024]{1,0:T(8,128)(2,1)S(1)}, u32[]{:S(2)}, u32[]{:S(2)}) collective-permute-start(bf16[160,1024]{1,0:T(8,128)(2,1)S(1)} %pad_maximum_fusion.9), channel_id=1, source_target_pairs={{0,1},{1,0},{2,3},{3,2},{4,5},{5,4},{6,7},{7,6},{8,9},{9,8},{10,11... | collective-permute-start | bytes 983048 | tf_op jit(solution)/shard_map/ppermute | solution.py:30
  (9 other events, 30.1 us)

commit v6 on v5

--- a/solution.py
+++ b/solution.py
@@ -113,26 +113,36 @@
     return jnp.concatenate([each[:n] for each in back] + [other], axis=0)
 
 
-def scatter_far(first, second):
+def join_halves(near_rows, far_rows):
+    cols = near_rows.shape[1]
+    both = jnp.concatenate([near_rows.reshape(4, -1, cols), far_rows.reshape(4, -1, cols)], axis=1)
+    return both.reshape(-1, cols)
+
+
+def split_halves(rows):
+    cols = rows.shape[1]
+    near_rows, far_rows = jnp.split(rows.reshape(4, -1, cols), 2, axis=1)
+    return near_rows.reshape(-1, cols), far_rows.reshape(-1, cols)
+
+
+def scatter_half(first, second):
     n = first.shape[0] // 4
-    return swap(first[3 * n:], "dp", 1), swap(second[3 * n:], "dp", 2)
-
-
-def scatter_add(first, second, via_x, via_y):
+    from_x = swap(jnp.concatenate([first[n:2 * n], first[3 * n:]], axis=0), "dp", 1)
+    from_y = swap(second[2 * n:], "dp", 2)
+    return from_x, from_y
+
+
+def scatter_quarter(first, second, from_x, from_y, together):
     n = first.shape[0] // 4
-    to_x = jnp.concatenate([first[n:2 * n], add_round(second[n:2 * n], via_y)], axis=1)
-    to_y = jnp.concatenate([add_round(first[2 * n:3 * n], via_x), second[2 * n:3 * n]], axis=1)
-    return to_x, to_y
-
-
-def scatter_near(first, second, to_x, to_y):
-    n = first.shape[0] // 4
-    c = first.shape[1]
-    from_x = swap(to_x, "dp", 1)
-    from_y = swap(to_y, "dp", 2)
+    to_x, to_y = add_round(second[n:2 * n], from_y[n:]), add_round(first[2 * n:3 * n], from_x[n:])
+    if together:
+        to_x, to_y = after((to_x, to_y))
+    last_x, last_y = swap(to_x, "dp", 1), swap(to_y, "dp", 2)
+    if together:
+        last_x, last_y = after((last_x, last_y))
     return tuple(
-        own[:n].astype(F32) + x.astype(F32) + y.astype(F32)
-        for own, x, y in ((first, from_x[:, :c], from_y[:, :c]), (second, from_x[:, c:], from_y[:, c:]))
+        own[:n].astype(F32) + one[:n].astype(F32) + other.astype(F32)
+        for own, one, other in ((first, from_x, last_y), (second, from_y, last_x))
     )
 
 
@@ -202,13 +212,9 @@
         in_rows = to_chips(*pair_core(send_rows))
         cot_send, in_rows[1] = after((by_chip(cot_send), in_rows[1]))
         cot_next = swap(cot_send[1], "expert", 2)
-        cot_send, in_rows = after((cot_send, in_rows))
-        cot_rows = [cot_send[0], cot_next, swap(cot_send[2], "expert", 4), swap(cot_send[3], "expert", 6)]
     else:
-        in_rows = [all_to_all(send_rows, experts)]
+        in_rows = jnp.split(all_to_all(send_rows, experts), 2, axis=0)
         cot_rows = [all_to_all(cot_send, experts)]
-    in_rows = reorder(jnp.concatenate(in_rows, axis=0), me, 4)
-
     pieces = (w_gate, w_up, w_down)
     for bit_index in range(levels):
         partner = from_partner(as_sent(pieces), "expert", bit_index)
@@ -220,31 +226,42 @@
         return lax.dot_general(rows, weights, CONTRACT_FEATS, preferred_element_type=F32).astype(BF)
 
     half = gate_w.shape[0] // 2
-    part_gate, part_up = partial_product(in_rows, gate_w), partial_product(in_rows, up_w)
-    to_x, to_y = scatter_add(part_gate, part_up, *scatter_far(part_gate, part_up))
-    gate_sum, up_sum = scatter_near(part_gate, part_up, to_x, to_y)
-    cot_rows, zeros = after_start(cot_rows, to_x[:, -1:] + to_y[:, :1])
+    n = buckets // 4
+    middle = len(in_rows) // 2
+    near_rows = reorder(jnp.concatenate(in_rows[:middle], axis=0), me, 4)
+    near_parts = partial_product(near_rows, gate_w), partial_product(near_rows, up_w)
+    near_parts, far_rows = after((near_parts, in_rows[middle:]))
+    if near:
+        cot_send, far_rows = after((cot_send, far_rows))
+        cot_rows = [cot_send[0], cot_next, swap(cot_send[2], "expert", 4), swap(cot_send[3], "expert", 6)]
+    far_rows = reorder(jnp.concatenate(far_rows, axis=0), me, 4)
+    in_rows = join_halves(near_rows, far_rows)
+    part_gate = join_halves(near_parts[0], partial_product(far_rows, gate_w))
+    part_up = join_halves(near_parts[1], partial_product(far_rows, up_w))
+    halves = scatter_half(part_gate, part_up)
+    gate_sum, up_sum = scatter_quarter(part_gate, part_up, *halves, False)
+    cot_rows, zeros = after_start(cot_rows, halves[0][:n, :1] + halves[1][:n, :1])
     if near:
         cot_rows = core_last(cot_rows)
-    cot_rows = reorder(jnp.concatenate(cot_rows, axis=0), me, 4)
+    cot_halves = jnp.split(jnp.concatenate(cot_rows, axis=0), 2, axis=0)
+    cot_rows = join_halves(*(reorder(rows, me, 4) for rows in cot_halves))
 
     active, slope_term = silu_parts(gate_sum)
     own_hidden = (active * up_sum).astype(BF)
 
     part_hidden = partial_product(cot_rows, down_w)
     part_first, part_second = part_hidden[:, :half], part_hidden[:, half:]
-    via, more_zeros = after_start(scatter_far(part_first, part_second), own_hidden[:, :1])
-    to_x, to_y = scatter_add(part_first, part_second, *via)
+    halves, more_zeros = after_start(scatter_half(part_first, part_second), own_hidden[:, :1])
     own_hidden = (own_hidden[:, :half], own_hidden[:, half:])
     near_hidden = gather_near(*own_hidden)
     hidden = jnp.concatenate(gather_far(*own_hidden, *near_hidden), axis=1)
-    grad_hidden = jnp.concatenate(scatter_near(part_first, part_second, to_x, to_y), axis=1) + zeros + more_zeros
+    grad_hidden = jnp.concatenate(scatter_quarter(part_first, part_second, *halves, True), axis=1) + zeros + more_zeros
     out_rows = jnp.dot(hidden, down_w, preferred_element_type=F32).astype(BF)
 
     own_grads = ((grad_hidden * up_sum * slope_term).astype(BF), (grad_hidden * active).astype(BF))
     hidden, near_grads = after((hidden, gather_near(*own_grads)))
     grad_rows = gather_far(*own_grads, *near_grads)
-    back = reorder(out_rows, me, 4)
+    back = jnp.concatenate([reorder(rows, me, 4) for rows in split_halves(out_rows)], axis=0)
     if near:
         back, grad_rows = after((from_chips(back), grad_rows))
         returned = from_core(back)

time: 106 us -> 110 us (1.038)
  waiting for transfers between devices: 41.6 us -> 45.6 us
  starting transfers between devices: 37 us -> 33.4 us
  local copies, waits for them, and re-layouts: 0.77 us -> 3.25 us
    ppermute x28, waiting for transfers between devices: 41.6 us -> 45.6 us  [swap(): return lax.ppermute(block, axis, [(i, i ^ mask) for i in range(count)])]
    ppermute x28, starting transfers between devices: 37 us -> 33.4 us  [swap(): return lax.ppermute(block, axis, [(i, i ^ mask) for i in range(count)])]
    unnamed x16 -> x12, local copies, waits for them, and re-layouts: 0.08 us -> 2.53 us
    dot_general x3 -> x5, matrix products: 6.37 us -> 6.83 us  [partial_product(): lax.dot_general(rows, weights, CONTRACT_FEATS, preferred_element_type=F32)]
  transfers between devices with their start and end apart: 28 -> 28, of which waited for: 14 -> 15; matrix products, arithmetic and copies ran while one was open for 22% -> 22% of each run, Pallas kernels for 0% -> 0%
where the time goes in v6:
time: 110 us; the launch traced here: 109 us
  waiting for transfers between devices  45.6 us (41%)
  starting transfers between devices  33.4 us (30%)
  matrix products  22.8 us (21%)
  local copies, waits for them, and re-layouts  3.25 us (3%)
  other arithmetic  3.1 us (3%)
  between operations  1.33 us (1%)
    ppermute x28, waiting for transfers between devices, swap(): return lax.ppermute(block, axis, [(i, i ^ mask) for i in range(count)])  45.6 us
    ppermute x28, starting transfers between devices, swap(): return lax.ppermute(block, axis, [(i, i ^ mask) for i in range(count)])  33.4 us
    dot_general x3, matrix products, term(): lax.dot_general(left, right, CONTRACT_ROWS, preferred_element_type=F32)  12 us
    dot_general x5, matrix products, partial_product(): lax.dot_general(rows, weights, CONTRACT_FEATS, preferred_element_type=F32)  6.83 us
    unnamed x12, local copies, waits for them, and re-layouts  2.53 us
  transfers between devices with their start and end apart: 28, of which 15 were waited for; matrix products, arithmetic and copies ran while one was open for 22% of the time, Pallas kernels for 0%

profile of v6, /device:TPU:0, one launch (start us, length us, event | category | flops | bytes accessed | tf_op | source)
XLA Modules:
  0.0 109.5 jit_solution(8208180546677538846)
XLA Ops:
  3.9 3.0 %collective-permute-start.1 = (bf16[80,1024]{1,0:T(8,128)(2,1)S(1)}, bf16[80,1024]{1,0:T(8,128)(2,1)S(1)}, u32[]{:S(2)}, u32[]{:S(2)}) collective-permute-start(bf16[80,1024]{1,0:T(8,128)(2,1)S(1)} %pad_maximum_fusion.23), channel_id=1, source_target_pairs={{0,2},{1,3},{2,0},{3,1},{4,6},{5,7},{6,4},{7,5},{8,10},{9,11},{10,... | collective-permute-start | bytes 491528 | tf_op jit(solution)/shard_map/ppermute | solution.py:30
  6.9 2.7 %collective-permute-start.2 = (bf16[80,1024]{1,0:T(8,128)(2,1)S(1)}, bf16[80,1024]{1,0:T(8,128)(2,1)S(1)}, u32[]{:S(2)}, u32[]{:S(2)}) collective-permute-start(bf16[80,1024]{1,0:T(8,128)(2,1)S(1)} %pad_maximum_fusion.24), channel_id=1, source_target_pairs={{0,4},{1,5},{2,6},{3,7},{4,0},{5,1},{6,2},{7,3},{8,12},{9,13},{10,... | collective-permute-start | bytes 491528 | tf_op jit(solution)/shard_map/ppermute | solution.py:30
  9.7 4.5 %collective-permute-done.1 = bf16[80,1024]{1,0:T(8,128)(2,1)S(1)} collective-permute-done((bf16[80,1024]{1,0:T(8,128)(2,1)S(1)}, bf16[80,1024]{1,0:T(8,128)(2,1)S(1)}, u32[]{:S(2)}, u32[]{:S(2)}) %collective-permute-start.1) | collective-permute-done | bytes 163872 | tf_op jit(solution)/shard_map/ppermute | solution.py:30
  17.7 4.4 %collective-permute-done.2 = bf16[80,1024]{1,0:T(8,128)(2,1)S(1)} collective-permute-done((bf16[80,1024]{1,0:T(8,128)(2,1)S(1)}, bf16[80,1024]{1,0:T(8,128)(2,1)S(1)}, u32[]{:S(2)}, u32[]{:S(2)}) %collective-permute-start.2) | collective-permute-done | bytes 163872 | tf_op jit(solution)/shard_map/ppermute | solution.py:30
  24.8 4.1 %collective-permute-start.16 = (bf16[80,1024]{1,0:T(8,128)(2,1)S(1)}, bf16[80,1024]{1,0:T(8,128)(2,1)S(1)}, u32[]{:S(2)}, u32[]{:S(2)}) collective-permute-start(bf16[80,1024]{1,0:T(8,128)(2,1)S(1)} %get-tuple-element.51), channel_id=1, source_target_pairs={{0,4},{1,5},{2,6},{3,7},{4,0},{5,1},{6,2},{7,3},{8,12},{9,13},{10,... | collective-permute-start | bytes 491528 | tf_op jit(solution)/shard_map/ppermute | solution.py:30
  31.9 1.6 %collective-permute-start.6 = (bf16[160,1792]{1,0:T(8,128)(2,1)S(1)}, bf16[160,1792]{1,0:T(8,128)(2,1)S(1)}, u32[]{:S(2)}, u32[]{:S(2)}) collective-permute-start(bf16[160,1792]{1,0:T(8,128)(2,1)S(1)} %bitcast.153), channel_id=1, source_target_pairs={{0,16},{8,24},{16,0},{24,8},{1,17},{9,25},{17,1},{25,9},{2,18},{10... | collective-permute-start | bytes 1720328 | tf_op jit(solution)/shard_map/ppermute | solution.py:30
  33.6 10.1 %collective-permute-done.4 = bf16[160,1792]{1,0:T(8,128)(2,1)S(1)} collective-permute-done((bf16[160,1792]{1,0:T(8,128)(2,1)S(1)}, bf16[160,1792]{1,0:T(8,128)(2,1)S(1)}, u32[]{:S(2)}, u32[]{:S(2)}) %collective-permute-start.4) | collective-permute-done | bytes 573472 | tf_op jit(solution)/shard_map/ppermute | solution.py:30
  43.8 1.6 %collective-permute-start.5 = (bf16[80,1792]{1,0:T(8,128)(2,1)S(1)}, bf16[80,1792]{1,0:T(8,128)(2,1)S(1)}, u32[]{:S(2)}, u32[]{:S(2)}) collective-permute-start(bf16[80,1792]{1,0:T(8,128)(2,1)S(1)} %fusion.5), channel_id=1, source_target_pairs={{0,16},{8,24},{16,0},{24,8},{1,17},{9,25},{17,1},{25,9},{2,18},{10... | collective-permute-start | bytes 860168 | tf_op jit(solution)/shard_map/ppermute | solution.py:30
  47.4 3.8 %collective-permute-done.5 = bf16[80,1792]{1,0:T(8,128)(2,1)S(1)} collective-permute-done((bf16[80,1792]{1,0:T(8,128)(2,1)S(1)}, bf16[80,1792]{1,0:T(8,128)(2,1)S(1)}, u32[]{:S(2)}, u32[]{:S(2)}) %collective-permute-start.5) | collective-permute-done | bytes 286752 | tf_op jit(solution)/shard_map/ppermute | solution.py:30
  51.2 1.7 %collective-permute-done.7 = bf16[80,1792]{1,0:T(8,128)(2,1)S(1)} collective-permute-done((bf16[80,1792]{1,0:T(8,128)(2,1)S(1)}, bf16[80,1792]{1,0:T(8,128)(2,1)S(1)}, u32[]{:S(2)}, u32[]{:S(2)}) %collective-permute-start.7) | collective-permute-done | bytes 286752 | tf_op jit(solution)/shard_map/ppermute | solution.py:30
  53.3 2.3 %collective-permute-start.9 = (bf16[80,1792]{1,0:T(8,128)(2,1)S(1)}, bf16[80,1792]{1,0:T(8,128)(2,1)S(1)}, u32[]{:S(2)}, u32[]{:S(2)}) collective-permute-start(bf16[80,1792]{1,0:T(8,128)(2,1)S(1)} %get-tuple-element.76), channel_id=1, source_target_pairs={{0,16},{8,24},{16,0},{24,8},{1,17},{9,25},{17,1},{25,9},{2,18},{10... | collective-permute-start | bytes 860168 | tf_op jit(solution)/shard_map/ppermute | solution.py:30
  55.9 1.8 %copy-done.5 = bf16[1792,1024]{1,0:T(8,128)(2,1)S(1)} copy-done((bf16[1792,1024]{1,0:T(8,128)(2,1)S(1)}, bf16[1792,1024]{1,0:T(8,128)(2,1)}, u32[]{:S(2)}) %copy-start.5) | copy-done | bytes 3670040
  59.3 2.1 %collective-permute-start.19 = (bf16[160,896]{1,0:T(8,128)(2,1)S(1)}, bf16[160,896]{1,0:T(8,128)(2,1)S(1)}, u32[]{:S(2)}, u32[]{:S(2)}) collective-permute-start(bf16[160,896]{1,0:T(8,128)(2,1)S(1)} %pad_maximum_fusion.18), channel_id=1, source_target_pairs={{0,8},{8,0},{16,24},{24,16},{1,9},{9,1},{17,25},{25,17},{2,10},{10... | collective-permute-start | bytes 860168 | tf_op jit(solution)/shard_map/ppermute | solution.py:30
  65.5 3.6 %collective-permute-done.19 = bf16[160,896]{1,0:T(8,128)(2,1)S(1)} collective-permute-done((bf16[160,896]{1,0:T(8,128)(2,1)S(1)}, bf16[160,896]{1,0:T(8,128)(2,1)S(1)}, u32[]{:S(2)}, u32[]{:S(2)}) %collective-permute-start.19) | collective-permute-done | bytes 286752 | tf_op jit(solution)/shard_map/ppermute | solution.py:30
  69.2 1.8 %collective-permute-start.21 = (bf16[80,896]{1,0:T(8,128)(2,1)S(1)}, bf16[80,896]{1,0:T(8,128)(2,1)S(1)}, u32[]{:S(2)}, u32[]{:S(2)}) collective-permute-start(bf16[80,896]{1,0:T(8,128)(2,1)S(1)} %get-tuple-element.59), channel_id=1, source_target_pairs={{0,8},{8,0},{16,24},{24,16},{1,9},{9,1},{17,25},{25,17},{2,10},{10... | collective-permute-start | bytes 430088 | tf_op jit(solution)/shard_map/ppermute | solution.py:30
  73.4 2.5 %collective-permute-start.14 = (bf16[80,1024]{1,0:T(8,128)(2,1)S(1)}, bf16[80,1024]{1,0:T(8,128)(2,1)S(1)}, u32[]{:S(2)}, u32[]{:S(2)}) collective-permute-start(bf16[80,1024]{1,0:T(8,128)(2,1)S(1)} %pad_maximum_fusion.29), channel_id=1, source_target_pairs={{0,6},{1,7},{2,4},{3,5},{4,2},{5,3},{6,0},{7,1},{8,14},{9,15},{10,... | collective-permute-start | bytes 491528 | tf_op jit(solution)/shard_map/ppermute | solution.py:30
  75.9 1.8 %collective-permute-done.22 = bf16[80,896]{1,0:T(8,128)(2,1)S(1)} collective-permute-done((bf16[80,896]{1,0:T(8,128)(2,1)S(1)}, bf16[80,896]{1,0:T(8,128)(2,1)S(1)}, u32[]{:S(2)}, u32[]{:S(2)}) %collective-permute-start.22) | collective-permute-done | bytes 143392 | tf_op jit(solution)/shard_map/ppermute | solution.py:30
  79.0 1.9 %collective-permute-start.23 = (bf16[80,3584]{1,0:T(8,128)(2,1)S(1)}, bf16[80,3584]{1,0:T(8,128)(2,1)S(1)}, u32[]{:S(2)}, u32[]{:S(2)}) collective-permute-start(bf16[80,3584]{1,0:T(8,128)(2,1)S(1)} %pad_maximum_fusion.5), channel_id=1, source_target_pairs={{0,8},{8,0},{16,24},{24,16},{1,9},{9,1},{17,25},{25,17},{2,10},{10... | collective-permute-start | bytes 1720328 | tf_op jit(solution)/shard_map/ppermute | solution.py:30
  81.1 10.2 %collective-permute-done.24 = bf16[80,3584]{1,0:T(8,128)(2,1)S(1)} collective-permute-done((bf16[80,3584]{1,0:T(8,128)(2,1)S(1)}, bf16[80,3584]{1,0:T(8,128)(2,1)S(1)}, u32[]{:S(2)}, u32[]{:S(2)}) %collective-permute-start.24) | collective-permute-done | bytes 573472 | tf_op jit(solution)/shard_map/ppermute | solution.py:30
  91.6 1.8 %collective-permute-start.26 = (bf16[80,1792]{1,0:T(8,128)(2,1)S(1)}, bf16[80,1792]{1,0:T(8,128)(2,1)S(1)}, u32[]{:S(2)}, u32[]{:S(2)}) collective-permute-start(bf16[80,1792]{1,0:T(8,128)(2,1)S(1)} %get-tuple-element.104), channel_id=1, source_target_pairs={{0,16},{8,24},{16,0},{24,8},{1,17},{9,25},{17,1},{25,9},{2,18},{10... | collective-permute-start | bytes 860168 | tf_op jit(solution)/shard_map/ppermute | solution.py:30
  93.9 4.1 %convolution_convert_fusion = bf16[1792,1024]{1,0:T(8,128)(2,1)} fusion(bf16[320,1792]{1,0:T(8,128)(2,1)S(1)} %maximum_maximum_fusion, bf16[320,1024]{1,0:T(8,128)(2,1)S(1)} %bitcast.151), kind=kOutput, calls=%fused_computation | convolution fusion | flops 1176240128 | bytes 5472256 | tf_op jit(solution)/shard_map/dot_general | solution.py:274
  98.4 1.8 %collective-permute-done.25 = bf16[80,1792]{1,0:T(8,128)(2,1)S(1)} collective-permute-done((bf16[80,1792]{1,0:T(8,128)(2,1)S(1)}, bf16[80,1792]{1,0:T(8,128)(2,1)S(1)}, u32[]{:S(2)}, u32[]{:S(2)}) %collective-permute-start.25) | collective-permute-done | bytes 286752 | tf_op jit(solution)/shard_map/ppermute | solution.py:30
  100.5 3.9 %convolution_convert_fusion.2 = bf16[1792,1024]{1,0:T(8,128)(2,1)} fusion(bf16[320,1792]{1,0:T(8,128)(2,1)S(1)} %pad_maximum_fusion, bf16[320,1024]{1,0:T(8,128)(2,1)S(1)} %bitcast.148), kind=kOutput, calls=%fused_computation.2 | convolution fusion | flops 1176240128 | bytes 5472256 | tf_op jit(solution)/shard_map/dot_general | solution.py:274
  104.4 3.9 %convolution_convert_fusion.1 = bf16[1792,1024]{1,0:T(8,128)(2,1)} fusion(bf16[320,1792]{1,0:T(8,128)(2,1)S(1)} %pad_maximum_fusion.1, bf16[320,1024]{1,0:T(8,128)(2,1)S(1)} %bitcast.149), kind=kOutput, calls=%fused_computation.1 | convolution fusion | flops 1176240128 | bytes 5472256 | tf_op jit(solution)/shard_map/dot_general | solution.py:274
  (129 shorter events, 26.9 us)
Async XLA Ops:
  3.9 10.3 %collective-permute-start.1 = (bf16[80,1024]{1,0:T(8,128)(2,1)S(1)}, bf16[80,1024]{1,0:T(8,128)(2,1)S(1)}, u32[]{:S(2)}, u32[]{:S(2)}) collective-permute-start(bf16[80,1024]{1,0:T(8,128)(2,1)S(1)} %pad_maximum_fusion.23), channel_id=1, source_target_pairs={{0,2},{1,3},{2,0},{3,1},{4,6},{5,7},{6,4},{7,5},{8,10},{9,11},{10,... | collective-permute-start | bytes 491528 | tf_op jit(solution)/shard_map/ppermute | solution.py:30
  6.9 15.1 %collective-permute-start.2 = (bf16[80,1024]{1,0:T(8,128)(2,1)S(1)}, bf16[80,1024]{1,0:T(8,128)(2,1)S(1)}, u32[]{:S(2)}, u32[]{:S(2)}) collective-permute-start(bf16[80,1024]{1,0:T(8,128)(2,1)S(1)} %pad_maximum_fusion.24), channel_id=1, source_target_pairs={{0,4},{1,5},{2,6},{3,7},{4,0},{5,1},{6,2},{7,3},{8,12},{9,13},{10,... | collective-permute-start | bytes 491528 | tf_op jit(solution)/shard_map/ppermute | solution.py:30
  9.6 12.5 %collective-permute-start.3 = (bf16[80,1024]{1,0:T(8,128)(2,1)S(1)}, bf16[80,1024]{1,0:T(8,128)(2,1)S(1)}, u32[]{:S(2)}, u32[]{:S(2)}) collective-permute-start(bf16[80,1024]{1,0:T(8,128)(2,1)S(1)} %pad_maximum_fusion.25), channel_id=1, source_target_pairs={{0,6},{1,7},{2,4},{3,5},{4,2},{5,3},{6,0},{7,1},{8,14},{9,15},{10,... | collective-permute-start | bytes 491528 | tf_op jit(solution)/shard_map/ppermute | solution.py:30
  14.2 31.9 %collective-permute-start.15 = (bf16[80,1024]{1,0:T(8,128)(2,1)S(1)}, bf16[80,1024]{1,0:T(8,128)(2,1)S(1)}, u32[]{:S(2)}, u32[]{:S(2)}) collective-permute-start(bf16[80,1024]{1,0:T(8,128)(2,1)S(1)} %get-tuple-element.42), channel_id=1, source_target_pairs={{0,2},{1,3},{2,0},{3,1},{4,6},{5,7},{6,4},{7,5},{8,10},{9,11},{10,... | collective-permute-start | bytes 491528 | tf_op jit(solution)/shard_map/ppermute | solution.py:30
  24.8 21.2 %collective-permute-start.16 = (bf16[80,1024]{1,0:T(8,128)(2,1)S(1)}, bf16[80,1024]{1,0:T(8,128)(2,1)S(1)}, u32[]{:S(2)}, u32[]{:S(2)}) collective-permute-start(bf16[80,1024]{1,0:T(8,128)(2,1)S(1)} %get-tuple-element.51), channel_id=1, source_target_pairs={{0,4},{1,5},{2,6},{3,7},{4,0},{5,1},{6,2},{7,3},{8,12},{9,13},{10,... | collective-permute-start | bytes 491528 | tf_op jit(solution)/shard_map/ppermute | solution.py:30
  28.9 17.2 %collective-permute-start.17 = (bf16[80,1024]{1,0:T(8,128)(2,1)S(1)}, bf16[80,1024]{1,0:T(8,128)(2,1)S(1)}, u32[]{:S(2)}, u32[]{:S(2)}) collective-permute-start(bf16[80,1024]{1,0:T(8,128)(2,1)S(1)} %get-tuple-element.52), channel_id=1, source_target_pairs={{0,6},{1,7},{2,4},{3,5},{4,2},{5,3},{6,0},{7,1},{8,14},{9,15},{10,... | collective-permute-start | bytes 491528 | tf_op jit(solution)/shard_map/ppermute | solution.py:30
  30.3 13.4 %collective-permute-start.4 = (bf16[160,1792]{1,0:T(8,128)(2,1)S(1)}, bf16[160,1792]{1,0:T(8,128)(2,1)S(1)}, u32[]{:S(2)}, u32[]{:S(2)}) collective-permute-start(bf16[160,1792]{1,0:T(8,128)(2,1)S(1)} %pad_maximum_fusion.4), channel_id=1, source_target_pairs={{0,8},{8,0},{16,24},{24,16},{1,9},{9,1},{17,25},{25,17},{2,10},{10... | collective-permute-start | bytes 1720328 | tf_op jit(solution)/shard_map/ppermute | solution.py:30
  31.9 14.1 %collective-permute-start.6 = (bf16[160,1792]{1,0:T(8,128)(2,1)S(1)}, bf16[160,1792]{1,0:T(8,128)(2,1)S(1)}, u32[]{:S(2)}, u32[]{:S(2)}) collective-permute-start(bf16[160,1792]{1,0:T(8,128)(2,1)S(1)} %bitcast.153), channel_id=1, source_target_pairs={{0,16},{8,24},{16,0},{24,8},{1,17},{9,25},{17,1},{25,9},{2,18},{10... | collective-permute-start | bytes 1720328 | tf_op jit(solution)/shard_map/ppermute | solution.py:30
  43.8 7.4 %collective-permute-start.5 = (bf16[80,1792]{1,0:T(8,128)(2,1)S(1)}, bf16[80,1792]{1,0:T(8,128)(2,1)S(1)}, u32[]{:S(2)}, u32[]{:S(2)}) collective-permute-start(bf16[80,1792]{1,0:T(8,128)(2,1)S(1)} %fusion.5), channel_id=1, source_target_pairs={{0,16},{8,24},{16,0},{24,8},{1,17},{9,25},{17,1},{25,9},{2,18},{10... | collective-permute-start | bytes 860168 | tf_op jit(solution)/shard_map/ppermute | solution.py:30
  46.2 6.7 %collective-permute-start.7 = (bf16[80,1792]{1,0:T(8,128)(2,1)S(1)}, bf16[80,1792]{1,0:T(8,128)(2,1)S(1)}, u32[]{:S(2)}, u32[]{:S(2)}) collective-permute-start(bf16[80,1792]{1,0:T(8,128)(2,1)S(1)} %fusion.3), channel_id=1, source_target_pairs={{0,8},{8,0},{16,24},{24,16},{1,9},{9,1},{17,25},{25,17},{2,10},{10... | collective-permute-start | bytes 860168 | tf_op jit(solution)/shard_map/ppermute | solution.py:30
  47.2 8.4 %collective-permute-start.18 = (bf16[160,1024]{1,0:T(8,128)(2,1)S(1)}, bf16[160,1024]{1,0:T(8,128)(2,1)S(1)}, u32[]{:S(2)}, u32[]{:S(2)}) collective-permute-start(bf16[160,1024]{1,0:T(8,128)(2,1)S(1)} %pad_maximum_fusion.10), channel_id=1, source_target_pairs={{0,1},{1,0},{2,3},{3,2},{4,5},{5,4},{6,7},{7,6},{8,9},{9,8},{10,11... | collective-permute-start | bytes 983048 | tf_op jit(solution)/shard_map/ppermute | solution.py:30
  53.3 9.5 %collective-permute-start.9 = (bf16[80,1792]{1,0:T(8,128)(2,1)S(1)}, bf16[80,1792]{1,0:T(8,128)(2,1)S(1)}, u32[]{:S(2)}, u32[]{:S(2)}) collective-permute-start(bf16[80,1792]{1,0:T(8,128)(2,1)S(1)} %get-tuple-element.76), channel_id=1, source_target_pairs={{0,16},{8,24},{16,0},{24,8},{1,17},{9,25},{17,1},{25,9},{2,18},{10... | collective-permute-start | bytes 860168 | tf_op jit(solution)/shard_map/ppermute | solution.py:30
  55.6 9.0 %collective-permute-start.8 = (bf16[80,1792]{1,0:T(8,128)(2,1)S(1)}, bf16[80,1792]{1,0:T(8,128)(2,1)S(1)}, u32[]{:S(2)}, u32[]{:S(2)}) collective-permute-start(bf16[80,1792]{1,0:T(8,128)(2,1)S(1)} %get-tuple-element.76), channel_id=1, source_target_pairs={{0,8},{8,0},{16,24},{24,16},{1,9},{9,1},{17,25},{25,17},{2,10},{10... | collective-permute-start | bytes 860168 | tf_op jit(solution)/shard_map/ppermute | solution.py:30
  59.3 9.9 %collective-permute-start.19 = (bf16[160,896]{1,0:T(8,128)(2,1)S(1)}, bf16[160,896]{1,0:T(8,128)(2,1)S(1)}, u32[]{:S(2)}, u32[]{:S(2)}) collective-permute-start(bf16[160,896]{1,0:T(8,128)(2,1)S(1)} %pad_maximum_fusion.18), channel_id=1, source_target_pairs={{0,8},{8,0},{16,24},{24,16},{1,9},{9,1},{17,25},{25,17},{2,10},{10... | collective-permute-start | bytes 860168 | tf_op jit(solution)/shard_map/ppermute | solution.py:30
  61.4 7.8 %collective-permute-start.20 = (bf16[160,896]{1,0:T(8,128)(2,1)S(1)}, bf16[160,896]{1,0:T(8,128)(2,1)S(1)}, u32[]{:S(2)}, u32[]{:S(2)}) collective-permute-start(bf16[160,896]{1,0:T(8,128)(2,1)S(1)} %slice.397), channel_id=1, source_target_pairs={{0,16},{8,24},{16,0},{24,8},{1,17},{9,25},{17,1},{25,9},{2,18},{10... | collective-permute-start | bytes 860168 | tf_op jit(solution)/shard_map/ppermute | solution.py:30
  62.8 8.9 %collective-permute-start.10 = (bf16[80,896]{1,0:T(8,128)(2,1)S(1)}, bf16[80,896]{1,0:T(8,128)(2,1)S(1)}, u32[]{:S(2)}, u32[]{:S(2)}) collective-permute-start(bf16[80,896]{1,0:T(8,128)(2,1)S(1)} %get-tuple-element.142), channel_id=1, source_target_pairs={{0,8},{8,0},{16,24},{24,16},{1,9},{9,1},{17,25},{25,17},{2,10},{10... | collective-permute-start | bytes 430088 | tf_op jit(solution)/shard_map/ppermute | solution.py:30
  64.6 7.1 %collective-permute-start.11 = (bf16[80,896]{1,0:T(8,128)(2,1)S(1)}, bf16[80,896]{1,0:T(8,128)(2,1)S(1)}, u32[]{:S(2)}, u32[]{:S(2)}) collective-permute-start(bf16[80,896]{1,0:T(8,128)(2,1)S(1)} %get-tuple-element.141), channel_id=1, source_target_pairs={{0,16},{8,24},{16,0},{24,8},{1,17},{9,25},{17,1},{25,9},{2,18},{10... | collective-permute-start | bytes 430088 | tf_op jit(solution)/shard_map/ppermute | solution.py:30
  73.3 27.0 %collective-permute-start.13 = (bf16[80,1024]{1,0:T(8,128)(2,1)S(1)}, bf16[80,1024]{1,0:T(8,128)(2,1)S(1)}, u32[]{:S(2)}, u32[]{:S(2)}) collective-permute-start(bf16[80,1024]{1,0:T(8,128)(2,1)S(1)} %pad_maximum_fusion.28), channel_id=1, source_target_pairs={{0,4},{1,5},{2,6},{3,7},{4,0},{5,1},{6,2},{7,3},{8,12},{9,13},{10,... | collective-permute-start | bytes 491528 | tf_op jit(solution)/shard_map/ppermute | solution.py:30
  73.4 26.9 %collective-permute-start.14 = (bf16[80,1024]{1,0:T(8,128)(2,1)S(1)}, bf16[80,1024]{1,0:T(8,128)(2,1)S(1)}, u32[]{:S(2)}, u32[]{:S(2)}) collective-permute-start(bf16[80,1024]{1,0:T(8,128)(2,1)S(1)} %pad_maximum_fusion.29), channel_id=1, source_target_pairs={{0,6},{1,7},{2,4},{3,5},{4,2},{5,3},{6,0},{7,1},{8,14},{9,15},{10,... | collective-permute-start | bytes 491528 | tf_op jit(solution)/shard_map/ppermute | solution.py:30
  78.4 12.8 %collective-permute-start.24 = (bf16[80,3584]{1,0:T(8,128)(2,1)S(1)}, bf16[80,3584]{1,0:T(8,128)(2,1)S(1)}, u32[]{:S(2)}, u32[]{:S(2)}) collective-permute-start(bf16[80,3584]{1,0:T(8,128)(2,1)S(1)} %pad_maximum_fusion.5), channel_id=1, source_target_pairs={{0,16},{8,24},{16,0},{24,8},{1,17},{9,25},{17,1},{25,9},{2,18},{10... | collective-permute-start | bytes 1720328 | tf_op jit(solution)/shard_map/ppermute | solution.py:30
  79.0 12.6 %collective-permute-start.23 = (bf16[80,3584]{1,0:T(8,128)(2,1)S(1)}, bf16[80,3584]{1,0:T(8,128)(2,1)S(1)}, u32[]{:S(2)}, u32[]{:S(2)}) collective-permute-start(bf16[80,3584]{1,0:T(8,128)(2,1)S(1)} %pad_maximum_fusion.5), channel_id=1, source_target_pairs={{0,8},{8,0},{16,24},{24,16},{1,9},{9,1},{17,25},{25,17},{2,10},{10... | collective-permute-start | bytes 1720328 | tf_op jit(solution)/shard_map/ppermute | solution.py:30
  80.9 19.4 %collective-permute-start.12 = (bf16[80,1024]{1,0:T(8,128)(2,1)S(1)}, bf16[80,1024]{1,0:T(8,128)(2,1)S(1)}, u32[]{:S(2)}, u32[]{:S(2)}) collective-permute-start(bf16[80,1024]{1,0:T(8,128)(2,1)S(1)} %pad_maximum_fusion.27), channel_id=1, source_target_pairs={{0,2},{1,3},{2,0},{3,1},{4,6},{5,7},{6,4},{7,5},{8,10},{9,11},{10,... | collective-permute-start | bytes 491528 | tf_op jit(solution)/shard_map/ppermute | solution.py:30
  91.6 6.7 %collective-permute-start.26 = (bf16[80,1792]{1,0:T(8,128)(2,1)S(1)}, bf16[80,1792]{1,0:T(8,128)(2,1)S(1)}, u32[]{:S(2)}, u32[]{:S(2)}) collective-permute-start(bf16[80,1792]{1,0:T(8,128)(2,1)S(1)} %get-tuple-element.104), channel_id=1, source_target_pairs={{0,16},{8,24},{16,0},{24,8},{1,17},{9,25},{17,1},{25,9},{2,18},{10... | collective-permute-start | bytes 860168 | tf_op jit(solution)/shard_map/ppermute | solution.py:30
  100.4 8.0 %collective-permute-start.27 = (bf16[160,1024]{1,0:T(8,128)(2,1)S(1)}, bf16[160,1024]{1,0:T(8,128)(2,1)S(1)}, u32[]{:S(2)}, u32[]{:S(2)}) collective-permute-start(bf16[160,1024]{1,0:T(8,128)(2,1)S(1)} %pad_maximum_fusion.15), channel_id=1, source_target_pairs={{0,1},{1,0},{2,3},{3,2},{4,5},{5,4},{6,7},{7,6},{8,9},{9,8},{10,11... | collective-permute-start | bytes 983048 | tf_op jit(solution)/shard_map/ppermute | solution.py:30
  (10 other events, 41.3 us)

commit v7 on v6

--- a/solution.py
+++ b/solution.py
@@ -125,6 +125,29 @@
     return near_rows.reshape(-1, cols), far_rows.reshape(-1, cols)
 
 
+def scatter_far(first, second):
+    n = first.shape[0] // 4
+    return swap(first[3 * n:], "dp", 1), swap(second[3 * n:], "dp", 2)
+
+
+def scatter_add(first, second, via_x, via_y):
+    n = first.shape[0] // 4
+    to_x = jnp.concatenate([first[n:2 * n], add_round(second[n:2 * n], via_y)], axis=1)
+    to_y = jnp.concatenate([add_round(first[2 * n:3 * n], via_x), second[2 * n:3 * n]], axis=1)
+    return to_x, to_y
+
+
+def scatter_near(first, second, to_x, to_y):
+    n = first.shape[0] // 4
+    c = first.shape[1]
+    from_x = swap(to_x, "dp", 1)
+    from_y = swap(to_y, "dp", 2)
+    return tuple(
+        own[:n].astype(F32) + x.astype(F32) + y.astype(F32)
+        for own, x, y in ((first, from_x[:, :c], from_y[:, :c]), (second, from_x[:, c:], from_y[:, c:]))
+    )
+
+
 def scatter_half(first, second):
     n = first.shape[0] // 4
     from_x = swap(jnp.concatenate([first[n:2 * n], first[3 * n:]], axis=0), "dp", 1)
@@ -132,18 +155,16 @@
     return from_x, from_y
 
 
-def scatter_quarter(first, second, from_x, from_y, together):
-    n = first.shape[0] // 4
-    to_x, to_y = add_round(second[n:2 * n], from_y[n:]), add_round(first[2 * n:3 * n], from_x[n:])
-    if together:
-        to_x, to_y = after((to_x, to_y))
-    last_x, last_y = swap(to_x, "dp", 1), swap(to_y, "dp", 2)
-    if together:
-        last_x, last_y = after((last_x, last_y))
-    return tuple(
-        own[:n].astype(F32) + one[:n].astype(F32) + other.astype(F32)
-        for own, one, other in ((first, from_x, last_y), (second, from_y, last_x))
-    )
+def scatter_quarter(first, second, from_x, from_y):
+    n = first.shape[0] // 4
+    last_x = swap(add_round(second[n:2 * n], from_y[n:]), "dp", 1)
+    last_y = swap(add_round(first[2 * n:3 * n], from_x[n:]), "dp", 2)
+    return last_x, last_y
+
+
+def sum_quarter(own, one, other):
+    n = other.shape[0]
+    return own[:n].astype(F32) + one[:n].astype(F32) + other.astype(F32)
 
 
 def gather_near(first, second):
@@ -239,23 +260,27 @@
     part_gate = join_halves(near_parts[0], partial_product(far_rows, gate_w))
     part_up = join_halves(near_parts[1], partial_product(far_rows, up_w))
     halves = scatter_half(part_gate, part_up)
-    gate_sum, up_sum = scatter_quarter(part_gate, part_up, *halves, False)
+    last = scatter_quarter(part_gate, part_up, *halves)
     cot_rows, zeros = after_start(cot_rows, halves[0][:n, :1] + halves[1][:n, :1])
     if near:
         cot_rows = core_last(cot_rows)
     cot_halves = jnp.split(jnp.concatenate(cot_rows, axis=0), 2, axis=0)
     cot_rows = join_halves(*(reorder(rows, me, 4) for rows in cot_halves))
 
+    part_hidden = partial_product(cot_rows, down_w)
+    last, late_zeros = after_start(last, part_hidden[:n, :1])
+    gate_sum = sum_quarter(part_gate, halves[0], last[1])
+    up_sum = sum_quarter(part_up, halves[1], last[0])
     active, slope_term = silu_parts(gate_sum)
     own_hidden = (active * up_sum).astype(BF)
 
-    part_hidden = partial_product(cot_rows, down_w)
     part_first, part_second = part_hidden[:, :half], part_hidden[:, half:]
-    halves, more_zeros = after_start(scatter_half(part_first, part_second), own_hidden[:, :1])
+    via, more_zeros = after_start(scatter_far(part_first, part_second), own_hidden[:, :1])
+    to_x, to_y = scatter_add(part_first, part_second, *via)
     own_hidden = (own_hidden[:, :half], own_hidden[:, half:])
     near_hidden = gather_near(*own_hidden)
     hidden = jnp.concatenate(gather_far(*own_hidden, *near_hidden), axis=1)
-    grad_hidden = jnp.concatenate(scatter_quarter(part_first, part_second, *halves, True), axis=1) + zeros + more_zeros
+    grad_hidden = jnp.concatenate(scatter_near(part_first, part_second, to_x, to_y), axis=1) + zeros + late_zeros + more_zeros
     out_rows = jnp.dot(hidden, down_w, preferred_element_type=F32).astype(BF)
 
     own_grads = ((grad_hidden * up_sum * slope_term).astype(BF), (grad_hidden * active).astype(BF))

time: 110 us -> 107 us (0.973)
  starting transfers between devices: 33.4 us -> 30.2 us
    ppermute x28, starting transfers between devices: 33.4 us -> 30.2 us  [swap(): return lax.ppermute(block, axis, [(i, i ^ mask) for i in range(count)])]
  transfers between devices with their start and end apart: 28 -> 28, of which waited for: 15 -> 17; matrix products, arithmetic and copies ran while one was open for 22% -> 22% of each run, Pallas kernels for 0% -> 0%
where the time goes in v7:
time: 107 us
  waiting for transfers between devices  46 us (43%)
  starting transfers between devices  30.2 us (28%)
  matrix products  22.6 us (21%)
  local copies, waits for them, and re-layouts  3.25 us (3%)
  other arithmetic  3.24 us (3%)
  between operations  1.31 us (1%)
    ppermute x28, waiting for transfers between devices, swap(): return lax.ppermute(block, axis, [(i, i ^ mask) for i in range(count)])  46 us
    ppermute x28, starting transfers between devices, swap(): return lax.ppermute(block, axis, [(i, i ^ mask) for i in range(count)])  30.2 us
    dot_general x3, matrix products, term(): lax.dot_general(left, right, CONTRACT_ROWS, preferred_element_type=F32)  11.8 us
    dot_general x5, matrix products, partial_product(): lax.dot_general(rows, weights, CONTRACT_FEATS, preferred_element_type=F32)  6.83 us
    unnamed x12, local copies, waits for them, and re-layouts  2.53 us
  transfers between devices with their start and end apart: 28, of which 17 were waited for; matrix products, arithmetic and copies ran while one was open for 22% of the time, Pallas kernels for 0%

profile of v7, /device:TPU:0, one launch (start us, length us, event | category | flops | bytes accessed | tf_op | source)
XLA Modules:
  0.0 106.7 jit_solution(7340151818871636445)
XLA Ops:
  3.9 3.0 %collective-permute-start.1 = (bf16[80,1024]{1,0:T(8,128)(2,1)S(1)}, bf16[80,1024]{1,0:T(8,128)(2,1)S(1)}, u32[]{:S(2)}, u32[]{:S(2)}) collective-permute-start(bf16[80,1024]{1,0:T(8,128)(2,1)S(1)} %pad_maximum_fusion.24), channel_id=1, source_target_pairs={{0,2},{1,3},{2,0},{3,1},{4,6},{5,7},{6,4},{7,5},{8,10},{9,11},{10,... | collective-permute-start | bytes 491528 | tf_op jit(solution)/shard_map/ppermute | solution.py:30
  6.9 2.7 %collective-permute-start.2 = (bf16[80,1024]{1,0:T(8,128)(2,1)S(1)}, bf16[80,1024]{1,0:T(8,128)(2,1)S(1)}, u32[]{:S(2)}, u32[]{:S(2)}) collective-permute-start(bf16[80,1024]{1,0:T(8,128)(2,1)S(1)} %pad_maximum_fusion.25), channel_id=1, source_target_pairs={{0,4},{1,5},{2,6},{3,7},{4,0},{5,1},{6,2},{7,3},{8,12},{9,13},{10,... | collective-permute-start | bytes 491528 | tf_op jit(solution)/shard_map/ppermute | solution.py:30
  9.7 4.5 %collective-permute-done.1 = bf16[80,1024]{1,0:T(8,128)(2,1)S(1)} collective-permute-done((bf16[80,1024]{1,0:T(8,128)(2,1)S(1)}, bf16[80,1024]{1,0:T(8,128)(2,1)S(1)}, u32[]{:S(2)}, u32[]{:S(2)}) %collective-permute-start.1) | collective-permute-done | bytes 163872 | tf_op jit(solution)/shard_map/ppermute | solution.py:30
  17.7 4.4 %collective-permute-done.2 = bf16[80,1024]{1,0:T(8,128)(2,1)S(1)} collective-permute-done((bf16[80,1024]{1,0:T(8,128)(2,1)S(1)}, bf16[80,1024]{1,0:T(8,128)(2,1)S(1)}, u32[]{:S(2)}, u32[]{:S(2)}) %collective-permute-start.2) | collective-permute-done | bytes 163872 | tf_op jit(solution)/shard_map/ppermute | solution.py:30
  24.8 4.1 %collective-permute-start.9 = (bf16[80,1024]{1,0:T(8,128)(2,1)S(1)}, bf16[80,1024]{1,0:T(8,128)(2,1)S(1)}, u32[]{:S(2)}, u32[]{:S(2)}) collective-permute-start(bf16[80,1024]{1,0:T(8,128)(2,1)S(1)} %get-tuple-element.50), channel_id=1, source_target_pairs={{0,4},{1,5},{2,6},{3,7},{4,0},{5,1},{6,2},{7,3},{8,12},{9,13},{10,... | collective-permute-start | bytes 491528 | tf_op jit(solution)/shard_map/ppermute | solution.py:30
  30.3 1.6 %collective-permute-start.4 = (bf16[160,1792]{1,0:T(8,128)(2,1)S(1)}, bf16[160,1792]{1,0:T(8,128)(2,1)S(1)}, u32[]{:S(2)}, u32[]{:S(2)}) collective-permute-start(bf16[160,1792]{1,0:T(8,128)(2,1)S(1)} %pad_maximum_fusion.4), channel_id=1, source_target_pairs={{0,8},{8,0},{16,24},{24,16},{1,9},{9,1},{17,25},{25,17},{2,10},{10... | collective-permute-start | bytes 1720328 | tf_op jit(solution)/shard_map/ppermute | solution.py:30
  31.9 1.6 %collective-permute-start.5 = (bf16[160,1792]{1,0:T(8,128)(2,1)S(1)}, bf16[160,1792]{1,0:T(8,128)(2,1)S(1)}, u32[]{:S(2)}, u32[]{:S(2)}) collective-permute-start(bf16[160,1792]{1,0:T(8,128)(2,1)S(1)} %bitcast.153), channel_id=1, source_target_pairs={{0,16},{8,24},{16,0},{24,8},{1,17},{9,25},{17,1},{25,9},{2,18},{10... | collective-permute-start | bytes 1720328 | tf_op jit(solution)/shard_map/ppermute | solution.py:30
  33.6 10.1 %collective-permute-done.4 = bf16[160,1792]{1,0:T(8,128)(2,1)S(1)} collective-permute-done((bf16[160,1792]{1,0:T(8,128)(2,1)S(1)}, bf16[160,1792]{1,0:T(8,128)(2,1)S(1)}, u32[]{:S(2)}, u32[]{:S(2)}) %collective-permute-start.4) | collective-permute-done | bytes 573472 | tf_op jit(solution)/shard_map/ppermute | solution.py:30
  43.8 1.6 %collective-permute-start.7 = (bf16[80,1792]{1,0:T(8,128)(2,1)S(1)}, bf16[80,1792]{1,0:T(8,128)(2,1)S(1)}, u32[]{:S(2)}, u32[]{:S(2)}) collective-permute-start(bf16[80,1792]{1,0:T(8,128)(2,1)S(1)} %fusion.5), channel_id=1, source_target_pairs={{0,16},{8,24},{16,0},{24,8},{1,17},{9,25},{17,1},{25,9},{2,18},{10... | collective-permute-start | bytes 860168 | tf_op jit(solution)/shard_map/ppermute | solution.py:30
  48.2 1.8 %copy-done.5 = bf16[1792,1024]{1,0:T(8,128)(2,1)S(1)} copy-done((bf16[1792,1024]{1,0:T(8,128)(2,1)S(1)}, bf16[1792,1024]{1,0:T(8,128)(2,1)}, u32[]{:S(2)}) %copy-start.5) | copy-done | bytes 3670040
  50.0 1.4 %convolution_convert_fusion.3 = bf16[320,1792]{1,0:T(8,128)(2,1)S(1)} fusion(bf16[320,1024]{1,0:T(8,128)(2,1)S(1)} %bitcast.150, bf16[1792,1024]{1,0:T(8,128)(2,1)S(1)} %copy-done.5), kind=kOutput, calls=%fused_computation.3 | convolution fusion | flops 1174978560 | bytes 5472256 | tf_op jit(solution)/shard_map/dot_general | solution.py:247
  51.5 4.1 %collective-permute-done.6 = bf16[80,1792]{1,0:T(8,128)(2,1)S(1)} collective-permute-done((bf16[80,1792]{1,0:T(8,128)(2,1)S(1)}, bf16[80,1792]{1,0:T(8,128)(2,1)S(1)}, u32[]{:S(2)}, u32[]{:S(2)}) %collective-permute-start.6) | collective-permute-done | bytes 286752 | tf_op jit(solution)/shard_map/ppermute | solution.py:30
  55.7 1.5 %collective-permute-start.20 = (bf16[80,896]{1,0:T(8,128)(2,1)S(1)}, bf16[80,896]{1,0:T(8,128)(2,1)S(1)}, u32[]{:S(2)}, u32[]{:S(2)}) collective-permute-start(bf16[80,896]{1,0:T(8,128)(2,1)S(1)} %get-tuple-element.82), channel_id=1, source_target_pairs={{0,16},{8,24},{16,0},{24,8},{1,17},{9,25},{17,1},{25,9},{2,18},{10... | collective-permute-start | bytes 430088 | tf_op jit(solution)/shard_map/ppermute | solution.py:30
  60.3 2.0 %collective-permute-done.20 = bf16[80,896]{1,0:T(8,128)(2,1)S(1)} collective-permute-done((bf16[80,896]{1,0:T(8,128)(2,1)S(1)}, bf16[80,896]{1,0:T(8,128)(2,1)S(1)}, u32[]{:S(2)}, u32[]{:S(2)}) %collective-permute-start.20) | collective-permute-done | bytes 143392 | tf_op jit(solution)/shard_map/ppermute | solution.py:30
  62.3 1.6 %collective-permute-done.19 = bf16[80,896]{1,0:T(8,128)(2,1)S(1)} collective-permute-done((bf16[80,896]{1,0:T(8,128)(2,1)S(1)}, bf16[80,896]{1,0:T(8,128)(2,1)S(1)}, u32[]{:S(2)}, u32[]{:S(2)}) %collective-permute-start.19) | collective-permute-done | bytes 143392 | tf_op jit(solution)/shard_map/ppermute | solution.py:30
  64.6 3.9 %collective-permute-done.13 = bf16[80,1792]{1,0:T(8,128)(2,1)S(1)} collective-permute-done((bf16[80,1792]{1,0:T(8,128)(2,1)S(1)}, bf16[80,1792]{1,0:T(8,128)(2,1)S(1)}, u32[]{:S(2)}, u32[]{:S(2)}) %collective-permute-start.13) | collective-permute-done | bytes 286752 | tf_op jit(solution)/shard_map/ppermute | solution.py:30
  70.4 4.1 %collective-permute-done.22 = bf16[80,1792]{1,0:T(8,128)(2,1)S(1)} collective-permute-done((bf16[80,1792]{1,0:T(8,128)(2,1)S(1)}, bf16[80,1792]{1,0:T(8,128)(2,1)S(1)}, u32[]{:S(2)}, u32[]{:S(2)}) %collective-permute-start.22) | collective-permute-done | bytes 286752 | tf_op jit(solution)/shard_map/ppermute | solution.py:30
  74.5 1.5 %collective-permute-done.21 = bf16[80,1792]{1,0:T(8,128)(2,1)S(1)} collective-permute-done((bf16[80,1792]{1,0:T(8,128)(2,1)S(1)}, bf16[80,1792]{1,0:T(8,128)(2,1)S(1)}, u32[]{:S(2)}, u32[]{:S(2)}) %collective-permute-start.21) | collective-permute-done | bytes 286752 | tf_op jit(solution)/shard_map/ppermute | solution.py:30
  78.3 1.4 %convolution_convert_fusion.9 = bf16[320,1024]{1,0:T(8,128)(2,1)S(1)} fusion(bf16[1792,1024]{1,0:T(8,128)(2,1)S(1)} %copy-done.5, bf16[80,896]{1,0:T(8,128)(2,1)S(1)} %collective-permute-done.15, bf16[80,896]{1,0:T(8,128)(2,1)S(1)} %get-tuple-element.143, bf16[80,896]{1,0:T(8,128)(2,1)S(1)} %get-tuple-element.141, ...), kind=kOutput, calls=%fused_computation.17 | convolution fusion | flops 1183907840 | bytes 5472256 | tf_op jit(solution)/shard_map/dot_general | solution.py:284
  79.9 2.5 %collective-permute-start.18 = (bf16[80,1024]{1,0:T(8,128)(2,1)S(1)}, bf16[80,1024]{1,0:T(8,128)(2,1)S(1)}, u32[]{:S(2)}, u32[]{:S(2)}) collective-permute-start(bf16[80,1024]{1,0:T(8,128)(2,1)S(1)} %pad_maximum_fusion.30), channel_id=1, source_target_pairs={{0,6},{1,7},{2,4},{3,5},{4,2},{5,3},{6,0},{7,1},{8,14},{9,15},{10,... | collective-permute-start | bytes 491528 | tf_op jit(solution)/shard_map/ppermute | solution.py:30
  83.7 5.1 %collective-permute-done.24 = bf16[80,3584]{1,0:T(8,128)(2,1)S(1)} collective-permute-done((bf16[80,3584]{1,0:T(8,128)(2,1)S(1)}, bf16[80,3584]{1,0:T(8,128)(2,1)S(1)}, u32[]{:S(2)}, u32[]{:S(2)}) %collective-permute-start.24) | collective-permute-done | bytes 573472 | tf_op jit(solution)/shard_map/ppermute | solution.py:30
  91.6 3.9 %convolution_convert_fusion = bf16[1792,1024]{1,0:T(8,128)(2,1)} fusion(bf16[320,1792]{1,0:T(8,128)(2,1)S(1)} %maximum_maximum_fusion, bf16[320,1024]{1,0:T(8,128)(2,1)S(1)} %bitcast.151), kind=kOutput, calls=%fused_computation | convolution fusion | flops 1176240128 | bytes 5472256 | tf_op jit(solution)/shard_map/dot_general | solution.py:299
  97.7 3.9 %convolution_convert_fusion.2 = bf16[1792,1024]{1,0:T(8,128)(2,1)} fusion(bf16[320,1792]{1,0:T(8,128)(2,1)S(1)} %pad_maximum_fusion, bf16[320,1024]{1,0:T(8,128)(2,1)S(1)} %bitcast.148), kind=kOutput, calls=%fused_computation.2 | convolution fusion | flops 1176240128 | bytes 5472256 | tf_op jit(solution)/shard_map/dot_general | solution.py:299
  101.6 3.9 %convolution_convert_fusion.1 = bf16[1792,1024]{1,0:T(8,128)(2,1)} fusion(bf16[320,1792]{1,0:T(8,128)(2,1)S(1)} %pad_maximum_fusion.1, bf16[320,1024]{1,0:T(8,128)(2,1)S(1)} %bitcast.149), kind=kOutput, calls=%fused_computation.1 | convolution fusion | flops 1176240128 | bytes 5472256 | tf_op jit(solution)/shard_map/dot_general | solution.py:299
  (131 shorter events, 29.0 us)
Async XLA Ops:
  3.9 10.3 %collective-permute-start.1 = (bf16[80,1024]{1,0:T(8,128)(2,1)S(1)}, bf16[80,1024]{1,0:T(8,128)(2,1)S(1)}, u32[]{:S(2)}, u32[]{:S(2)}) collective-permute-start(bf16[80,1024]{1,0:T(8,128)(2,1)S(1)} %pad_maximum_fusion.24), channel_id=1, source_target_pairs={{0,2},{1,3},{2,0},{3,1},{4,6},{5,7},{6,4},{7,5},{8,10},{9,11},{10,... | collective-permute-start | bytes 491528 | tf_op jit(solution)/shard_map/ppermute | solution.py:30
  6.9 15.1 %collective-permute-start.2 = (bf16[80,1024]{1,0:T(8,128)(2,1)S(1)}, bf16[80,1024]{1,0:T(8,128)(2,1)S(1)}, u32[]{:S(2)}, u32[]{:S(2)}) collective-permute-start(bf16[80,1024]{1,0:T(8,128)(2,1)S(1)} %pad_maximum_fusion.25), channel_id=1, source_target_pairs={{0,4},{1,5},{2,6},{3,7},{4,0},{5,1},{6,2},{7,3},{8,12},{9,13},{10,... | collective-permute-start | bytes 491528 | tf_op jit(solution)/shard_map/ppermute | solution.py:30
  9.6 12.5 %collective-permute-start.3 = (bf16[80,1024]{1,0:T(8,128)(2,1)S(1)}, bf16[80,1024]{1,0:T(8,128)(2,1)S(1)}, u32[]{:S(2)}, u32[]{:S(2)}) collective-permute-start(bf16[80,1024]{1,0:T(8,128)(2,1)S(1)} %pad_maximum_fusion.26), channel_id=1, source_target_pairs={{0,6},{1,7},{2,4},{3,5},{4,2},{5,3},{6,0},{7,1},{8,14},{9,15},{10,... | collective-permute-start | bytes 491528 | tf_op jit(solution)/shard_map/ppermute | solution.py:30
  14.2 31.9 %collective-permute-start.8 = (bf16[80,1024]{1,0:T(8,128)(2,1)S(1)}, bf16[80,1024]{1,0:T(8,128)(2,1)S(1)}, u32[]{:S(2)}, u32[]{:S(2)}) collective-permute-start(bf16[80,1024]{1,0:T(8,128)(2,1)S(1)} %get-tuple-element.41), channel_id=1, source_target_pairs={{0,2},{1,3},{2,0},{3,1},{4,6},{5,7},{6,4},{7,5},{8,10},{9,11},{10,... | collective-permute-start | bytes 491528 | tf_op jit(solution)/shard_map/ppermute | solution.py:30
  24.8 21.2 %collective-permute-start.9 = (bf16[80,1024]{1,0:T(8,128)(2,1)S(1)}, bf16[80,1024]{1,0:T(8,128)(2,1)S(1)}, u32[]{:S(2)}, u32[]{:S(2)}) collective-permute-start(bf16[80,1024]{1,0:T(8,128)(2,1)S(1)} %get-tuple-element.50), channel_id=1, source_target_pairs={{0,4},{1,5},{2,6},{3,7},{4,0},{5,1},{6,2},{7,3},{8,12},{9,13},{10,... | collective-permute-start | bytes 491528 | tf_op jit(solution)/shard_map/ppermute | solution.py:30
  28.9 17.2 %collective-permute-start.10 = (bf16[80,1024]{1,0:T(8,128)(2,1)S(1)}, bf16[80,1024]{1,0:T(8,128)(2,1)S(1)}, u32[]{:S(2)}, u32[]{:S(2)}) collective-permute-start(bf16[80,1024]{1,0:T(8,128)(2,1)S(1)} %get-tuple-element.51), channel_id=1, source_target_pairs={{0,6},{1,7},{2,4},{3,5},{4,2},{5,3},{6,0},{7,1},{8,14},{9,15},{10,... | collective-permute-start | bytes 491528 | tf_op jit(solution)/shard_map/ppermute | solution.py:30
  30.3 13.4 %collective-permute-start.4 = (bf16[160,1792]{1,0:T(8,128)(2,1)S(1)}, bf16[160,1792]{1,0:T(8,128)(2,1)S(1)}, u32[]{:S(2)}, u32[]{:S(2)}) collective-permute-start(bf16[160,1792]{1,0:T(8,128)(2,1)S(1)} %pad_maximum_fusion.4), channel_id=1, source_target_pairs={{0,8},{8,0},{16,24},{24,16},{1,9},{9,1},{17,25},{25,17},{2,10},{10... | collective-permute-start | bytes 1720328 | tf_op jit(solution)/shard_map/ppermute | solution.py:30
  31.9 14.1 %collective-permute-start.5 = (bf16[160,1792]{1,0:T(8,128)(2,1)S(1)}, bf16[160,1792]{1,0:T(8,128)(2,1)S(1)}, u32[]{:S(2)}, u32[]{:S(2)}) collective-permute-start(bf16[160,1792]{1,0:T(8,128)(2,1)S(1)} %bitcast.153), channel_id=1, source_target_pairs={{0,16},{8,24},{16,0},{24,8},{1,17},{9,25},{17,1},{25,9},{2,18},{10... | collective-permute-start | bytes 1720328 | tf_op jit(solution)/shard_map/ppermute | solution.py:30
  43.8 7.7 %collective-permute-start.7 = (bf16[80,1792]{1,0:T(8,128)(2,1)S(1)}, bf16[80,1792]{1,0:T(8,128)(2,1)S(1)}, u32[]{:S(2)}, u32[]{:S(2)}) collective-permute-start(bf16[80,1792]{1,0:T(8,128)(2,1)S(1)} %fusion.5), channel_id=1, source_target_pairs={{0,16},{8,24},{16,0},{24,8},{1,17},{9,25},{17,1},{25,9},{2,18},{10... | collective-permute-start | bytes 860168 | tf_op jit(solution)/shard_map/ppermute | solution.py:30
  46.4 9.3 %collective-permute-start.6 = (bf16[80,1792]{1,0:T(8,128)(2,1)S(1)}, bf16[80,1792]{1,0:T(8,128)(2,1)S(1)}, u32[]{:S(2)}, u32[]{:S(2)}) collective-permute-start(bf16[80,1792]{1,0:T(8,128)(2,1)S(1)} %fusion.6), channel_id=1, source_target_pairs={{0,8},{8,0},{16,24},{24,16},{1,9},{9,1},{17,25},{25,17},{2,10},{10... | collective-permute-start | bytes 860168 | tf_op jit(solution)/shard_map/ppermute | solution.py:30
  57.8 10.6 %collective-permute-start.13 = (bf16[80,1792]{1,0:T(8,128)(2,1)S(1)}, bf16[80,1792]{1,0:T(8,128)(2,1)S(1)}, u32[]{:S(2)}, u32[]{:S(2)}) collective-permute-start(bf16[80,1792]{1,0:T(8,128)(2,1)S(1)} %get-tuple-element.74), channel_id=1, source_target_pairs={{0,16},{8,24},{16,0},{24,8},{1,17},{9,25},{17,1},{25,9},{2,18},{10... | collective-permute-start | bytes 860168 | tf_op jit(solution)/shard_map/ppermute | solution.py:30
  59.0 11.0 %collective-permute-start.12 = (bf16[80,1792]{1,0:T(8,128)(2,1)S(1)}, bf16[80,1792]{1,0:T(8,128)(2,1)S(1)}, u32[]{:S(2)}, u32[]{:S(2)}) collective-permute-start(bf16[80,1792]{1,0:T(8,128)(2,1)S(1)} %get-tuple-element.74), channel_id=1, source_target_pairs={{0,8},{8,0},{16,24},{24,16},{1,9},{9,1},{17,25},{25,17},{2,10},{10... | collective-permute-start | bytes 860168 | tf_op jit(solution)/shard_map/ppermute | solution.py:30
  64.1 10.5 %collective-permute-start.22 = (bf16[80,1792]{1,0:T(8,128)(2,1)S(1)}, bf16[80,1792]{1,0:T(8,128)(2,1)S(1)}, u32[]{:S(2)}, u32[]{:S(2)}) collective-permute-start(bf16[80,1792]{1,0:T(8,128)(2,1)S(1)} %pad_maximum_fusion.19), channel_id=1, source_target_pairs={{0,16},{8,24},{16,0},{24,8},{1,17},{9,25},{17,1},{25,9},{2,18},{10... | collective-permute-start | bytes 860168 | tf_op jit(solution)/shard_map/ppermute | solution.py:30
  64.4 11.7 %collective-permute-start.21 = (bf16[80,1792]{1,0:T(8,128)(2,1)S(1)}, bf16[80,1792]{1,0:T(8,128)(2,1)S(1)}, u32[]{:S(2)}, u32[]{:S(2)}) collective-permute-start(bf16[80,1792]{1,0:T(8,128)(2,1)S(1)} %pad_maximum_fusion.18), channel_id=1, source_target_pairs={{0,8},{8,0},{16,24},{24,16},{1,9},{9,1},{17,25},{25,17},{2,10},{10... | collective-permute-start | bytes 860168 | tf_op jit(solution)/shard_map/ppermute | solution.py:30
  68.4 9.9 %collective-permute-start.14 = (bf16[80,896]{1,0:T(8,128)(2,1)S(1)}, bf16[80,896]{1,0:T(8,128)(2,1)S(1)}, u32[]{:S(2)}, u32[]{:S(2)}) collective-permute-start(bf16[80,896]{1,0:T(8,128)(2,1)S(1)} %get-tuple-element.142), channel_id=1, source_target_pairs={{0,8},{8,0},{16,24},{24,16},{1,9},{9,1},{17,25},{25,17},{2,10},{10... | collective-permute-start | bytes 430088 | tf_op jit(solution)/shard_map/ppermute | solution.py:30
  70.0 8.3 %collective-permute-start.15 = (bf16[80,896]{1,0:T(8,128)(2,1)S(1)}, bf16[80,896]{1,0:T(8,128)(2,1)S(1)}, u32[]{:S(2)}, u32[]{:S(2)}) collective-permute-start(bf16[80,896]{1,0:T(8,128)(2,1)S(1)} %get-tuple-element.141), channel_id=1, source_target_pairs={{0,16},{8,24},{16,0},{24,8},{1,17},{9,25},{17,1},{25,9},{2,18},{10... | collective-permute-start | bytes 430088 | tf_op jit(solution)/shard_map/ppermute | solution.py:30
  76.9 11.9 %collective-permute-start.24 = (bf16[80,3584]{1,0:T(8,128)(2,1)S(1)}, bf16[80,3584]{1,0:T(8,128)(2,1)S(1)}, u32[]{:S(2)}, u32[]{:S(2)}) collective-permute-start(bf16[80,3584]{1,0:T(8,128)(2,1)S(1)} %pad_maximum_fusion.5), channel_id=1, source_target_pairs={{0,16},{8,24},{16,0},{24,8},{1,17},{9,25},{17,1},{25,9},{2,18},{10... | collective-permute-start | bytes 1720328 | tf_op jit(solution)/shard_map/ppermute | solution.py:30
  77.2 12.7 %collective-permute-start.23 = (bf16[80,3584]{1,0:T(8,128)(2,1)S(1)}, bf16[80,3584]{1,0:T(8,128)(2,1)S(1)}, u32[]{:S(2)}, u32[]{:S(2)}) collective-permute-start(bf16[80,3584]{1,0:T(8,128)(2,1)S(1)} %pad_maximum_fusion.5), channel_id=1, source_target_pairs={{0,8},{8,0},{16,24},{24,16},{1,9},{9,1},{17,25},{25,17},{2,10},{10... | collective-permute-start | bytes 1720328 | tf_op jit(solution)/shard_map/ppermute | solution.py:30
  79.8 17.6 %collective-permute-start.17 = (bf16[80,1024]{1,0:T(8,128)(2,1)S(1)}, bf16[80,1024]{1,0:T(8,128)(2,1)S(1)}, u32[]{:S(2)}, u32[]{:S(2)}) collective-permute-start(bf16[80,1024]{1,0:T(8,128)(2,1)S(1)} %pad_maximum_fusion.29), channel_id=1, source_target_pairs={{0,4},{1,5},{2,6},{3,7},{4,0},{5,1},{6,2},{7,3},{8,12},{9,13},{10,... | collective-permute-start | bytes 491528 | tf_op jit(solution)/shard_map/ppermute | solution.py:30
  79.9 17.5 %collective-permute-start.18 = (bf16[80,1024]{1,0:T(8,128)(2,1)S(1)}, bf16[80,1024]{1,0:T(8,128)(2,1)S(1)}, u32[]{:S(2)}, u32[]{:S(2)}) collective-permute-start(bf16[80,1024]{1,0:T(8,128)(2,1)S(1)} %pad_maximum_fusion.30), channel_id=1, source_target_pairs={{0,6},{1,7},{2,4},{3,5},{4,2},{5,3},{6,0},{7,1},{8,14},{9,15},{10,... | collective-permute-start | bytes 491528 | tf_op jit(solution)/shard_map/ppermute | solution.py:30
  82.5 14.9 %collective-permute-start.16 = (bf16[80,1024]{1,0:T(8,128)(2,1)S(1)}, bf16[80,1024]{1,0:T(8,128)(2,1)S(1)}, u32[]{:S(2)}, u32[]{:S(2)}) collective-permute-start(bf16[80,1024]{1,0:T(8,128)(2,1)S(1)} %pad_maximum_fusion.28), channel_id=1, source_target_pairs={{0,2},{1,3},{2,0},{3,1},{4,6},{5,7},{6,4},{7,5},{8,10},{9,11},{10,... | collective-permute-start | bytes 491528 | tf_op jit(solution)/shard_map/ppermute | solution.py:30
  90.0 6.7 %collective-permute-start.26 = (bf16[80,1792]{1,0:T(8,128)(2,1)S(1)}, bf16[80,1792]{1,0:T(8,128)(2,1)S(1)}, u32[]{:S(2)}, u32[]{:S(2)}) collective-permute-start(bf16[80,1792]{1,0:T(8,128)(2,1)S(1)} %get-tuple-element.104), channel_id=1, source_target_pairs={{0,16},{8,24},{16,0},{24,8},{1,17},{9,25},{17,1},{25,9},{2,18},{10... | collective-permute-start | bytes 860168 | tf_op jit(solution)/shard_map/ppermute | solution.py:30
  90.7 6.7 %collective-permute-start.25 = (bf16[80,1792]{1,0:T(8,128)(2,1)S(1)}, bf16[80,1792]{1,0:T(8,128)(2,1)S(1)}, u32[]{:S(2)}, u32[]{:S(2)}) collective-permute-start(bf16[80,1792]{1,0:T(8,128)(2,1)S(1)} %get-tuple-element.103), channel_id=1, source_target_pairs={{0,8},{8,0},{16,24},{24,16},{1,9},{9,1},{17,25},{25,17},{2,10},{10... | collective-permute-start | bytes 860168 | tf_op jit(solution)/shard_map/ppermute | solution.py:30
  97.6 8.0 %collective-permute-start.27 = (bf16[160,1024]{1,0:T(8,128)(2,1)S(1)}, bf16[160,1024]{1,0:T(8,128)(2,1)S(1)}, u32[]{:S(2)}, u32[]{:S(2)}) collective-permute-start(bf16[160,1024]{1,0:T(8,128)(2,1)S(1)} %pad_maximum_fusion.15), channel_id=1, source_target_pairs={{0,1},{1,0},{2,3},{3,2},{4,5},{5,4},{6,7},{7,6},{8,9},{9,8},{10,11... | collective-permute-start | bytes 983048 | tf_op jit(solution)/shard_map/ppermute | solution.py:30
  (10 other events, 36.3 us)

commit v8 on v3

--- a/solution.py
+++ b/solution.py
@@ -1,6 +1,8 @@
 import jax
 import jax.numpy as jnp
 from jax import lax
+from jax.experimental import pallas as pl
+from jax.experimental.pallas import tpu as pltpu
 from jax.sharding import PartitionSpec as P
 
 BF = jnp.bfloat16
@@ -153,6 +155,36 @@
 
 CONTRACT_FEATS = (((1,), (1,)), ((), ()))
 CONTRACT_ROWS = (((0,), (0,)), ((), ()))
+
+
+def two_terms(first, second, rows):
+    count, width = first.shape
+    feats = rows.shape[1]
+    block = 256
+
+    def kernel(first_ref, second_ref, rows_ref, first_out, second_out):
+        lines = lax.broadcasted_iota(jnp.int32, (block, block), 0)
+        identity = (lines == lax.broadcasted_iota(jnp.int32, (block, block), 1)).astype(BF)
+        for left_ref, out in ((first_ref, first_out), (second_ref, second_out)):
+            turned = lax.dot_general(identity, left_ref[...], CONTRACT_FEATS, preferred_element_type=F32)
+            out[...] = jnp.dot(turned.astype(BF), rows_ref[...], preferred_element_type=F32).astype(BF)
+
+    left_spec = pl.BlockSpec((count, block), lambda i: (0, i))
+    out_spec = pl.BlockSpec((block, feats), lambda i: (i, 0))
+    out = jax.ShapeDtypeStruct((width, feats), BF)
+    return pl.pallas_call(
+        kernel,
+        grid=(width // block,),
+        in_specs=[left_spec, left_spec, pl.BlockSpec((count, feats), lambda i: (0, 0))],
+        out_specs=[out_spec, out_spec],
+        out_shape=[out, out],
+        compiler_params=pltpu.CompilerParams(vmem_limit_bytes=24 * 2**20),
+        cost_estimate=pl.CostEstimate(
+            flops=16 * count * width * feats,
+            bytes_accessed=16 * (count + feats) * width,
+            transcendentals=0,
+        ),
+    )(first, second, rows)
 
 
 def per_device(tokens, expert_ids, route_weights, w_gate, w_up, w_down, out_grad):
@@ -248,14 +280,14 @@
         returned = from_core(back)
     else:
         returned = all_to_all(back, experts)
-    picked_0 = jnp.dot(place_0, returned, preferred_element_type=F32)
-    picked_1 = jnp.dot(place_1, returned, preferred_element_type=F32)
-    output = (route_weights[:, :1] * picked_0 + route_weights[:, 1:] * picked_1).astype(BF)
+    weighted = (route_weights[:, :1] * place_0 + route_weights[:, 1:] * place_1).astype(BF)
+    output = jnp.dot(weighted, returned, preferred_element_type=F32).astype(BF)
 
     def term(left, right):
         return lax.dot_general(left, right, CONTRACT_ROWS, preferred_element_type=F32).astype(BF)
 
-    grad_terms = (term(grad_rows[0], in_rows), term(grad_rows[1], in_rows), term(hidden, cot_rows))
+    down_term, grad_rows = after((term(hidden, cot_rows), grad_rows))
+    grad_terms = (*two_terms(*grad_rows, in_rows), down_term)
     for bit_index in range(levels):
         partner = from_partner(grad_terms, "expert", bit_index)
         grad_terms = tuple(add_round(own, their) for own, their in zip(grad_terms, partner))

time: 105 us -> 106 us (level)
  Pallas kernels: 0 us -> 8.44 us
  matrix products: 20.5 us -> 12.2 us
  waiting for transfers between devices: 43.9 us -> 42.8 us
    pallas_call x0 -> x1, Pallas kernels: none -> 8.44 us  [two_terms(): pl.pallas_call(kernel, grid=(width // block,), in_specs=[left_spec, left_...]
    dot_general x3 -> x1, matrix products: 12 us -> 3.95 us  [term(): lax.dot_general(left, right, CONTRACT_ROWS, preferred_element_type=F32)]
    ppermute x28, waiting for transfers between devices: 43.9 us -> 42.8 us  [swap(): return lax.ppermute(block, axis, [(i, i ^ mask) for i in range(count)])]
  transfers between devices with their start and end apart: 28 -> 28, of which waited for: 15 -> 13; matrix products, arithmetic and copies ran while one was open for 20% -> 12% of each run, Pallas kernels for 0% -> 8%
where the time goes in v8:
time: 106 us; the launch traced here: 105 us
  waiting for transfers between devices  42.8 us (40%)
  starting transfers between devices  36.5 us (34%)
  matrix products  12.2 us (12%)
  Pallas kernels  8.44 us (8%)
  other arithmetic  2.82 us (3%)
  local copies, waits for them, and re-layouts  1.37 us (1%)
  between operations  1.27 us (1%)
    ppermute x28, waiting for transfers between devices, swap(): return lax.ppermute(block, axis, [(i, i ^ mask) for i in range(count)])  42.8 us
    ppermute x28, starting transfers between devices, swap(): return lax.ppermute(block, axis, [(i, i ^ mask) for i in range(count)])  36.5 us
    pallas_call x1, Pallas kernels, two_terms(): pl.pallas_call(kernel, grid=(width // block,), in_specs=[left_spec, left_...  8.44 us
    dot_general x3, matrix products, partial_product(): lax.dot_general(rows, weights, CONTRACT_FEATS, preferred_element_type=F32)  4.24 us
    dot_general x1, matrix products, term(): lax.dot_general(left, right, CONTRACT_ROWS, preferred_element_type=F32)  3.95 us
  transfers between devices with their start and end apart: 28, of which 13 were waited for; matrix products, arithmetic and copies ran while one was open for 12% of the time, Pallas kernels for 8%

profile of v8, /device:TPU:0, one launch (start us, length us, event | category | flops | bytes accessed | tf_op | source)
XLA Modules:
  0.0 105.4 jit_solution(15752896346185907186)
XLA Ops:
  3.9 3.0 %collective-permute-start.1 = (bf16[80,1024]{1,0:T(8,128)(2,1)S(1)}, bf16[80,1024]{1,0:T(8,128)(2,1)S(1)}, u32[]{:S(2)}, u32[]{:S(2)}) collective-permute-start(bf16[80,1024]{1,0:T(8,128)(2,1)S(1)} %pad_maximum_fusion.13), channel_id=1, source_target_pairs={{0,2},{1,3},{2,0},{3,1},{4,6},{5,7},{6,4},{7,5},{8,10},{9,11},{10,... | collective-permute-start | bytes 491528 | tf_op jit(solution)/shard_map/ppermute | solution.py:32
  6.9 2.7 %collective-permute-start.2 = (bf16[80,1024]{1,0:T(8,128)(2,1)S(1)}, bf16[80,1024]{1,0:T(8,128)(2,1)S(1)}, u32[]{:S(2)}, u32[]{:S(2)}) collective-permute-start(bf16[80,1024]{1,0:T(8,128)(2,1)S(1)} %pad_maximum_fusion.14), channel_id=1, source_target_pairs={{0,4},{1,5},{2,6},{3,7},{4,0},{5,1},{6,2},{7,3},{8,12},{9,13},{10,... | collective-permute-start | bytes 491528 | tf_op jit(solution)/shard_map/ppermute | solution.py:32
  10.2 4.0 %collective-permute-done.1 = bf16[80,1024]{1,0:T(8,128)(2,1)S(1)} collective-permute-done((bf16[80,1024]{1,0:T(8,128)(2,1)S(1)}, bf16[80,1024]{1,0:T(8,128)(2,1)S(1)}, u32[]{:S(2)}, u32[]{:S(2)}) %collective-permute-start.1) | collective-permute-done | bytes 163872 | tf_op jit(solution)/shard_map/ppermute | solution.py:32
  14.2 7.8 %collective-permute-done.2 = bf16[80,1024]{1,0:T(8,128)(2,1)S(1)} collective-permute-done((bf16[80,1024]{1,0:T(8,128)(2,1)S(1)}, bf16[80,1024]{1,0:T(8,128)(2,1)S(1)}, u32[]{:S(2)}, u32[]{:S(2)}) %collective-permute-start.2) | collective-permute-done | bytes 163872 | tf_op jit(solution)/shard_map/ppermute | solution.py:32
  22.1 3.1 %collective-permute-start.15 = (bf16[80,1024]{1,0:T(8,128)(2,1)S(1)}, bf16[80,1024]{1,0:T(8,128)(2,1)S(1)}, u32[]{:S(2)}, u32[]{:S(2)}) collective-permute-start(bf16[80,1024]{1,0:T(8,128)(2,1)S(1)} %pad_maximum_fusion.17), channel_id=1, source_target_pairs={{0,2},{1,3},{2,0},{3,1},{4,6},{5,7},{6,4},{7,5},{8,10},{9,11},{10,... | collective-permute-start | bytes 491528 | tf_op jit(solution)/shard_map/ppermute | solution.py:32
  26.2 1.5 %collective-permute-start.17 = (bf16[80,1024]{1,0:T(8,128)(2,1)S(1)}, bf16[80,1024]{1,0:T(8,128)(2,1)S(1)}, u32[]{:S(2)}, u32[]{:S(2)}) collective-permute-start(bf16[80,1024]{1,0:T(8,128)(2,1)S(1)} %pad_maximum_fusion.19), channel_id=1, source_target_pairs={{0,6},{1,7},{2,4},{3,5},{4,2},{5,3},{6,0},{7,1},{8,14},{9,15},{10,... | collective-permute-start | bytes 491528 | tf_op jit(solution)/shard_map/ppermute | solution.py:32
  27.9 1.4 %convolution_convert_fusion.3 = bf16[320,1792]{1,0:T(8,128)(2,1)S(1)} fusion(bf16[1792,1024]{1,0:T(8,128)(2,1)S(1)} %copy-done.3, bf16[80,1024]{1,0:T(8,128)(2,1)S(1)} %get-tuple-element.91, bf16[80,1024]{1,0:T(8,128)(2,1)S(1)} %get-tuple-element.92, bf16[80,1024]{1,0:T(8,128)(2,1)S(1)} %get-tuple-element.93, bf16[80,1024]{1,0:T(8,128)(2,1)S(1)} %get-tuple-element.90), kind=kOutput, calls=%fused_computation.3 | convolution fusion | flops 1177600000 | bytes 5472256 | tf_op jit(solution)/shard_map/dot_general | solution.py:250
  31.4 1.6 %collective-permute-start.4 = (bf16[80,1792]{1,0:T(8,128)(2,1)S(1)}, bf16[80,1792]{1,0:T(8,128)(2,1)S(1)}, u32[]{:S(2)}, u32[]{:S(2)}) collective-permute-start(bf16[80,1792]{1,0:T(8,128)(2,1)S(1)} %get-tuple-element.72), channel_id=1, source_target_pairs={{0,16},{8,24},{16,0},{24,8},{1,17},{9,25},{17,1},{25,9},{2,18},{10... | collective-permute-start | bytes 860168 | tf_op jit(solution)/shard_map/ppermute | solution.py:32
  33.0 1.6 %collective-permute-start.6 = (bf16[80,1792]{1,0:T(8,128)(2,1)S(1)}, bf16[80,1792]{1,0:T(8,128)(2,1)S(1)}, u32[]{:S(2)}, u32[]{:S(2)}) collective-permute-start(bf16[80,1792]{1,0:T(8,128)(2,1)S(1)} %get-tuple-element.71), channel_id=1, source_target_pairs={{0,8},{8,0},{16,24},{24,16},{1,9},{9,1},{17,25},{25,17},{2,10},{10... | collective-permute-start | bytes 860168 | tf_op jit(solution)/shard_map/ppermute | solution.py:32
  34.7 4.0 %collective-permute-done.4 = bf16[80,1792]{1,0:T(8,128)(2,1)S(1)} collective-permute-done((bf16[80,1792]{1,0:T(8,128)(2,1)S(1)}, bf16[80,1792]{1,0:T(8,128)(2,1)S(1)}, u32[]{:S(2)}, u32[]{:S(2)}) %collective-permute-start.4) | collective-permute-done | bytes 286752 | tf_op jit(solution)/shard_map/ppermute | solution.py:32
  41.6 1.5 %collective-permute-start.5 = (bf16[80,3584]{1,0:T(8,128)(2,1)S(1)}, bf16[80,3584]{1,0:T(8,128)(2,1)S(1)}, u32[]{:S(2)}, u32[]{:S(2)}) collective-permute-start(bf16[80,3584]{1,0:T(8,128)(2,1)S(1)} %pad_maximum_fusion.5), channel_id=1, source_target_pairs={{0,8},{8,0},{16,24},{24,16},{1,9},{9,1},{17,25},{25,17},{2,10},{10... | collective-permute-start | bytes 1720328 | tf_op jit(solution)/shard_map/ppermute | solution.py:32
  46.4 9.8 %collective-permute-done.7 = bf16[80,3584]{1,0:T(8,128)(2,1)S(1)} collective-permute-done((bf16[80,3584]{1,0:T(8,128)(2,1)S(1)}, bf16[80,3584]{1,0:T(8,128)(2,1)S(1)}, u32[]{:S(2)}, u32[]{:S(2)}) %collective-permute-start.7) | collective-permute-done | bytes 573472 | tf_op jit(solution)/shard_map/ppermute | solution.py:32
  58.7 1.5 %collective-permute-start.8 = (bf16[80,1792]{1,0:T(8,128)(2,1)S(1)}, bf16[80,1792]{1,0:T(8,128)(2,1)S(1)}, u32[]{:S(2)}, u32[]{:S(2)}) collective-permute-start(bf16[80,1792]{1,0:T(8,128)(2,1)S(1)} %multiply_convert_fusion.2), channel_id=1, source_target_pairs={{0,8},{8,0},{16,24},{24,16},{1,9},{9,1},{17,25},{25,17},{2,10},{10... | collective-permute-start | bytes 860168 | tf_op jit(solution)/shard_map/ppermute | solution.py:32
  62.6 5.0 %collective-permute-done.9 = bf16[80,1792]{1,0:T(8,128)(2,1)S(1)} collective-permute-done((bf16[80,1792]{1,0:T(8,128)(2,1)S(1)}, bf16[80,1792]{1,0:T(8,128)(2,1)S(1)}, u32[]{:S(2)}, u32[]{:S(2)}) %collective-permute-start.9) | collective-permute-done | bytes 286752 | tf_op jit(solution)/shard_map/ppermute | solution.py:32
  67.6 1.6 %collective-permute-start.10 = (bf16[80,896]{1,0:T(8,128)(2,1)S(1)}, bf16[80,896]{1,0:T(8,128)(2,1)S(1)}, u32[]{:S(2)}, u32[]{:S(2)}) collective-permute-start(bf16[80,896]{1,0:T(8,128)(2,1)S(1)} %get-tuple-element.110), channel_id=1, source_target_pairs={{0,8},{8,0},{16,24},{24,16},{1,9},{9,1},{17,25},{25,17},{2,10},{10... | collective-permute-start | bytes 430088 | tf_op jit(solution)/shard_map/ppermute | solution.py:32
  70.2 2.7 %collective-permute-done.22 = bf16[80,1792]{1,0:T(8,128)(2,1)S(1)} collective-permute-done((bf16[80,1792]{1,0:T(8,128)(2,1)S(1)}, bf16[80,1792]{1,0:T(8,128)(2,1)S(1)}, u32[]{:S(2)}, u32[]{:S(2)}) %collective-permute-start.22) | collective-permute-done | bytes 286752 | tf_op jit(solution)/shard_map/ppermute | solution.py:32
  75.4 1.5 %collective-permute-start.23 = (bf16[80,3584]{1,0:T(8,128)(2,1)S(1)}, bf16[80,3584]{1,0:T(8,128)(2,1)S(1)}, u32[]{:S(2)}, u32[]{:S(2)}) collective-permute-start(bf16[80,3584]{1,0:T(8,128)(2,1)S(1)} %pad_maximum_fusion.7), channel_id=1, source_target_pairs={{0,8},{8,0},{16,24},{24,16},{1,9},{9,1},{17,25},{25,17},{2,10},{10... | collective-permute-start | bytes 1720328 | tf_op jit(solution)/shard_map/ppermute | solution.py:32
  76.9 1.4 %convolution_convert_fusion.5 = bf16[320,1024]{1,0:T(8,128)(2,1)S(1)} fusion(bf16[1792,1024]{1,0:T(8,128)(2,1)S(1)} %copy-done.5, bf16[80,896]{1,0:T(8,128)(2,1)S(1)} %collective-permute-done.11, bf16[80,896]{1,0:T(8,128)(2,1)S(1)} %get-tuple-element.111, bf16[80,896]{1,0:T(8,128)(2,1)S(1)} %get-tuple-element.109, ...), kind=kOutput, calls=%fused_computation.7 | convolution fusion | flops 1183907840 | bytes 5472256 | tf_op jit(solution)/shard_map/dot_general | solution.py:272
  78.4 2.3 %collective-permute-start.14 = (bf16[80,1024]{1,0:T(8,128)(2,1)S(1)}, bf16[80,1024]{1,0:T(8,128)(2,1)S(1)}, u32[]{:S(2)}, u32[]{:S(2)}) collective-permute-start(bf16[80,1024]{1,0:T(8,128)(2,1)S(1)} %get-tuple-element.86), channel_id=1, source_target_pairs={{0,6},{1,7},{2,4},{3,5},{4,2},{5,3},{6,0},{7,1},{8,14},{9,15},{10,... | collective-permute-start | bytes 491528 | tf_op jit(solution)/shard_map/ppermute | solution.py:32
  80.7 1.5 %collective-permute-start.13 = (bf16[80,1024]{1,0:T(8,128)(2,1)S(1)}, bf16[80,1024]{1,0:T(8,128)(2,1)S(1)}, u32[]{:S(2)}, u32[]{:S(2)}) collective-permute-start(bf16[80,1024]{1,0:T(8,128)(2,1)S(1)} %get-tuple-element.87), channel_id=1, source_target_pairs={{0,4},{1,5},{2,6},{3,7},{4,0},{5,1},{6,2},{7,3},{8,12},{9,13},{10,... | collective-permute-start | bytes 491528 | tf_op jit(solution)/shard_map/ppermute | solution.py:32
  82.9 4.1 %collective-permute-done.24 = bf16[80,3584]{1,0:T(8,128)(2,1)S(1)} collective-permute-done((bf16[80,3584]{1,0:T(8,128)(2,1)S(1)}, bf16[80,3584]{1,0:T(8,128)(2,1)S(1)}, u32[]{:S(2)}, u32[]{:S(2)}) %collective-permute-start.24) | collective-permute-done | bytes 573472 | tf_op jit(solution)/shard_map/ppermute | solution.py:32
  88.8 1.6 %collective-permute-start.25 = (bf16[80,1792]{1,0:T(8,128)(2,1)S(1)}, bf16[80,1792]{1,0:T(8,128)(2,1)S(1)}, u32[]{:S(2)}, u32[]{:S(2)}) collective-permute-start(bf16[80,1792]{1,0:T(8,128)(2,1)S(1)} %get-tuple-element.99), channel_id=1, source_target_pairs={{0,8},{8,0},{16,24},{24,16},{1,9},{9,1},{17,25},{25,17},{2,10},{10... | collective-permute-start | bytes 860168 | tf_op jit(solution)/shard_map/ppermute | solution.py:32
  90.4 3.9 %convolution_convert_fusion = bf16[1792,1024]{1,0:T(8,128)(2,1)} fusion(bf16[320,1792]{1,0:T(8,128)(2,1)S(1)} %maximum_maximum_fusion, bf16[80,1024]{1,0:T(8,128)(2,1)S(1)} %get-tuple-element.75, bf16[80,1024]{1,0:T(8,128)(2,1)S(1)} %get-tuple-element.76, bf16[80,1024]{1,0:T(8,128)(2,1)S(1)} %get-tuple-element.77, bf16[80,1024]{1,0:T(8,128)(2,1)S(1)} %get-tuple-element.74), kind=kOutput, calls=%fused_computation | convolution fusion | flops 1178861568 | bytes 5472256 | tf_op jit(solution)/shard_map/dot_general | solution.py:287
  95.8 8.4 %shard_map.102 = (bf16[1792,1024]{1,0:T(8,128)(2,1)}, bf16[1792,1024]{1,0:T(8,128)(2,1)}) custom-call(bf16[320,1792]{1,0:T(8,128)(2,1)S(1)} %pad_maximum_fusion.first_ref, bf16[320,1792]{1,0:T(8,128)(2,1)S(1)} %pad_maximum_fusion.1.second_ref, bf16[320,1024]{1,0:T(8,128)(2,1)S(1)} %pad_maximum_fusion.3.rows_ref), custom_call_target="tpu_custom_call" | custom-call | flops 9395240960 | bytes 38535168 | tf_op jit(solution)/shard_map/pallas_call | solution.py:175
  (120 shorter events, 26.5 us)
Async XLA Ops:
  3.9 10.3 %collective-permute-start.1 = (bf16[80,1024]{1,0:T(8,128)(2,1)S(1)}, bf16[80,1024]{1,0:T(8,128)(2,1)S(1)}, u32[]{:S(2)}, u32[]{:S(2)}) collective-permute-start(bf16[80,1024]{1,0:T(8,128)(2,1)S(1)} %pad_maximum_fusion.13), channel_id=1, source_target_pairs={{0,2},{1,3},{2,0},{3,1},{4,6},{5,7},{6,4},{7,5},{8,10},{9,11},{10,... | collective-permute-start | bytes 491528 | tf_op jit(solution)/shard_map/ppermute | solution.py:32
  6.9 15.1 %collective-permute-start.2 = (bf16[80,1024]{1,0:T(8,128)(2,1)S(1)}, bf16[80,1024]{1,0:T(8,128)(2,1)S(1)}, u32[]{:S(2)}, u32[]{:S(2)}) collective-permute-start(bf16[80,1024]{1,0:T(8,128)(2,1)S(1)} %pad_maximum_fusion.14), channel_id=1, source_target_pairs={{0,4},{1,5},{2,6},{3,7},{4,0},{5,1},{6,2},{7,3},{8,12},{9,13},{10,... | collective-permute-start | bytes 491528 | tf_op jit(solution)/shard_map/ppermute | solution.py:32
  9.6 12.4 %collective-permute-start.3 = (bf16[80,1024]{1,0:T(8,128)(2,1)S(1)}, bf16[80,1024]{1,0:T(8,128)(2,1)S(1)}, u32[]{:S(2)}, u32[]{:S(2)}) collective-permute-start(bf16[80,1024]{1,0:T(8,128)(2,1)S(1)} %pad_maximum_fusion.15), channel_id=1, source_target_pairs={{0,6},{1,7},{2,4},{3,5},{4,2},{5,3},{6,0},{7,1},{8,14},{9,15},{10,... | collective-permute-start | bytes 491528 | tf_op jit(solution)/shard_map/ppermute | solution.py:32
  22.1 18.1 %collective-permute-start.15 = (bf16[80,1024]{1,0:T(8,128)(2,1)S(1)}, bf16[80,1024]{1,0:T(8,128)(2,1)S(1)}, u32[]{:S(2)}, u32[]{:S(2)}) collective-permute-start(bf16[80,1024]{1,0:T(8,128)(2,1)S(1)} %pad_maximum_fusion.17), channel_id=1, source_target_pairs={{0,2},{1,3},{2,0},{3,1},{4,6},{5,7},{6,4},{7,5},{8,10},{9,11},{10,... | collective-permute-start | bytes 491528 | tf_op jit(solution)/shard_map/ppermute | solution.py:32
  25.1 15.1 %collective-permute-start.16 = (bf16[80,1024]{1,0:T(8,128)(2,1)S(1)}, bf16[80,1024]{1,0:T(8,128)(2,1)S(1)}, u32[]{:S(2)}, u32[]{:S(2)}) collective-permute-start(bf16[80,1024]{1,0:T(8,128)(2,1)S(1)} %pad_maximum_fusion.18), channel_id=1, source_target_pairs={{0,4},{1,5},{2,6},{3,7},{4,0},{5,1},{6,2},{7,3},{8,12},{9,13},{10,... | collective-permute-start | bytes 491528 | tf_op jit(solution)/shard_map/ppermute | solution.py:32
  26.2 13.9 %collective-permute-start.17 = (bf16[80,1024]{1,0:T(8,128)(2,1)S(1)}, bf16[80,1024]{1,0:T(8,128)(2,1)S(1)}, u32[]{:S(2)}, u32[]{:S(2)}) collective-permute-start(bf16[80,1024]{1,0:T(8,128)(2,1)S(1)} %pad_maximum_fusion.19), channel_id=1, source_target_pairs={{0,6},{1,7},{2,4},{3,5},{4,2},{5,3},{6,0},{7,1},{8,14},{9,15},{10,... | collective-permute-start | bytes 491528 | tf_op jit(solution)/shard_map/ppermute | solution.py:32
  31.4 7.3 %collective-permute-start.4 = (bf16[80,1792]{1,0:T(8,128)(2,1)S(1)}, bf16[80,1792]{1,0:T(8,128)(2,1)S(1)}, u32[]{:S(2)}, u32[]{:S(2)}) collective-permute-start(bf16[80,1792]{1,0:T(8,128)(2,1)S(1)} %get-tuple-element.72), channel_id=1, source_target_pairs={{0,16},{8,24},{16,0},{24,8},{1,17},{9,25},{17,1},{25,9},{2,18},{10... | collective-permute-start | bytes 860168 | tf_op jit(solution)/shard_map/ppermute | solution.py:32
  33.0 7.0 %collective-permute-start.6 = (bf16[80,1792]{1,0:T(8,128)(2,1)S(1)}, bf16[80,1792]{1,0:T(8,128)(2,1)S(1)}, u32[]{:S(2)}, u32[]{:S(2)}) collective-permute-start(bf16[80,1792]{1,0:T(8,128)(2,1)S(1)} %get-tuple-element.71), channel_id=1, source_target_pairs={{0,8},{8,0},{16,24},{24,16},{1,9},{9,1},{17,25},{25,17},{2,10},{10... | collective-permute-start | bytes 860168 | tf_op jit(solution)/shard_map/ppermute | solution.py:32
  40.4 15.8 %collective-permute-start.7 = (bf16[80,3584]{1,0:T(8,128)(2,1)S(1)}, bf16[80,3584]{1,0:T(8,128)(2,1)S(1)}, u32[]{:S(2)}, u32[]{:S(2)}) collective-permute-start(bf16[80,3584]{1,0:T(8,128)(2,1)S(1)} %pad_maximum_fusion.6), channel_id=1, source_target_pairs={{0,16},{8,24},{16,0},{24,8},{1,17},{9,25},{17,1},{25,9},{2,18},{10... | collective-permute-start | bytes 1720328 | tf_op jit(solution)/shard_map/ppermute | solution.py:32
  41.6 15.8 %collective-permute-start.5 = (bf16[80,3584]{1,0:T(8,128)(2,1)S(1)}, bf16[80,3584]{1,0:T(8,128)(2,1)S(1)}, u32[]{:S(2)}, u32[]{:S(2)}) collective-permute-start(bf16[80,3584]{1,0:T(8,128)(2,1)S(1)} %pad_maximum_fusion.5), channel_id=1, source_target_pairs={{0,8},{8,0},{16,24},{24,16},{1,9},{9,1},{17,25},{25,17},{2,10},{10... | collective-permute-start | bytes 1720328 | tf_op jit(solution)/shard_map/ppermute | solution.py:32
  44.9 15.4 %collective-permute-start.20 = (bf16[80,896]{1,0:T(8,128)(2,1)S(1)}, bf16[80,896]{1,0:T(8,128)(2,1)S(1)}, u32[]{:S(2)}, u32[]{:S(2)}) collective-permute-start(bf16[80,896]{1,0:T(8,128)(2,1)S(1)} %get-tuple-element.66), channel_id=1, source_target_pairs={{0,16},{8,24},{16,0},{24,8},{1,17},{9,25},{17,1},{25,9},{2,18},{10... | collective-permute-start | bytes 430088 | tf_op jit(solution)/shard_map/ppermute | solution.py:32
  45.9 14.4 %collective-permute-start.19 = (bf16[80,896]{1,0:T(8,128)(2,1)S(1)}, bf16[80,896]{1,0:T(8,128)(2,1)S(1)}, u32[]{:S(2)}, u32[]{:S(2)}) collective-permute-start(bf16[80,896]{1,0:T(8,128)(2,1)S(1)} %get-tuple-element.67), channel_id=1, source_target_pairs={{0,8},{8,0},{16,24},{24,16},{1,9},{9,1},{17,25},{25,17},{2,10},{10... | collective-permute-start | bytes 430088 | tf_op jit(solution)/shard_map/ppermute | solution.py:32
  57.7 9.8 %collective-permute-start.9 = (bf16[80,1792]{1,0:T(8,128)(2,1)S(1)}, bf16[80,1792]{1,0:T(8,128)(2,1)S(1)}, u32[]{:S(2)}, u32[]{:S(2)}) collective-permute-start(bf16[80,1792]{1,0:T(8,128)(2,1)S(1)} %multiply_convert_fusion.2), channel_id=1, source_target_pairs={{0,16},{8,24},{16,0},{24,8},{1,17},{9,25},{17,1},{25,9},{2,18},{10... | collective-permute-start | bytes 860168 | tf_op jit(solution)/shard_map/ppermute | solution.py:32
  58.7 10.4 %collective-permute-start.8 = (bf16[80,1792]{1,0:T(8,128)(2,1)S(1)}, bf16[80,1792]{1,0:T(8,128)(2,1)S(1)}, u32[]{:S(2)}, u32[]{:S(2)}) collective-permute-start(bf16[80,1792]{1,0:T(8,128)(2,1)S(1)} %multiply_convert_fusion.2), channel_id=1, source_target_pairs={{0,8},{8,0},{16,24},{24,16},{1,9},{9,1},{17,25},{25,17},{2,10},{10... | collective-permute-start | bytes 860168 | tf_op jit(solution)/shard_map/ppermute | solution.py:32
  60.5 12.4 %collective-permute-start.22 = (bf16[80,1792]{1,0:T(8,128)(2,1)S(1)}, bf16[80,1792]{1,0:T(8,128)(2,1)S(1)}, u32[]{:S(2)}, u32[]{:S(2)}) collective-permute-start(bf16[80,1792]{1,0:T(8,128)(2,1)S(1)} %pad_maximum_fusion.11), channel_id=1, source_target_pairs={{0,16},{8,24},{16,0},{24,8},{1,17},{9,25},{17,1},{25,9},{2,18},{10... | collective-permute-start | bytes 860168 | tf_op jit(solution)/shard_map/ppermute | solution.py:32
  61.7 11.9 %collective-permute-start.21 = (bf16[80,1792]{1,0:T(8,128)(2,1)S(1)}, bf16[80,1792]{1,0:T(8,128)(2,1)S(1)}, u32[]{:S(2)}, u32[]{:S(2)}) collective-permute-start(bf16[80,1792]{1,0:T(8,128)(2,1)S(1)} %pad_maximum_fusion.10), channel_id=1, source_target_pairs={{0,8},{8,0},{16,24},{24,16},{1,9},{9,1},{17,25},{25,17},{2,10},{10... | collective-permute-start | bytes 860168 | tf_op jit(solution)/shard_map/ppermute | solution.py:32
  67.6 9.3 %collective-permute-start.10 = (bf16[80,896]{1,0:T(8,128)(2,1)S(1)}, bf16[80,896]{1,0:T(8,128)(2,1)S(1)}, u32[]{:S(2)}, u32[]{:S(2)}) collective-permute-start(bf16[80,896]{1,0:T(8,128)(2,1)S(1)} %get-tuple-element.110), channel_id=1, source_target_pairs={{0,8},{8,0},{16,24},{24,16},{1,9},{9,1},{17,25},{25,17},{2,10},{10... | collective-permute-start | bytes 430088 | tf_op jit(solution)/shard_map/ppermute | solution.py:32
  69.2 7.7 %collective-permute-start.11 = (bf16[80,896]{1,0:T(8,128)(2,1)S(1)}, bf16[80,896]{1,0:T(8,128)(2,1)S(1)}, u32[]{:S(2)}, u32[]{:S(2)}) collective-permute-start(bf16[80,896]{1,0:T(8,128)(2,1)S(1)} %get-tuple-element.109), channel_id=1, source_target_pairs={{0,16},{8,24},{16,0},{24,8},{1,17},{9,25},{17,1},{25,9},{2,18},{10... | collective-permute-start | bytes 430088 | tf_op jit(solution)/shard_map/ppermute | solution.py:32
  74.2 12.8 %collective-permute-start.24 = (bf16[80,3584]{1,0:T(8,128)(2,1)S(1)}, bf16[80,3584]{1,0:T(8,128)(2,1)S(1)}, u32[]{:S(2)}, u32[]{:S(2)}) collective-permute-start(bf16[80,3584]{1,0:T(8,128)(2,1)S(1)} %pad_maximum_fusion.7), channel_id=1, source_target_pairs={{0,16},{8,24},{16,0},{24,8},{1,17},{9,25},{17,1},{25,9},{2,18},{10... | collective-permute-start | bytes 1720328 | tf_op jit(solution)/shard_map/ppermute | solution.py:32
  75.4 12.1 %collective-permute-start.23 = (bf16[80,3584]{1,0:T(8,128)(2,1)S(1)}, bf16[80,3584]{1,0:T(8,128)(2,1)S(1)}, u32[]{:S(2)}, u32[]{:S(2)}) collective-permute-start(bf16[80,3584]{1,0:T(8,128)(2,1)S(1)} %pad_maximum_fusion.7), channel_id=1, source_target_pairs={{0,8},{8,0},{16,24},{24,16},{1,9},{9,1},{17,25},{25,17},{2,10},{10... | collective-permute-start | bytes 1720328 | tf_op jit(solution)/shard_map/ppermute | solution.py:32
  78.4 17.2 %collective-permute-start.14 = (bf16[80,1024]{1,0:T(8,128)(2,1)S(1)}, bf16[80,1024]{1,0:T(8,128)(2,1)S(1)}, u32[]{:S(2)}, u32[]{:S(2)}) collective-permute-start(bf16[80,1024]{1,0:T(8,128)(2,1)S(1)} %get-tuple-element.86), channel_id=1, source_target_pairs={{0,6},{1,7},{2,4},{3,5},{4,2},{5,3},{6,0},{7,1},{8,14},{9,15},{10,... | collective-permute-start | bytes 491528 | tf_op jit(solution)/shard_map/ppermute | solution.py:32
  80.7 15.0 %collective-permute-start.13 = (bf16[80,1024]{1,0:T(8,128)(2,1)S(1)}, bf16[80,1024]{1,0:T(8,128)(2,1)S(1)}, u32[]{:S(2)}, u32[]{:S(2)}) collective-permute-start(bf16[80,1024]{1,0:T(8,128)(2,1)S(1)} %get-tuple-element.87), channel_id=1, source_target_pairs={{0,4},{1,5},{2,6},{3,7},{4,0},{5,1},{6,2},{7,3},{8,12},{9,13},{10,... | collective-permute-start | bytes 491528 | tf_op jit(solution)/shard_map/ppermute | solution.py:32
  82.2 13.4 %collective-permute-start.12 = (bf16[80,1024]{1,0:T(8,128)(2,1)S(1)}, bf16[80,1024]{1,0:T(8,128)(2,1)S(1)}, u32[]{:S(2)}, u32[]{:S(2)}) collective-permute-start(bf16[80,1024]{1,0:T(8,128)(2,1)S(1)} %get-tuple-element.88), channel_id=1, source_target_pairs={{0,2},{1,3},{2,0},{3,1},{4,6},{5,7},{6,4},{7,5},{8,10},{9,11},{10,... | collective-permute-start | bytes 491528 | tf_op jit(solution)/shard_map/ppermute | solution.py:32
  95.7 8.5 %collective-permute-start.27 = (bf16[160,1024]{1,0:T(8,128)(2,1)S(1)}, bf16[160,1024]{1,0:T(8,128)(2,1)S(1)}, u32[]{:S(2)}, u32[]{:S(2)}) collective-permute-start(bf16[160,1024]{1,0:T(8,128)(2,1)S(1)} %pad_maximum_fusion.9), channel_id=1, source_target_pairs={{0,1},{1,0},{2,3},{3,2},{4,5},{5,4},{6,7},{7,6},{8,9},{9,8},{10,11... | collective-permute-start | bytes 983048 | tf_op jit(solution)/shard_map/ppermute | solution.py:32
  (10 other events, 34.2 us)

commit v9 on v8

--- a/solution.py
+++ b/solution.py
@@ -160,14 +160,13 @@
 def two_terms(first, second, rows):
     count, width = first.shape
     feats = rows.shape[1]
-    block = 256
+    block = width // 2
 
     def kernel(first_ref, second_ref, rows_ref, first_out, second_out):
-        lines = lax.broadcasted_iota(jnp.int32, (block, block), 0)
-        identity = (lines == lax.broadcasted_iota(jnp.int32, (block, block), 1)).astype(BF)
         for left_ref, out in ((first_ref, first_out), (second_ref, second_out)):
-            turned = lax.dot_general(identity, left_ref[...], CONTRACT_FEATS, preferred_element_type=F32)
-            out[...] = jnp.dot(turned.astype(BF), rows_ref[...], preferred_element_type=F32).astype(BF)
+            out[...] = lax.dot_general(
+                left_ref[...], rows_ref[...], CONTRACT_ROWS, preferred_element_type=F32
+            ).astype(BF)
 
     left_spec = pl.BlockSpec((count, block), lambda i: (0, i))
     out_spec = pl.BlockSpec((block, feats), lambda i: (i, 0))
@@ -178,7 +177,7 @@
         in_specs=[left_spec, left_spec, pl.BlockSpec((count, feats), lambda i: (0, 0))],
         out_specs=[out_spec, out_spec],
         out_shape=[out, out],
-        compiler_params=pltpu.CompilerParams(vmem_limit_bytes=24 * 2**20),
+        compiler_params=pltpu.CompilerParams(vmem_limit_bytes=36 * 2**20),
         cost_estimate=pl.CostEstimate(
             flops=16 * count * width * feats,
             bytes_accessed=16 * (count + feats) * width,

time: 106 us -> 103 us (0.972)
  Pallas kernels: 8.44 us -> 5.67 us
    pallas_call x1, Pallas kernels: 8.44 us -> 5.67 us  [two_terms(): pl.pallas_call(kernel, grid=(width // block,), in_specs=[left_spec, left_...]
  transfers between devices with their start and end apart: 28 -> 28, of which waited for: 13 -> 13; matrix products, arithmetic and copies ran while one was open for 12% -> 13% of each run, Pallas kernels for 8% -> 6%
where the time goes in v9:
time: 103 us
  waiting for transfers between devices  42.9 us (42%)
  starting transfers between devices  36.5 us (35%)
  matrix products  12.1 us (12%)
  Pallas kernels  5.67 us (6%)
  other arithmetic  2.81 us (3%)
  local copies, waits for them, and re-layouts  1.37 us (1%)
  between operations  1.28 us (1%)
    ppermute x28, waiting for transfers between devices, swap(): return lax.ppermute(block, axis, [(i, i ^ mask) for i in range(count)])  42.9 us
    ppermute x28, starting transfers between devices, swap(): return lax.ppermute(block, axis, [(i, i ^ mask) for i in range(count)])  36.5 us
    pallas_call x1, Pallas kernels, two_terms(): pl.pallas_call(kernel, grid=(width // block,), in_specs=[left_spec, left_...  5.67 us
    dot_general x3, matrix products, partial_product(): lax.dot_general(rows, weights, CONTRACT_FEATS, preferred_element_type=F32)  4.22 us
    dot_general x1, matrix products, term(): lax.dot_general(left, right, CONTRACT_ROWS, preferred_element_type=F32)  3.94 us
  transfers between devices with their start and end apart: 28, of which 13 were waited for; matrix products, arithmetic and copies ran while one was open for 13% of the time, Pallas kernels for 6%

profile of v9, /device:TPU:0, one launch (start us, length us, event | category | flops | bytes accessed | tf_op | source)
XLA Modules:
  0.0 102.6 jit_solution(9173567225339355076)
XLA Ops:
  3.9 3.0 %collective-permute-start.1 = (bf16[80,1024]{1,0:T(8,128)(2,1)S(1)}, bf16[80,1024]{1,0:T(8,128)(2,1)S(1)}, u32[]{:S(2)}, u32[]{:S(2)}) collective-permute-start(bf16[80,1024]{1,0:T(8,128)(2,1)S(1)} %pad_maximum_fusion.13), channel_id=1, source_target_pairs={{0,2},{1,3},{2,0},{3,1},{4,6},{5,7},{6,4},{7,5},{8,10},{9,11},{10,... | collective-permute-start | bytes 491528 | tf_op jit(solution)/shard_map/ppermute | solution.py:32
  6.9 2.7 %collective-permute-start.2 = (bf16[80,1024]{1,0:T(8,128)(2,1)S(1)}, bf16[80,1024]{1,0:T(8,128)(2,1)S(1)}, u32[]{:S(2)}, u32[]{:S(2)}) collective-permute-start(bf16[80,1024]{1,0:T(8,128)(2,1)S(1)} %pad_maximum_fusion.14), channel_id=1, source_target_pairs={{0,4},{1,5},{2,6},{3,7},{4,0},{5,1},{6,2},{7,3},{8,12},{9,13},{10,... | collective-permute-start | bytes 491528 | tf_op jit(solution)/shard_map/ppermute | solution.py:32
  10.2 4.0 %collective-permute-done.1 = bf16[80,1024]{1,0:T(8,128)(2,1)S(1)} collective-permute-done((bf16[80,1024]{1,0:T(8,128)(2,1)S(1)}, bf16[80,1024]{1,0:T(8,128)(2,1)S(1)}, u32[]{:S(2)}, u32[]{:S(2)}) %collective-permute-start.1) | collective-permute-done | bytes 163872 | tf_op jit(solution)/shard_map/ppermute | solution.py:32
  14.2 7.8 %collective-permute-done.2 = bf16[80,1024]{1,0:T(8,128)(2,1)S(1)} collective-permute-done((bf16[80,1024]{1,0:T(8,128)(2,1)S(1)}, bf16[80,1024]{1,0:T(8,128)(2,1)S(1)}, u32[]{:S(2)}, u32[]{:S(2)}) %collective-permute-start.2) | collective-permute-done | bytes 163872 | tf_op jit(solution)/shard_map/ppermute | solution.py:32
  22.1 3.1 %collective-permute-start.15 = (bf16[80,1024]{1,0:T(8,128)(2,1)S(1)}, bf16[80,1024]{1,0:T(8,128)(2,1)S(1)}, u32[]{:S(2)}, u32[]{:S(2)}) collective-permute-start(bf16[80,1024]{1,0:T(8,128)(2,1)S(1)} %pad_maximum_fusion.17), channel_id=1, source_target_pairs={{0,2},{1,3},{2,0},{3,1},{4,6},{5,7},{6,4},{7,5},{8,10},{9,11},{10,... | collective-permute-start | bytes 491528 | tf_op jit(solution)/shard_map/ppermute | solution.py:32
  26.3 1.5 %collective-permute-start.17 = (bf16[80,1024]{1,0:T(8,128)(2,1)S(1)}, bf16[80,1024]{1,0:T(8,128)(2,1)S(1)}, u32[]{:S(2)}, u32[]{:S(2)}) collective-permute-start(bf16[80,1024]{1,0:T(8,128)(2,1)S(1)} %pad_maximum_fusion.19), channel_id=1, source_target_pairs={{0,6},{1,7},{2,4},{3,5},{4,2},{5,3},{6,0},{7,1},{8,14},{9,15},{10,... | collective-permute-start | bytes 491528 | tf_op jit(solution)/shard_map/ppermute | solution.py:32
  27.9 1.4 %convolution_convert_fusion.3 = bf16[320,1792]{1,0:T(8,128)(2,1)S(1)} fusion(bf16[1792,1024]{1,0:T(8,128)(2,1)S(1)} %copy-done.3, bf16[80,1024]{1,0:T(8,128)(2,1)S(1)} %get-tuple-element.91, bf16[80,1024]{1,0:T(8,128)(2,1)S(1)} %get-tuple-element.92, bf16[80,1024]{1,0:T(8,128)(2,1)S(1)} %get-tuple-element.93, bf16[80,1024]{1,0:T(8,128)(2,1)S(1)} %get-tuple-element.90), kind=kOutput, calls=%fused_computation.3 | convolution fusion | flops 1177600000 | bytes 5472256 | tf_op jit(solution)/shard_map/dot_general | solution.py:249
  31.4 1.6 %collective-permute-start.4 = (bf16[80,1792]{1,0:T(8,128)(2,1)S(1)}, bf16[80,1792]{1,0:T(8,128)(2,1)S(1)}, u32[]{:S(2)}, u32[]{:S(2)}) collective-permute-start(bf16[80,1792]{1,0:T(8,128)(2,1)S(1)} %get-tuple-element.72), channel_id=1, source_target_pairs={{0,16},{8,24},{16,0},{24,8},{1,17},{9,25},{17,1},{25,9},{2,18},{10... | collective-permute-start | bytes 860168 | tf_op jit(solution)/shard_map/ppermute | solution.py:32
  33.0 1.6 %collective-permute-start.6 = (bf16[80,1792]{1,0:T(8,128)(2,1)S(1)}, bf16[80,1792]{1,0:T(8,128)(2,1)S(1)}, u32[]{:S(2)}, u32[]{:S(2)}) collective-permute-start(bf16[80,1792]{1,0:T(8,128)(2,1)S(1)} %get-tuple-element.71), channel_id=1, source_target_pairs={{0,8},{8,0},{16,24},{24,16},{1,9},{9,1},{17,25},{25,17},{2,10},{10... | collective-permute-start | bytes 860168 | tf_op jit(solution)/shard_map/ppermute | solution.py:32
  34.7 4.0 %collective-permute-done.4 = bf16[80,1792]{1,0:T(8,128)(2,1)S(1)} collective-permute-done((bf16[80,1792]{1,0:T(8,128)(2,1)S(1)}, bf16[80,1792]{1,0:T(8,128)(2,1)S(1)}, u32[]{:S(2)}, u32[]{:S(2)}) %collective-permute-start.4) | collective-permute-done | bytes 286752 | tf_op jit(solution)/shard_map/ppermute | solution.py:32
  41.6 1.5 %collective-permute-start.5 = (bf16[80,3584]{1,0:T(8,128)(2,1)S(1)}, bf16[80,3584]{1,0:T(8,128)(2,1)S(1)}, u32[]{:S(2)}, u32[]{:S(2)}) collective-permute-start(bf16[80,3584]{1,0:T(8,128)(2,1)S(1)} %pad_maximum_fusion.5), channel_id=1, source_target_pairs={{0,8},{8,0},{16,24},{24,16},{1,9},{9,1},{17,25},{25,17},{2,10},{10... | collective-permute-start | bytes 1720328 | tf_op jit(solution)/shard_map/ppermute | solution.py:32
  46.4 9.9 %collective-permute-done.7 = bf16[80,3584]{1,0:T(8,128)(2,1)S(1)} collective-permute-done((bf16[80,3584]{1,0:T(8,128)(2,1)S(1)}, bf16[80,3584]{1,0:T(8,128)(2,1)S(1)}, u32[]{:S(2)}, u32[]{:S(2)}) %collective-permute-start.7) | collective-permute-done | bytes 573472 | tf_op jit(solution)/shard_map/ppermute | solution.py:32
  58.8 1.5 %collective-permute-start.8 = (bf16[80,1792]{1,0:T(8,128)(2,1)S(1)}, bf16[80,1792]{1,0:T(8,128)(2,1)S(1)}, u32[]{:S(2)}, u32[]{:S(2)}) collective-permute-start(bf16[80,1792]{1,0:T(8,128)(2,1)S(1)} %multiply_convert_fusion.2), channel_id=1, source_target_pairs={{0,8},{8,0},{16,24},{24,16},{1,9},{9,1},{17,25},{25,17},{2,10},{10... | collective-permute-start | bytes 860168 | tf_op jit(solution)/shard_map/ppermute | solution.py:32
  62.6 5.0 %collective-permute-done.9 = bf16[80,1792]{1,0:T(8,128)(2,1)S(1)} collective-permute-done((bf16[80,1792]{1,0:T(8,128)(2,1)S(1)}, bf16[80,1792]{1,0:T(8,128)(2,1)S(1)}, u32[]{:S(2)}, u32[]{:S(2)}) %collective-permute-start.9) | collective-permute-done | bytes 286752 | tf_op jit(solution)/shard_map/ppermute | solution.py:32
  67.6 1.6 %collective-permute-start.10 = (bf16[80,896]{1,0:T(8,128)(2,1)S(1)}, bf16[80,896]{1,0:T(8,128)(2,1)S(1)}, u32[]{:S(2)}, u32[]{:S(2)}) collective-permute-start(bf16[80,896]{1,0:T(8,128)(2,1)S(1)} %get-tuple-element.110), channel_id=1, source_target_pairs={{0,8},{8,0},{16,24},{24,16},{1,9},{9,1},{17,25},{25,17},{2,10},{10... | collective-permute-start | bytes 430088 | tf_op jit(solution)/shard_map/ppermute | solution.py:32
  70.2 2.7 %collective-permute-done.22 = bf16[80,1792]{1,0:T(8,128)(2,1)S(1)} collective-permute-done((bf16[80,1792]{1,0:T(8,128)(2,1)S(1)}, bf16[80,1792]{1,0:T(8,128)(2,1)S(1)}, u32[]{:S(2)}, u32[]{:S(2)}) %collective-permute-start.22) | collective-permute-done | bytes 286752 | tf_op jit(solution)/shard_map/ppermute | solution.py:32
  75.4 1.5 %collective-permute-start.23 = (bf16[80,3584]{1,0:T(8,128)(2,1)S(1)}, bf16[80,3584]{1,0:T(8,128)(2,1)S(1)}, u32[]{:S(2)}, u32[]{:S(2)}) collective-permute-start(bf16[80,3584]{1,0:T(8,128)(2,1)S(1)} %pad_maximum_fusion.7), channel_id=1, source_target_pairs={{0,8},{8,0},{16,24},{24,16},{1,9},{9,1},{17,25},{25,17},{2,10},{10... | collective-permute-start | bytes 1720328 | tf_op jit(solution)/shard_map/ppermute | solution.py:32
  76.9 1.4 %convolution_convert_fusion.5 = bf16[320,1024]{1,0:T(8,128)(2,1)S(1)} fusion(bf16[1792,1024]{1,0:T(8,128)(2,1)S(1)} %copy-done.5, bf16[80,896]{1,0:T(8,128)(2,1)S(1)} %collective-permute-done.11, bf16[80,896]{1,0:T(8,128)(2,1)S(1)} %get-tuple-element.111, bf16[80,896]{1,0:T(8,128)(2,1)S(1)} %get-tuple-element.109, ...), kind=kOutput, calls=%fused_computation.7 | convolution fusion | flops 1183907840 | bytes 5472256 | tf_op jit(solution)/shard_map/dot_general | solution.py:271
  78.3 2.3 %collective-permute-start.14 = (bf16[80,1024]{1,0:T(8,128)(2,1)S(1)}, bf16[80,1024]{1,0:T(8,128)(2,1)S(1)}, u32[]{:S(2)}, u32[]{:S(2)}) collective-permute-start(bf16[80,1024]{1,0:T(8,128)(2,1)S(1)} %get-tuple-element.86), channel_id=1, source_target_pairs={{0,6},{1,7},{2,4},{3,5},{4,2},{5,3},{6,0},{7,1},{8,14},{9,15},{10,... | collective-permute-start | bytes 491528 | tf_op jit(solution)/shard_map/ppermute | solution.py:32
  80.6 1.5 %collective-permute-start.13 = (bf16[80,1024]{1,0:T(8,128)(2,1)S(1)}, bf16[80,1024]{1,0:T(8,128)(2,1)S(1)}, u32[]{:S(2)}, u32[]{:S(2)}) collective-permute-start(bf16[80,1024]{1,0:T(8,128)(2,1)S(1)} %get-tuple-element.87), channel_id=1, source_target_pairs={{0,4},{1,5},{2,6},{3,7},{4,0},{5,1},{6,2},{7,3},{8,12},{9,13},{10,... | collective-permute-start | bytes 491528 | tf_op jit(solution)/shard_map/ppermute | solution.py:32
  82.9 4.1 %collective-permute-done.24 = bf16[80,3584]{1,0:T(8,128)(2,1)S(1)} collective-permute-done((bf16[80,3584]{1,0:T(8,128)(2,1)S(1)}, bf16[80,3584]{1,0:T(8,128)(2,1)S(1)}, u32[]{:S(2)}, u32[]{:S(2)}) %collective-permute-start.24) | collective-permute-done | bytes 573472 | tf_op jit(solution)/shard_map/ppermute | solution.py:32
  88.8 1.6 %collective-permute-start.25 = (bf16[80,1792]{1,0:T(8,128)(2,1)S(1)}, bf16[80,1792]{1,0:T(8,128)(2,1)S(1)}, u32[]{:S(2)}, u32[]{:S(2)}) collective-permute-start(bf16[80,1792]{1,0:T(8,128)(2,1)S(1)} %get-tuple-element.99), channel_id=1, source_target_pairs={{0,8},{8,0},{16,24},{24,16},{1,9},{9,1},{17,25},{25,17},{2,10},{10... | collective-permute-start | bytes 860168 | tf_op jit(solution)/shard_map/ppermute | solution.py:32
  90.4 3.9 %convolution_convert_fusion = bf16[1792,1024]{1,0:T(8,128)(2,1)} fusion(bf16[320,1792]{1,0:T(8,128)(2,1)S(1)} %maximum_maximum_fusion, bf16[80,1024]{1,0:T(8,128)(2,1)S(1)} %get-tuple-element.75, bf16[80,1024]{1,0:T(8,128)(2,1)S(1)} %get-tuple-element.76, bf16[80,1024]{1,0:T(8,128)(2,1)S(1)} %get-tuple-element.77, bf16[80,1024]{1,0:T(8,128)(2,1)S(1)} %get-tuple-element.74), kind=kOutput, calls=%fused_computation | convolution fusion | flops 1178861568 | bytes 5472256 | tf_op jit(solution)/shard_map/dot_general | solution.py:286
  95.8 5.7 %shard_map.102 = (bf16[1792,1024]{1,0:T(8,128)(2,1)}, bf16[1792,1024]{1,0:T(8,128)(2,1)}) custom-call(bf16[320,1792]{1,0:T(8,128)(2,1)S(1)} %pad_maximum_fusion.first_ref, bf16[320,1792]{1,0:T(8,128)(2,1)S(1)} %pad_maximum_fusion.1.second_ref, bf16[320,1024]{1,0:T(8,128)(2,1)S(1)} %pad_maximum_fusion.3.rows_ref), custom_call_target="tpu_custom_call" | custom-call | flops 9395240960 | bytes 38535168 | tf_op jit(solution)/shard_map/pallas_call | solution.py:174
  (120 shorter events, 26.5 us)
Async XLA Ops:
  3.9 10.3 %collective-permute-start.1 = (bf16[80,1024]{1,0:T(8,128)(2,1)S(1)}, bf16[80,1024]{1,0:T(8,128)(2,1)S(1)}, u32[]{:S(2)}, u32[]{:S(2)}) collective-permute-start(bf16[80,1024]{1,0:T(8,128)(2,1)S(1)} %pad_maximum_fusion.13), channel_id=1, source_target_pairs={{0,2},{1,3},{2,0},{3,1},{4,6},{5,7},{6,4},{7,5},{8,10},{9,11},{10,... | collective-permute-start | bytes 491528 | tf_op jit(solution)/shard_map/ppermute | solution.py:32
  6.9 15.1 %collective-permute-start.2 = (bf16[80,1024]{1,0:T(8,128)(2,1)S(1)}, bf16[80,1024]{1,0:T(8,128)(2,1)S(1)}, u32[]{:S(2)}, u32[]{:S(2)}) collective-permute-start(bf16[80,1024]{1,0:T(8,128)(2,1)S(1)} %pad_maximum_fusion.14), channel_id=1, source_target_pairs={{0,4},{1,5},{2,6},{3,7},{4,0},{5,1},{6,2},{7,3},{8,12},{9,13},{10,... | collective-permute-start | bytes 491528 | tf_op jit(solution)/shard_map/ppermute | solution.py:32
  9.6 12.4 %collective-permute-start.3 = (bf16[80,1024]{1,0:T(8,128)(2,1)S(1)}, bf16[80,1024]{1,0:T(8,128)(2,1)S(1)}, u32[]{:S(2)}, u32[]{:S(2)}) collective-permute-start(bf16[80,1024]{1,0:T(8,128)(2,1)S(1)} %pad_maximum_fusion.15), channel_id=1, source_target_pairs={{0,6},{1,7},{2,4},{3,5},{4,2},{5,3},{6,0},{7,1},{8,14},{9,15},{10,... | collective-permute-start | bytes 491528 | tf_op jit(solution)/shard_map/ppermute | solution.py:32
  22.1 18.1 %collective-permute-start.15 = (bf16[80,1024]{1,0:T(8,128)(2,1)S(1)}, bf16[80,1024]{1,0:T(8,128)(2,1)S(1)}, u32[]{:S(2)}, u32[]{:S(2)}) collective-permute-start(bf16[80,1024]{1,0:T(8,128)(2,1)S(1)} %pad_maximum_fusion.17), channel_id=1, source_target_pairs={{0,2},{1,3},{2,0},{3,1},{4,6},{5,7},{6,4},{7,5},{8,10},{9,11},{10,... | collective-permute-start | bytes 491528 | tf_op jit(solution)/shard_map/ppermute | solution.py:32
  25.1 15.1 %collective-permute-start.16 = (bf16[80,1024]{1,0:T(8,128)(2,1)S(1)}, bf16[80,1024]{1,0:T(8,128)(2,1)S(1)}, u32[]{:S(2)}, u32[]{:S(2)}) collective-permute-start(bf16[80,1024]{1,0:T(8,128)(2,1)S(1)} %pad_maximum_fusion.18), channel_id=1, source_target_pairs={{0,4},{1,5},{2,6},{3,7},{4,0},{5,1},{6,2},{7,3},{8,12},{9,13},{10,... | collective-permute-start | bytes 491528 | tf_op jit(solution)/shard_map/ppermute | solution.py:32
  26.3 14.0 %collective-permute-start.17 = (bf16[80,1024]{1,0:T(8,128)(2,1)S(1)}, bf16[80,1024]{1,0:T(8,128)(2,1)S(1)}, u32[]{:S(2)}, u32[]{:S(2)}) collective-permute-start(bf16[80,1024]{1,0:T(8,128)(2,1)S(1)} %pad_maximum_fusion.19), channel_id=1, source_target_pairs={{0,6},{1,7},{2,4},{3,5},{4,2},{5,3},{6,0},{7,1},{8,14},{9,15},{10,... | collective-permute-start | bytes 491528 | tf_op jit(solution)/shard_map/ppermute | solution.py:32
  31.4 7.3 %collective-permute-start.4 = (bf16[80,1792]{1,0:T(8,128)(2,1)S(1)}, bf16[80,1792]{1,0:T(8,128)(2,1)S(1)}, u32[]{:S(2)}, u32[]{:S(2)}) collective-permute-start(bf16[80,1792]{1,0:T(8,128)(2,1)S(1)} %get-tuple-element.72), channel_id=1, source_target_pairs={{0,16},{8,24},{16,0},{24,8},{1,17},{9,25},{17,1},{25,9},{2,18},{10... | collective-permute-start | bytes 860168 | tf_op jit(solution)/shard_map/ppermute | solution.py:32
  33.0 7.0 %collective-permute-start.6 = (bf16[80,1792]{1,0:T(8,128)(2,1)S(1)}, bf16[80,1792]{1,0:T(8,128)(2,1)S(1)}, u32[]{:S(2)}, u32[]{:S(2)}) collective-permute-start(bf16[80,1792]{1,0:T(8,128)(2,1)S(1)} %get-tuple-element.71), channel_id=1, source_target_pairs={{0,8},{8,0},{16,24},{24,16},{1,9},{9,1},{17,25},{25,17},{2,10},{10... | collective-permute-start | bytes 860168 | tf_op jit(solution)/shard_map/ppermute | solution.py:32
  40.5 15.8 %collective-permute-start.7 = (bf16[80,3584]{1,0:T(8,128)(2,1)S(1)}, bf16[80,3584]{1,0:T(8,128)(2,1)S(1)}, u32[]{:S(2)}, u32[]{:S(2)}) collective-permute-start(bf16[80,3584]{1,0:T(8,128)(2,1)S(1)} %pad_maximum_fusion.6), channel_id=1, source_target_pairs={{0,16},{8,24},{16,0},{24,8},{1,17},{9,25},{17,1},{25,9},{2,18},{10... | collective-permute-start | bytes 1720328 | tf_op jit(solution)/shard_map/ppermute | solution.py:32
  41.6 15.8 %collective-permute-start.5 = (bf16[80,3584]{1,0:T(8,128)(2,1)S(1)}, bf16[80,3584]{1,0:T(8,128)(2,1)S(1)}, u32[]{:S(2)}, u32[]{:S(2)}) collective-permute-start(bf16[80,3584]{1,0:T(8,128)(2,1)S(1)} %pad_maximum_fusion.5), channel_id=1, source_target_pairs={{0,8},{8,0},{16,24},{24,16},{1,9},{9,1},{17,25},{25,17},{2,10},{10... | collective-permute-start | bytes 1720328 | tf_op jit(solution)/shard_map/ppermute | solution.py:32
  44.9 15.4 %collective-permute-start.20 = (bf16[80,896]{1,0:T(8,128)(2,1)S(1)}, bf16[80,896]{1,0:T(8,128)(2,1)S(1)}, u32[]{:S(2)}, u32[]{:S(2)}) collective-permute-start(bf16[80,896]{1,0:T(8,128)(2,1)S(1)} %get-tuple-element.66), channel_id=1, source_target_pairs={{0,16},{8,24},{16,0},{24,8},{1,17},{9,25},{17,1},{25,9},{2,18},{10... | collective-permute-start | bytes 430088 | tf_op jit(solution)/shard_map/ppermute | solution.py:32
  45.9 14.4 %collective-permute-start.19 = (bf16[80,896]{1,0:T(8,128)(2,1)S(1)}, bf16[80,896]{1,0:T(8,128)(2,1)S(1)}, u32[]{:S(2)}, u32[]{:S(2)}) collective-permute-start(bf16[80,896]{1,0:T(8,128)(2,1)S(1)} %get-tuple-element.67), channel_id=1, source_target_pairs={{0,8},{8,0},{16,24},{24,16},{1,9},{9,1},{17,25},{25,17},{2,10},{10... | collective-permute-start | bytes 430088 | tf_op jit(solution)/shard_map/ppermute | solution.py:32
  57.7 9.8 %collective-permute-start.9 = (bf16[80,1792]{1,0:T(8,128)(2,1)S(1)}, bf16[80,1792]{1,0:T(8,128)(2,1)S(1)}, u32[]{:S(2)}, u32[]{:S(2)}) collective-permute-start(bf16[80,1792]{1,0:T(8,128)(2,1)S(1)} %multiply_convert_fusion.2), channel_id=1, source_target_pairs={{0,16},{8,24},{16,0},{24,8},{1,17},{9,25},{17,1},{25,9},{2,18},{10... | collective-permute-start | bytes 860168 | tf_op jit(solution)/shard_map/ppermute | solution.py:32
  58.8 10.4 %collective-permute-start.8 = (bf16[80,1792]{1,0:T(8,128)(2,1)S(1)}, bf16[80,1792]{1,0:T(8,128)(2,1)S(1)}, u32[]{:S(2)}, u32[]{:S(2)}) collective-permute-start(bf16[80,1792]{1,0:T(8,128)(2,1)S(1)} %multiply_convert_fusion.2), channel_id=1, source_target_pairs={{0,8},{8,0},{16,24},{24,16},{1,9},{9,1},{17,25},{25,17},{2,10},{10... | collective-permute-start | bytes 860168 | tf_op jit(solution)/shard_map/ppermute | solution.py:32
  60.5 12.4 %collective-permute-start.22 = (bf16[80,1792]{1,0:T(8,128)(2,1)S(1)}, bf16[80,1792]{1,0:T(8,128)(2,1)S(1)}, u32[]{:S(2)}, u32[]{:S(2)}) collective-permute-start(bf16[80,1792]{1,0:T(8,128)(2,1)S(1)} %pad_maximum_fusion.11), channel_id=1, source_target_pairs={{0,16},{8,24},{16,0},{24,8},{1,17},{9,25},{17,1},{25,9},{2,18},{10... | collective-permute-start | bytes 860168 | tf_op jit(solution)/shard_map/ppermute | solution.py:32
  61.7 11.9 %collective-permute-start.21 = (bf16[80,1792]{1,0:T(8,128)(2,1)S(1)}, bf16[80,1792]{1,0:T(8,128)(2,1)S(1)}, u32[]{:S(2)}, u32[]{:S(2)}) collective-permute-start(bf16[80,1792]{1,0:T(8,128)(2,1)S(1)} %pad_maximum_fusion.10), channel_id=1, source_target_pairs={{0,8},{8,0},{16,24},{24,16},{1,9},{9,1},{17,25},{25,17},{2,10},{10... | collective-permute-start | bytes 860168 | tf_op jit(solution)/shard_map/ppermute | solution.py:32
  67.6 9.2 %collective-permute-start.10 = (bf16[80,896]{1,0:T(8,128)(2,1)S(1)}, bf16[80,896]{1,0:T(8,128)(2,1)S(1)}, u32[]{:S(2)}, u32[]{:S(2)}) collective-permute-start(bf16[80,896]{1,0:T(8,128)(2,1)S(1)} %get-tuple-element.110), channel_id=1, source_target_pairs={{0,8},{8,0},{16,24},{24,16},{1,9},{9,1},{17,25},{25,17},{2,10},{10... | collective-permute-start | bytes 430088 | tf_op jit(solution)/shard_map/ppermute | solution.py:32
  69.2 7.7 %collective-permute-start.11 = (bf16[80,896]{1,0:T(8,128)(2,1)S(1)}, bf16[80,896]{1,0:T(8,128)(2,1)S(1)}, u32[]{:S(2)}, u32[]{:S(2)}) collective-permute-start(bf16[80,896]{1,0:T(8,128)(2,1)S(1)} %get-tuple-element.109), channel_id=1, source_target_pairs={{0,16},{8,24},{16,0},{24,8},{1,17},{9,25},{17,1},{25,9},{2,18},{10... | collective-permute-start | bytes 430088 | tf_op jit(solution)/shard_map/ppermute | solution.py:32
  74.2 12.8 %collective-permute-start.24 = (bf16[80,3584]{1,0:T(8,128)(2,1)S(1)}, bf16[80,3584]{1,0:T(8,128)(2,1)S(1)}, u32[]{:S(2)}, u32[]{:S(2)}) collective-permute-start(bf16[80,3584]{1,0:T(8,128)(2,1)S(1)} %pad_maximum_fusion.7), channel_id=1, source_target_pairs={{0,16},{8,24},{16,0},{24,8},{1,17},{9,25},{17,1},{25,9},{2,18},{10... | collective-permute-start | bytes 1720328 | tf_op jit(solution)/shard_map/ppermute | solution.py:32
  75.4 12.1 %collective-permute-start.23 = (bf16[80,3584]{1,0:T(8,128)(2,1)S(1)}, bf16[80,3584]{1,0:T(8,128)(2,1)S(1)}, u32[]{:S(2)}, u32[]{:S(2)}) collective-permute-start(bf16[80,3584]{1,0:T(8,128)(2,1)S(1)} %pad_maximum_fusion.7), channel_id=1, source_target_pairs={{0,8},{8,0},{16,24},{24,16},{1,9},{9,1},{17,25},{25,17},{2,10},{10... | collective-permute-start | bytes 1720328 | tf_op jit(solution)/shard_map/ppermute | solution.py:32
  78.3 17.2 %collective-permute-start.14 = (bf16[80,1024]{1,0:T(8,128)(2,1)S(1)}, bf16[80,1024]{1,0:T(8,128)(2,1)S(1)}, u32[]{:S(2)}, u32[]{:S(2)}) collective-permute-start(bf16[80,1024]{1,0:T(8,128)(2,1)S(1)} %get-tuple-element.86), channel_id=1, source_target_pairs={{0,6},{1,7},{2,4},{3,5},{4,2},{5,3},{6,0},{7,1},{8,14},{9,15},{10,... | collective-permute-start | bytes 491528 | tf_op jit(solution)/shard_map/ppermute | solution.py:32
  80.6 14.9 %collective-permute-start.13 = (bf16[80,1024]{1,0:T(8,128)(2,1)S(1)}, bf16[80,1024]{1,0:T(8,128)(2,1)S(1)}, u32[]{:S(2)}, u32[]{:S(2)}) collective-permute-start(bf16[80,1024]{1,0:T(8,128)(2,1)S(1)} %get-tuple-element.87), channel_id=1, source_target_pairs={{0,4},{1,5},{2,6},{3,7},{4,0},{5,1},{6,2},{7,3},{8,12},{9,13},{10,... | collective-permute-start | bytes 491528 | tf_op jit(solution)/shard_map/ppermute | solution.py:32
  82.2 13.4 %collective-permute-start.12 = (bf16[80,1024]{1,0:T(8,128)(2,1)S(1)}, bf16[80,1024]{1,0:T(8,128)(2,1)S(1)}, u32[]{:S(2)}, u32[]{:S(2)}) collective-permute-start(bf16[80,1024]{1,0:T(8,128)(2,1)S(1)} %get-tuple-element.88), channel_id=1, source_target_pairs={{0,2},{1,3},{2,0},{3,1},{4,6},{5,7},{6,4},{7,5},{8,10},{9,11},{10,... | collective-permute-start | bytes 491528 | tf_op jit(solution)/shard_map/ppermute | solution.py:32
  87.5 6.8 %collective-permute-start.26 = (bf16[80,1792]{1,0:T(8,128)(2,1)S(1)}, bf16[80,1792]{1,0:T(8,128)(2,1)S(1)}, u32[]{:S(2)}, u32[]{:S(2)}) collective-permute-start(bf16[80,1792]{1,0:T(8,128)(2,1)S(1)} %get-tuple-element.100), channel_id=1, source_target_pairs={{0,16},{8,24},{16,0},{24,8},{1,17},{9,25},{17,1},{25,9},{2,18},{10... | collective-permute-start | bytes 860168 | tf_op jit(solution)/shard_map/ppermute | solution.py:32
  (10 other events, 33.1 us)

commit v10 on v9

--- a/solution.py
+++ b/solution.py
@@ -160,23 +160,35 @@
 def two_terms(first, second, rows):
     count, width = first.shape
     feats = rows.shape[1]
-    block = width // 2
-
-    def kernel(first_ref, second_ref, rows_ref, first_out, second_out):
-        for left_ref, out in ((first_ref, first_out), (second_ref, second_out)):
-            out[...] = lax.dot_general(
-                left_ref[...], rows_ref[...], CONTRACT_ROWS, preferred_element_type=F32
-            ).astype(BF)
-
-    left_spec = pl.BlockSpec((count, block), lambda i: (0, i))
-    out_spec = pl.BlockSpec((block, feats), lambda i: (i, 0))
+    cuts = ((0, width // 2, width), (0, width // 2, width - 256, width))
+
+    def kernel(first_ref, second_ref, rows_ref, first_out, second_out, first_held, second_held, sems):
+        copies = []
+        refs = ((first_ref, first_out, first_held), (second_ref, second_out, second_held))
+        for (left_ref, out, held), ends in zip(refs, cuts):
+            for low, high in zip(ends, ends[1:]):
+                held[low:high, :] = lax.dot_general(
+                    left_ref[:, low:high], rows_ref[...], CONTRACT_ROWS, preferred_element_type=F32
+                ).astype(BF)
+                copy = pltpu.make_async_copy(held.at[low:high], out.at[low:high], sems.at[len(copies)])
+                copy.start()
+                copies.append(copy)
+        for copy in copies:
+            copy.wait()
+
+    whole = pl.BlockSpec(memory_space=pltpu.VMEM)
+    anywhere = pl.BlockSpec(memory_space=pl.ANY)
     out = jax.ShapeDtypeStruct((width, feats), BF)
     return pl.pallas_call(
         kernel,
-        grid=(width // block,),
-        in_specs=[left_spec, left_spec, pl.BlockSpec((count, feats), lambda i: (0, 0))],
-        out_specs=[out_spec, out_spec],
+        in_specs=[whole, whole, whole],
+        out_specs=[anywhere, anywhere],
         out_shape=[out, out],
+        scratch_shapes=[
+            pltpu.VMEM((width, feats), BF),
+            pltpu.VMEM((width, feats), BF),
+            pltpu.SemaphoreType.DMA((5,)),
+        ],
         compiler_params=pltpu.CompilerParams(vmem_limit_bytes=36 * 2**20),
         cost_estimate=pl.CostEstimate(
             flops=16 * count * width * feats,

time: 103 us -> 102 us (level)
  transfers between devices with their start and end apart: 28 -> 28, of which waited for: 13 -> 13; matrix products, arithmetic and copies ran while one was open for 13% -> 13% of each run, Pallas kernels for 6% -> 5%
where the time goes in v10:
time: 102 us
  waiting for transfers between devices  42.7 us (42%)
  starting transfers between devices  36.5 us (36%)
  matrix products  12.3 us (12%)
  Pallas kernels  4.96 us (5%)
  other arithmetic  2.81 us (3%)
  local copies, waits for them, and re-layouts  1.37 us (1%)
  between operations  1.3 us (1%)
    ppermute x28, waiting for transfers between devices, swap(): return lax.ppermute(block, axis, [(i, i ^ mask) for i in range(count)])  42.7 us
    ppermute x28, starting transfers between devices, swap(): return lax.ppermute(block, axis, [(i, i ^ mask) for i in range(count)])  36.5 us
    pallas_call x1, Pallas kernels, two_terms(): pl.pallas_call(kernel, in_specs=[whole, whole, whole], out_specs=[anywher...  4.96 us
    dot_general x3, matrix products, partial_product(): lax.dot_general(rows, weights, CONTRACT_FEATS, preferred_element_type=F32)  4.22 us
    dot_general x1, matrix products, term(): lax.dot_general(left, right, CONTRACT_ROWS, preferred_element_type=F32)  4.1 us
  transfers between devices with their start and end apart: 28, of which 13 were waited for; matrix products, arithmetic and copies ran while one was open for 13% of the time, Pallas kernels for 5%

profile of v10, /device:TPU:0, one launch (start us, length us, event | category | flops | bytes accessed | tf_op | source)
XLA Modules:
  0.0 101.9 jit_solution(12066265300440612173)
XLA Ops:
  3.9 3.0 %collective-permute-start.1 = (bf16[80,1024]{1,0:T(8,128)(2,1)S(1)}, bf16[80,1024]{1,0:T(8,128)(2,1)S(1)}, u32[]{:S(2)}, u32[]{:S(2)}) collective-permute-start(bf16[80,1024]{1,0:T(8,128)(2,1)S(1)} %pad_maximum_fusion.13), channel_id=1, source_target_pairs={{0,2},{1,3},{2,0},{3,1},{4,6},{5,7},{6,4},{7,5},{8,10},{9,11},{10,... | collective-permute-start | bytes 491528 | tf_op jit(solution)/shard_map/ppermute | solution.py:32
  6.9 2.7 %collective-permute-start.2 = (bf16[80,1024]{1,0:T(8,128)(2,1)S(1)}, bf16[80,1024]{1,0:T(8,128)(2,1)S(1)}, u32[]{:S(2)}, u32[]{:S(2)}) collective-permute-start(bf16[80,1024]{1,0:T(8,128)(2,1)S(1)} %pad_maximum_fusion.14), channel_id=1, source_target_pairs={{0,4},{1,5},{2,6},{3,7},{4,0},{5,1},{6,2},{7,3},{8,12},{9,13},{10,... | collective-permute-start | bytes 491528 | tf_op jit(solution)/shard_map/ppermute | solution.py:32
  10.2 4.0 %collective-permute-done.1 = bf16[80,1024]{1,0:T(8,128)(2,1)S(1)} collective-permute-done((bf16[80,1024]{1,0:T(8,128)(2,1)S(1)}, bf16[80,1024]{1,0:T(8,128)(2,1)S(1)}, u32[]{:S(2)}, u32[]{:S(2)}) %collective-permute-start.1) | collective-permute-done | bytes 163872 | tf_op jit(solution)/shard_map/ppermute | solution.py:32
  14.2 7.8 %collective-permute-done.2 = bf16[80,1024]{1,0:T(8,128)(2,1)S(1)} collective-permute-done((bf16[80,1024]{1,0:T(8,128)(2,1)S(1)}, bf16[80,1024]{1,0:T(8,128)(2,1)S(1)}, u32[]{:S(2)}, u32[]{:S(2)}) %collective-permute-start.2) | collective-permute-done | bytes 163872 | tf_op jit(solution)/shard_map/ppermute | solution.py:32
  22.1 3.1 %collective-permute-start.15 = (bf16[80,1024]{1,0:T(8,128)(2,1)S(1)}, bf16[80,1024]{1,0:T(8,128)(2,1)S(1)}, u32[]{:S(2)}, u32[]{:S(2)}) collective-permute-start(bf16[80,1024]{1,0:T(8,128)(2,1)S(1)} %pad_maximum_fusion.17), channel_id=1, source_target_pairs={{0,2},{1,3},{2,0},{3,1},{4,6},{5,7},{6,4},{7,5},{8,10},{9,11},{10,... | collective-permute-start | bytes 491528 | tf_op jit(solution)/shard_map/ppermute | solution.py:32
  26.2 1.5 %collective-permute-start.17 = (bf16[80,1024]{1,0:T(8,128)(2,1)S(1)}, bf16[80,1024]{1,0:T(8,128)(2,1)S(1)}, u32[]{:S(2)}, u32[]{:S(2)}) collective-permute-start(bf16[80,1024]{1,0:T(8,128)(2,1)S(1)} %pad_maximum_fusion.19), channel_id=1, source_target_pairs={{0,6},{1,7},{2,4},{3,5},{4,2},{5,3},{6,0},{7,1},{8,14},{9,15},{10,... | collective-permute-start | bytes 491528 | tf_op jit(solution)/shard_map/ppermute | solution.py:32
  27.9 1.4 %convolution_convert_fusion.3 = bf16[320,1792]{1,0:T(8,128)(2,1)S(1)} fusion(bf16[1792,1024]{1,0:T(8,128)(2,1)S(1)} %copy-done.3, bf16[80,1024]{1,0:T(8,128)(2,1)S(1)} %get-tuple-element.91, bf16[80,1024]{1,0:T(8,128)(2,1)S(1)} %get-tuple-element.92, bf16[80,1024]{1,0:T(8,128)(2,1)S(1)} %get-tuple-element.93, bf16[80,1024]{1,0:T(8,128)(2,1)S(1)} %get-tuple-element.90), kind=kOutput, calls=%fused_computation.3 | convolution fusion | flops 1177600000 | bytes 5472256 | tf_op jit(solution)/shard_map/dot_general | solution.py:261
  31.4 1.6 %collective-permute-start.4 = (bf16[80,1792]{1,0:T(8,128)(2,1)S(1)}, bf16[80,1792]{1,0:T(8,128)(2,1)S(1)}, u32[]{:S(2)}, u32[]{:S(2)}) collective-permute-start(bf16[80,1792]{1,0:T(8,128)(2,1)S(1)} %get-tuple-element.72), channel_id=1, source_target_pairs={{0,16},{8,24},{16,0},{24,8},{1,17},{9,25},{17,1},{25,9},{2,18},{10... | collective-permute-start | bytes 860168 | tf_op jit(solution)/shard_map/ppermute | solution.py:32
  33.0 1.6 %collective-permute-start.6 = (bf16[80,1792]{1,0:T(8,128)(2,1)S(1)}, bf16[80,1792]{1,0:T(8,128)(2,1)S(1)}, u32[]{:S(2)}, u32[]{:S(2)}) collective-permute-start(bf16[80,1792]{1,0:T(8,128)(2,1)S(1)} %get-tuple-element.71), channel_id=1, source_target_pairs={{0,8},{8,0},{16,24},{24,16},{1,9},{9,1},{17,25},{25,17},{2,10},{10... | collective-permute-start | bytes 860168 | tf_op jit(solution)/shard_map/ppermute | solution.py:32
  34.7 4.0 %collective-permute-done.4 = bf16[80,1792]{1,0:T(8,128)(2,1)S(1)} collective-permute-done((bf16[80,1792]{1,0:T(8,128)(2,1)S(1)}, bf16[80,1792]{1,0:T(8,128)(2,1)S(1)}, u32[]{:S(2)}, u32[]{:S(2)}) %collective-permute-start.4) | collective-permute-done | bytes 286752 | tf_op jit(solution)/shard_map/ppermute | solution.py:32
  41.6 1.5 %collective-permute-start.5 = (bf16[80,3584]{1,0:T(8,128)(2,1)S(1)}, bf16[80,3584]{1,0:T(8,128)(2,1)S(1)}, u32[]{:S(2)}, u32[]{:S(2)}) collective-permute-start(bf16[80,3584]{1,0:T(8,128)(2,1)S(1)} %pad_maximum_fusion.5), channel_id=1, source_target_pairs={{0,8},{8,0},{16,24},{24,16},{1,9},{9,1},{17,25},{25,17},{2,10},{10... | collective-permute-start | bytes 1720328 | tf_op jit(solution)/shard_map/ppermute | solution.py:32
  46.4 9.9 %collective-permute-done.7 = bf16[80,3584]{1,0:T(8,128)(2,1)S(1)} collective-permute-done((bf16[80,3584]{1,0:T(8,128)(2,1)S(1)}, bf16[80,3584]{1,0:T(8,128)(2,1)S(1)}, u32[]{:S(2)}, u32[]{:S(2)}) %collective-permute-start.7) | collective-permute-done | bytes 573472 | tf_op jit(solution)/shard_map/ppermute | solution.py:32
  58.8 1.5 %collective-permute-start.8 = (bf16[80,1792]{1,0:T(8,128)(2,1)S(1)}, bf16[80,1792]{1,0:T(8,128)(2,1)S(1)}, u32[]{:S(2)}, u32[]{:S(2)}) collective-permute-start(bf16[80,1792]{1,0:T(8,128)(2,1)S(1)} %multiply_convert_fusion.2), channel_id=1, source_target_pairs={{0,8},{8,0},{16,24},{24,16},{1,9},{9,1},{17,25},{25,17},{2,10},{10... | collective-permute-start | bytes 860168 | tf_op jit(solution)/shard_map/ppermute | solution.py:32
  62.6 5.0 %collective-permute-done.9 = bf16[80,1792]{1,0:T(8,128)(2,1)S(1)} collective-permute-done((bf16[80,1792]{1,0:T(8,128)(2,1)S(1)}, bf16[80,1792]{1,0:T(8,128)(2,1)S(1)}, u32[]{:S(2)}, u32[]{:S(2)}) %collective-permute-start.9) | collective-permute-done | bytes 286752 | tf_op jit(solution)/shard_map/ppermute | solution.py:32
  67.6 1.6 %collective-permute-start.10 = (bf16[80,896]{1,0:T(8,128)(2,1)S(1)}, bf16[80,896]{1,0:T(8,128)(2,1)S(1)}, u32[]{:S(2)}, u32[]{:S(2)}) collective-permute-start(bf16[80,896]{1,0:T(8,128)(2,1)S(1)} %get-tuple-element.110), channel_id=1, source_target_pairs={{0,8},{8,0},{16,24},{24,16},{1,9},{9,1},{17,25},{25,17},{2,10},{10... | collective-permute-start | bytes 430088 | tf_op jit(solution)/shard_map/ppermute | solution.py:32
  70.2 2.7 %collective-permute-done.22 = bf16[80,1792]{1,0:T(8,128)(2,1)S(1)} collective-permute-done((bf16[80,1792]{1,0:T(8,128)(2,1)S(1)}, bf16[80,1792]{1,0:T(8,128)(2,1)S(1)}, u32[]{:S(2)}, u32[]{:S(2)}) %collective-permute-start.22) | collective-permute-done | bytes 286752 | tf_op jit(solution)/shard_map/ppermute | solution.py:32
  75.4 1.5 %collective-permute-start.23 = (bf16[80,3584]{1,0:T(8,128)(2,1)S(1)}, bf16[80,3584]{1,0:T(8,128)(2,1)S(1)}, u32[]{:S(2)}, u32[]{:S(2)}) collective-permute-start(bf16[80,3584]{1,0:T(8,128)(2,1)S(1)} %pad_maximum_fusion.7), channel_id=1, source_target_pairs={{0,8},{8,0},{16,24},{24,16},{1,9},{9,1},{17,25},{25,17},{2,10},{10... | collective-permute-start | bytes 1720328 | tf_op jit(solution)/shard_map/ppermute | solution.py:32
  76.9 1.4 %convolution_convert_fusion.5 = bf16[320,1024]{1,0:T(8,128)(2,1)S(1)} fusion(bf16[1792,1024]{1,0:T(8,128)(2,1)S(1)} %copy-done.5, bf16[80,896]{1,0:T(8,128)(2,1)S(1)} %collective-permute-done.11, bf16[80,896]{1,0:T(8,128)(2,1)S(1)} %get-tuple-element.111, bf16[80,896]{1,0:T(8,128)(2,1)S(1)} %get-tuple-element.109, ...), kind=kOutput, calls=%fused_computation.7 | convolution fusion | flops 1183907840 | bytes 5472256 | tf_op jit(solution)/shard_map/dot_general | solution.py:283
  78.3 2.3 %collective-permute-start.14 = (bf16[80,1024]{1,0:T(8,128)(2,1)S(1)}, bf16[80,1024]{1,0:T(8,128)(2,1)S(1)}, u32[]{:S(2)}, u32[]{:S(2)}) collective-permute-start(bf16[80,1024]{1,0:T(8,128)(2,1)S(1)} %get-tuple-element.86), channel_id=1, source_target_pairs={{0,6},{1,7},{2,4},{3,5},{4,2},{5,3},{6,0},{7,1},{8,14},{9,15},{10,... | collective-permute-start | bytes 491528 | tf_op jit(solution)/shard_map/ppermute | solution.py:32
  80.6 1.5 %collective-permute-start.13 = (bf16[80,1024]{1,0:T(8,128)(2,1)S(1)}, bf16[80,1024]{1,0:T(8,128)(2,1)S(1)}, u32[]{:S(2)}, u32[]{:S(2)}) collective-permute-start(bf16[80,1024]{1,0:T(8,128)(2,1)S(1)} %get-tuple-element.87), channel_id=1, source_target_pairs={{0,4},{1,5},{2,6},{3,7},{4,0},{5,1},{6,2},{7,3},{8,12},{9,13},{10,... | collective-permute-start | bytes 491528 | tf_op jit(solution)/shard_map/ppermute | solution.py:32
  82.9 4.1 %collective-permute-done.24 = bf16[80,3584]{1,0:T(8,128)(2,1)S(1)} collective-permute-done((bf16[80,3584]{1,0:T(8,128)(2,1)S(1)}, bf16[80,3584]{1,0:T(8,128)(2,1)S(1)}, u32[]{:S(2)}, u32[]{:S(2)}) %collective-permute-start.24) | collective-permute-done | bytes 573472 | tf_op jit(solution)/shard_map/ppermute | solution.py:32
  88.8 1.6 %collective-permute-start.25 = (bf16[80,1792]{1,0:T(8,128)(2,1)S(1)}, bf16[80,1792]{1,0:T(8,128)(2,1)S(1)}, u32[]{:S(2)}, u32[]{:S(2)}) collective-permute-start(bf16[80,1792]{1,0:T(8,128)(2,1)S(1)} %get-tuple-element.99), channel_id=1, source_target_pairs={{0,8},{8,0},{16,24},{24,16},{1,9},{9,1},{17,25},{25,17},{2,10},{10... | collective-permute-start | bytes 860168 | tf_op jit(solution)/shard_map/ppermute | solution.py:32
  90.4 4.1 %convolution_convert_fusion = bf16[1792,1024]{1,0:T(8,128)(2,1)} fusion(bf16[320,1792]{1,0:T(8,128)(2,1)S(1)} %maximum_maximum_fusion, bf16[80,1024]{1,0:T(8,128)(2,1)S(1)} %get-tuple-element.75, bf16[80,1024]{1,0:T(8,128)(2,1)S(1)} %get-tuple-element.76, bf16[80,1024]{1,0:T(8,128)(2,1)S(1)} %get-tuple-element.77, bf16[80,1024]{1,0:T(8,128)(2,1)S(1)} %get-tuple-element.74), kind=kOutput, calls=%fused_computation | convolution fusion | flops 1178861568 | bytes 5472256 | tf_op jit(solution)/shard_map/dot_general | solution.py:298
  95.8 5.0 %shard_map.102 = (bf16[1792,1024]{1,0:T(8,128)(2,1)}, bf16[1792,1024]{1,0:T(8,128)(2,1)}) custom-call(bf16[320,1792]{1,0:T(8,128)(2,1)S(1)} %pad_maximum_fusion.first_ref, bf16[320,1792]{1,0:T(8,128)(2,1)S(1)} %pad_maximum_fusion.1.second_ref, bf16[320,1024]{1,0:T(8,128)(2,1)S(1)} %pad_maximum_fusion.3.rows_ref), custom_call_target="tpu_custom_call" | custom-call | flops 9395240960 | bytes 38535168 | tf_op jit(solution)/shard_map/pallas_call | solution.py:182
  (120 shorter events, 26.4 us)
Async XLA Ops:
  3.9 10.3 %collective-permute-start.1 = (bf16[80,1024]{1,0:T(8,128)(2,1)S(1)}, bf16[80,1024]{1,0:T(8,128)(2,1)S(1)}, u32[]{:S(2)}, u32[]{:S(2)}) collective-permute-start(bf16[80,1024]{1,0:T(8,128)(2,1)S(1)} %pad_maximum_fusion.13), channel_id=1, source_target_pairs={{0,2},{1,3},{2,0},{3,1},{4,6},{5,7},{6,4},{7,5},{8,10},{9,11},{10,... | collective-permute-start | bytes 491528 | tf_op jit(solution)/shard_map/ppermute | solution.py:32
  6.9 15.1 %collective-permute-start.2 = (bf16[80,1024]{1,0:T(8,128)(2,1)S(1)}, bf16[80,1024]{1,0:T(8,128)(2,1)S(1)}, u32[]{:S(2)}, u32[]{:S(2)}) collective-permute-start(bf16[80,1024]{1,0:T(8,128)(2,1)S(1)} %pad_maximum_fusion.14), channel_id=1, source_target_pairs={{0,4},{1,5},{2,6},{3,7},{4,0},{5,1},{6,2},{7,3},{8,12},{9,13},{10,... | collective-permute-start | bytes 491528 | tf_op jit(solution)/shard_map/ppermute | solution.py:32
  9.6 12.4 %collective-permute-start.3 = (bf16[80,1024]{1,0:T(8,128)(2,1)S(1)}, bf16[80,1024]{1,0:T(8,128)(2,1)S(1)}, u32[]{:S(2)}, u32[]{:S(2)}) collective-permute-start(bf16[80,1024]{1,0:T(8,128)(2,1)S(1)} %pad_maximum_fusion.15), channel_id=1, source_target_pairs={{0,6},{1,7},{2,4},{3,5},{4,2},{5,3},{6,0},{7,1},{8,14},{9,15},{10,... | collective-permute-start | bytes 491528 | tf_op jit(solution)/shard_map/ppermute | solution.py:32
  22.1 18.1 %collective-permute-start.15 = (bf16[80,1024]{1,0:T(8,128)(2,1)S(1)}, bf16[80,1024]{1,0:T(8,128)(2,1)S(1)}, u32[]{:S(2)}, u32[]{:S(2)}) collective-permute-start(bf16[80,1024]{1,0:T(8,128)(2,1)S(1)} %pad_maximum_fusion.17), channel_id=1, source_target_pairs={{0,2},{1,3},{2,0},{3,1},{4,6},{5,7},{6,4},{7,5},{8,10},{9,11},{10,... | collective-permute-start | bytes 491528 | tf_op jit(solution)/shard_map/ppermute | solution.py:32
  25.1 15.1 %collective-permute-start.16 = (bf16[80,1024]{1,0:T(8,128)(2,1)S(1)}, bf16[80,1024]{1,0:T(8,128)(2,1)S(1)}, u32[]{:S(2)}, u32[]{:S(2)}) collective-permute-start(bf16[80,1024]{1,0:T(8,128)(2,1)S(1)} %pad_maximum_fusion.18), channel_id=1, source_target_pairs={{0,4},{1,5},{2,6},{3,7},{4,0},{5,1},{6,2},{7,3},{8,12},{9,13},{10,... | collective-permute-start | bytes 491528 | tf_op jit(solution)/shard_map/ppermute | solution.py:32
  26.2 14.0 %collective-permute-start.17 = (bf16[80,1024]{1,0:T(8,128)(2,1)S(1)}, bf16[80,1024]{1,0:T(8,128)(2,1)S(1)}, u32[]{:S(2)}, u32[]{:S(2)}) collective-permute-start(bf16[80,1024]{1,0:T(8,128)(2,1)S(1)} %pad_maximum_fusion.19), channel_id=1, source_target_pairs={{0,6},{1,7},{2,4},{3,5},{4,2},{5,3},{6,0},{7,1},{8,14},{9,15},{10,... | collective-permute-start | bytes 491528 | tf_op jit(solution)/shard_map/ppermute | solution.py:32
  31.4 7.3 %collective-permute-start.4 = (bf16[80,1792]{1,0:T(8,128)(2,1)S(1)}, bf16[80,1792]{1,0:T(8,128)(2,1)S(1)}, u32[]{:S(2)}, u32[]{:S(2)}) collective-permute-start(bf16[80,1792]{1,0:T(8,128)(2,1)S(1)} %get-tuple-element.72), channel_id=1, source_target_pairs={{0,16},{8,24},{16,0},{24,8},{1,17},{9,25},{17,1},{25,9},{2,18},{10... | collective-permute-start | bytes 860168 | tf_op jit(solution)/shard_map/ppermute | solution.py:32
  33.0 7.0 %collective-permute-start.6 = (bf16[80,1792]{1,0:T(8,128)(2,1)S(1)}, bf16[80,1792]{1,0:T(8,128)(2,1)S(1)}, u32[]{:S(2)}, u32[]{:S(2)}) collective-permute-start(bf16[80,1792]{1,0:T(8,128)(2,1)S(1)} %get-tuple-element.71), channel_id=1, source_target_pairs={{0,8},{8,0},{16,24},{24,16},{1,9},{9,1},{17,25},{25,17},{2,10},{10... | collective-permute-start | bytes 860168 | tf_op jit(solution)/shard_map/ppermute | solution.py:32
  40.5 15.8 %collective-permute-start.7 = (bf16[80,3584]{1,0:T(8,128)(2,1)S(1)}, bf16[80,3584]{1,0:T(8,128)(2,1)S(1)}, u32[]{:S(2)}, u32[]{:S(2)}) collective-permute-start(bf16[80,3584]{1,0:T(8,128)(2,1)S(1)} %pad_maximum_fusion.6), channel_id=1, source_target_pairs={{0,16},{8,24},{16,0},{24,8},{1,17},{9,25},{17,1},{25,9},{2,18},{10... | collective-permute-start | bytes 1720328 | tf_op jit(solution)/shard_map/ppermute | solution.py:32
  41.6 15.8 %collective-permute-start.5 = (bf16[80,3584]{1,0:T(8,128)(2,1)S(1)}, bf16[80,3584]{1,0:T(8,128)(2,1)S(1)}, u32[]{:S(2)}, u32[]{:S(2)}) collective-permute-start(bf16[80,3584]{1,0:T(8,128)(2,1)S(1)} %pad_maximum_fusion.5), channel_id=1, source_target_pairs={{0,8},{8,0},{16,24},{24,16},{1,9},{9,1},{17,25},{25,17},{2,10},{10... | collective-permute-start | bytes 1720328 | tf_op jit(solution)/shard_map/ppermute | solution.py:32
  44.9 15.4 %collective-permute-start.20 = (bf16[80,896]{1,0:T(8,128)(2,1)S(1)}, bf16[80,896]{1,0:T(8,128)(2,1)S(1)}, u32[]{:S(2)}, u32[]{:S(2)}) collective-permute-start(bf16[80,896]{1,0:T(8,128)(2,1)S(1)} %get-tuple-element.66), channel_id=1, source_target_pairs={{0,16},{8,24},{16,0},{24,8},{1,17},{9,25},{17,1},{25,9},{2,18},{10... | collective-permute-start | bytes 430088 | tf_op jit(solution)/shard_map/ppermute | solution.py:32
  45.9 14.4 %collective-permute-start.19 = (bf16[80,896]{1,0:T(8,128)(2,1)S(1)}, bf16[80,896]{1,0:T(8,128)(2,1)S(1)}, u32[]{:S(2)}, u32[]{:S(2)}) collective-permute-start(bf16[80,896]{1,0:T(8,128)(2,1)S(1)} %get-tuple-element.67), channel_id=1, source_target_pairs={{0,8},{8,0},{16,24},{24,16},{1,9},{9,1},{17,25},{25,17},{2,10},{10... | collective-permute-start | bytes 430088 | tf_op jit(solution)/shard_map/ppermute | solution.py:32
  57.8 9.8 %collective-permute-start.9 = (bf16[80,1792]{1,0:T(8,128)(2,1)S(1)}, bf16[80,1792]{1,0:T(8,128)(2,1)S(1)}, u32[]{:S(2)}, u32[]{:S(2)}) collective-permute-start(bf16[80,1792]{1,0:T(8,128)(2,1)S(1)} %multiply_convert_fusion.2), channel_id=1, source_target_pairs={{0,16},{8,24},{16,0},{24,8},{1,17},{9,25},{17,1},{25,9},{2,18},{10... | collective-permute-start | bytes 860168 | tf_op jit(solution)/shard_map/ppermute | solution.py:32
  58.8 10.4 %collective-permute-start.8 = (bf16[80,1792]{1,0:T(8,128)(2,1)S(1)}, bf16[80,1792]{1,0:T(8,128)(2,1)S(1)}, u32[]{:S(2)}, u32[]{:S(2)}) collective-permute-start(bf16[80,1792]{1,0:T(8,128)(2,1)S(1)} %multiply_convert_fusion.2), channel_id=1, source_target_pairs={{0,8},{8,0},{16,24},{24,16},{1,9},{9,1},{17,25},{25,17},{2,10},{10... | collective-permute-start | bytes 860168 | tf_op jit(solution)/shard_map/ppermute | solution.py:32
  60.5 12.4 %collective-permute-start.22 = (bf16[80,1792]{1,0:T(8,128)(2,1)S(1)}, bf16[80,1792]{1,0:T(8,128)(2,1)S(1)}, u32[]{:S(2)}, u32[]{:S(2)}) collective-permute-start(bf16[80,1792]{1,0:T(8,128)(2,1)S(1)} %pad_maximum_fusion.11), channel_id=1, source_target_pairs={{0,16},{8,24},{16,0},{24,8},{1,17},{9,25},{17,1},{25,9},{2,18},{10... | collective-permute-start | bytes 860168 | tf_op jit(solution)/shard_map/ppermute | solution.py:32
  61.7 11.9 %collective-permute-start.21 = (bf16[80,1792]{1,0:T(8,128)(2,1)S(1)}, bf16[80,1792]{1,0:T(8,128)(2,1)S(1)}, u32[]{:S(2)}, u32[]{:S(2)}) collective-permute-start(bf16[80,1792]{1,0:T(8,128)(2,1)S(1)} %pad_maximum_fusion.10), channel_id=1, source_target_pairs={{0,8},{8,0},{16,24},{24,16},{1,9},{9,1},{17,25},{25,17},{2,10},{10... | collective-permute-start | bytes 860168 | tf_op jit(solution)/shard_map/ppermute | solution.py:32
  67.6 9.2 %collective-permute-start.10 = (bf16[80,896]{1,0:T(8,128)(2,1)S(1)}, bf16[80,896]{1,0:T(8,128)(2,1)S(1)}, u32[]{:S(2)}, u32[]{:S(2)}) collective-permute-start(bf16[80,896]{1,0:T(8,128)(2,1)S(1)} %get-tuple-element.110), channel_id=1, source_target_pairs={{0,8},{8,0},{16,24},{24,16},{1,9},{9,1},{17,25},{25,17},{2,10},{10... | collective-permute-start | bytes 430088 | tf_op jit(solution)/shard_map/ppermute | solution.py:32
  69.2 7.7 %collective-permute-start.11 = (bf16[80,896]{1,0:T(8,128)(2,1)S(1)}, bf16[80,896]{1,0:T(8,128)(2,1)S(1)}, u32[]{:S(2)}, u32[]{:S(2)}) collective-permute-start(bf16[80,896]{1,0:T(8,128)(2,1)S(1)} %get-tuple-element.109), channel_id=1, source_target_pairs={{0,16},{8,24},{16,0},{24,8},{1,17},{9,25},{17,1},{25,9},{2,18},{10... | collective-permute-start | bytes 430088 | tf_op jit(solution)/shard_map/ppermute | solution.py:32
  74.2 12.8 %collective-permute-start.24 = (bf16[80,3584]{1,0:T(8,128)(2,1)S(1)}, bf16[80,3584]{1,0:T(8,128)(2,1)S(1)}, u32[]{:S(2)}, u32[]{:S(2)}) collective-permute-start(bf16[80,3584]{1,0:T(8,128)(2,1)S(1)} %pad_maximum_fusion.7), channel_id=1, source_target_pairs={{0,16},{8,24},{16,0},{24,8},{1,17},{9,25},{17,1},{25,9},{2,18},{10... | collective-permute-start | bytes 1720328 | tf_op jit(solution)/shard_map/ppermute | solution.py:32
  75.4 12.1 %collective-permute-start.23 = (bf16[80,3584]{1,0:T(8,128)(2,1)S(1)}, bf16[80,3584]{1,0:T(8,128)(2,1)S(1)}, u32[]{:S(2)}, u32[]{:S(2)}) collective-permute-start(bf16[80,3584]{1,0:T(8,128)(2,1)S(1)} %pad_maximum_fusion.7), channel_id=1, source_target_pairs={{0,8},{8,0},{16,24},{24,16},{1,9},{9,1},{17,25},{25,17},{2,10},{10... | collective-permute-start | bytes 1720328 | tf_op jit(solution)/shard_map/ppermute | solution.py:32
  78.3 17.2 %collective-permute-start.14 = (bf16[80,1024]{1,0:T(8,128)(2,1)S(1)}, bf16[80,1024]{1,0:T(8,128)(2,1)S(1)}, u32[]{:S(2)}, u32[]{:S(2)}) collective-permute-start(bf16[80,1024]{1,0:T(8,128)(2,1)S(1)} %get-tuple-element.86), channel_id=1, source_target_pairs={{0,6},{1,7},{2,4},{3,5},{4,2},{5,3},{6,0},{7,1},{8,14},{9,15},{10,... | collective-permute-start | bytes 491528 | tf_op jit(solution)/shard_map/ppermute | solution.py:32
  80.6 15.0 %collective-permute-start.13 = (bf16[80,1024]{1,0:T(8,128)(2,1)S(1)}, bf16[80,1024]{1,0:T(8,128)(2,1)S(1)}, u32[]{:S(2)}, u32[]{:S(2)}) collective-permute-start(bf16[80,1024]{1,0:T(8,128)(2,1)S(1)} %get-tuple-element.87), channel_id=1, source_target_pairs={{0,4},{1,5},{2,6},{3,7},{4,0},{5,1},{6,2},{7,3},{8,12},{9,13},{10,... | collective-permute-start | bytes 491528 | tf_op jit(solution)/shard_map/ppermute | solution.py:32
  82.2 13.4 %collective-permute-start.12 = (bf16[80,1024]{1,0:T(8,128)(2,1)S(1)}, bf16[80,1024]{1,0:T(8,128)(2,1)S(1)}, u32[]{:S(2)}, u32[]{:S(2)}) collective-permute-start(bf16[80,1024]{1,0:T(8,128)(2,1)S(1)} %get-tuple-element.88), channel_id=1, source_target_pairs={{0,2},{1,3},{2,0},{3,1},{4,6},{5,7},{6,4},{7,5},{8,10},{9,11},{10,... | collective-permute-start | bytes 491528 | tf_op jit(solution)/shard_map/ppermute | solution.py:32
  87.5 7.0 %collective-permute-start.26 = (bf16[80,1792]{1,0:T(8,128)(2,1)S(1)}, bf16[80,1792]{1,0:T(8,128)(2,1)S(1)}, u32[]{:S(2)}, u32[]{:S(2)}) collective-permute-start(bf16[80,1792]{1,0:T(8,128)(2,1)S(1)} %get-tuple-element.100), channel_id=1, source_target_pairs={{0,16},{8,24},{16,0},{24,8},{1,17},{9,25},{17,1},{25,9},{2,18},{10... | collective-permute-start | bytes 860168 | tf_op jit(solution)/shard_map/ppermute | solution.py:32
  (10 other events, 32.4 us)

commit v11 on v10

--- a/solution.py
+++ b/solution.py
@@ -243,7 +243,7 @@
     ).astype(BF)
     if near:
         in_rows = to_chips(*pair_core(send_rows))
-        cot_send, in_rows = after((cot_send, in_rows))
+        cot_send, in_rows[2] = after((cot_send, in_rows[2]))
         cot_rows = to_chips_first(cot_send)
     else:
         in_rows = [all_to_all(send_rows, experts)]

time: 102 us -> 98.4 us (0.965); the launches traced: 102 us -> 96.5 us
  waiting for transfers between devices: 42.7 us -> 36.5 us
    ppermute x28, waiting for transfers between devices: 42.7 us -> 36.5 us  [swap(): return lax.ppermute(block, axis, [(i, i ^ mask) for i in range(count)])]
  transfers between devices with their start and end apart: 28 -> 28, of which waited for: 13 -> 12; matrix products, arithmetic and copies ran while one was open for 13% -> 14% of each run, Pallas kernels for 5% -> 5%
where the time goes in v11:
time: 98.4 us; the launch traced here: 96.5 us
  starting transfers between devices  37.2 us (38%)
  waiting for transfers between devices  36.5 us (37%)
  matrix products  12.3 us (12%)
  Pallas kernels  4.96 us (5%)
  other arithmetic  2.75 us (3%)
  local copies, waits for them, and re-layouts  1.41 us (1%)
  between operations  1.3 us (1%)
    ppermute x28, starting transfers between devices, swap(): return lax.ppermute(block, axis, [(i, i ^ mask) for i in range(count)])  37.2 us
    ppermute x28, waiting for transfers between devices, swap(): return lax.ppermute(block, axis, [(i, i ^ mask) for i in range(count)])  36.5 us
    pallas_call x1, Pallas kernels, two_terms(): pl.pallas_call(kernel, in_specs=[whole, whole, whole], out_specs=[anywher...  4.96 us
    dot_general x3, matrix products, partial_product(): lax.dot_general(rows, weights, CONTRACT_FEATS, preferred_element_type=F32)  4.22 us
    dot_general x1, matrix products, term(): lax.dot_general(left, right, CONTRACT_ROWS, preferred_element_type=F32)  4.11 us
  transfers between devices with their start and end apart: 28, of which 12 were waited for; matrix products, arithmetic and copies ran while one was open for 14% of the time, Pallas kernels for 5%

profile of v11, /device:TPU:0, one launch (start us, length us, event | category | flops | bytes accessed | tf_op | source)
XLA Modules:
  0.0 96.5 jit_solution(14026841758037014942)
XLA Ops:
  3.9 4.0 %collective-permute-start.2 = (bf16[80,1024]{1,0:T(8,128)(2,1)S(1)}, bf16[80,1024]{1,0:T(8,128)(2,1)S(1)}, u32[]{:S(2)}, u32[]{:S(2)}) collective-permute-start(bf16[80,1024]{1,0:T(8,128)(2,1)S(1)} %pad_maximum_fusion.12), channel_id=1, source_target_pairs={{0,4},{1,5},{2,6},{3,7},{4,0},{5,1},{6,2},{7,3},{8,12},{9,13},{10,... | collective-permute-start | bytes 491528 | tf_op jit(solution)/shard_map/ppermute | solution.py:32
  7.9 1.6 %collective-permute-start.1 = (bf16[80,1024]{1,0:T(8,128)(2,1)S(1)}, bf16[80,1024]{1,0:T(8,128)(2,1)S(1)}, u32[]{:S(2)}, u32[]{:S(2)}) collective-permute-start(bf16[80,1024]{1,0:T(8,128)(2,1)S(1)} %pad_maximum_fusion.11), channel_id=1, source_target_pairs={{0,2},{1,3},{2,0},{3,1},{4,6},{5,7},{6,4},{7,5},{8,10},{9,11},{10,... | collective-permute-start | bytes 491528 | tf_op jit(solution)/shard_map/ppermute | solution.py:32
  9.7 7.0 %collective-permute-done.2 = bf16[80,1024]{1,0:T(8,128)(2,1)S(1)} collective-permute-done((bf16[80,1024]{1,0:T(8,128)(2,1)S(1)}, bf16[80,1024]{1,0:T(8,128)(2,1)S(1)}, u32[]{:S(2)}, u32[]{:S(2)}) %collective-permute-start.2) | collective-permute-done | bytes 163872 | tf_op jit(solution)/shard_map/ppermute | solution.py:32
  17.4 3.7 %collective-permute-start.16 = (bf16[80,1024]{1,0:T(8,128)(2,1)S(1)}, bf16[80,1024]{1,0:T(8,128)(2,1)S(1)}, u32[]{:S(2)}, u32[]{:S(2)}) collective-permute-start(bf16[80,1024]{1,0:T(8,128)(2,1)S(1)} %pad_maximum_fusion.16), channel_id=1, source_target_pairs={{0,4},{1,5},{2,6},{3,7},{4,0},{5,1},{6,2},{7,3},{8,12},{9,13},{10,... | collective-permute-start | bytes 491528 | tf_op jit(solution)/shard_map/ppermute | solution.py:32
  21.5 1.4 %convolution_convert_fusion.3 = bf16[320,1792]{1,0:T(8,128)(2,1)S(1)} fusion(bf16[1792,1024]{1,0:T(8,128)(2,1)S(1)} %copy-done.3, bf16[80,1024]{1,0:T(8,128)(2,1)S(1)} %get-tuple-element.85, bf16[80,1024]{1,0:T(8,128)(2,1)S(1)} %get-tuple-element.86, bf16[80,1024]{1,0:T(8,128)(2,1)S(1)} %get-tuple-element.87, bf16[80,1024]{1,0:T(8,128)(2,1)S(1)} %get-tuple-element.84), kind=kOutput, calls=%fused_computation.3 | convolution fusion | flops 1177600000 | bytes 5472256 | tf_op jit(solution)/shard_map/dot_general | solution.py:261
  23.5 1.4 %convolution_convert_fusion.2 = bf16[320,1792]{1,0:T(8,128)(2,1)S(1)} fusion(bf16[1792,1024]{1,0:T(8,128)(2,1)S(1)} %copy-done.4, bf16[80,1024]{1,0:T(8,128)(2,1)S(1)} %get-tuple-element.85, bf16[80,1024]{1,0:T(8,128)(2,1)S(1)} %get-tuple-element.86, bf16[80,1024]{1,0:T(8,128)(2,1)S(1)} %get-tuple-element.87, bf16[80,1024]{1,0:T(8,128)(2,1)S(1)} %get-tuple-element.84), kind=kOutput, calls=%fused_computation.2 | convolution fusion | flops 1177600000 | bytes 5472256 | tf_op jit(solution)/shard_map/dot_general | solution.py:261
  25.0 2.2 %collective-permute-start.4 = (bf16[80,1792]{1,0:T(8,128)(2,1)S(1)}, bf16[80,1792]{1,0:T(8,128)(2,1)S(1)}, u32[]{:S(2)}, u32[]{:S(2)}) collective-permute-start(bf16[80,1792]{1,0:T(8,128)(2,1)S(1)} %get-tuple-element.66), channel_id=1, source_target_pairs={{0,16},{8,24},{16,0},{24,8},{1,17},{9,25},{17,1},{25,9},{2,18},{10... | collective-permute-start | bytes 860168 | tf_op jit(solution)/shard_map/ppermute | solution.py:32
  27.3 1.6 %collective-permute-start.6 = (bf16[80,1792]{1,0:T(8,128)(2,1)S(1)}, bf16[80,1792]{1,0:T(8,128)(2,1)S(1)}, u32[]{:S(2)}, u32[]{:S(2)}) collective-permute-start(bf16[80,1792]{1,0:T(8,128)(2,1)S(1)} %get-tuple-element.65), channel_id=1, source_target_pairs={{0,8},{8,0},{16,24},{24,16},{1,9},{9,1},{17,25},{25,17},{2,10},{10... | collective-permute-start | bytes 860168 | tf_op jit(solution)/shard_map/ppermute | solution.py:32
  28.9 4.0 %collective-permute-done.4 = bf16[80,1792]{1,0:T(8,128)(2,1)S(1)} collective-permute-done((bf16[80,1792]{1,0:T(8,128)(2,1)S(1)}, bf16[80,1792]{1,0:T(8,128)(2,1)S(1)}, u32[]{:S(2)}, u32[]{:S(2)}) %collective-permute-start.4) | collective-permute-done | bytes 286752 | tf_op jit(solution)/shard_map/ppermute | solution.py:32
  34.7 1.4 %collective-permute-start.7 = (bf16[80,3584]{1,0:T(8,128)(2,1)S(1)}, bf16[80,3584]{1,0:T(8,128)(2,1)S(1)}, u32[]{:S(2)}, u32[]{:S(2)}) collective-permute-start(bf16[80,3584]{1,0:T(8,128)(2,1)S(1)} %pad_maximum_fusion.5), channel_id=1, source_target_pairs={{0,16},{8,24},{16,0},{24,8},{1,17},{9,25},{17,1},{25,9},{2,18},{10... | collective-permute-start | bytes 1720328 | tf_op jit(solution)/shard_map/ppermute | solution.py:32
  36.2 1.5 %collective-permute-start.5 = (bf16[80,3584]{1,0:T(8,128)(2,1)S(1)}, bf16[80,3584]{1,0:T(8,128)(2,1)S(1)}, u32[]{:S(2)}, u32[]{:S(2)}) collective-permute-start(bf16[80,3584]{1,0:T(8,128)(2,1)S(1)} %pad_maximum_fusion.4), channel_id=1, source_target_pairs={{0,8},{8,0},{16,24},{24,16},{1,9},{9,1},{17,25},{25,17},{2,10},{10... | collective-permute-start | bytes 1720328 | tf_op jit(solution)/shard_map/ppermute | solution.py:32
  41.0 9.6 %collective-permute-done.7 = bf16[80,3584]{1,0:T(8,128)(2,1)S(1)} collective-permute-done((bf16[80,3584]{1,0:T(8,128)(2,1)S(1)}, bf16[80,3584]{1,0:T(8,128)(2,1)S(1)}, u32[]{:S(2)}, u32[]{:S(2)}) %collective-permute-start.7) | collective-permute-done | bytes 573472 | tf_op jit(solution)/shard_map/ppermute | solution.py:32
  53.0 1.5 %collective-permute-start.8 = (bf16[80,1792]{1,0:T(8,128)(2,1)S(1)}, bf16[80,1792]{1,0:T(8,128)(2,1)S(1)}, u32[]{:S(2)}, u32[]{:S(2)}) collective-permute-start(bf16[80,1792]{1,0:T(8,128)(2,1)S(1)} %multiply_convert_fusion.2), channel_id=1, source_target_pairs={{0,8},{8,0},{16,24},{24,16},{1,9},{9,1},{17,25},{25,17},{2,10},{10... | collective-permute-start | bytes 860168 | tf_op jit(solution)/shard_map/ppermute | solution.py:32
  54.8 1.4 %collective-permute-start.22 = (bf16[80,1792]{1,0:T(8,128)(2,1)S(1)}, bf16[80,1792]{1,0:T(8,128)(2,1)S(1)}, u32[]{:S(2)}, u32[]{:S(2)}) collective-permute-start(bf16[80,1792]{1,0:T(8,128)(2,1)S(1)} %pad_maximum_fusion.10), channel_id=1, source_target_pairs={{0,16},{8,24},{16,0},{24,8},{1,17},{9,25},{17,1},{25,9},{2,18},{10... | collective-permute-start | bytes 860168 | tf_op jit(solution)/shard_map/ppermute | solution.py:32
  56.9 5.3 %collective-permute-done.9 = bf16[80,1792]{1,0:T(8,128)(2,1)S(1)} collective-permute-done((bf16[80,1792]{1,0:T(8,128)(2,1)S(1)}, bf16[80,1792]{1,0:T(8,128)(2,1)S(1)}, u32[]{:S(2)}, u32[]{:S(2)}) %collective-permute-start.9) | collective-permute-done | bytes 286752 | tf_op jit(solution)/shard_map/ppermute | solution.py:32
  62.2 1.6 %collective-permute-start.10 = (bf16[80,896]{1,0:T(8,128)(2,1)S(1)}, bf16[80,896]{1,0:T(8,128)(2,1)S(1)}, u32[]{:S(2)}, u32[]{:S(2)}) collective-permute-start(bf16[80,896]{1,0:T(8,128)(2,1)S(1)} %get-tuple-element.104), channel_id=1, source_target_pairs={{0,8},{8,0},{16,24},{24,16},{1,9},{9,1},{17,25},{25,17},{2,10},{10... | collective-permute-start | bytes 430088 | tf_op jit(solution)/shard_map/ppermute | solution.py:32
  64.5 3.0 %collective-permute-done.22 = bf16[80,1792]{1,0:T(8,128)(2,1)S(1)} collective-permute-done((bf16[80,1792]{1,0:T(8,128)(2,1)S(1)}, bf16[80,1792]{1,0:T(8,128)(2,1)S(1)}, u32[]{:S(2)}, u32[]{:S(2)}) %collective-permute-start.22) | collective-permute-done | bytes 286752 | tf_op jit(solution)/shard_map/ppermute | solution.py:32
  69.9 1.5 %collective-permute-start.23 = (bf16[80,3584]{1,0:T(8,128)(2,1)S(1)}, bf16[80,3584]{1,0:T(8,128)(2,1)S(1)}, u32[]{:S(2)}, u32[]{:S(2)}) collective-permute-start(bf16[80,3584]{1,0:T(8,128)(2,1)S(1)} %pad_maximum_fusion.6), channel_id=1, source_target_pairs={{0,8},{8,0},{16,24},{24,16},{1,9},{9,1},{17,25},{25,17},{2,10},{10... | collective-permute-start | bytes 1720328 | tf_op jit(solution)/shard_map/ppermute | solution.py:32
  72.9 3.2 %collective-permute-start.14 = (bf16[80,1024]{1,0:T(8,128)(2,1)S(1)}, bf16[80,1024]{1,0:T(8,128)(2,1)S(1)}, u32[]{:S(2)}, u32[]{:S(2)}) collective-permute-start(bf16[80,1024]{1,0:T(8,128)(2,1)S(1)} %get-tuple-element.80), channel_id=1, source_target_pairs={{0,6},{1,7},{2,4},{3,5},{4,2},{5,3},{6,0},{7,1},{8,14},{9,15},{10,... | collective-permute-start | bytes 491528 | tf_op jit(solution)/shard_map/ppermute | solution.py:32
  76.1 2.3 %collective-permute-start.13 = (bf16[80,1024]{1,0:T(8,128)(2,1)S(1)}, bf16[80,1024]{1,0:T(8,128)(2,1)S(1)}, u32[]{:S(2)}, u32[]{:S(2)}) collective-permute-start(bf16[80,1024]{1,0:T(8,128)(2,1)S(1)} %get-tuple-element.81), channel_id=1, source_target_pairs={{0,4},{1,5},{2,6},{3,7},{4,0},{5,1},{6,2},{7,3},{8,12},{9,13},{10,... | collective-permute-start | bytes 491528 | tf_op jit(solution)/shard_map/ppermute | solution.py:32
  78.9 2.6 %collective-permute-done.24 = bf16[80,3584]{1,0:T(8,128)(2,1)S(1)} collective-permute-done((bf16[80,3584]{1,0:T(8,128)(2,1)S(1)}, bf16[80,3584]{1,0:T(8,128)(2,1)S(1)}, u32[]{:S(2)}, u32[]{:S(2)}) %collective-permute-start.24) | collective-permute-done | bytes 573472 | tf_op jit(solution)/shard_map/ppermute | solution.py:32
  83.4 1.6 %collective-permute-start.25 = (bf16[80,1792]{1,0:T(8,128)(2,1)S(1)}, bf16[80,1792]{1,0:T(8,128)(2,1)S(1)}, u32[]{:S(2)}, u32[]{:S(2)}) collective-permute-start(bf16[80,1792]{1,0:T(8,128)(2,1)S(1)} %get-tuple-element.93), channel_id=1, source_target_pairs={{0,8},{8,0},{16,24},{24,16},{1,9},{9,1},{17,25},{25,17},{2,10},{10... | collective-permute-start | bytes 860168 | tf_op jit(solution)/shard_map/ppermute | solution.py:32
  84.9 4.1 %convolution_convert_fusion = bf16[1792,1024]{1,0:T(8,128)(2,1)} fusion(bf16[320,1792]{1,0:T(8,128)(2,1)S(1)} %maximum_maximum_fusion, bf16[80,1024]{1,0:T(8,128)(2,1)S(1)} %get-tuple-element.69, bf16[80,1024]{1,0:T(8,128)(2,1)S(1)} %get-tuple-element.70, bf16[80,1024]{1,0:T(8,128)(2,1)S(1)} %get-tuple-element.71, bf16[80,1024]{1,0:T(8,128)(2,1)S(1)} %get-tuple-element.68), kind=kOutput, calls=%fused_computation | convolution fusion | flops 1178861568 | bytes 5472256 | tf_op jit(solution)/shard_map/dot_general | solution.py:298
  90.4 5.0 %shard_map.102 = (bf16[1792,1024]{1,0:T(8,128)(2,1)}, bf16[1792,1024]{1,0:T(8,128)(2,1)}) custom-call(bf16[320,1792]{1,0:T(8,128)(2,1)S(1)} %pad_maximum_fusion.first_ref, bf16[320,1792]{1,0:T(8,128)(2,1)S(1)} %pad_maximum_fusion.1.second_ref, bf16[320,1024]{1,0:T(8,128)(2,1)S(1)} %pad_maximum_fusion.2.rows_ref), custom_call_target="tpu_custom_call" | custom-call | flops 9395240960 | bytes 38535168 | tf_op jit(solution)/shard_map/pallas_call | solution.py:182
  (121 shorter events, 22.7 us)
Async XLA Ops:
  3.9 12.8 %collective-permute-start.2 = (bf16[80,1024]{1,0:T(8,128)(2,1)S(1)}, bf16[80,1024]{1,0:T(8,128)(2,1)S(1)}, u32[]{:S(2)}, u32[]{:S(2)}) collective-permute-start(bf16[80,1024]{1,0:T(8,128)(2,1)S(1)} %pad_maximum_fusion.12), channel_id=1, source_target_pairs={{0,4},{1,5},{2,6},{3,7},{4,0},{5,1},{6,2},{7,3},{8,12},{9,13},{10,... | collective-permute-start | bytes 491528 | tf_op jit(solution)/shard_map/ppermute | solution.py:32
  7.9 13.4 %collective-permute-start.1 = (bf16[80,1024]{1,0:T(8,128)(2,1)S(1)}, bf16[80,1024]{1,0:T(8,128)(2,1)S(1)}, u32[]{:S(2)}, u32[]{:S(2)}) collective-permute-start(bf16[80,1024]{1,0:T(8,128)(2,1)S(1)} %pad_maximum_fusion.11), channel_id=1, source_target_pairs={{0,2},{1,3},{2,0},{3,1},{4,6},{5,7},{6,4},{7,5},{8,10},{9,11},{10,... | collective-permute-start | bytes 491528 | tf_op jit(solution)/shard_map/ppermute | solution.py:32
  9.6 11.8 %collective-permute-start.3 = (bf16[80,1024]{1,0:T(8,128)(2,1)S(1)}, bf16[80,1024]{1,0:T(8,128)(2,1)S(1)}, u32[]{:S(2)}, u32[]{:S(2)}) collective-permute-start(bf16[80,1024]{1,0:T(8,128)(2,1)S(1)} %pad_maximum_fusion.13), channel_id=1, source_target_pairs={{0,6},{1,7},{2,4},{3,5},{4,2},{5,3},{6,0},{7,1},{8,14},{9,15},{10,... | collective-permute-start | bytes 491528 | tf_op jit(solution)/shard_map/ppermute | solution.py:32
  16.7 17.7 %collective-permute-start.15 = (bf16[80,1024]{1,0:T(8,128)(2,1)S(1)}, bf16[80,1024]{1,0:T(8,128)(2,1)S(1)}, u32[]{:S(2)}, u32[]{:S(2)}) collective-permute-start(bf16[80,1024]{1,0:T(8,128)(2,1)S(1)} %pad_maximum_fusion.15), channel_id=1, source_target_pairs={{0,2},{1,3},{2,0},{3,1},{4,6},{5,7},{6,4},{7,5},{8,10},{9,11},{10,... | collective-permute-start | bytes 491528 | tf_op jit(solution)/shard_map/ppermute | solution.py:32
  17.4 17.1 %collective-permute-start.16 = (bf16[80,1024]{1,0:T(8,128)(2,1)S(1)}, bf16[80,1024]{1,0:T(8,128)(2,1)S(1)}, u32[]{:S(2)}, u32[]{:S(2)}) collective-permute-start(bf16[80,1024]{1,0:T(8,128)(2,1)S(1)} %pad_maximum_fusion.16), channel_id=1, source_target_pairs={{0,4},{1,5},{2,6},{3,7},{4,0},{5,1},{6,2},{7,3},{8,12},{9,13},{10,... | collective-permute-start | bytes 491528 | tf_op jit(solution)/shard_map/ppermute | solution.py:32
  21.2 13.3 %collective-permute-start.17 = (bf16[80,1024]{1,0:T(8,128)(2,1)S(1)}, bf16[80,1024]{1,0:T(8,128)(2,1)S(1)}, u32[]{:S(2)}, u32[]{:S(2)}) collective-permute-start(bf16[80,1024]{1,0:T(8,128)(2,1)S(1)} %pad_maximum_fusion.17), channel_id=1, source_target_pairs={{0,6},{1,7},{2,4},{3,5},{4,2},{5,3},{6,0},{7,1},{8,14},{9,15},{10,... | collective-permute-start | bytes 491528 | tf_op jit(solution)/shard_map/ppermute | solution.py:32
  25.0 7.9 %collective-permute-start.4 = (bf16[80,1792]{1,0:T(8,128)(2,1)S(1)}, bf16[80,1792]{1,0:T(8,128)(2,1)S(1)}, u32[]{:S(2)}, u32[]{:S(2)}) collective-permute-start(bf16[80,1792]{1,0:T(8,128)(2,1)S(1)} %get-tuple-element.66), channel_id=1, source_target_pairs={{0,16},{8,24},{16,0},{24,8},{1,17},{9,25},{17,1},{25,9},{2,18},{10... | collective-permute-start | bytes 860168 | tf_op jit(solution)/shard_map/ppermute | solution.py:32
  27.3 7.0 %collective-permute-start.6 = (bf16[80,1792]{1,0:T(8,128)(2,1)S(1)}, bf16[80,1792]{1,0:T(8,128)(2,1)S(1)}, u32[]{:S(2)}, u32[]{:S(2)}) collective-permute-start(bf16[80,1792]{1,0:T(8,128)(2,1)S(1)} %get-tuple-element.65), channel_id=1, source_target_pairs={{0,8},{8,0},{16,24},{24,16},{1,9},{9,1},{17,25},{25,17},{2,10},{10... | collective-permute-start | bytes 860168 | tf_op jit(solution)/shard_map/ppermute | solution.py:32
  34.7 15.8 %collective-permute-start.7 = (bf16[80,3584]{1,0:T(8,128)(2,1)S(1)}, bf16[80,3584]{1,0:T(8,128)(2,1)S(1)}, u32[]{:S(2)}, u32[]{:S(2)}) collective-permute-start(bf16[80,3584]{1,0:T(8,128)(2,1)S(1)} %pad_maximum_fusion.5), channel_id=1, source_target_pairs={{0,16},{8,24},{16,0},{24,8},{1,17},{9,25},{17,1},{25,9},{2,18},{10... | collective-permute-start | bytes 1720328 | tf_op jit(solution)/shard_map/ppermute | solution.py:32
  36.2 15.8 %collective-permute-start.5 = (bf16[80,3584]{1,0:T(8,128)(2,1)S(1)}, bf16[80,3584]{1,0:T(8,128)(2,1)S(1)}, u32[]{:S(2)}, u32[]{:S(2)}) collective-permute-start(bf16[80,3584]{1,0:T(8,128)(2,1)S(1)} %pad_maximum_fusion.4), channel_id=1, source_target_pairs={{0,8},{8,0},{16,24},{24,16},{1,9},{9,1},{17,25},{25,17},{2,10},{10... | collective-permute-start | bytes 1720328 | tf_op jit(solution)/shard_map/ppermute | solution.py:32
  39.4 15.1 %collective-permute-start.20 = (bf16[80,896]{1,0:T(8,128)(2,1)S(1)}, bf16[80,896]{1,0:T(8,128)(2,1)S(1)}, u32[]{:S(2)}, u32[]{:S(2)}) collective-permute-start(bf16[80,896]{1,0:T(8,128)(2,1)S(1)} %get-tuple-element.60), channel_id=1, source_target_pairs={{0,16},{8,24},{16,0},{24,8},{1,17},{9,25},{17,1},{25,9},{2,18},{10... | collective-permute-start | bytes 430088 | tf_op jit(solution)/shard_map/ppermute | solution.py:32
  40.1 14.4 %collective-permute-start.19 = (bf16[80,896]{1,0:T(8,128)(2,1)S(1)}, bf16[80,896]{1,0:T(8,128)(2,1)S(1)}, u32[]{:S(2)}, u32[]{:S(2)}) collective-permute-start(bf16[80,896]{1,0:T(8,128)(2,1)S(1)} %get-tuple-element.61), channel_id=1, source_target_pairs={{0,8},{8,0},{16,24},{24,16},{1,9},{9,1},{17,25},{25,17},{2,10},{10... | collective-permute-start | bytes 430088 | tf_op jit(solution)/shard_map/ppermute | solution.py:32
  52.3 9.8 %collective-permute-start.9 = (bf16[80,1792]{1,0:T(8,128)(2,1)S(1)}, bf16[80,1792]{1,0:T(8,128)(2,1)S(1)}, u32[]{:S(2)}, u32[]{:S(2)}) collective-permute-start(bf16[80,1792]{1,0:T(8,128)(2,1)S(1)} %multiply_convert_fusion.2), channel_id=1, source_target_pairs={{0,16},{8,24},{16,0},{24,8},{1,17},{9,25},{17,1},{25,9},{2,18},{10... | collective-permute-start | bytes 860168 | tf_op jit(solution)/shard_map/ppermute | solution.py:32
  53.0 10.7 %collective-permute-start.8 = (bf16[80,1792]{1,0:T(8,128)(2,1)S(1)}, bf16[80,1792]{1,0:T(8,128)(2,1)S(1)}, u32[]{:S(2)}, u32[]{:S(2)}) collective-permute-start(bf16[80,1792]{1,0:T(8,128)(2,1)S(1)} %multiply_convert_fusion.2), channel_id=1, source_target_pairs={{0,8},{8,0},{16,24},{24,16},{1,9},{9,1},{17,25},{25,17},{2,10},{10... | collective-permute-start | bytes 860168 | tf_op jit(solution)/shard_map/ppermute | solution.py:32
  54.8 12.7 %collective-permute-start.22 = (bf16[80,1792]{1,0:T(8,128)(2,1)S(1)}, bf16[80,1792]{1,0:T(8,128)(2,1)S(1)}, u32[]{:S(2)}, u32[]{:S(2)}) collective-permute-start(bf16[80,1792]{1,0:T(8,128)(2,1)S(1)} %pad_maximum_fusion.10), channel_id=1, source_target_pairs={{0,16},{8,24},{16,0},{24,8},{1,17},{9,25},{17,1},{25,9},{2,18},{10... | collective-permute-start | bytes 860168 | tf_op jit(solution)/shard_map/ppermute | solution.py:32
  56.2 11.9 %collective-permute-start.21 = (bf16[80,1792]{1,0:T(8,128)(2,1)S(1)}, bf16[80,1792]{1,0:T(8,128)(2,1)S(1)}, u32[]{:S(2)}, u32[]{:S(2)}) collective-permute-start(bf16[80,1792]{1,0:T(8,128)(2,1)S(1)} %pad_maximum_fusion.9), channel_id=1, source_target_pairs={{0,8},{8,0},{16,24},{24,16},{1,9},{9,1},{17,25},{25,17},{2,10},{10... | collective-permute-start | bytes 860168 | tf_op jit(solution)/shard_map/ppermute | solution.py:32
  62.2 9.2 %collective-permute-start.10 = (bf16[80,896]{1,0:T(8,128)(2,1)S(1)}, bf16[80,896]{1,0:T(8,128)(2,1)S(1)}, u32[]{:S(2)}, u32[]{:S(2)}) collective-permute-start(bf16[80,896]{1,0:T(8,128)(2,1)S(1)} %get-tuple-element.104), channel_id=1, source_target_pairs={{0,8},{8,0},{16,24},{24,16},{1,9},{9,1},{17,25},{25,17},{2,10},{10... | collective-permute-start | bytes 430088 | tf_op jit(solution)/shard_map/ppermute | solution.py:32
  63.7 7.7 %collective-permute-start.11 = (bf16[80,896]{1,0:T(8,128)(2,1)S(1)}, bf16[80,896]{1,0:T(8,128)(2,1)S(1)}, u32[]{:S(2)}, u32[]{:S(2)}) collective-permute-start(bf16[80,896]{1,0:T(8,128)(2,1)S(1)} %get-tuple-element.103), channel_id=1, source_target_pairs={{0,16},{8,24},{16,0},{24,8},{1,17},{9,25},{17,1},{25,9},{2,18},{10... | collective-permute-start | bytes 430088 | tf_op jit(solution)/shard_map/ppermute | solution.py:32
  68.8 12.8 %collective-permute-start.24 = (bf16[80,3584]{1,0:T(8,128)(2,1)S(1)}, bf16[80,3584]{1,0:T(8,128)(2,1)S(1)}, u32[]{:S(2)}, u32[]{:S(2)}) collective-permute-start(bf16[80,3584]{1,0:T(8,128)(2,1)S(1)} %pad_maximum_fusion.6), channel_id=1, source_target_pairs={{0,16},{8,24},{16,0},{24,8},{1,17},{9,25},{17,1},{25,9},{2,18},{10... | collective-permute-start | bytes 1720328 | tf_op jit(solution)/shard_map/ppermute | solution.py:32
  69.9 12.1 %collective-permute-start.23 = (bf16[80,3584]{1,0:T(8,128)(2,1)S(1)}, bf16[80,3584]{1,0:T(8,128)(2,1)S(1)}, u32[]{:S(2)}, u32[]{:S(2)}) collective-permute-start(bf16[80,3584]{1,0:T(8,128)(2,1)S(1)} %pad_maximum_fusion.6), channel_id=1, source_target_pairs={{0,8},{8,0},{16,24},{24,16},{1,9},{9,1},{17,25},{25,17},{2,10},{10... | collective-permute-start | bytes 1720328 | tf_op jit(solution)/shard_map/ppermute | solution.py:32
  72.9 17.3 %collective-permute-start.14 = (bf16[80,1024]{1,0:T(8,128)(2,1)S(1)}, bf16[80,1024]{1,0:T(8,128)(2,1)S(1)}, u32[]{:S(2)}, u32[]{:S(2)}) collective-permute-start(bf16[80,1024]{1,0:T(8,128)(2,1)S(1)} %get-tuple-element.80), channel_id=1, source_target_pairs={{0,6},{1,7},{2,4},{3,5},{4,2},{5,3},{6,0},{7,1},{8,14},{9,15},{10,... | collective-permute-start | bytes 491528 | tf_op jit(solution)/shard_map/ppermute | solution.py:32
  76.1 14.1 %collective-permute-start.13 = (bf16[80,1024]{1,0:T(8,128)(2,1)S(1)}, bf16[80,1024]{1,0:T(8,128)(2,1)S(1)}, u32[]{:S(2)}, u32[]{:S(2)}) collective-permute-start(bf16[80,1024]{1,0:T(8,128)(2,1)S(1)} %get-tuple-element.81), channel_id=1, source_target_pairs={{0,4},{1,5},{2,6},{3,7},{4,0},{5,1},{6,2},{7,3},{8,12},{9,13},{10,... | collective-permute-start | bytes 491528 | tf_op jit(solution)/shard_map/ppermute | solution.py:32
  78.3 11.8 %collective-permute-start.12 = (bf16[80,1024]{1,0:T(8,128)(2,1)S(1)}, bf16[80,1024]{1,0:T(8,128)(2,1)S(1)}, u32[]{:S(2)}, u32[]{:S(2)}) collective-permute-start(bf16[80,1024]{1,0:T(8,128)(2,1)S(1)} %get-tuple-element.82), channel_id=1, source_target_pairs={{0,2},{1,3},{2,0},{3,1},{4,6},{5,7},{6,4},{7,5},{8,10},{9,11},{10,... | collective-permute-start | bytes 491528 | tf_op jit(solution)/shard_map/ppermute | solution.py:32
  82.0 7.0 %collective-permute-start.26 = (bf16[80,1792]{1,0:T(8,128)(2,1)S(1)}, bf16[80,1792]{1,0:T(8,128)(2,1)S(1)}, u32[]{:S(2)}, u32[]{:S(2)}) collective-permute-start(bf16[80,1792]{1,0:T(8,128)(2,1)S(1)} %get-tuple-element.94), channel_id=1, source_target_pairs={{0,16},{8,24},{16,0},{24,8},{1,17},{9,25},{17,1},{25,9},{2,18},{10... | collective-permute-start | bytes 860168 | tf_op jit(solution)/shard_map/ppermute | solution.py:32
  (10 other events, 31.8 us)

commit v12 on v11

--- a/solution.py
+++ b/solution.py
@@ -243,7 +243,7 @@
     ).astype(BF)
     if near:
         in_rows = to_chips(*pair_core(send_rows))
-        cot_send, in_rows[2] = after((cot_send, in_rows[2]))
+        cot_send, in_rows[1] = after((cot_send, in_rows[1]))
         cot_rows = to_chips_first(cot_send)
     else:
         in_rows = [all_to_all(send_rows, experts)]

time: 98.4 us -> 104 us (1.057)
  the two profiles are of different devices: /device:TPU:0 before, /device:TPU:19 now
where the time goes in v12:
time: 104 us
  waiting for transfers between devices  51.5 us (50%)
  starting transfers between devices  30.1 us (29%)
  matrix products  12.3 us (12%)
  Pallas kernels  4.96 us (5%)
  other arithmetic  2.75 us (3%)
  local copies, waits for them, and re-layouts  1.41 us (1%)
  between operations  1.24 us (1%)
    ppermute x28, waiting for transfers between devices, swap(): return lax.ppermute(block, axis, [(i, i ^ mask) for i in range(count)])  51.5 us
    ppermute x28, starting transfers between devices, swap(): return lax.ppermute(block, axis, [(i, i ^ mask) for i in range(count)])  30.1 us
    pallas_call x1, Pallas kernels, two_terms(): pl.pallas_call(kernel, in_specs=[whole, whole, whole], out_specs=[anywher...  4.96 us
    dot_general x3, matrix products, partial_product(): lax.dot_general(rows, weights, CONTRACT_FEATS, preferred_element_type=F32)  4.21 us
    dot_general x1, matrix products, term(): lax.dot_general(left, right, CONTRACT_ROWS, preferred_element_type=F32)  4.11 us
  transfers between devices with their start and end apart: 28, of which 15 were waited for; matrix products, arithmetic and copies ran while one was open for 13% of the time, Pallas kernels for 5%

profile of v12, /device:TPU:19, one launch (start us, length us, event | category | flops | bytes accessed | tf_op | source)
XLA Modules:
  0.0 104.3 jit_solution(7935942995553192740)
XLA Ops:
  4.1 1.4 %collective-permute-start.1 = (bf16[80,1024]{1,0:T(8,128)(2,1)S(1)}, bf16[80,1024]{1,0:T(8,128)(2,1)S(1)}, u32[]{:S(2)}, u32[]{:S(2)}) collective-permute-start(bf16[80,1024]{1,0:T(8,128)(2,1)S(1)} %pad_maximum_fusion.11), channel_id=1, source_target_pairs={{0,2},{1,3},{2,0},{3,1},{4,6},{5,7},{6,4},{7,5},{8,10},{9,11},{10,... | collective-permute-start | bytes 491528 | tf_op jit(solution)/shard_map/ppermute | solution.py:32
  5.6 1.4 %collective-permute-start.3 = (bf16[80,1024]{1,0:T(8,128)(2,1)S(1)}, bf16[80,1024]{1,0:T(8,128)(2,1)S(1)}, u32[]{:S(2)}, u32[]{:S(2)}) collective-permute-start(bf16[80,1024]{1,0:T(8,128)(2,1)S(1)} %pad_maximum_fusion.13), channel_id=1, source_target_pairs={{0,6},{1,7},{2,4},{3,5},{4,2},{5,3},{6,0},{7,1},{8,14},{9,15},{10,... | collective-permute-start | bytes 491528 | tf_op jit(solution)/shard_map/ppermute | solution.py:32
  7.0 3.7 %collective-permute-done.1 = bf16[80,1024]{1,0:T(8,128)(2,1)S(1)} collective-permute-done((bf16[80,1024]{1,0:T(8,128)(2,1)S(1)}, bf16[80,1024]{1,0:T(8,128)(2,1)S(1)}, u32[]{:S(2)}, u32[]{:S(2)}) %collective-permute-start.1) | collective-permute-done | bytes 163872 | tf_op jit(solution)/shard_map/ppermute | solution.py:32
  10.8 2.4 %collective-permute-start.15 = (bf16[80,1024]{1,0:T(8,128)(2,1)S(1)}, bf16[80,1024]{1,0:T(8,128)(2,1)S(1)}, u32[]{:S(2)}, u32[]{:S(2)}) collective-permute-start(bf16[80,1024]{1,0:T(8,128)(2,1)S(1)} %pad_maximum_fusion.15), channel_id=1, source_target_pairs={{0,2},{1,3},{2,0},{3,1},{4,6},{5,7},{6,4},{7,5},{8,10},{9,11},{10,... | collective-permute-start | bytes 491528 | tf_op jit(solution)/shard_map/ppermute | solution.py:32
  13.3 1.2 %collective-permute-start.17 = (bf16[80,1024]{1,0:T(8,128)(2,1)S(1)}, bf16[80,1024]{1,0:T(8,128)(2,1)S(1)}, u32[]{:S(2)}, u32[]{:S(2)}) collective-permute-start(bf16[80,1024]{1,0:T(8,128)(2,1)S(1)} %pad_maximum_fusion.17), channel_id=1, source_target_pairs={{0,6},{1,7},{2,4},{3,5},{4,2},{5,3},{6,0},{7,1},{8,14},{9,15},{10,... | collective-permute-start | bytes 491528 | tf_op jit(solution)/shard_map/ppermute | solution.py:32
  14.6 13.6 %collective-permute-done.3 = bf16[80,1024]{1,0:T(8,128)(2,1)S(1)} collective-permute-done((bf16[80,1024]{1,0:T(8,128)(2,1)S(1)}, bf16[80,1024]{1,0:T(8,128)(2,1)S(1)}, u32[]{:S(2)}, u32[]{:S(2)}) %collective-permute-start.3) | collective-permute-done | bytes 163872 | tf_op jit(solution)/shard_map/ppermute | solution.py:32
  28.3 1.4 %convolution_convert_fusion.3 = bf16[320,1792]{1,0:T(8,128)(2,1)S(1)} fusion(bf16[1792,1024]{1,0:T(8,128)(2,1)S(1)} %copy-done.3, bf16[80,1024]{1,0:T(8,128)(2,1)S(1)} %get-tuple-element.85, bf16[80,1024]{1,0:T(8,128)(2,1)S(1)} %get-tuple-element.86, bf16[80,1024]{1,0:T(8,128)(2,1)S(1)} %get-tuple-element.87, bf16[80,1024]{1,0:T(8,128)(2,1)S(1)} %get-tuple-element.84), kind=kOutput, calls=%fused_computation.3 | convolution fusion | flops 1177600000 | bytes 5472256 | tf_op jit(solution)/shard_map/dot_general | solution.py:261
  30.4 1.4 %convolution_convert_fusion.2 = bf16[320,1792]{1,0:T(8,128)(2,1)S(1)} fusion(bf16[1792,1024]{1,0:T(8,128)(2,1)S(1)} %copy-done.4, bf16[80,1024]{1,0:T(8,128)(2,1)S(1)} %get-tuple-element.85, bf16[80,1024]{1,0:T(8,128)(2,1)S(1)} %get-tuple-element.86, bf16[80,1024]{1,0:T(8,128)(2,1)S(1)} %get-tuple-element.87, bf16[80,1024]{1,0:T(8,128)(2,1)S(1)} %get-tuple-element.84), kind=kOutput, calls=%fused_computation.2 | convolution fusion | flops 1177600000 | bytes 5472256 | tf_op jit(solution)/shard_map/dot_general | solution.py:261
  31.8 1.3 %collective-permute-start.4 = (bf16[80,1792]{1,0:T(8,128)(2,1)S(1)}, bf16[80,1792]{1,0:T(8,128)(2,1)S(1)}, u32[]{:S(2)}, u32[]{:S(2)}) collective-permute-start(bf16[80,1792]{1,0:T(8,128)(2,1)S(1)} %get-tuple-element.66), channel_id=1, source_target_pairs={{0,16},{8,24},{16,0},{24,8},{1,17},{9,25},{17,1},{25,9},{2,18},{10... | collective-permute-start | bytes 860168 | tf_op jit(solution)/shard_map/ppermute | solution.py:32
  33.6 3.8 %collective-permute-done.4 = bf16[80,1792]{1,0:T(8,128)(2,1)S(1)} collective-permute-done((bf16[80,1792]{1,0:T(8,128)(2,1)S(1)}, bf16[80,1792]{1,0:T(8,128)(2,1)S(1)}, u32[]{:S(2)}, u32[]{:S(2)}) %collective-permute-start.4) | collective-permute-done | bytes 286752 | tf_op jit(solution)/shard_map/ppermute | solution.py:32
  37.5 1.5 %collective-permute-done.6 = bf16[80,1792]{1,0:T(8,128)(2,1)S(1)} collective-permute-done((bf16[80,1792]{1,0:T(8,128)(2,1)S(1)}, bf16[80,1792]{1,0:T(8,128)(2,1)S(1)}, u32[]{:S(2)}, u32[]{:S(2)}) %collective-permute-start.6) | collective-permute-done | bytes 286752 | tf_op jit(solution)/shard_map/ppermute | solution.py:32
  39.3 3.8 %collective-permute-start.18 = (bf16[160,1024]{1,0:T(8,128)(2,1)S(1)}, bf16[160,1024]{1,0:T(8,128)(2,1)S(1)}, u32[]{:S(2)}, u32[]{:S(2)}) collective-permute-start(bf16[160,1024]{1,0:T(8,128)(2,1)S(1)} %pad_maximum_fusion.7), channel_id=1, source_target_pairs={{0,1},{1,0},{2,3},{3,2},{4,5},{5,4},{6,7},{7,6},{8,9},{9,8},{10,11... | collective-permute-start | bytes 983048 | tf_op jit(solution)/shard_map/ppermute | solution.py:32
  44.5 1.4 %convolution_convert_fusion.1 = bf16[320,1792]{1,0:T(8,128)(2,1)S(1)} fusion(bf16[1792,1024]{1,0:T(8,128)(2,1)S(1)} %copy-done.5, bf16[80,1024]{1,0:T(8,128)(2,1)S(1)} %get-tuple-element.69, bf16[80,1024]{1,0:T(8,128)(2,1)S(1)} %get-tuple-element.70, bf16[80,1024]{1,0:T(8,128)(2,1)S(1)} %get-tuple-element.71, bf16[80,1024]{1,0:T(8,128)(2,1)S(1)} %get-tuple-element.68), kind=kOutput, calls=%fused_computation.1 | convolution fusion | flops 1177600000 | bytes 5472256 | tf_op jit(solution)/shard_map/dot_general | solution.py:261
  46.7 1.2 %collective-permute-start.19 = (bf16[80,896]{1,0:T(8,128)(2,1)S(1)}, bf16[80,896]{1,0:T(8,128)(2,1)S(1)}, u32[]{:S(2)}, u32[]{:S(2)}) collective-permute-start(bf16[80,896]{1,0:T(8,128)(2,1)S(1)} %get-tuple-element.61), channel_id=1, source_target_pairs={{0,8},{8,0},{16,24},{24,16},{1,9},{9,1},{17,25},{25,17},{2,10},{10... | collective-permute-start | bytes 430088 | tf_op jit(solution)/shard_map/ppermute | solution.py:32
  47.9 9.8 %collective-permute-done.7 = bf16[80,3584]{1,0:T(8,128)(2,1)S(1)} collective-permute-done((bf16[80,3584]{1,0:T(8,128)(2,1)S(1)}, bf16[80,3584]{1,0:T(8,128)(2,1)S(1)}, u32[]{:S(2)}, u32[]{:S(2)}) %collective-permute-start.7) | collective-permute-done | bytes 573472 | tf_op jit(solution)/shard_map/ppermute | solution.py:32
  59.6 1.2 %collective-permute-done.20 = bf16[80,896]{1,0:T(8,128)(2,1)S(1)} collective-permute-done((bf16[80,896]{1,0:T(8,128)(2,1)S(1)}, bf16[80,896]{1,0:T(8,128)(2,1)S(1)}, u32[]{:S(2)}, u32[]{:S(2)}) %collective-permute-start.20) | collective-permute-done | bytes 143392 | tf_op jit(solution)/shard_map/ppermute | solution.py:32
  62.6 2.9 %collective-permute-done.9 = bf16[80,1792]{1,0:T(8,128)(2,1)S(1)} collective-permute-done((bf16[80,1792]{1,0:T(8,128)(2,1)S(1)}, bf16[80,1792]{1,0:T(8,128)(2,1)S(1)}, u32[]{:S(2)}, u32[]{:S(2)}) %collective-permute-start.9) | collective-permute-done | bytes 286752 | tf_op jit(solution)/shard_map/ppermute | solution.py:32
  66.8 4.9 %collective-permute-done.22 = bf16[80,1792]{1,0:T(8,128)(2,1)S(1)} collective-permute-done((bf16[80,1792]{1,0:T(8,128)(2,1)S(1)}, bf16[80,1792]{1,0:T(8,128)(2,1)S(1)}, u32[]{:S(2)}, u32[]{:S(2)}) %collective-permute-start.22) | collective-permute-done | bytes 286752 | tf_op jit(solution)/shard_map/ppermute | solution.py:32
  74.7 1.4 %convolution_convert_fusion.5 = bf16[320,1024]{1,0:T(8,128)(2,1)S(1)} fusion(bf16[1792,1024]{1,0:T(8,128)(2,1)S(1)} %copy-done.5, bf16[80,896]{1,0:T(8,128)(2,1)S(1)} %collective-permute-done.11, bf16[80,896]{1,0:T(8,128)(2,1)S(1)} %get-tuple-element.105, bf16[80,896]{1,0:T(8,128)(2,1)S(1)} %get-tuple-element.103, ...), kind=kOutput, calls=%fused_computation.7 | convolution fusion | flops 1183907840 | bytes 5472256 | tf_op jit(solution)/shard_map/dot_general | solution.py:283
  76.5 2.5 %collective-permute-start.12 = (bf16[80,1024]{1,0:T(8,128)(2,1)S(1)}, bf16[80,1024]{1,0:T(8,128)(2,1)S(1)}, u32[]{:S(2)}, u32[]{:S(2)}) collective-permute-start(bf16[80,1024]{1,0:T(8,128)(2,1)S(1)} %get-tuple-element.82), channel_id=1, source_target_pairs={{0,2},{1,3},{2,0},{3,1},{4,6},{5,7},{6,4},{7,5},{8,10},{9,11},{10,... | collective-permute-start | bytes 491528 | tf_op jit(solution)/shard_map/ppermute | solution.py:32
  79.0 6.3 %collective-permute-done.24 = bf16[80,3584]{1,0:T(8,128)(2,1)S(1)} collective-permute-done((bf16[80,3584]{1,0:T(8,128)(2,1)S(1)}, bf16[80,3584]{1,0:T(8,128)(2,1)S(1)}, u32[]{:S(2)}, u32[]{:S(2)}) %collective-permute-start.24) | collective-permute-done | bytes 573472 | tf_op jit(solution)/shard_map/ppermute | solution.py:32
  87.0 4.1 %convolution_convert_fusion = bf16[1792,1024]{1,0:T(8,128)(2,1)} fusion(bf16[320,1792]{1,0:T(8,128)(2,1)S(1)} %maximum_maximum_fusion, bf16[80,1024]{1,0:T(8,128)(2,1)S(1)} %get-tuple-element.69, bf16[80,1024]{1,0:T(8,128)(2,1)S(1)} %get-tuple-element.70, bf16[80,1024]{1,0:T(8,128)(2,1)S(1)} %get-tuple-element.71, bf16[80,1024]{1,0:T(8,128)(2,1)S(1)} %get-tuple-element.68), kind=kOutput, calls=%fused_computation | convolution fusion | flops 1178861568 | bytes 5472256 | tf_op jit(solution)/shard_map/dot_general | solution.py:298
  92.7 5.5 %collective-permute-start.27 = (bf16[160,1024]{1,0:T(8,128)(2,1)S(1)}, bf16[160,1024]{1,0:T(8,128)(2,1)S(1)}, u32[]{:S(2)}, u32[]{:S(2)}) collective-permute-start(bf16[160,1024]{1,0:T(8,128)(2,1)S(1)} %pad_maximum_fusion.8), channel_id=1, source_target_pairs={{0,1},{1,0},{2,3},{3,2},{4,5},{5,4},{6,7},{7,6},{8,9},{9,8},{10,11... | collective-permute-start | bytes 983048 | tf_op jit(solution)/shard_map/ppermute | solution.py:32
  98.2 5.0 %shard_map.102 = (bf16[1792,1024]{1,0:T(8,128)(2,1)}, bf16[1792,1024]{1,0:T(8,128)(2,1)}) custom-call(bf16[320,1792]{1,0:T(8,128)(2,1)S(1)} %pad_maximum_fusion.first_ref, bf16[320,1792]{1,0:T(8,128)(2,1)S(1)} %pad_maximum_fusion.1.second_ref, bf16[320,1024]{1,0:T(8,128)(2,1)S(1)} %pad_maximum_fusion.2.rows_ref), custom_call_target="tpu_custom_call" | custom-call | flops 9395240960 | bytes 38535168 | tf_op jit(solution)/shard_map/pallas_call | solution.py:182
  (121 shorter events, 19.9 us)
Async XLA Ops:
  4.1 6.6 %collective-permute-start.1 = (bf16[80,1024]{1,0:T(8,128)(2,1)S(1)}, bf16[80,1024]{1,0:T(8,128)(2,1)S(1)}, u32[]{:S(2)}, u32[]{:S(2)}) collective-permute-start(bf16[80,1024]{1,0:T(8,128)(2,1)S(1)} %pad_maximum_fusion.11), channel_id=1, source_target_pairs={{0,2},{1,3},{2,0},{3,1},{4,6},{5,7},{6,4},{7,5},{8,10},{9,11},{10,... | collective-permute-start | bytes 491528 | tf_op jit(solution)/shard_map/ppermute | solution.py:32
  5.5 9.1 %collective-permute-start.2 = (bf16[80,1024]{1,0:T(8,128)(2,1)S(1)}, bf16[80,1024]{1,0:T(8,128)(2,1)S(1)}, u32[]{:S(2)}, u32[]{:S(2)}) collective-permute-start(bf16[80,1024]{1,0:T(8,128)(2,1)S(1)} %pad_maximum_fusion.12), channel_id=1, source_target_pairs={{0,4},{1,5},{2,6},{3,7},{4,0},{5,1},{6,2},{7,3},{8,12},{9,13},{10,... | collective-permute-start | bytes 491528 | tf_op jit(solution)/shard_map/ppermute | solution.py:32
  5.6 22.6 %collective-permute-start.3 = (bf16[80,1024]{1,0:T(8,128)(2,1)S(1)}, bf16[80,1024]{1,0:T(8,128)(2,1)S(1)}, u32[]{:S(2)}, u32[]{:S(2)}) collective-permute-start(bf16[80,1024]{1,0:T(8,128)(2,1)S(1)} %pad_maximum_fusion.13), channel_id=1, source_target_pairs={{0,6},{1,7},{2,4},{3,5},{4,2},{5,3},{6,0},{7,1},{8,14},{9,15},{10,... | collective-permute-start | bytes 491528 | tf_op jit(solution)/shard_map/ppermute | solution.py:32
  10.8 28.4 %collective-permute-start.15 = (bf16[80,1024]{1,0:T(8,128)(2,1)S(1)}, bf16[80,1024]{1,0:T(8,128)(2,1)S(1)}, u32[]{:S(2)}, u32[]{:S(2)}) collective-permute-start(bf16[80,1024]{1,0:T(8,128)(2,1)S(1)} %pad_maximum_fusion.15), channel_id=1, source_target_pairs={{0,2},{1,3},{2,0},{3,1},{4,6},{5,7},{6,4},{7,5},{8,10},{9,11},{10,... | collective-permute-start | bytes 491528 | tf_op jit(solution)/shard_map/ppermute | solution.py:32
  13.2 25.9 %collective-permute-start.16 = (bf16[80,1024]{1,0:T(8,128)(2,1)S(1)}, bf16[80,1024]{1,0:T(8,128)(2,1)S(1)}, u32[]{:S(2)}, u32[]{:S(2)}) collective-permute-start(bf16[80,1024]{1,0:T(8,128)(2,1)S(1)} %pad_maximum_fusion.16), channel_id=1, source_target_pairs={{0,4},{1,5},{2,6},{3,7},{4,0},{5,1},{6,2},{7,3},{8,12},{9,13},{10,... | collective-permute-start | bytes 491528 | tf_op jit(solution)/shard_map/ppermute | solution.py:32
  13.3 25.9 %collective-permute-start.17 = (bf16[80,1024]{1,0:T(8,128)(2,1)S(1)}, bf16[80,1024]{1,0:T(8,128)(2,1)S(1)}, u32[]{:S(2)}, u32[]{:S(2)}) collective-permute-start(bf16[80,1024]{1,0:T(8,128)(2,1)S(1)} %pad_maximum_fusion.17), channel_id=1, source_target_pairs={{0,6},{1,7},{2,4},{3,5},{4,2},{5,3},{6,0},{7,1},{8,14},{9,15},{10,... | collective-permute-start | bytes 491528 | tf_op jit(solution)/shard_map/ppermute | solution.py:32
  33.2 5.8 %collective-permute-start.6 = (bf16[80,1792]{1,0:T(8,128)(2,1)S(1)}, bf16[80,1792]{1,0:T(8,128)(2,1)S(1)}, u32[]{:S(2)}, u32[]{:S(2)}) collective-permute-start(bf16[80,1792]{1,0:T(8,128)(2,1)S(1)} %get-tuple-element.65), channel_id=1, source_target_pairs={{0,8},{8,0},{16,24},{24,16},{1,9},{9,1},{17,25},{25,17},{2,10},{10... | collective-permute-start | bytes 860168 | tf_op jit(solution)/shard_map/ppermute | solution.py:32
  43.1 14.7 %collective-permute-start.7 = (bf16[80,3584]{1,0:T(8,128)(2,1)S(1)}, bf16[80,3584]{1,0:T(8,128)(2,1)S(1)}, u32[]{:S(2)}, u32[]{:S(2)}) collective-permute-start(bf16[80,3584]{1,0:T(8,128)(2,1)S(1)} %pad_maximum_fusion.5), channel_id=1, source_target_pairs={{0,16},{8,24},{16,0},{24,8},{1,17},{9,25},{17,1},{25,9},{2,18},{10... | collective-permute-start | bytes 1720328 | tf_op jit(solution)/shard_map/ppermute | solution.py:32
  43.4 14.4 %collective-permute-start.5 = (bf16[80,3584]{1,0:T(8,128)(2,1)S(1)}, bf16[80,3584]{1,0:T(8,128)(2,1)S(1)}, u32[]{:S(2)}, u32[]{:S(2)}) collective-permute-start(bf16[80,3584]{1,0:T(8,128)(2,1)S(1)} %pad_maximum_fusion.4), channel_id=1, source_target_pairs={{0,8},{8,0},{16,24},{24,16},{1,9},{9,1},{17,25},{25,17},{2,10},{10... | collective-permute-start | bytes 1720328 | tf_op jit(solution)/shard_map/ppermute | solution.py:32
  45.9 14.9 %collective-permute-start.20 = (bf16[80,896]{1,0:T(8,128)(2,1)S(1)}, bf16[80,896]{1,0:T(8,128)(2,1)S(1)}, u32[]{:S(2)}, u32[]{:S(2)}) collective-permute-start(bf16[80,896]{1,0:T(8,128)(2,1)S(1)} %get-tuple-element.60), channel_id=1, source_target_pairs={{0,16},{8,24},{16,0},{24,8},{1,17},{9,25},{17,1},{25,9},{2,18},{10... | collective-permute-start | bytes 430088 | tf_op jit(solution)/shard_map/ppermute | solution.py:32
  46.7 14.1 %collective-permute-start.19 = (bf16[80,896]{1,0:T(8,128)(2,1)S(1)}, bf16[80,896]{1,0:T(8,128)(2,1)S(1)}, u32[]{:S(2)}, u32[]{:S(2)}) collective-permute-start(bf16[80,896]{1,0:T(8,128)(2,1)S(1)} %get-tuple-element.61), channel_id=1, source_target_pairs={{0,8},{8,0},{16,24},{24,16},{1,9},{9,1},{17,25},{25,17},{2,10},{10... | collective-permute-start | bytes 430088 | tf_op jit(solution)/shard_map/ppermute | solution.py:32
  58.1 7.4 %collective-permute-start.9 = (bf16[80,1792]{1,0:T(8,128)(2,1)S(1)}, bf16[80,1792]{1,0:T(8,128)(2,1)S(1)}, u32[]{:S(2)}, u32[]{:S(2)}) collective-permute-start(bf16[80,1792]{1,0:T(8,128)(2,1)S(1)} %multiply_convert_fusion.2), channel_id=1, source_target_pairs={{0,16},{8,24},{16,0},{24,8},{1,17},{9,25},{17,1},{25,9},{2,18},{10... | collective-permute-start | bytes 860168 | tf_op jit(solution)/shard_map/ppermute | solution.py:32
  59.3 6.5 %collective-permute-start.8 = (bf16[80,1792]{1,0:T(8,128)(2,1)S(1)}, bf16[80,1792]{1,0:T(8,128)(2,1)S(1)}, u32[]{:S(2)}, u32[]{:S(2)}) collective-permute-start(bf16[80,1792]{1,0:T(8,128)(2,1)S(1)} %multiply_convert_fusion.2), channel_id=1, source_target_pairs={{0,8},{8,0},{16,24},{24,16},{1,9},{9,1},{17,25},{25,17},{2,10},{10... | collective-permute-start | bytes 860168 | tf_op jit(solution)/shard_map/ppermute | solution.py:32
  61.1 10.6 %collective-permute-start.22 = (bf16[80,1792]{1,0:T(8,128)(2,1)S(1)}, bf16[80,1792]{1,0:T(8,128)(2,1)S(1)}, u32[]{:S(2)}, u32[]{:S(2)}) collective-permute-start(bf16[80,1792]{1,0:T(8,128)(2,1)S(1)} %pad_maximum_fusion.10), channel_id=1, source_target_pairs={{0,16},{8,24},{16,0},{24,8},{1,17},{9,25},{17,1},{25,9},{2,18},{10... | collective-permute-start | bytes 860168 | tf_op jit(solution)/shard_map/ppermute | solution.py:32
  62.3 9.4 %collective-permute-start.21 = (bf16[80,1792]{1,0:T(8,128)(2,1)S(1)}, bf16[80,1792]{1,0:T(8,128)(2,1)S(1)}, u32[]{:S(2)}, u32[]{:S(2)}) collective-permute-start(bf16[80,1792]{1,0:T(8,128)(2,1)S(1)} %pad_maximum_fusion.9), channel_id=1, source_target_pairs={{0,8},{8,0},{16,24},{24,16},{1,9},{9,1},{17,25},{25,17},{2,10},{10... | collective-permute-start | bytes 860168 | tf_op jit(solution)/shard_map/ppermute | solution.py:32
  65.5 9.2 %collective-permute-start.10 = (bf16[80,896]{1,0:T(8,128)(2,1)S(1)}, bf16[80,896]{1,0:T(8,128)(2,1)S(1)}, u32[]{:S(2)}, u32[]{:S(2)}) collective-permute-start(bf16[80,896]{1,0:T(8,128)(2,1)S(1)} %get-tuple-element.104), channel_id=1, source_target_pairs={{0,8},{8,0},{16,24},{24,16},{1,9},{9,1},{17,25},{25,17},{2,10},{10... | collective-permute-start | bytes 430088 | tf_op jit(solution)/shard_map/ppermute | solution.py:32
  65.8 8.9 %collective-permute-start.11 = (bf16[80,896]{1,0:T(8,128)(2,1)S(1)}, bf16[80,896]{1,0:T(8,128)(2,1)S(1)}, u32[]{:S(2)}, u32[]{:S(2)}) collective-permute-start(bf16[80,896]{1,0:T(8,128)(2,1)S(1)} %get-tuple-element.103), channel_id=1, source_target_pairs={{0,16},{8,24},{16,0},{24,8},{1,17},{9,25},{17,1},{25,9},{2,18},{10... | collective-permute-start | bytes 430088 | tf_op jit(solution)/shard_map/ppermute | solution.py:32
  72.3 13.0 %collective-permute-start.24 = (bf16[80,3584]{1,0:T(8,128)(2,1)S(1)}, bf16[80,3584]{1,0:T(8,128)(2,1)S(1)}, u32[]{:S(2)}, u32[]{:S(2)}) collective-permute-start(bf16[80,3584]{1,0:T(8,128)(2,1)S(1)} %pad_maximum_fusion.6), channel_id=1, source_target_pairs={{0,16},{8,24},{16,0},{24,8},{1,17},{9,25},{17,1},{25,9},{2,18},{10... | collective-permute-start | bytes 1720328 | tf_op jit(solution)/shard_map/ppermute | solution.py:32
  73.5 12.4 %collective-permute-start.23 = (bf16[80,3584]{1,0:T(8,128)(2,1)S(1)}, bf16[80,3584]{1,0:T(8,128)(2,1)S(1)}, u32[]{:S(2)}, u32[]{:S(2)}) collective-permute-start(bf16[80,3584]{1,0:T(8,128)(2,1)S(1)} %pad_maximum_fusion.6), channel_id=1, source_target_pairs={{0,8},{8,0},{16,24},{24,16},{1,9},{9,1},{17,25},{25,17},{2,10},{10... | collective-permute-start | bytes 1720328 | tf_op jit(solution)/shard_map/ppermute | solution.py:32
  76.2 16.3 %collective-permute-start.14 = (bf16[80,1024]{1,0:T(8,128)(2,1)S(1)}, bf16[80,1024]{1,0:T(8,128)(2,1)S(1)}, u32[]{:S(2)}, u32[]{:S(2)}) collective-permute-start(bf16[80,1024]{1,0:T(8,128)(2,1)S(1)} %get-tuple-element.80), channel_id=1, source_target_pairs={{0,6},{1,7},{2,4},{3,5},{4,2},{5,3},{6,0},{7,1},{8,14},{9,15},{10,... | collective-permute-start | bytes 491528 | tf_op jit(solution)/shard_map/ppermute | solution.py:32
  76.4 16.1 %collective-permute-start.13 = (bf16[80,1024]{1,0:T(8,128)(2,1)S(1)}, bf16[80,1024]{1,0:T(8,128)(2,1)S(1)}, u32[]{:S(2)}, u32[]{:S(2)}) collective-permute-start(bf16[80,1024]{1,0:T(8,128)(2,1)S(1)} %get-tuple-element.81), channel_id=1, source_target_pairs={{0,4},{1,5},{2,6},{3,7},{4,0},{5,1},{6,2},{7,3},{8,12},{9,13},{10,... | collective-permute-start | bytes 491528 | tf_op jit(solution)/shard_map/ppermute | solution.py:32
  76.5 16.1 %collective-permute-start.12 = (bf16[80,1024]{1,0:T(8,128)(2,1)S(1)}, bf16[80,1024]{1,0:T(8,128)(2,1)S(1)}, u32[]{:S(2)}, u32[]{:S(2)}) collective-permute-start(bf16[80,1024]{1,0:T(8,128)(2,1)S(1)} %get-tuple-element.82), channel_id=1, source_target_pairs={{0,2},{1,3},{2,0},{3,1},{4,6},{5,7},{6,4},{7,5},{8,10},{9,11},{10,... | collective-permute-start | bytes 491528 | tf_op jit(solution)/shard_map/ppermute | solution.py:32
  86.6 5.8 %collective-permute-start.25 = (bf16[80,1792]{1,0:T(8,128)(2,1)S(1)}, bf16[80,1792]{1,0:T(8,128)(2,1)S(1)}, u32[]{:S(2)}, u32[]{:S(2)}) collective-permute-start(bf16[80,1792]{1,0:T(8,128)(2,1)S(1)} %get-tuple-element.93), channel_id=1, source_target_pairs={{0,8},{8,0},{16,24},{24,16},{1,9},{9,1},{17,25},{25,17},{2,10},{10... | collective-permute-start | bytes 860168 | tf_op jit(solution)/shard_map/ppermute | solution.py:32
  92.7 10.5 %collective-permute-start.27 = (bf16[160,1024]{1,0:T(8,128)(2,1)S(1)}, bf16[160,1024]{1,0:T(8,128)(2,1)S(1)}, u32[]{:S(2)}, u32[]{:S(2)}) collective-permute-start(bf16[160,1024]{1,0:T(8,128)(2,1)S(1)} %pad_maximum_fusion.8), channel_id=1, source_target_pairs={{0,1},{1,0},{2,3},{3,2},{4,5},{5,4},{6,7},{7,6},{8,9},{9,8},{10,11... | collective-permute-start | bytes 983048 | tf_op jit(solution)/shard_map/ppermute | solution.py:32
  (10 other events, 48.4 us)
